TPU v7x, 256 devices: a whole 4x4x8 slice. The times are simulated.
256 devices in a mesh: seq: 16 (over z, y_lo), mp: 16 (over x, y_hi, core).
Axes of the slice: x: 4, y: 4 (y_hi: 2, y_lo: 2; y = y_hi * 2 + y_lo), z: 8, core: 2. Of those that a mesh axis runs over, the one named last changes fastest.
Arguments:
- stream: bfloat16 [32768, 4096], P(('seq', 'mp')), may hold values from -6 to 6
- doc_start: int32 [32768], P(('seq', 'mp')), may hold values 0 or 1
- norm_gain: float32 [4096], replicated, may hold values from 0.1 to 1.9
- weight_in: bfloat16 [4096, 7168], P('seq', 'mp'), may hold values from -0.09375 to 0.09375
- weight_out: bfloat16 [7168, 4096], P('mp', 'seq'), may hold values from -0.0625 to 0.0625
- upstream: bfloat16 [32768, 4096], P(('seq', 'mp')), may hold values from -24 to 24
Outputs:
- mixed_stream: bfloat16 [32768, 4096], P(('seq', 'mp'))
- grad_stream: bfloat16 [32768, 4096], P(('seq', 'mp'))
- grad_gain: float32 [4096], replicated
- grad_weight_in: float32 [4096, 7168], P('seq', 'mp')
- grad_weight_out: float32 [7168, 4096], P('mp', 'seq')
All inputs are finite; a program needn't handle non-finite values. No bound on the sum of `doc_start` on one device may be relied on, other than what follows from the above.
Results may differ from a plain program's by a relative error of at most 0.02.
Values may be sent and summed in bfloat16 or wider, within the bound.
No kernel may reach another device: no remote copies, remote signals or barrier semaphores. Data moves between devices by JAX's collectives and lax.ppermute only.
A program may use at most 128 MiB of HBM per device.

v0:
```python
import jax
import jax.numpy as jnp
from jax import lax
from jax.sharding import PartitionSpec as P


def from_behind(value, axis, by):
    peers = lax.axis_size(axis)
    pairs = [(i, i + by) for i in range(peers) if 0 <= i + by < peers]
    return lax.ppermute(value, axis, pairs)


def gelu_tanh(tensor):
    return jax.nn.gelu(tensor, approximate=True)


def contract(left, right, left_dim, right_dim):
    return lax.dot_general(
        left, right, (((left_dim,), (right_dim,)), ((), ())), preferred_element_type=jnp.float32
    )


def shards(stream, doc_start, norm_gain, weight_in, weight_out, upstream):
    tok_rows, feat_width = stream.shape
    groups = tok_rows // 4
    grouped = stream.reshape(groups, 4, feat_width).astype(jnp.float32)
    pooled = (jnp.sum(grouped, axis=1) * 0.25).astype(jnp.bfloat16)
    pooled_f = pooled.astype(jnp.float32)
    inv_rms = lax.rsqrt(jnp.mean(pooled_f * pooled_f, axis=1, keepdims=True) + 1e-05)
    gathered = lax.all_gather(pooled, "mp", axis=0, tiled=True).astype(jnp.float32)
    inv_group = lax.rsqrt(jnp.mean(gathered * gathered, axis=1, keepdims=True) + 1e-05)
    normed = (gathered * inv_group * norm_gain).astype(jnp.bfloat16)
    full_in = lax.all_gather(weight_in, "seq", axis=0, tiled=True)
    full_out = lax.all_gather(weight_out, "seq", axis=1, tiled=True)
    hidden_pre = jnp.dot(normed, full_in, preferred_element_type=jnp.float32)
    activated = gelu_tanh(hidden_pre).astype(jnp.bfloat16)
    down_sum = lax.psum_scatter(
        jnp.dot(activated, full_out, preferred_element_type=jnp.float32).astype(jnp.bfloat16),
        "mp",
        scatter_dimension=0,
        tiled=True,
    ).astype(jnp.float32)
    coarse = (pooled_f + down_sum).astype(jnp.bfloat16)
    carried = from_behind(coarse[groups - 1 :], ("seq", "mp"), 1)
    earlier = jnp.concatenate([carried, coarse[:-1]], axis=0)
    starts = doc_start.reshape(groups, 4).astype(jnp.float32)
    keep_mask = jnp.cumprod(1.0 - starts, axis=1)
    mixed_stream = (
        (grouped + keep_mask[:, :, None] * earlier.astype(jnp.float32)[:, None, :])
        .reshape(tok_rows, feat_width)
        .astype(jnp.bfloat16)
    )
    up_grouped = upstream.reshape(groups, 4, feat_width).astype(jnp.float32)
    group_sums = jnp.sum(up_grouped * keep_mask[:, :, None], axis=1)
    following = from_behind(group_sums[:1].astype(jnp.bfloat16), ("seq", "mp"), -1)
    grad_coarse = jnp.concatenate([group_sums[1:].astype(jnp.bfloat16), following], axis=0)
    grad_group = lax.all_gather(grad_coarse, "mp", axis=0, tiled=True)
    grad_act = contract(grad_group, full_out, 1, 1)
    pullback = jax.vjp(gelu_tanh, hidden_pre)[1]
    grad_pre = pullback(grad_act)[0].astype(jnp.bfloat16)
    out_term = contract(activated, grad_group, 0, 0)
    grad_weight_out = lax.psum_scatter(
        out_term.astype(jnp.bfloat16), "seq", scatter_dimension=1, tiled=True
    ).astype(jnp.float32)
    grad_weight_in = lax.psum_scatter(
        contract(normed, grad_pre, 0, 0).astype(jnp.bfloat16),
        "seq",
        scatter_dimension=0,
        tiled=True,
    ).astype(jnp.float32)
    grad_normed = lax.psum_scatter(
        contract(grad_pre, full_in, 1, 1).astype(jnp.bfloat16),
        "mp",
        scatter_dimension=0,
        tiled=True,
    ).astype(jnp.float32)
    grad_gain = lax.psum(jnp.sum(grad_normed * pooled_f * inv_rms, axis=0), ("seq", "mp"))
    scaled = norm_gain * grad_normed
    grad_pooled = grad_coarse.astype(jnp.float32) + inv_rms * (
        scaled - pooled_f * inv_rms * inv_rms * jnp.mean(scaled * pooled_f, axis=1, keepdims=True)
    )
    grad_stream = (
        (up_grouped + 0.25 * grad_pooled[:, None, :])
        .reshape(tok_rows, feat_width)
        .astype(jnp.bfloat16)
    )
    return (mixed_stream, grad_stream, grad_gain, grad_weight_in, grad_weight_out)


def solution(mesh):
    in_specs = (
        P(("seq", "mp"), None),
        P(("seq", "mp")),
        P(),
        P("seq", "mp"),
        P("mp", "seq"),
        P(("seq", "mp"), None),
    )
    out_specs = (
        P(("seq", "mp"), None),
        P(("seq", "mp"), None),
        P(),
        P("seq", "mp"),
        P("mp", "seq"),
    )
    return jax.shard_map(shards, mesh=mesh, in_specs=in_specs, out_specs=out_specs, check_vma=False)
```

profile of v0, /device:TPU:1, one launch (start us, length us, event | category | flops | bytes accessed | tf_op | source)
XLA Modules:
  0.0 742.4 jit_solution(7729088938047629296)
XLA Ops:
  7.2 0.0 copy-start.5
  7.2 0.0 copy-start.1
  7.2 0.0 all-gather.5.cloned.1.call-start
  7.2 1.8 reshape.74
  9.0 2.2 reduce_sum.54
  11.2 1.9 fusion.18
  13.1 0.0 all-gather.5.cloned.1.call-update
  13.2 0.0 all-gather.7.cloned.1.call-start
  13.2 0.7 all-gather.7.cloned.1.call-update
  13.9 0.0 all-gather.9.cloned.1.call-start
  14.0 0.7 all-gather.9.cloned.1.call-update
  14.6 0.0 all-gather.11.cloned.1.call-start
  14.7 0.0 copy-done.5
  14.7 0.1 sub.22
  14.8 0.0 copy-done.1
  14.8 0.7 reshape.75
  15.5 0.0 copy-start.4
  15.5 0.2 reduce_window.9
  15.7 1.4 multiply_reduce_fusion
  17.2 5.1 collective-permute-start.1
  22.3 0.1 slice.20
  22.4 2.4 collective-permute-done.1
  24.8 0.7 pad_maximum_fusion
  25.5 0.0 all-gather.11.cloned.1.call-update
  25.6 0.0 reduce-scatter.7.cloned.1.call-start
  25.6 53.0 %all-gather.5.cloned.1.call-done = bf16[512,4096]{1,0:T(8,128)(2,1)} async-done(((bf16[32,4096]{1,0:T(8,128)(2,1)}), bf16[512,4096]{1,0:T(8,128)(2,1)}) %all-gather.5.cloned.1.call-update) | async-done | bytes 4194320 | tf_op jit(solution)/shard_map/all_gather | solution.py:30
  78.7 3.1 fusion
  81.7 95.6 %all-gather.7.cloned.1.call-done = bf16[4096,448]{0,1:T(8,128)(2,1)} async-done(((bf16[256,448]{0,1:T(8,128)(2,1)}), bf16[4096,448]{0,1:T(8,128)(2,1)}) %all-gather.7.cloned.1.call-update) | async-done | bytes 3670032 | tf_op jit(solution)/shard_map/all_gather | solution.py:33
  177.4 0.0 copy-done.4
  177.4 5.5 fusion.4
  182.9 105.0 %all-gather.9.cloned.1.call-done = bf16[448,4096]{1,0:T(8,128)(2,1)} async-done(((bf16[448,256]{1,0:T(8,128)(2,1)}), bf16[448,4096]{1,0:T(8,128)(2,1)}) %all-gather.9.cloned.1.call-update) | async-done | bytes 3670032 | tf_op jit(solution)/shard_map/all_gather | solution.py:34
  287.9 74.9 %all-gather.11.cloned.1.call-done = bf16[512,4096]{1,0:T(8,128)(2,1)} async-done(((bf16[32,4096]{1,0:T(8,128)(2,1)}), bf16[512,4096]{1,0:T(8,128)(2,1)}) %all-gather.11.cloned.1.call-update) | async-done | bytes 4194320 | tf_op jit(solution)/shard_map/all_gather | solution.py:57
  362.8 6.0 fusion.12
  368.8 4.3 convolution_convert_fusion
  373.1 0.0 reduce-scatter.7.cloned.1.call-update
  373.1 0.2 reduce-scatter.5.cloned.1.call-start
  373.4 6.5 convolution_convert_fusion.1
  379.8 0.0 reduce-scatter.5.cloned.1.call-update
  379.9 0.0 reduce-scatter.9.cloned.1.call-start
  379.9 6.2 convolution_convert_fusion.2
  386.1 0.0 reduce-scatter.9.cloned.1.call-update
  386.1 0.0 copy-start.2
  386.1 0.0 reduce-scatter.11.cloned.1.call-start
  386.2 6.4 convolution_convert_fusion.3
  392.6 0.0 reduce-scatter.11.cloned.1.call-update
  392.6 65.7 %reduce-scatter.7.cloned.1.call-done = bf16[32,4096]{1,0:T(8,128)(2,1)} async-done(((bf16[512,4096]{1,0:T(8,128)(2,1)}), bf16[32,4096]{1,0:T(8,128)(2,1)}) %reduce-scatter.7.cloned.1.call-update) | async-done | bytes 262160 | tf_op jit(solution)/shard_map/reduce_scatter | solution.py:71
  458.4 0.0 copy-done.2
  458.4 1.2 fusion.23
  459.6 90.6 %reduce-scatter.5.cloned.1.call-done = bf16[32,4096]{1,0:T(8,128)(2,1)} async-done(((bf16[512,4096]{1,0:T(8,128)(2,1)}), bf16[32,4096]{1,0:T(8,128)(2,1)}) %reduce-scatter.5.cloned.1.call-update) | async-done | bytes 262160 | tf_op jit(solution)/shard_map/reduce_scatter | solution.py:37
  550.2 1.3 fusion.16
  551.6 5.4 collective-permute-start
  557.0 0.1 mul.158
  557.1 0.6 add.71
  557.7 1.8 add.72
  559.4 80.3 %psum.7 = f32[4096]{0:T(1024)} all-reduce(f32[4096]{0:T(1024)S(1)} %get-tuple-element.5), channel_id=1, replica_groups=mesh['seq'=16,'mp'=16] {'seq','mp'}, use_global_device_ids=true, to_apply=%region_9.10 | all-reduce | flops 4096 | bytes 32768 | tf_op jit(solution)/shard_map/psum | solution.py:77
  639.7 0.0 collective-permute-done
  639.7 0.1 maximum_convert_fusion
  639.8 0.6 mul.171
  640.4 1.7 mul.172
  642.1 0.0 copy-done
  642.1 4.5 add_convert_fusion
  646.6 1.7 convert_element_type.113
  648.3 85.5 %reduce-scatter.11.cloned.1.call-done = bf16[448,256]{1,0:T(8,128)(2,1)} async-done(((bf16[448,4096]{1,0:T(8,128)(2,1)}), bf16[448,256]{1,0:T(8,128)(2,1)}) %reduce-scatter.11.cloned.1.call-update) | async-done | bytes 229392 | tf_op jit(solution)/shard_map/reduce_scatter | solution.py:62
  733.8 1.7 convert_element_type.115
  (10 shorter events, 0.1 us)
Async XLA Ops:
  7.2 7.5 %copy-start.5 = (s32[128]{0:T(128)S(1)}, s32[128]{0:T(128)}, u32[]{:S(2)}) copy-start(s32[128]{0:T(128)} %param.7) | copy-start | bytes 1540
  7.2 7.6 %copy-start.1 = (bf16[128,4096]{1,0:T(8,128)(2,1)S(1)}, bf16[128,4096]{1,0:T(8,128)(2,1)}, u32[]{:S(2)}) copy-start(bf16[128,4096]{1,0:T(8,128)(2,1)} %param.11) | copy-start | bytes 3145732
  7.2 71.5 %all-gather.5.cloned.1.call-start = ((), (), s32[]{:S(2)}) async-start(), calls=%async_computation.4 | async-start | bytes 4456448 | tf_op jit(solution)/shard_map/all_gather | solution.py:30
  13.2 164.2 %all-gather.7.cloned.1.call-start = ((), (), s32[]{:S(2)}) async-start(), calls=%async_computation.5 | async-start | bytes 3899392 | tf_op jit(solution)/shard_map/all_gather | solution.py:33
  13.9 274.0 %all-gather.9.cloned.1.call-start = ((), (), s32[]{:S(2)}) async-start(), calls=%async_computation.6 | async-start | bytes 3899392 | tf_op jit(solution)/shard_map/all_gather | solution.py:34
  14.6 348.1 %all-gather.11.cloned.1.call-start = ((), (), s32[]{:S(2)}) async-start(), calls=%async_computation.8 | async-start | bytes 4456448 | tf_op jit(solution)/shard_map/all_gather | solution.py:57
  15.5 161.9 %copy-start.4 = (f32[4096]{0:T(1024)S(1)}, f32[4096]{0:T(1024)}, u32[]{:S(2)}) copy-start(f32[4096]{0:T(1024)} %param.8) | copy-start | bytes 49156
  17.2 7.6 %collective-permute-start.1 = (bf16[1,4096]{1,0:T(2,128)(2,1)S(1)}, bf16[1,4096]{1,0:T(2,128)(2,1)S(1)}, u32[]{:S(2)}, u32[]{:S(2)}) collective-permute-start(bf16[1,4096]{1,0:T(2,128)(2,1)S(1)} %slice.21), channel_id=1, source_target_pairs={{1,0},{2,1},{3,2},{4,3},{5,4},{6,5},{7,6},{8,7},{9,8},{10,9},{11,1... | collective-permute-start | bytes 24584 | tf_op jit(solution)/shard_map/ppermute | solution.py:10
  25.6 432.8 %reduce-scatter.7.cloned.1.call-start = ((), (), s32[]{:S(2)}) async-start(), calls=%async_computation.9 | async-start | bytes 4456448 | tf_op jit(solution)/shard_map/reduce_scatter | solution.py:71
  362.8 6.0 copy-start.3
  373.1 177.1 %reduce-scatter.5.cloned.1.call-start = ((), (), s32[]{:S(2)}) async-start(), calls=%async_computation.7 | async-start | bytes 4456448 | tf_op jit(solution)/shard_map/reduce_scatter | solution.py:37
  379.9 266.7 %reduce-scatter.9.cloned.1.call-start = ((), (), s32[]{:S(2)}) async-start(), calls=%async_computation.10 | async-start | bytes 3899392 | tf_op jit(solution)/shard_map/reduce_scatter | solution.py:65
  386.1 72.2 %copy-start.2 = (bf16[32,4096]{1,0:T(8,128)(2,1)S(1)}, bf16[32,4096]{1,0:T(8,128)(2,1)}, u32[]{:S(2)}) copy-start(bf16[32,4096]{1,0:T(8,128)(2,1)} %get-tuple-element.8) | copy-start | bytes 786436
  386.1 347.6 %reduce-scatter.11.cloned.1.call-start = ((), (), s32[]{:S(2)}) async-start(), calls=%async_computation.11 | async-start | bytes 3899392 | tf_op jit(solution)/shard_map/reduce_scatter | solution.py:62
  551.6 88.2 %collective-permute-start = (bf16[1,4096]{1,0:T(2,128)(2,1)S(1)}, bf16[1,4096]{1,0:T(2,128)(2,1)S(1)}, u32[]{:S(2)}, u32[]{:S(2)}) collective-permute-start(bf16[1,4096]{1,0:T(2,128)(2,1)S(1)} %slice.18), channel_id=1, source_target_pairs={{0,1},{1,2},{2,3},{3,4},{4,5},{5,6},{6,7},{7,8},{8,9},{9,10},{10,1... | collective-permute-start | bytes 24584 | tf_op jit(solution)/shard_map/ppermute | solution.py:10
  559.4 82.6 %copy-start = (bf16[128,4096]{1,0:T(8,128)(2,1)S(1)}, bf16[128,4096]{1,0:T(8,128)(2,1)}, u32[]{:S(2)}) copy-start(bf16[128,4096]{1,0:T(8,128)(2,1)} %param.6) | copy-start | bytes 3145732
Sparse Core Ops, SparseCore 0:
  13.3 65.3 all-gather.4
  80.4 96.9 all-gather.6
  179.1 108.7 all-gather.8
  291.0 71.7 all-gather.10
  373.3 85.0 reduce-scatter.6
  463.2 86.9 reduce-scatter.4
  552.8 89.2 reduce-scatter.8
  644.6 89.0 reduce-scatter.10
where the time goes:
time: 745 us; the launch traced here: 742 us
  waiting for transfers between devices  574 us (77%)
  blocking collectives  80.3 us (11%)
  matrix products  34.9 us (5%)
  other arithmetic  20.1 us (3%)
  between operations  14.3 us (2%)
  starting transfers between devices  11.1 us (1%)
    all_gather x1, waiting for transfers between devices, shards(): full_out = lax.all_gather(weight_out, 'seq', axis=1, tiled=True)  105 us
    all_gather x1, waiting for transfers between devices, shards(): full_in = lax.all_gather(weight_in, 'seq', axis=0, tiled=True)  95.6 us
    reduce_scatter x1, waiting for transfers between devices, shards(): lax.psum_scatter(jnp.dot(activated, full_out, preferred_element_type=jnp....  90.6 us
    reduce_scatter x1, waiting for transfers between devices, shards(): lax.psum_scatter(out_term.astype(jnp.bfloat16), 'seq', scatter_dimension=...  85.5 us
    psum x1, blocking collectives, shards(): lax.psum(jnp.sum(grad_normed * pooled_f * inv_rms, axis=0), ('seq', 'mp'))  80.3 us
    all_gather x1, waiting for transfers between devices, shards(): grad_group = lax.all_gather(grad_coarse, 'mp', axis=0, tiled=True)  74.9 us
    reduce_scatter x1, waiting for transfers between devices, shards(): lax.psum_scatter(contract(grad_pre, full_in, 1, 1).astype(jnp.bfloat16),...  65.7 us
    all_gather x1, waiting for transfers between devices, shards(): lax.all_gather(pooled, 'mp', axis=0, tiled=True).astype(jnp.float32)  53 us
  transfers between devices with their start and end apart: 10, of which 8 were waited for; matrix products, arithmetic and copies ran while one was open for 6% of the time, Pallas kernels for 0%

commit v1 on v0

v1 whole, which is shorter than its diff:
```python
import functools

import jax
import jax.numpy as jnp
from jax import lax
from jax.experimental import pallas as pl
from jax.experimental.pallas import tpu as pltpu
from jax.sharding import Mesh, PartitionSpec as P

AXES = ("z", "yl", "x", "yh", "c")
NZ, NY, NX = 8, 4, 4


def linear(z, y, x, c):
    return (((z * 2 + y % 2) * NX + x) * 2 + y // 2) * 2 + c


def places():
    return [
        (z, y, x, c) for z in range(NZ) for y in range(NY) for x in range(NX) for c in range(2)
    ]


def shift(value, dx=0, dy=0):
    pairs = [
        (linear(z, y, x, c), linear(z, (y + dy) % NY, (x + dx) % NX, c)) for z, y, x, c in places()
    ]
    return lax.ppermute(value, AXES, pairs)


def other_core(value):
    pairs = [(linear(z, y, x, c), linear(z, y, x, 1 - c)) for z, y, x, c in places()]
    return lax.ppermute(value, AXES, pairs)


def swap_low(value):
    pairs = [
        (linear(z, y, x, c), linear(z, (y // 2) * 2 + c, x, y % 2)) for z, y, x, c in places()
    ]
    return lax.ppermute(value, AXES, pairs)


def from_behind(value, by):
    count = NZ * NY * NX * 2
    pairs = [(i, i + by) for i in range(count) if 0 <= i + by < count]
    return lax.ppermute(value, AXES, pairs)


def nt(a, b):
    return lax.dot_general(a, b, (((1,), (1,)), ((), ())), preferred_element_type=jnp.float32)


def nn(a, b):
    return jnp.dot(a, b, preferred_element_type=jnp.float32)


def block_kernel(n_blocks, chunks, *refs):
    acts = refs[:n_blocks]
    w_own, w_oth = refs[n_blocks : n_blocks + 2]
    outs = refs[n_blocks + 2 : 2 * n_blocks + 2]
    g_own, g_oth, gain = refs[2 * n_blocks + 2 : 2 * n_blocks + 5]
    (p_s, g_s, wi_s, wo_s, d_s, n_s, gi_s, go_s, h_s, ga_s, sq_s, act, gp, act_t, gp_t, in_sem,
     out_sem) = refs[2 * n_blocks + 5 :]
    core = lax.axis_index("c")
    rows = acts[0].shape[1]
    hidden = wi_s.shape[0]
    half = w_own.shape[2]
    width = 2 * half
    feats = chunks * width

    def cols(z):
        return pl.ds(pl.multiple_of(z * width, width), width)

    def w_cols(z, which):
        return pl.ds(pl.multiple_of(z * width + which * half, half), half)

    def fetch(z, carry):
        for i in range(n_blocks):
            at = pl.ds(i * rows, rows)
            pltpu.make_async_copy(
                acts[i].at[0, :, cols(z)], p_s.at[at, cols(z)], in_sem.at[0, z]
            ).start()
            pltpu.make_async_copy(
                acts[i].at[1, :, cols(z)], g_s.at[at, cols(z)], in_sem.at[1, z]
            ).start()
        for source, which in ((w_own, core), (w_oth, 1 - core)):
            pltpu.make_async_copy(
                source.at[z, pl.ds(0, hidden), :], wi_s.at[:, w_cols(z, which)], in_sem.at[2, z]
            ).start()
            pltpu.make_async_copy(
                source.at[z, pl.ds(hidden, hidden), :],
                wo_s.at[:, w_cols(z, which)],
                in_sem.at[3, z],
            ).start()
        return carry

    lax.fori_loop(0, chunks, fetch, 0)
    h_s[...] = jnp.zeros_like(h_s)
    ga_s[...] = jnp.zeros_like(ga_s)
    sq_s[...] = jnp.zeros_like(sq_s)

    def first(z, carry):
        for k, buf in enumerate((p_s, g_s, wi_s, wo_s)):
            view = buf.at[:, cols(z)]
            pltpu.make_async_copy(view, view, in_sem.at[k, z]).wait()
        p = p_s[:, cols(z)]
        h_s[...] += nt(p, wi_s[:, cols(z)])
        ga_s[...] += nt(g_s[:, cols(z)], wo_s[:, cols(z)])
        pf = p.astype(jnp.float32)
        sq_s[...] += jnp.sum(pf * pf, axis=1, keepdims=True)
        return carry

    lax.fori_loop(0, chunks, first, 0)
    inv = lax.rsqrt(sq_s[...] * (1.0 / feats) + 1e-05)
    v = h_s[...] * inv
    v2 = v * v
    t = jnp.tanh(0.7978845608 * v * (1.0 + 0.044715 * v2))
    up = 0.5 * (1.0 + t)
    a = (v * up).astype(jnp.bfloat16)
    slope = up + 0.5 * v * (1.0 - t * t) * (0.7978845608 * (1.0 + 0.134145 * v2))
    b = (ga_s[...] * slope * inv).astype(jnp.bfloat16)
    act[...] = a
    gp[...] = b
    act_t[...] = a.T
    gp_t[...] = b.T

    def second(z, carry):
        wi = wi_s[:, cols(z)]
        d_s[:, cols(z)] = nn(act[...], wo_s[:, cols(z)]).astype(jnp.bfloat16)
        n_s[:, cols(z)] = nn(gp[...], wi).astype(jnp.bfloat16)
        go_s[:, cols(z)] = nn(act_t[...], g_s[:, cols(z)]).astype(jnp.bfloat16)
        gi = nn(gp_t[...], p_s[:, cols(z)])
        gi_s[:, cols(z)] = gi.astype(jnp.bfloat16)
        gain[:, cols(z)] = jnp.sum(gi * wi.astype(jnp.float32), axis=0, keepdims=True)
        for i in range(n_blocks):
            at = pl.ds(i * rows, rows)
            pltpu.make_async_copy(
                d_s.at[at, cols(z)], outs[i].at[0, :, cols(z)], out_sem.at[0, z]
            ).start()
            pltpu.make_async_copy(
                n_s.at[at, cols(z)], outs[i].at[1, :, cols(z)], out_sem.at[1, z]
            ).start()
        for dest, which in ((g_own, core), (g_oth, 1 - core)):
            pltpu.make_async_copy(
                gi_s.at[:, w_cols(z, which)], dest.at[z, pl.ds(0, hidden), :], out_sem.at[2, z]
            ).start()
            pltpu.make_async_copy(
                go_s.at[:, w_cols(z, which)], dest.at[z, pl.ds(hidden, hidden), :], out_sem.at[3, z]
            ).start()
        return carry

    lax.fori_loop(0, chunks, second, 0)

    def drain(z, carry):
        for k, buf in enumerate((d_s, n_s, gi_s, go_s)):
            view = buf.at[:, cols(z)]
            pltpu.make_async_copy(view, view, out_sem.at[k, z]).wait()
        return carry

    lax.fori_loop(0, chunks, drain, 0)


def block(acts, w_own, w_oth):
    n = len(acts)
    _, rows, feats = acts[0].shape
    chunks, hidden2, half = w_own.shape
    hidden = hidden2 // 2
    total = n * rows
    bf = jnp.bfloat16
    anywhere = pl.BlockSpec(memory_space=pl.ANY)
    flops = 12 * total * feats * hidden
    return pl.pallas_call(
        functools.partial(block_kernel, n, chunks),
        out_shape=[jax.ShapeDtypeStruct(acts[0].shape, bf)] * n
        + [jax.ShapeDtypeStruct(w_own.shape, bf)] * 2
        + [jax.ShapeDtypeStruct((1, feats), jnp.float32)],
        in_specs=[anywhere] * (n + 2),
        out_specs=[anywhere] * (n + 2) + [pl.BlockSpec(memory_space=pltpu.VMEM)],
        scratch_shapes=[pltpu.VMEM((total, feats), bf)] * 2
        + [pltpu.VMEM((hidden, feats), bf)] * 2
        + [pltpu.VMEM((total, feats), bf)] * 2
        + [pltpu.VMEM((hidden, feats), bf)] * 2
        + [pltpu.VMEM((total, hidden), jnp.float32)] * 2
        + [pltpu.VMEM((total, 1), jnp.float32)]
        + [pltpu.VMEM((total, hidden), bf)] * 2
        + [pltpu.VMEM((hidden, total), bf)] * 2
        + [pltpu.SemaphoreType.DMA((4, chunks)), pltpu.SemaphoreType.DMA((4, chunks))],
        compiler_params=pltpu.CompilerParams(vmem_limit_bytes=48 * 1024 * 1024),
        cost_estimate=pl.CostEstimate(
            flops=flops, bytes_accessed=8 * (total + hidden) * feats * 2, transcendentals=0
        ),
    )(*acts, w_own, w_oth)


def gather_plane(first, second):
    a = jnp.concatenate([first] + [shift(first, dy=d) for d in (1, 2, 3)], axis=1)
    b = jnp.concatenate([second] + [shift(second, dx=d) for d in (1, 2, 3)], axis=1)
    return [a] + [shift(a, dx=d) for d in (1, 2, 3)] + [b] + [shift(b, dy=d) for d in (1, 2, 3)]


def add_all(parts):
    total = parts[0].astype(jnp.float32)
    for part in parts[1:]:
        total = total + part.astype(jnp.float32)
    return total


def scatter_plane(blocks, rows):
    a = add_all([blocks[0]] + [shift(blocks[d], dx=-d) for d in (1, 2, 3)]).astype(jnp.bfloat16)
    b = add_all([blocks[4]] + [shift(blocks[4 + d], dy=-d) for d in (1, 2, 3)]).astype(jnp.bfloat16)
    a = [a[:, d * rows : (d + 1) * rows] for d in range(4)]
    b = [b[:, d * rows : (d + 1) * rows] for d in range(4)]
    a = add_all([a[0]] + [shift(a[d], dy=-d) for d in (1, 2, 3)])
    b = add_all([b[0]] + [shift(b[d], dx=-d) for d in (1, 2, 3)])
    return jnp.concatenate([a, b], axis=1)


def shards(stream, doc_start, norm_gain, weight_in, weight_out, upstream):
    tok_rows, feats = stream.shape
    groups = tok_rows // 4
    hidden = weight_out.shape[0]
    k_rows = weight_in.shape[0]
    bf = jnp.bfloat16
    seq = lax.axis_index("z") * 2 + lax.axis_index("yl")
    gain = lax.dynamic_slice(norm_gain, (seq * k_rows,), (k_rows,))

    scaled_in = (weight_in.T.astype(jnp.float32) * gain[None, :]).astype(bf)
    both = swap_low(jnp.concatenate([scaled_in, weight_out], axis=0))
    w_own = lax.all_gather(both, "z", axis=0, tiled=False)

    starts = doc_start.reshape(groups, 4).astype(jnp.float32)
    keep = jnp.cumprod(1.0 - starts, axis=1).reshape(tok_rows)
    group_of = lax.broadcasted_iota(jnp.int32, (groups, tok_rows), 1) // 4
    here = lax.broadcasted_iota(jnp.int32, (groups, tok_rows), 0)
    pool = jnp.where(group_of == here, 0.25, 0.0).astype(bf)
    pooled = nn(pool, stream).astype(bf)
    pick = jnp.where(group_of == here, keep[None, :], 0.0).astype(bf)
    group_sums = nn(pick, upstream).astype(bf)
    following = from_behind(group_sums[:1], -1)
    grad_coarse = jnp.concatenate([group_sums[1:], following], axis=0)

    acts = jnp.stack([pooled, grad_coarse], axis=0)
    rows = groups // 2
    blocks = gather_plane(acts[:, :rows], acts[:, rows:])
    w_oth = other_core(w_own)
    results = block(blocks, w_own, w_oth)
    outs, (g_own, g_oth, gain_part) = results[:8], results[8:]

    mine = (g_own.astype(jnp.float32) + other_core(g_oth).astype(jnp.float32)).astype(bf)
    grads = swap_low(lax.psum_scatter(mine, "z", scatter_dimension=0, tiled=False))
    grad_weight_in = (grads[:hidden].astype(jnp.float32) * gain[None, :]).T
    grad_weight_out = grads[hidden:].astype(jnp.float32)
    grad_gain = lax.psum(gain_part[0] / norm_gain, AXES)

    down_sum, scaled = scatter_plane(outs, rows)
    pooled_f = pooled.astype(jnp.float32)
    inv_sq = 1.0 / (jnp.mean(pooled_f * pooled_f, axis=1, keepdims=True) + 1e-05)
    coarse = (pooled_f + down_sum).astype(bf)
    carried = from_behind(coarse[groups - 1 :], 1)
    earlier = jnp.concatenate([carried, coarse[:-1]], axis=0)
    mixed_stream = (stream.astype(jnp.float32) + nn(pick.T, earlier)).astype(bf)
    grad_pooled = grad_coarse.astype(jnp.float32) + (
        scaled - pooled_f * inv_sq * jnp.mean(scaled * pooled_f, axis=1, keepdims=True)
    )
    grad_stream = (upstream.astype(jnp.float32) + nn(pool.T, grad_pooled.astype(bf))).astype(bf)
    return (mixed_stream, grad_stream, grad_gain, grad_weight_in, grad_weight_out)


def solution(mesh):
    fine = Mesh(mesh.devices.reshape(NZ, 2, NX, 2, 2), AXES)
    rows = P(AXES, None)
    seq, mp = ("z", "yl"), ("x", "yh", "c")
    in_specs = (rows, P(AXES), P(), P(seq, mp), P(mp, seq), rows)
    out_specs = (rows, rows, P(), P(seq, mp), P(mp, seq))
    return jax.shard_map(shards, mesh=fine, in_specs=in_specs, out_specs=out_specs, check_vma=False)
```

time: 745 us -> 427 us (0.57)
  waiting for transfers between devices: 574 us -> 207 us
  starting transfers between devices: 11.1 us -> 45.5 us
  blocking collectives: 80.3 us -> 114 us
  matrix products: 34.9 us -> 4.4 us
  Pallas kernels: 0 us -> 20.6 us
    all_gather x4 -> x1, waiting for transfers between devices: 329 us -> 49 us  [shards(): w_own = lax.all_gather(both, 'z', axis=0, tiled=False)]
    reduce_scatter x4 -> x1, waiting for transfers between devices: 242 us -> 0.02 us  [shards(): lax.psum_scatter(mine, 'z', scatter_dimension=0, tiled=False)]
    ppermute x2 -> x30, waiting for transfers between devices: 2.4 us -> 158 us  [the longest x24 144 us: shift(): return lax.ppermute(value, AXES, pairs)]
    ppermute x2 -> x30, starting transfers between devices: 10.6 us -> 45.4 us  [the longest x24 28.1 us: shift(): return lax.ppermute(value, AXES, pairs)]
    psum x1, blocking collectives: 80.3 us -> 114 us  [shards(): grad_gain = lax.psum(gain_part[0] / norm_gain, AXES)]
    dot_general x6 -> x4, matrix products: 34.9 us -> 4.4 us  [nn(): return jnp.dot(a, b, preferred_element_type=jnp.float32)]
    pallas_call x0 -> x1, Pallas kernels: none -> 20.6 us  [block(): pl.pallas_call(functools.partial(block_kernel, n, chunks), out_shape=[jax...]
    reduce_sum x4 -> x0, other arithmetic: 7.92 us -> none  [the longest x1 3.08 us: shards(): jnp.mean(gathered * gathered, axis=1, keepdims=True) + 1e-05]
  transfers between devices with their start and end apart: 10 -> 32, of which waited for: 8 -> 16; matrix products, arithmetic and copies ran while one was open for 6% -> 4% of each run, Pallas kernels for 0% -> 0%
where the time goes in v1:
time: 427 us
  waiting for transfers between devices  207 us (48%)
  blocking collectives  114 us (27%)
  starting transfers between devices  45.5 us (11%)
  Pallas kernels  20.6 us (5%)
  other arithmetic  14.6 us (3%)
  between operations  14.4 us (3%)
  local copies, waits for them, and re-layouts  6.39 us (1%)
  matrix products  4.4 us (1%)
    ppermute x24, waiting for transfers between devices, shift(): return lax.ppermute(value, AXES, pairs)  144 us
    psum x1, blocking collectives, shards(): grad_gain = lax.psum(gain_part[0] / norm_gain, AXES)  114 us
    all_gather x1, waiting for transfers between devices, shards(): w_own = lax.all_gather(both, 'z', axis=0, tiled=False)  49 us
    ppermute x24, starting transfers between devices, shift(): return lax.ppermute(value, AXES, pairs)  28.1 us
    pallas_call x1, Pallas kernels, block(): pl.pallas_call(functools.partial(block_kernel, n, chunks), out_shape=[jax...  20.6 us
    ppermute x2, waiting for transfers between devices, swap_low(): return lax.ppermute(value, AXES, pairs)  10 us
    ppermute x2, starting transfers between devices, from_behind(): return lax.ppermute(value, AXES, pairs)  9.1 us
  transfers between devices with their start and end apart: 32, of which 16 were waited for; matrix products, arithmetic and copies ran while one was open for 4% of the time, Pallas kernels for 0%

profile of v1, /device:TPU:1, one launch (start us, length us, event | category | flops | bytes accessed | tf_op | source)
XLA Modules:
  0.0 426.8 jit_solution(3424012528342574023)
XLA Ops:
  7.2 0.9 dynamic_slice.3
  8.1 1.0 fusion.19
  9.1 1.0 pad_maximum_fusion.3
  10.1 4.6 %collective-permute-start.13 = (bf16[896,256]{1,0:T(8,128)(2,1)S(1)}, bf16[896,256]{1,0:T(8,128)(2,1)S(1)}, u32[]{:S(2)}, u32[]{:S(2)}) collective-permute-start(bf16[896,256]{1,0:T(8,128)(2,1)S(1)} %pad_maximum_fusion.3), channel_id=1, source_target_pairs={{0,0},{1,16},{4,4},{5,20},{8,8},{9,24},{12,12},{13,28},{16,1},{17,... | collective-permute-start | bytes 1376264 | tf_op jit(solution)/shard_map/ppermute | solution.py:40
  14.7 6.1 %collective-permute-done.13 = bf16[896,256]{1,0:T(8,128)(2,1)S(1)} collective-permute-done((bf16[896,256]{1,0:T(8,128)(2,1)S(1)}, bf16[896,256]{1,0:T(8,128)(2,1)S(1)}, u32[]{:S(2)}, u32[]{:S(2)}) %collective-permute-start.13) | collective-permute-done | bytes 458784 | tf_op jit(solution)/shard_map/ppermute | solution.py:40
  20.8 0.8 copy-done.9
  21.7 0.7 convert_subtract_fusion
  22.5 0.2 reduce_window.9
  22.8 0.3 convolution_convert_fusion
  23.1 1.9 collective-permute-start
  25.0 0.3 convolution_convert_fusion.1
  25.4 49.0 %all-gather.3.cloned.1.call-done = bf16[7168,256]{1,0:T(8,128)(2,1)} async-done(((bf16[896,256]{1,0:T(8,128)(2,1)}), bf16[7168,256]{1,0:T(8,128)(2,1)}) %all-gather.3.cloned.1.call-update) | async-done | bytes 3670032 | tf_op jit(solution)/shard_map/all_gather | solution.py:229
  74.4 0.7 collective-permute-start.14
  75.2 2.5 collective-permute-start.3
  77.7 0.5 collective-permute-start.2
  78.2 0.6 collective-permute-start.1
  78.8 10.1 %collective-permute-done.3 = bf16[2,16,4096]{2,1,0:T(8,128)(2,1)S(1)} collective-permute-done((bf16[2,16,4096]{2,1,0:T(8,128)(2,1)S(1)}, bf16[2,16,4096]{2,1,0:T(8,128)(2,1)S(1)}, u32[]{:S(2)}, u32[]{:S(2)}) %collective-permute-start.3) | collective-permute-done | bytes 262176 | tf_op jit(solution)/shard_map/ppermute | solution.py:28
  88.9 4.1 collective-permute-done.1
  93.2 2.5 collective-permute-start.6
  95.7 0.6 collective-permute-start.5
  96.2 0.9 collective-permute-start.9
  97.1 1.5 collective-permute-start.8
  98.6 47.8 %collective-permute-done.9 = bf16[2,16,4096]{2,1,0:T(8,128)(2,1)S(1)} collective-permute-done((bf16[2,16,4096]{2,1,0:T(8,128)(2,1)S(1)}, bf16[2,16,4096]{2,1,0:T(8,128)(2,1)S(1)}, u32[]{:S(2)}, u32[]{:S(2)}) %collective-permute-start.9) | collective-permute-done | bytes 262176 | tf_op jit(solution)/shard_map/ppermute | solution.py:28
  146.5 0.3 collective-permute-start.7
  146.8 6.6 %collective-permute-start.4 = (bf16[2,64,4096]{2,1,0:T(8,128)(2,1)S(1)}, bf16[2,64,4096]{2,1,0:T(8,128)(2,1)S(1)}, u32[]{:S(2)}, u32[]{:S(2)}) collective-permute-start(bf16[2,64,4096]{2,1,0:T(8,128)(2,1)S(1)} %pad_maximum_fusion.refs_0_), channel_id=1, source_target_pairs={{0,4},{1,5},{4,8},{5,9},{8,12},{9,13},{12,0},{13,1},{16,20},{17,21... | collective-permute-start | bytes 3145736 | tf_op jit(solution)/shard_map/ppermute | solution.py:28
  153.3 6.8 %collective-permute-done.7 = bf16[2,16,4096]{2,1,0:T(8,128)(2,1)S(1)} collective-permute-done((bf16[2,16,4096]{2,1,0:T(8,128)(2,1)S(1)}, bf16[2,16,4096]{2,1,0:T(8,128)(2,1)S(1)}, u32[]{:S(2)}, u32[]{:S(2)}) %collective-permute-start.7) | collective-permute-done | bytes 262176 | tf_op jit(solution)/shard_map/ppermute | solution.py:28
  160.3 0.6 collective-permute-start.11
  160.9 1.1 collective-permute-start.10
  162.0 20.5 %collective-permute-done.4.refs_1_ = bf16[2,64,4096]{2,1,0:T(8,128)(2,1)S(1)} collective-permute-done((bf16[2,64,4096]{2,1,0:T(8,128)(2,1)S(1)}, bf16[2,64,4096]{2,1,0:T(8,128)(2,1)S(1)}, u32[]{:S(2)}, u32[]{:S(2)}) %collective-permute-start.4) | collective-permute-done | bytes 1048608 | tf_op jit(solution)/shard_map/ppermute | solution.py:28
  182.6 0.5 collective-permute-done.11.refs_6_
  183.1 26.4 %collective-permute-done.10.refs_5_ = bf16[2,64,4096]{2,1,0:T(8,128)(2,1)S(1)} collective-permute-done((bf16[2,64,4096]{2,1,0:T(8,128)(2,1)S(1)}, bf16[2,64,4096]{2,1,0:T(8,128)(2,1)S(1)}, u32[]{:S(2)}, u32[]{:S(2)}) %collective-permute-start.10) | collective-permute-done | bytes 1048608 | tf_op jit(solution)/shard_map/ppermute | solution.py:28
  209.5 1.0 copy-done.17
  210.5 1.9 copy-done.11
  212.4 20.6 %shard_map.101 = (bf16[2,64,4096]{2,1,0:T(8,128)(2,1)S(1)}, bf16[2,64,4096]{2,1,0:T(8,128)(2,1)}, bf16[2,64,4096]{2,1,0:T(8,128)(2,1)}, bf16[2,64,4096]{2,1,0:T(...) custom-call(bf16[2,64,4096]{2,1,0:T(8,128)(2,1)} %copy-done.7, ...), custom_call_target="tpu_custom_call" | custom-call | flops 11274289152 | bytes 62914560 | tf_op jit(solution)/shard_map/pallas_call | solution.py:172
  233.0 0.6 collective-permute-start.28
  233.6 1.2 collective-permute-start.15
  234.8 0.6 collective-permute-start.17
  235.3 4.5 %collective-permute-done.28 = bf16[8,896,256]{2,1,0:T(8,128)(2,1)S(1)} collective-permute-done((bf16[8,896,256]{2,1,0:T(8,128)(2,1)}, bf16[8,896,256]{2,1,0:T(8,128)(2,1)S(1)}, u32[]{:S(2)}, u32[]{:S(2)}) %collective-permute-start.28) | collective-permute-done | bytes 3670048 | tf_op jit(solution)/shard_map/ppermute | solution.py:33
  239.8 4.8 %add_convert_fusion = bf16[8,896,256]{2,1,0:T(8,128)(2,1)} fusion(bf16[8,896,256]{2,1,0:T(8,128)(2,1)S(1)} %collective-permute-done.28, bf16[8,896,256]{2,1,0:T(8,128)(2,1)} %get-tuple-element.25), kind=kLoop, calls=%fused_computation | loop fusion | flops 7340032 | bytes 11010048 | tf_op jit(solution)/shard_map/convert_element_type | solution.py:249
  244.6 0.7 copy-done.10
  245.3 1.8 collective-permute-start.21
  247.1 113.6 %psum.7 = f32[4096]{0:T(1024)} all-reduce(f32[4096]{0:T(1024)S(1)} %div.39), channel_id=1, replica_groups=mesh['z'=8,'yl'=2,'x'=4,'yh'=2,'c'=2] {'z','yl','x','yh','c'}, use_global_device_ids=true, to_apply=%region_3.4 | all-reduce | flops 4096 | bytes 32768 | tf_op jit(solution)/shard_map/psum | solution.py:253
  360.7 0.6 collective-permute-start.23
  361.3 2.5 add_convert_fusion.2
  363.8 2.2 collective-permute-start.18
  366.0 1.3 collective-permute-start.19
  367.3 18.8 %collective-permute-done.23 = bf16[2,64,4096]{2,1,0:T(8,128)(2,1)S(1)} collective-permute-done((bf16[2,64,4096]{2,1,0:T(8,128)(2,1)}, bf16[2,64,4096]{2,1,0:T(8,128)(2,1)S(1)}, u32[]{:S(2)}, u32[]{:S(2)}) %collective-permute-start.23) | collective-permute-done | bytes 1048608 | tf_op jit(solution)/shard_map/ppermute | solution.py:28
  386.2 2.2 add_convert_fusion.1
  388.4 1.3 collective-permute-start.24
  389.7 0.3 collective-permute-start.26
  390.0 1.2 collective-permute-start.25
  391.1 1.0 collective-permute-done.20
  392.1 5.0 %collective-permute-done.19 = bf16[2,16,4096]{2,1,0:T(8,128)(2,1)S(1)} collective-permute-done((bf16[2,16,4096]{2,1,0:T(8,128)(2,1)S(1)}, bf16[2,16,4096]{2,1,0:T(8,128)(2,1)S(1)}, u32[]{:S(2)}, u32[]{:S(2)}) %collective-permute-start.19) | collective-permute-done | bytes 262176 | tf_op jit(solution)/shard_map/ppermute | solution.py:28
  397.2 2.2 collective-permute-done.26
  399.4 0.4 collective-permute-done.25
  400.0 0.2 fusion.3
  400.2 0.7 copy-done.5
  400.9 7.2 %collective-permute-start.27 = (bf16[1,4096]{1,0:T(2,128)(2,1)S(1)}, bf16[1,4096]{1,0:T(2,128)(2,1)S(1)}, u32[]{:S(2)}, u32[]{:S(2)}) collective-permute-start(bf16[1,4096]{1,0:T(2,128)(2,1)S(1)} %slice.76), channel_id=1, source_target_pairs={{0,1},{1,2},{2,3},{3,4},{4,5},{5,6},{6,7},{7,8},{8,9},{9,10},{10,1... | collective-permute-start | bytes 24584 | tf_op jit(solution)/shard_map/ppermute | solution.py:46
  408.2 2.4 collective-permute-start.29
  410.6 2.4 fusion.1
  413.0 1.4 fusion
  414.5 3.9 collective-permute-done.29
  418.3 0.8 multiply_bitcast_fusion
  419.1 0.8 slice_convert_fusion
  (73 shorter events, 1.3 us)
Async XLA Ops:
  7.2 15.6 %copy-start = (bf16[128,4096]{1,0:T(8,128)(2,1)S(1)}, bf16[128,4096]{1,0:T(8,128)(2,1)}, u32[]{:S(2)}) copy-start(bf16[128,4096]{1,0:T(8,128)(2,1)} %param.11) | copy-start | bytes 3145732
  7.2 17.8 %copy-start.2 = (bf16[128,4096]{1,0:T(8,128)(2,1)S(1)}, bf16[128,4096]{1,0:T(8,128)(2,1)}, u32[]{:S(2)}) copy-start(bf16[128,4096]{1,0:T(8,128)(2,1)} %param.6) | copy-start | bytes 3145732
  7.2 67.2 %all-gather.3.cloned.1.call-start = ((), (), s32[]{:S(2)}) async-start(), calls=%async_computation.2 | async-start | bytes 4128768 | tf_op jit(solution)/shard_map/all_gather | solution.py:229
  10.1 10.8 %collective-permute-start.13 = (bf16[896,256]{1,0:T(8,128)(2,1)S(1)}, bf16[896,256]{1,0:T(8,128)(2,1)S(1)}, u32[]{:S(2)}, u32[]{:S(2)}) collective-permute-start(bf16[896,256]{1,0:T(8,128)(2,1)S(1)} %pad_maximum_fusion.3), channel_id=1, source_target_pairs={{0,0},{1,16},{4,4},{5,20},{8,8},{9,24},{12,12},{13,28},{16,1},{17,... | collective-permute-start | bytes 1376264 | tf_op jit(solution)/shard_map/ppermute | solution.py:40
  20.8 0.8 copy-start.9
  21.6 386.5 %reduce-scatter.2.cloned.1.call-start = ((), (), s32[]{:S(2)}) async-start(), calls=%async_computation.1 | async-start | bytes 4128768 | tf_op jit(solution)/shard_map/reduce_scatter | solution.py:250
  23.1 52.0 %collective-permute-start = (bf16[1,4096]{1,0:T(2,128)(2,1)S(1)}, bf16[1,4096]{1,0:T(2,128)(2,1)S(1)}, u32[]{:S(2)}, u32[]{:S(2)}) collective-permute-start(bf16[1,4096]{1,0:T(2,128)(2,1)S(1)} %slice.65), channel_id=1, source_target_pairs={{1,0},{2,1},{3,2},{4,3},{5,4},{6,5},{7,6},{8,7},{9,8},{10,9},{11,1... | collective-permute-start | bytes 24584 | tf_op jit(solution)/shard_map/ppermute | solution.py:46
  25.4 134.8 %copy-start.4 = (bf16[31,4096]{1,0:T(8,128)(2,1)}, bf16[31,4096]{1,0:T(8,128)(2,1)S(1)}, u32[]{:S(2)}) copy-start(bf16[31,4096]{1,0:T(8,128)(2,1)S(1)} %slice.64) | copy-start | bytes 761860
  74.4 136.0 %collective-permute-start.14 = (bf16[8,896,256]{2,1,0:T(8,128)(2,1)}, bf16[8,896,256]{2,1,0:T(8,128)(2,1)S(1)}, u32[]{:S(2)}, u32[]{:S(2)}) collective-permute-start(bf16[8,896,256]{2,1,0:T(8,128)(2,1)} %bitcast.27), channel_id=1, source_target_pairs={{0,1},{1,0},{4,5},{5,4},{8,9},{9,8},{12,13},{13,12},{16,17},{17,16... | collective-permute-start | bytes 11010056 | tf_op jit(solution)/shard_map/ppermute | solution.py:33
  75.2 13.8 %collective-permute-start.3 = (bf16[2,16,4096]{2,1,0:T(8,128)(2,1)S(1)}, bf16[2,16,4096]{2,1,0:T(8,128)(2,1)S(1)}, u32[]{:S(2)}, u32[]{:S(2)}) collective-permute-start(bf16[2,16,4096]{2,1,0:T(8,128)(2,1)S(1)} %get-tuple-element.37), channel_id=1, source_target_pairs={{0,18},{1,19},{4,22},{5,23},{8,26},{9,27},{12,30},{13,31},{16,0},{... | collective-permute-start | bytes 786440 | tf_op jit(solution)/shard_map/ppermute | solution.py:28
  77.7 11.2 %collective-permute-start.2 = (bf16[2,16,4096]{2,1,0:T(8,128)(2,1)S(1)}, bf16[2,16,4096]{2,1,0:T(8,128)(2,1)S(1)}, u32[]{:S(2)}, u32[]{:S(2)}) collective-permute-start(bf16[2,16,4096]{2,1,0:T(8,128)(2,1)S(1)} %get-tuple-element.37), channel_id=1, source_target_pairs={{0,2},{1,3},{4,6},{5,7},{8,10},{9,11},{12,14},{13,15},{16,18},{17,... | collective-permute-start | bytes 786440 | tf_op jit(solution)/shard_map/ppermute | solution.py:28
  78.2 14.8 %collective-permute-start.1 = (bf16[2,16,4096]{2,1,0:T(8,128)(2,1)S(1)}, bf16[2,16,4096]{2,1,0:T(8,128)(2,1)S(1)}, u32[]{:S(2)}, u32[]{:S(2)}) collective-permute-start(bf16[2,16,4096]{2,1,0:T(8,128)(2,1)S(1)} %get-tuple-element.37), channel_id=1, source_target_pairs={{0,16},{1,17},{4,20},{5,21},{8,24},{9,25},{12,28},{13,29},{16,2},{... | collective-permute-start | bytes 786440 | tf_op jit(solution)/shard_map/ppermute | solution.py:28
  93.2 117.3 %copy-start.7 = (bf16[2,64,4096]{2,1,0:T(8,128)(2,1)}, bf16[2,64,4096]{2,1,0:T(8,128)(2,1)S(1)}, u32[]{:S(2)}) copy-start(bf16[2,64,4096]{2,1,0:T(8,128)(2,1)S(1)} %pad_maximum_fusion.refs_0_) | copy-start | bytes 3145732
  93.2 67.1 %collective-permute-start.6 = (bf16[2,64,4096]{2,1,0:T(8,128)(2,1)S(1)}, bf16[2,64,4096]{2,1,0:T(8,128)(2,1)S(1)}, u32[]{:S(2)}, u32[]{:S(2)}) collective-permute-start(bf16[2,64,4096]{2,1,0:T(8,128)(2,1)S(1)} %pad_maximum_fusion.refs_0_), channel_id=1, source_target_pairs={{0,12},{1,13},{4,0},{5,1},{8,4},{9,5},{12,8},{13,9},{16,28},{17,29... | collective-permute-start | bytes 3145736 | tf_op jit(solution)/shard_map/ppermute | solution.py:28
  95.7 65.3 %collective-permute-start.5 = (bf16[2,64,4096]{2,1,0:T(8,128)(2,1)S(1)}, bf16[2,64,4096]{2,1,0:T(8,128)(2,1)S(1)}, u32[]{:S(2)}, u32[]{:S(2)}) collective-permute-start(bf16[2,64,4096]{2,1,0:T(8,128)(2,1)S(1)} %pad_maximum_fusion.refs_0_), channel_id=1, source_target_pairs={{0,8},{1,9},{4,12},{5,13},{8,0},{9,1},{12,4},{13,5},{16,24},{17,25... | collective-permute-start | bytes 3145736 | tf_op jit(solution)/shard_map/ppermute | solution.py:28
  96.2 50.2 %collective-permute-start.9 = (bf16[2,16,4096]{2,1,0:T(8,128)(2,1)S(1)}, bf16[2,16,4096]{2,1,0:T(8,128)(2,1)S(1)}, u32[]{:S(2)}, u32[]{:S(2)}) collective-permute-start(bf16[2,16,4096]{2,1,0:T(8,128)(2,1)S(1)} %get-tuple-element.36), channel_id=1, source_target_pairs={{0,12},{1,13},{4,0},{5,1},{8,4},{9,5},{12,8},{13,9},{16,28},{17,29... | collective-permute-start | bytes 786440 | tf_op jit(solution)/shard_map/ppermute | solution.py:28
  97.1 49.7 %collective-permute-start.8 = (bf16[2,16,4096]{2,1,0:T(8,128)(2,1)S(1)}, bf16[2,16,4096]{2,1,0:T(8,128)(2,1)S(1)}, u32[]{:S(2)}, u32[]{:S(2)}) collective-permute-start(bf16[2,16,4096]{2,1,0:T(8,128)(2,1)S(1)} %get-tuple-element.36), channel_id=1, source_target_pairs={{0,8},{1,9},{4,12},{5,13},{8,0},{9,1},{12,4},{13,5},{16,24},{17,25... | collective-permute-start | bytes 786440 | tf_op jit(solution)/shard_map/ppermute | solution.py:28
  146.5 13.6 %collective-permute-start.7 = (bf16[2,16,4096]{2,1,0:T(8,128)(2,1)S(1)}, bf16[2,16,4096]{2,1,0:T(8,128)(2,1)S(1)}, u32[]{:S(2)}, u32[]{:S(2)}) collective-permute-start(bf16[2,16,4096]{2,1,0:T(8,128)(2,1)S(1)} %get-tuple-element.36), channel_id=1, source_target_pairs={{0,4},{1,5},{4,8},{5,9},{8,12},{9,13},{12,0},{13,1},{16,20},{17,21... | collective-permute-start | bytes 786440 | tf_op jit(solution)/shard_map/ppermute | solution.py:28
  146.8 35.8 %collective-permute-start.4 = (bf16[2,64,4096]{2,1,0:T(8,128)(2,1)S(1)}, bf16[2,64,4096]{2,1,0:T(8,128)(2,1)S(1)}, u32[]{:S(2)}, u32[]{:S(2)}) collective-permute-start(bf16[2,64,4096]{2,1,0:T(8,128)(2,1)S(1)} %pad_maximum_fusion.refs_0_), channel_id=1, source_target_pairs={{0,4},{1,5},{4,8},{5,9},{8,12},{9,13},{12,0},{13,1},{16,20},{17,21... | collective-permute-start | bytes 3145736 | tf_op jit(solution)/shard_map/ppermute | solution.py:28
  160.2 50.3 %copy-start.8 = (bf16[2,64,4096]{2,1,0:T(8,128)(2,1)}, bf16[2,64,4096]{2,1,0:T(8,128)(2,1)S(1)}, u32[]{:S(2)}) copy-start(bf16[2,64,4096]{2,1,0:T(8,128)(2,1)S(1)} %pad_maximum_fusion.1.refs_4_) | copy-start | bytes 3145732
  160.2 22.4 %collective-permute-start.12 = (bf16[2,64,4096]{2,1,0:T(8,128)(2,1)S(1)}, bf16[2,64,4096]{2,1,0:T(8,128)(2,1)S(1)}, u32[]{:S(2)}, u32[]{:S(2)}) collective-permute-start(bf16[2,64,4096]{2,1,0:T(8,128)(2,1)S(1)} %pad_maximum_fusion.1.refs_4_), channel_id=1, source_target_pairs={{0,18},{1,19},{4,22},{5,23},{8,26},{9,27},{12,30},{13,31},{16,0},{... | collective-permute-start | bytes 3145736 | tf_op jit(solution)/shard_map/ppermute | solution.py:28
  160.3 50.1 %copy-start.12 = (bf16[2,64,4096]{2,1,0:T(8,128)(2,1)}, bf16[2,64,4096]{2,1,0:T(8,128)(2,1)S(1)}, u32[]{:S(2)}) copy-start(bf16[2,64,4096]{2,1,0:T(8,128)(2,1)S(1)} %collective-permute-done.6.refs_3_) | copy-start | bytes 3145732
  160.3 22.8 %collective-permute-start.11 = (bf16[2,64,4096]{2,1,0:T(8,128)(2,1)S(1)}, bf16[2,64,4096]{2,1,0:T(8,128)(2,1)S(1)}, u32[]{:S(2)}, u32[]{:S(2)}) collective-permute-start(bf16[2,64,4096]{2,1,0:T(8,128)(2,1)S(1)} %pad_maximum_fusion.1.refs_4_), channel_id=1, source_target_pairs={{0,2},{1,3},{4,6},{5,7},{8,10},{9,11},{12,14},{13,15},{16,18},{17,... | collective-permute-start | bytes 3145736 | tf_op jit(solution)/shard_map/ppermute | solution.py:28
  160.9 49.5 %copy-start.13 = (bf16[2,64,4096]{2,1,0:T(8,128)(2,1)}, bf16[2,64,4096]{2,1,0:T(8,128)(2,1)S(1)}, u32[]{:S(2)}) copy-start(bf16[2,64,4096]{2,1,0:T(8,128)(2,1)S(1)} %collective-permute-done.5.refs_2_) | copy-start | bytes 3145732
  160.9 48.5 %collective-permute-start.10 = (bf16[2,64,4096]{2,1,0:T(8,128)(2,1)S(1)}, bf16[2,64,4096]{2,1,0:T(8,128)(2,1)S(1)}, u32[]{:S(2)}, u32[]{:S(2)}) collective-permute-start(bf16[2,64,4096]{2,1,0:T(8,128)(2,1)S(1)} %pad_maximum_fusion.1.refs_4_), channel_id=1, source_target_pairs={{0,16},{1,17},{4,20},{5,21},{8,24},{9,25},{12,28},{13,29},{16,2},{... | collective-permute-start | bytes 3145736 | tf_op jit(solution)/shard_map/ppermute | solution.py:28
  182.6 27.9 %copy-start.14 = (bf16[2,64,4096]{2,1,0:T(8,128)(2,1)}, bf16[2,64,4096]{2,1,0:T(8,128)(2,1)S(1)}, u32[]{:S(2)}) copy-start(bf16[2,64,4096]{2,1,0:T(8,128)(2,1)S(1)} %collective-permute-done.4.refs_1_) | copy-start | bytes 3145732
  182.6 27.9 %copy-start.15 = (bf16[2,64,4096]{2,1,0:T(8,128)(2,1)}, bf16[2,64,4096]{2,1,0:T(8,128)(2,1)S(1)}, u32[]{:S(2)}) copy-start(bf16[2,64,4096]{2,1,0:T(8,128)(2,1)S(1)} %collective-permute-done.12.refs_7_) | copy-start | bytes 3145732
  183.1 26.4 %copy-start.16 = (bf16[2,64,4096]{2,1,0:T(8,128)(2,1)}, bf16[2,64,4096]{2,1,0:T(8,128)(2,1)S(1)}, u32[]{:S(2)}) copy-start(bf16[2,64,4096]{2,1,0:T(8,128)(2,1)S(1)} %collective-permute-done.11.refs_6_) | copy-start | bytes 3145732
  209.5 1.0 copy-start.17
  210.5 1.9 copy-start.11
  233.0 6.8 %collective-permute-start.28 = (bf16[8,896,256]{2,1,0:T(8,128)(2,1)}, bf16[8,896,256]{2,1,0:T(8,128)(2,1)S(1)}, u32[]{:S(2)}, u32[]{:S(2)}) collective-permute-start(bf16[8,896,256]{2,1,0:T(8,128)(2,1)} %get-tuple-element.26), channel_id=1, source_target_pairs={{0,1},{1,0},{4,5},{5,4},{8,9},{9,8},{12,13},{13,12},{16,17},{17,16... | collective-permute-start | bytes 11010056 | tf_op jit(solution)/shard_map/ppermute | solution.py:33
  233.6 127.1 %collective-permute-start.15 = (bf16[2,64,4096]{2,1,0:T(8,128)(2,1)}, bf16[2,64,4096]{2,1,0:T(8,128)(2,1)}, u32[]{:S(2)}, u32[]{:S(2)}) collective-permute-start(bf16[2,64,4096]{2,1,0:T(8,128)(2,1)} %get-tuple-element.17), channel_id=1, source_target_pairs={{0,12},{1,13},{4,0},{5,1},{8,4},{9,5},{12,8},{13,9},{16,28},{17,29... | collective-permute-start | bytes 3145736 | tf_op jit(solution)/shard_map/ppermute | solution.py:28
  234.8 126.5 %collective-permute-start.16 = (bf16[2,64,4096]{2,1,0:T(8,128)(2,1)}, bf16[2,64,4096]{2,1,0:T(8,128)(2,1)}, u32[]{:S(2)}, u32[]{:S(2)}) collective-permute-start(bf16[2,64,4096]{2,1,0:T(8,128)(2,1)} %get-tuple-element.18), channel_id=1, source_target_pairs={{0,8},{1,9},{4,12},{5,13},{8,0},{9,1},{12,4},{13,5},{16,24},{17,25... | collective-permute-start | bytes 3145736 | tf_op jit(solution)/shard_map/ppermute | solution.py:28
  234.8 126.5 %collective-permute-start.17 = (bf16[2,64,4096]{2,1,0:T(8,128)(2,1)S(1)}, bf16[2,64,4096]{2,1,0:T(8,128)(2,1)}, u32[]{:S(2)}, u32[]{:S(2)}) collective-permute-start(bf16[2,64,4096]{2,1,0:T(8,128)(2,1)S(1)} %get-tuple-element.19), channel_id=1, source_target_pairs={{0,4},{1,5},{4,8},{5,9},{8,12},{9,13},{12,0},{13,1},{16,20},{17,21... | collective-permute-start | bytes 3145736 | tf_op jit(solution)/shard_map/ppermute | solution.py:28
  244.6 0.7 copy-start.10
  245.3 120.7 %collective-permute-start.21 = (bf16[2,64,4096]{2,1,0:T(8,128)(2,1)}, bf16[2,64,4096]{2,1,0:T(8,128)(2,1)}, u32[]{:S(2)}, u32[]{:S(2)}) collective-permute-start(bf16[2,64,4096]{2,1,0:T(8,128)(2,1)} %get-tuple-element.21), channel_id=1, source_target_pairs={{0,18},{1,19},{4,22},{5,23},{8,26},{9,27},{12,30},{13,31},{16,0},{... | collective-permute-start | bytes 3145736 | tf_op jit(solution)/shard_map/ppermute | solution.py:28
  247.1 120.2 %collective-permute-start.22 = (bf16[2,64,4096]{2,1,0:T(8,128)(2,1)}, bf16[2,64,4096]{2,1,0:T(8,128)(2,1)}, u32[]{:S(2)}, u32[]{:S(2)}) collective-permute-start(bf16[2,64,4096]{2,1,0:T(8,128)(2,1)} %get-tuple-element.22), channel_id=1, source_target_pairs={{0,2},{1,3},{4,6},{5,7},{8,10},{9,11},{12,14},{13,15},{16,18},{17,... | collective-permute-start | bytes 3145736 | tf_op jit(solution)/shard_map/ppermute | solution.py:28
  360.7 25.5 %collective-permute-start.23 = (bf16[2,64,4096]{2,1,0:T(8,128)(2,1)}, bf16[2,64,4096]{2,1,0:T(8,128)(2,1)S(1)}, u32[]{:S(2)}, u32[]{:S(2)}) collective-permute-start(bf16[2,64,4096]{2,1,0:T(8,128)(2,1)} %get-tuple-element.23), channel_id=1, source_target_pairs={{0,16},{1,17},{4,20},{5,21},{8,24},{9,25},{12,28},{13,29},{16,2},{... | collective-permute-start | bytes 3145736 | tf_op jit(solution)/shard_map/ppermute | solution.py:28
  363.8 26.1 %collective-permute-start.18 = (bf16[2,16,4096]{2,1,0:T(8,128)(2,1)S(1)}, bf16[2,16,4096]{2,1,0:T(8,128)(2,1)S(1)}, u32[]{:S(2)}, u32[]{:S(2)}) collective-permute-start(bf16[2,16,4096]{2,1,0:T(8,128)(2,1)S(1)} %get-tuple-element.33), channel_id=1, source_target_pairs={{0,18},{1,19},{4,22},{5,23},{8,26},{9,27},{12,30},{13,31},{16,0},{... | collective-permute-start | bytes 786440 | tf_op jit(solution)/shard_map/ppermute | solution.py:28
  366.0 26.1 %collective-permute-start.20 = (bf16[2,16,4096]{2,1,0:T(8,128)(2,1)S(1)}, bf16[2,16,4096]{2,1,0:T(8,128)(2,1)S(1)}, u32[]{:S(2)}, u32[]{:S(2)}) collective-permute-start(bf16[2,16,4096]{2,1,0:T(8,128)(2,1)S(1)} %get-tuple-element.34), channel_id=1, source_target_pairs={{0,16},{1,17},{4,20},{5,21},{8,24},{9,25},{12,28},{13,29},{16,2},{... | collective-permute-start | bytes 786440 | tf_op jit(solution)/shard_map/ppermute | solution.py:28
  366.0 31.1 %collective-permute-start.19 = (bf16[2,16,4096]{2,1,0:T(8,128)(2,1)S(1)}, bf16[2,16,4096]{2,1,0:T(8,128)(2,1)S(1)}, u32[]{:S(2)}, u32[]{:S(2)}) collective-permute-start(bf16[2,16,4096]{2,1,0:T(8,128)(2,1)S(1)} %get-tuple-element.35), channel_id=1, source_target_pairs={{0,2},{1,3},{4,6},{5,7},{8,10},{9,11},{12,14},{13,15},{16,18},{17,... | collective-permute-start | bytes 786440 | tf_op jit(solution)/shard_map/ppermute | solution.py:28
  388.4 8.8 %collective-permute-start.24 = (bf16[2,16,4096]{2,1,0:T(8,128)(2,1)S(1)}, bf16[2,16,4096]{2,1,0:T(8,128)(2,1)S(1)}, u32[]{:S(2)}, u32[]{:S(2)}) collective-permute-start(bf16[2,16,4096]{2,1,0:T(8,128)(2,1)S(1)} %get-tuple-element.30), channel_id=1, source_target_pairs={{0,12},{1,13},{4,0},{5,1},{8,4},{9,5},{12,8},{13,9},{16,28},{17,29... | collective-permute-start | bytes 786440 | tf_op jit(solution)/shard_map/ppermute | solution.py:28
  389.7 9.8 %collective-permute-start.26 = (bf16[2,16,4096]{2,1,0:T(8,128)(2,1)S(1)}, bf16[2,16,4096]{2,1,0:T(8,128)(2,1)S(1)}, u32[]{:S(2)}, u32[]{:S(2)}) collective-permute-start(bf16[2,16,4096]{2,1,0:T(8,128)(2,1)S(1)} %get-tuple-element.31), channel_id=1, source_target_pairs={{0,4},{1,5},{4,8},{5,9},{8,12},{9,13},{12,0},{13,1},{16,20},{17,21... | collective-permute-start | bytes 786440 | tf_op jit(solution)/shard_map/ppermute | solution.py:28
  389.9 20.6 %copy-start.1 = (bf16[128,4096]{1,0:T(8,128)(2,1)S(1)}, bf16[128,4096]{1,0:T(8,128)(2,1)}, u32[]{:S(2)}) copy-start(bf16[128,4096]{1,0:T(8,128)(2,1)} %param.11) | copy-start | bytes 3145732
  390.0 9.9 %collective-permute-start.25 = (bf16[2,16,4096]{2,1,0:T(8,128)(2,1)S(1)}, bf16[2,16,4096]{2,1,0:T(8,128)(2,1)S(1)}, u32[]{:S(2)}, u32[]{:S(2)}) collective-permute-start(bf16[2,16,4096]{2,1,0:T(8,128)(2,1)S(1)} %get-tuple-element.32), channel_id=1, source_target_pairs={{0,8},{1,9},{4,12},{5,13},{8,0},{9,1},{12,4},{13,5},{16,24},{17,25... | collective-permute-start | bytes 786440 | tf_op jit(solution)/shard_map/ppermute | solution.py:28
  400.2 0.7 copy-start.5
  400.2 12.8 %copy-start.3 = (bf16[128,4096]{1,0:T(8,128)(2,1)S(1)}, bf16[128,4096]{1,0:T(8,128)(2,1)}, u32[]{:S(2)}) copy-start(bf16[128,4096]{1,0:T(8,128)(2,1)} %param.6) | copy-start | bytes 3145732
  400.9 12.1 %collective-permute-start.27 = (bf16[1,4096]{1,0:T(2,128)(2,1)S(1)}, bf16[1,4096]{1,0:T(2,128)(2,1)S(1)}, u32[]{:S(2)}, u32[]{:S(2)}) collective-permute-start(bf16[1,4096]{1,0:T(2,128)(2,1)S(1)} %slice.76), channel_id=1, source_target_pairs={{0,1},{1,2},{2,3},{3,4},{4,5},{5,6},{6,7},{7,8},{8,9},{9,10},{10,1... | collective-permute-start | bytes 24584 | tf_op jit(solution)/shard_map/ppermute | solution.py:46
  408.2 4.8 %copy-start.6 = (bf16[32,4096]{1,0:T(8,128)(2,1)S(1)}, bf16[32,4096]{1,0:T(8,128)(2,1)}, u32[]{:S(2)}) copy-start(bf16[32,4096]{1,0:T(8,128)(2,1)} %copy-done.5) | copy-start | bytes 786436
  408.2 10.1 %collective-permute-start.29 = (bf16[896,256]{1,0:T(8,128)(2,1)}, bf16[896,256]{1,0:T(8,128)(2,1)S(1)}, u32[]{:S(2)}, u32[]{:S(2)}) collective-permute-start(bf16[896,256]{1,0:T(8,128)(2,1)} %bitcast.29), channel_id=1, source_target_pairs={{0,0},{1,16},{4,4},{5,20},{8,8},{9,24},{12,12},{13,28},{16,1},{17,... | collective-permute-start | bytes 1376264 | tf_op jit(solution)/shard_map/ppermute | solution.py:40
Sparse Core Ops, SparseCore 0:
  21.8 52.6 all-gather.2
  244.7 46.2 reduce-scatter.1

commit v2 on v1

--- a/solution.py
+++ b/solution.py
@@ -54,15 +54,20 @@
     return jnp.dot(a, b, preferred_element_type=jnp.float32)
 
 
-def block_kernel(n_blocks, chunks, *refs):
-    acts = refs[:n_blocks]
-    w_own, w_oth = refs[n_blocks : n_blocks + 2]
-    outs = refs[n_blocks + 2 : 2 * n_blocks + 2]
-    g_own, g_oth, gain = refs[2 * n_blocks + 2 : 2 * n_blocks + 5]
+def slots(refs):
+    s0, s1, p2, g2, s3 = refs
+    return [(s0.at[0], s0.at[1]), (s1.at[0], s1.at[1]), (p2, g2), (s3.at[0], s3.at[1])]
+
+
+def block_kernel(chunks, *refs):
+    acts = slots(refs[:5]) + slots(refs[5:10])
+    w_own, w_oth = refs[10:12]
+    outs = slots(refs[12:17]) + slots(refs[17:22])
+    g_own, g_oth, gain = refs[22:25]
     (p_s, g_s, wi_s, wo_s, d_s, n_s, gi_s, go_s, h_s, ga_s, sq_s, act, gp, act_t, gp_t, in_sem,
-     out_sem) = refs[2 * n_blocks + 5 :]
+     out_sem) = refs[25:]
     core = lax.axis_index("c")
-    rows = acts[0].shape[1]
+    rows = refs[0].shape[1]
     hidden = wi_s.shape[0]
     half = w_own.shape[2]
     width = 2 * half
@@ -75,14 +80,12 @@
         return pl.ds(pl.multiple_of(z * width + which * half, half), half)
 
     def fetch(z, carry):
-        for i in range(n_blocks):
+        for i, pair in enumerate(acts):
             at = pl.ds(i * rows, rows)
-            pltpu.make_async_copy(
-                acts[i].at[0, :, cols(z)], p_s.at[at, cols(z)], in_sem.at[0, z]
-            ).start()
-            pltpu.make_async_copy(
-                acts[i].at[1, :, cols(z)], g_s.at[at, cols(z)], in_sem.at[1, z]
-            ).start()
+            for k, (source, buf) in enumerate(zip(pair, (p_s, g_s))):
+                pltpu.make_async_copy(
+                    source.at[:, cols(z)], buf.at[at, cols(z)], in_sem.at[k, z]
+                ).start()
         for source, which in ((w_own, core), (w_oth, 1 - core)):
             pltpu.make_async_copy(
                 source.at[z, pl.ds(0, hidden), :], wi_s.at[:, w_cols(z, which)], in_sem.at[2, z]
@@ -132,14 +135,12 @@
         gi = nn(gp_t[...], p_s[:, cols(z)])
         gi_s[:, cols(z)] = gi.astype(jnp.bfloat16)
         gain[:, cols(z)] = jnp.sum(gi * wi.astype(jnp.float32), axis=0, keepdims=True)
-        for i in range(n_blocks):
+        for i, pair in enumerate(outs):
             at = pl.ds(i * rows, rows)
-            pltpu.make_async_copy(
-                d_s.at[at, cols(z)], outs[i].at[0, :, cols(z)], out_sem.at[0, z]
-            ).start()
-            pltpu.make_async_copy(
-                n_s.at[at, cols(z)], outs[i].at[1, :, cols(z)], out_sem.at[1, z]
-            ).start()
+            for k, (dest, buf) in enumerate(zip(pair, (d_s, n_s))):
+                pltpu.make_async_copy(
+                    buf.at[at, cols(z)], dest.at[:, cols(z)], out_sem.at[k, z]
+                ).start()
         for dest, which in ((g_own, core), (g_oth, 1 - core)):
             pltpu.make_async_copy(
                 gi_s.at[:, w_cols(z, which)], dest.at[z, pl.ds(0, hidden), :], out_sem.at[2, z]
@@ -161,21 +162,20 @@
 
 
 def block(acts, w_own, w_oth):
-    n = len(acts)
     _, rows, feats = acts[0].shape
     chunks, hidden2, half = w_own.shape
     hidden = hidden2 // 2
-    total = n * rows
+    total = 8 * rows
     bf = jnp.bfloat16
     anywhere = pl.BlockSpec(memory_space=pl.ANY)
     flops = 12 * total * feats * hidden
     return pl.pallas_call(
-        functools.partial(block_kernel, n, chunks),
-        out_shape=[jax.ShapeDtypeStruct(acts[0].shape, bf)] * n
+        functools.partial(block_kernel, chunks),
+        out_shape=[jax.ShapeDtypeStruct(act.shape, bf) for act in acts]
         + [jax.ShapeDtypeStruct(w_own.shape, bf)] * 2
         + [jax.ShapeDtypeStruct((1, feats), jnp.float32)],
-        in_specs=[anywhere] * (n + 2),
-        out_specs=[anywhere] * (n + 2) + [pl.BlockSpec(memory_space=pltpu.VMEM)],
+        in_specs=[anywhere] * 12,
+        out_specs=[anywhere] * 12 + [pl.BlockSpec(memory_space=pltpu.VMEM)],
         scratch_shapes=[pltpu.VMEM((total, feats), bf)] * 2
         + [pltpu.VMEM((hidden, feats), bf)] * 2
         + [pltpu.VMEM((total, feats), bf)] * 2
@@ -192,12 +192,6 @@
     )(*acts, w_own, w_oth)
 
 
-def gather_plane(first, second):
-    a = jnp.concatenate([first] + [shift(first, dy=d) for d in (1, 2, 3)], axis=1)
-    b = jnp.concatenate([second] + [shift(second, dx=d) for d in (1, 2, 3)], axis=1)
-    return [a] + [shift(a, dx=d) for d in (1, 2, 3)] + [b] + [shift(b, dy=d) for d in (1, 2, 3)]
-
-
 def add_all(parts):
     total = parts[0].astype(jnp.float32)
     for part in parts[1:]:
@@ -205,14 +199,58 @@
     return total
 
 
-def scatter_plane(blocks, rows):
-    a = add_all([blocks[0]] + [shift(blocks[d], dx=-d) for d in (1, 2, 3)]).astype(jnp.bfloat16)
-    b = add_all([blocks[4]] + [shift(blocks[4 + d], dy=-d) for d in (1, 2, 3)]).astype(jnp.bfloat16)
+def by_x(value, d):
+    return shift(value, dx=d)
+
+
+def by_y(value, d):
+    return shift(value, dy=d)
+
+
+def gather_plane(first, second):
+    a = jnp.concatenate([first] + [by_y(first, d) for d in (1, 2, 3)], axis=1)
+    b = jnp.concatenate([second] + [by_x(second, d) for d in (1, 2, 3)], axis=1)
+    a, b = lax.optimization_barrier((a, b))
+    a1, a3, b1, b3 = by_x(a, 1), by_x(a, -1), by_y(b, 1), by_y(b, -1)
+    a2, b2 = (by_x(a1[0], 1), by_x(a3[1], -1)), (by_y(b1[0], 1), by_y(b3[1], -1))
+    return [a, a1, *a2, a3, b, b1, *b2, b3], (a, b)
+
+
+def fold(half, move):
+    s0, s1, d2, n2, s3 = half
+    bf = jnp.bfloat16
+    d2, n2 = move(d2, -1), move(n2, 1)
+    s1 = jnp.stack([add_all([s1[0], d2]).astype(bf), s1[1]])
+    s3 = jnp.stack([s3[0], add_all([s3[1], n2]).astype(bf)])
+    return s1, s3
+
+
+def scatter_plane(outs, rows, gain_part, weight_part):
+    sends = (*fold(outs[:5], by_x), *fold(outs[5:], by_y), gain_part, weight_part)
+    a1, a3, b1, b3, gain_part, weight_part = lax.optimization_barrier(sends)
+    weight_sum = lax.psum_scatter(weight_part, "z", scatter_dimension=0, tiled=False)
+    a1, a3, b1, b3 = by_x(a1, -1), by_x(a3, 1), by_y(b1, -1), by_y(b3, 1)
+    arrived = (a1, a3, b1, b3, total_over_all(gain_part), weight_sum)
+    a1, a3, b1, b3, grad_gain, weight_sum = lax.optimization_barrier(arrived)
+    a = add_all([outs[0], a1, a3]).astype(jnp.bfloat16)
+    b = add_all([outs[5], b1, b3]).astype(jnp.bfloat16)
     a = [a[:, d * rows : (d + 1) * rows] for d in range(4)]
     b = [b[:, d * rows : (d + 1) * rows] for d in range(4)]
-    a = add_all([a[0]] + [shift(a[d], dy=-d) for d in (1, 2, 3)])
-    b = add_all([b[0]] + [shift(b[d], dx=-d) for d in (1, 2, 3)])
-    return jnp.concatenate([a, b], axis=1)
+    a = add_all([a[0]] + [by_y(a[d], -d) for d in (1, 2, 3)])
+    b = add_all([b[0]] + [by_x(b[d], -d) for d in (1, 2, 3)])
+    return jnp.concatenate([a, b], axis=1), grad_gain, weight_sum
+
+
+def total_over_all(value):
+    moves = [lambda p, k=k: (p[0] ^ k, p[1], p[2], p[3]) for k in (1, 2, 4)]
+    moves += [lambda p: (p[0], p[1], p[2], 1 - p[3])]
+    moves += [lambda p, k=k: (p[0], p[1] ^ k, p[2], p[3]) for k in (1, 2)]
+    moves += [lambda p, k=k: (p[0], p[1], p[2] ^ k, p[3]) for k in (1, 2)]
+    for move in moves:
+        value = value + lax.ppermute(
+            value, AXES, [(linear(*p), linear(*move(p))) for p in places()]
+        )
+    return value
 
 
 def shards(stream, doc_start, norm_gain, weight_in, weight_out, upstream):
@@ -241,18 +279,17 @@
 
     acts = jnp.stack([pooled, grad_coarse], axis=0)
     rows = groups // 2
-    blocks = gather_plane(acts[:, :rows], acts[:, rows:])
+    blocks, begun = gather_plane(acts[:, :rows], acts[:, rows:])
+    w_own = lax.optimization_barrier((w_own, *begun))[0]
     w_oth = other_core(w_own)
     results = block(blocks, w_own, w_oth)
-    outs, (g_own, g_oth, gain_part) = results[:8], results[8:]
+    outs, (g_own, g_oth, gain_part) = results[:10], results[10:]
 
     mine = (g_own.astype(jnp.float32) + other_core(g_oth).astype(jnp.float32)).astype(bf)
-    grads = swap_low(lax.psum_scatter(mine, "z", scatter_dimension=0, tiled=False))
+    (down_sum, scaled), grad_gain, grads = scatter_plane(outs, rows, gain_part[0] / norm_gain, mine)
+    grads = swap_low(grads)
     grad_weight_in = (grads[:hidden].astype(jnp.float32) * gain[None, :]).T
     grad_weight_out = grads[hidden:].astype(jnp.float32)
-    grad_gain = lax.psum(gain_part[0] / norm_gain, AXES)
-
-    down_sum, scaled = scatter_plane(outs, rows)
     pooled_f = pooled.astype(jnp.float32)
     inv_sq = 1.0 / (jnp.mean(pooled_f * pooled_f, axis=1, keepdims=True) + 1e-05)
     coarse = (pooled_f + down_sum).astype(bf)

time: 427 us -> 246 us (0.58)
  blocking collectives: 114 us -> 0 us
  waiting for transfers between devices: 207 us -> 93.6 us
  starting transfers between devices: 45.5 us -> 82.8 us
  local copies, waits for them, and re-layouts: 6.39 us -> 11.8 us
    psum x1 -> x0, blocking collectives: 114 us -> none  [shards(): grad_gain = lax.psum(gain_part[0] / norm_gain, AXES)]
    ppermute x24 -> x28, waiting for transfers between devices: 144 us -> 37 us  [shift(): return lax.ppermute(value, AXES, pairs)]
    all_gather x1, waiting for transfers between devices: 49 us -> 16.8 us  [shards(): w_own = lax.all_gather(both, 'z', axis=0, tiled=False)]
    ppermute x0 -> x8, starting transfers between devices: none -> 22 us  [total_over_all(): lax.ppermute(value, AXES, [(linear(*p), linear(*move(p))) for p in places...]
    ppermute x0 -> x8, waiting for transfers between devices: none -> 17.6 us  [total_over_all(): lax.ppermute(value, AXES, [(linear(*p), linear(*move(p))) for p in places...]
    reduce_scatter x1, waiting for transfers between devices: 0.02 us -> 11.7 us  [scatter_plane(): lax.psum_scatter(weight_part, 'z', scatter_dimension=0, tiled=False)]
    ppermute x24 -> x28, starting transfers between devices: 28.1 us -> 35.8 us  [shift(): return lax.ppermute(value, AXES, pairs)]
    another operation x0 -> x8, other arithmetic: none -> 4.81 us  [the longest x4 2.45 us: fold(): s3 = jnp.stack([s3[0], add_all([s3[1], n2]).astype(bf)])]
  transfers between devices with their start and end apart: 32 -> 44, of which waited for: 16 -> 23; matrix products, arithmetic and copies ran while one was open for 4% -> 9% of each run, Pallas kernels for 0% -> 0%
where the time goes in v2:
time: 246 us; the launch traced here: 245 us
  waiting for transfers between devices  93.6 us (38%)
  starting transfers between devices  82.8 us (34%)
  Pallas kernels  20.5 us (8%)
  other arithmetic  18.3 us (7%)
  between operations  14.5 us (6%)
  local copies, waits for them, and re-layouts  11.8 us (5%)
  matrix products  3.44 us (1%)
    ppermute x28, waiting for transfers between devices, shift(): return lax.ppermute(value, AXES, pairs)  37 us
    ppermute x28, starting transfers between devices, shift(): return lax.ppermute(value, AXES, pairs)  35.8 us
    ppermute x8, starting transfers between devices, total_over_all(): lax.ppermute(value, AXES, [(linear(*p), linear(*move(p))) for p in places...  22 us
    pallas_call x1, Pallas kernels, block(): pl.pallas_call(functools.partial(block_kernel, chunks), out_shape=[jax.Sh...  20.5 us
    ppermute x8, waiting for transfers between devices, total_over_all(): lax.ppermute(value, AXES, [(linear(*p), linear(*move(p))) for p in places...  17.6 us
    all_gather x1, waiting for transfers between devices, shards(): w_own = lax.all_gather(both, 'z', axis=0, tiled=False)  16.8 us
    reduce_scatter x1, waiting for transfers between devices, scatter_plane(): lax.psum_scatter(weight_part, 'z', scatter_dimension=0, tiled=False)  11.7 us
    ppermute x2, starting transfers between devices, from_behind(): return lax.ppermute(value, AXES, pairs)  11 us
  transfers between devices with their start and end apart: 44, of which 23 were waited for; matrix products, arithmetic and copies ran while one was open for 9% of the time, Pallas kernels for 0%

profile of v2, /device:TPU:1, one launch (start us, length us, event | category | flops | bytes accessed | tf_op | source)
XLA Modules:
  0.0 245.0 jit_solution(7867472178458231792)
XLA Ops:
  8.1 1.0 fusion.27
  10.1 4.6 %collective-permute-start.15 = (bf16[896,256]{1,0:T(8,128)(2,1)S(1)}, bf16[896,256]{1,0:T(8,128)(2,1)S(1)}, u32[]{:S(2)}, u32[]{:S(2)}) collective-permute-start(bf16[896,256]{1,0:T(8,128)(2,1)S(1)} %pad_maximum_fusion.7), channel_id=1, source_target_pairs={{0,0},{1,16},{4,4},{5,20},{8,8},{9,24},{12,12},{13,28},{16,1},{17,... | collective-permute-start | bytes 1376264 | tf_op jit(solution)/shard_map/ppermute | solution.py:40
  14.7 6.1 %collective-permute-done.15 = bf16[896,256]{1,0:T(8,128)(2,1)S(1)} collective-permute-done((bf16[896,256]{1,0:T(8,128)(2,1)S(1)}, bf16[896,256]{1,0:T(8,128)(2,1)S(1)}, u32[]{:S(2)}, u32[]{:S(2)}) %collective-permute-start.15) | collective-permute-done | bytes 458784 | tf_op jit(solution)/shard_map/ppermute | solution.py:40
  23.1 1.9 collective-permute-start
  25.4 4.3 %collective-permute-done = bf16[1,4096]{1,0:T(2,128)(2,1)S(1)} collective-permute-done((bf16[1,4096]{1,0:T(2,128)(2,1)S(1)}, bf16[1,4096]{1,0:T(2,128)(2,1)S(1)}, u32[]{:S(2)}, u32[]{:S(2)}) %collective-permute-start) | collective-permute-done | bytes 8224 | tf_op jit(solution)/shard_map/ppermute | solution.py:46
  29.7 2.6 %collective-permute-start.6 = (bf16[2,16,4096]{2,1,0:T(8,128)(2,1)S(1)}, bf16[2,16,4096]{2,1,0:T(8,128)(2,1)S(1)}, u32[]{:S(2)}, u32[]{:S(2)}) collective-permute-start(bf16[2,16,4096]{2,1,0:T(8,128)(2,1)S(1)} %get-tuple-element.70), channel_id=1, source_target_pairs={{0,12},{1,13},{4,0},{5,1},{8,4},{9,5},{12,8},{13,9},{16,28},{17,29... | collective-permute-start | bytes 786440 | tf_op jit(solution)/shard_map/ppermute | solution.py:28
  33.4 1.5 collective-permute-start.3
  34.9 2.2 collective-permute-start.2
  37.1 6.1 %collective-permute-done.6 = bf16[2,16,4096]{2,1,0:T(8,128)(2,1)S(1)} collective-permute-done((bf16[2,16,4096]{2,1,0:T(8,128)(2,1)S(1)}, bf16[2,16,4096]{2,1,0:T(8,128)(2,1)S(1)}, u32[]{:S(2)}, u32[]{:S(2)}) %collective-permute-start.6) | collective-permute-done | bytes 262176 | tf_op jit(solution)/shard_map/ppermute | solution.py:28
  43.6 4.2 %collective-permute-done.4 = bf16[2,16,4096]{2,1,0:T(8,128)(2,1)S(1)} collective-permute-done((bf16[2,16,4096]{2,1,0:T(8,128)(2,1)S(1)}, bf16[2,16,4096]{2,1,0:T(8,128)(2,1)S(1)}, u32[]{:S(2)}, u32[]{:S(2)}) %collective-permute-start.4) | collective-permute-done | bytes 262176 | tf_op jit(solution)/shard_map/ppermute | solution.py:28
  47.9 3.3 %collective-permute-done.1 = bf16[2,16,4096]{2,1,0:T(8,128)(2,1)S(1)} collective-permute-done((bf16[2,16,4096]{2,1,0:T(8,128)(2,1)S(1)}, bf16[2,16,4096]{2,1,0:T(8,128)(2,1)S(1)}, u32[]{:S(2)}, u32[]{:S(2)}) %collective-permute-start.1) | collective-permute-done | bytes 262176 | tf_op jit(solution)/shard_map/ppermute | solution.py:28
  51.2 1.0 pad_maximum_fusion.refs_0_
  52.2 3.9 %collective-permute-start.9 = (bf16[2,64,4096]{2,1,0:T(8,128)(2,1)}, bf16[2,64,4096]{2,1,0:T(8,128)(2,1)}, u32[]{:S(2)}, u32[]{:S(2)}) collective-permute-start(bf16[2,64,4096]{2,1,0:T(8,128)(2,1)} %pad_maximum_fusion.refs_0_), channel_id=1, source_target_pairs={{0,12},{1,13},{4,0},{5,1},{8,4},{9,5},{12,8},{13,9},{16,28},{17,29... | collective-permute-start | bytes 3145736 | tf_op jit(solution)/shard_map/ppermute | solution.py:28
  56.1 1.5 collective-permute-start.11
  57.6 16.8 %all-gather.3.cloned.1.call-done = bf16[7168,256]{1,0:T(8,128)(2,1)} async-done(((bf16[896,256]{1,0:T(8,128)(2,1)}), bf16[7168,256]{1,0:T(8,128)(2,1)}) %all-gather.3.cloned.1.call-update) | async-done | bytes 3670032 | tf_op jit(solution)/shard_map/all_gather | solution.py:267
  75.1 2.1 collective-permute-done.9.refs_4_
  77.2 1.1 slice_bitcast_fusion.2
  78.2 3.5 %collective-permute-start.10 = (bf16[64,4096]{1,0:T(8,128)(2,1)S(1)}, bf16[64,4096]{1,0:T(8,128)(2,1)S(1)}, u32[]{:S(2)}, u32[]{:S(2)}) collective-permute-start(bf16[64,4096]{1,0:T(8,128)(2,1)S(1)} %slice_bitcast_fusion.2), channel_id=1, source_target_pairs={{0,12},{1,13},{4,0},{5,1},{8,4},{9,5},{12,8},{13,9},{16,28},{17,29... | collective-permute-start | bytes 1572872 | tf_op jit(solution)/shard_map/ppermute | solution.py:28
  81.7 1.1 slice_bitcast_fusion.3
  82.9 1.1 slice_bitcast_fusion
  84.1 1.1 slice_bitcast_fusion.1
  85.2 1.7 collective-permute-start.12
  86.9 3.4 %collective-permute-done.10.refs_3_ = bf16[64,4096]{1,0:T(8,128)(2,1)S(1)} collective-permute-done((bf16[64,4096]{1,0:T(8,128)(2,1)S(1)}, bf16[64,4096]{1,0:T(8,128)(2,1)S(1)}, u32[]{:S(2)}, u32[]{:S(2)}) %collective-permute-start.10) | collective-permute-done | bytes 524320 | tf_op jit(solution)/shard_map/ppermute | solution.py:28
  90.3 4.3 %collective-permute-done.8.refs_2_ = bf16[64,4096]{1,0:T(8,128)(2,1)S(1)} collective-permute-done((bf16[64,4096]{1,0:T(8,128)(2,1)S(1)}, bf16[64,4096]{1,0:T(8,128)(2,1)S(1)}, u32[]{:S(2)}, u32[]{:S(2)}) %collective-permute-start.8) | collective-permute-done | bytes 524320 | tf_op jit(solution)/shard_map/ppermute | solution.py:28
  94.6 2.6 %collective-permute-done.12.refs_7_ = bf16[64,4096]{1,0:T(8,128)(2,1)S(1)} collective-permute-done((bf16[64,4096]{1,0:T(8,128)(2,1)S(1)}, bf16[64,4096]{1,0:T(8,128)(2,1)S(1)}, u32[]{:S(2)}, u32[]{:S(2)}) %collective-permute-start.12) | collective-permute-done | bytes 524320 | tf_op jit(solution)/shard_map/ppermute | solution.py:28
  97.1 1.9 copy-done.13
  99.0 20.5 %shard_map.101 = (bf16[2,64,4096]{2,1,0:T(8,128)(2,1)S(1)}, bf16[2,64,4096]{2,1,0:T(8,128)(2,1)}, bf16[64,4096]{1,0:T(8,128)(2,1)S(1)}, bf16[64,4096]{1,0:T(8,12...) custom-call(bf16[2,64,4096]{2,1,0:T(8,128)(2,1)} %pad_maximum_fusion, ...), custom_call_target="tpu_custom_call" | custom-call | flops 11274289152 | bytes 62914560 | tf_op jit(solution)/shard_map/pallas_call | solution.py:172
  119.5 2.4 collective-permute-start.17
  122.0 1.2 slice.93
  123.2 1.1 slice.94
  124.6 1.5 collective-permute-start.20
  126.0 5.0 %collective-permute-start.21 = (bf16[8,896,256]{2,1,0:T(8,128)(2,1)}, bf16[8,896,256]{2,1,0:T(8,128)(2,1)S(1)}, u32[]{:S(2)}, u32[]{:S(2)}) collective-permute-start(bf16[8,896,256]{2,1,0:T(8,128)(2,1)} %get-tuple-element.47), channel_id=1, source_target_pairs={{0,1},{1,0},{4,5},{5,4},{8,9},{9,8},{12,13},{13,12},{16,17},{17,16... | collective-permute-start | bytes 11010056 | tf_op jit(solution)/shard_map/ppermute | solution.py:33
  131.1 3.5 %collective-permute-done.18 = bf16[64,4096]{1,0:T(8,128)(2,1)S(1)} collective-permute-done((bf16[64,4096]{1,0:T(8,128)(2,1)S(1)}, bf16[64,4096]{1,0:T(8,128)(2,1)S(1)}, u32[]{:S(2)}, u32[]{:S(2)}) %collective-permute-start.18) | collective-permute-done | bytes 524320 | tf_op jit(solution)/shard_map/ppermute | solution.py:28
  134.8 1.0 pad_maximum_fusion.2
  136.0 1.1 pad_maximum_fusion.3
  137.1 1.1 pad_maximum_fusion.4
  138.3 1.1 pad_maximum_fusion.5
  139.4 1.2 copy-done.2
  140.6 2.7 %add_convert_fusion = bf16[8,896,256]{2,1,0:T(8,128)(2,1)} fusion(bf16[8,896,256]{2,1,0:T(8,128)(2,1)S(1)} %collective-permute-done.21, bf16[8,896,256]{2,1,0:T(8,128)(2,1)S(1)} %copy-done.2), kind=kLoop, calls=%fused_computation | loop fusion | flops 7340032 | bytes 11010048 | tf_op jit(solution)/shard_map/convert_element_type | solution.py:288
  143.4 1.5 collective-permute-start.23
  146.3 2.5 %collective-permute-start.26 = (f32[4096]{0:T(1024)S(1)}, f32[4096]{0:T(1024)S(1)}, u32[]{:S(2)}, u32[]{:S(2)}) collective-permute-start(f32[4096]{0:T(1024)S(1)} %div.35), channel_id=1, source_target_pairs={{0,32},{1,33},{4,36},{5,37},{8,40},{9,41},{12,44},{13,45},{16,48},... | collective-permute-start | bytes 49160 | tf_op jit(solution)/shard_map/ppermute | solution.py:250
  148.8 1.1 collective-permute-done.26
  149.9 2.8 %collective-permute-start.27 = (f32[4096]{0:T(1024)S(1)}, f32[4096]{0:T(1024)S(1)}, u32[]{:S(2)}, u32[]{:S(2)}) collective-permute-start(f32[4096]{0:T(1024)S(1)} %add.109), channel_id=1, source_target_pairs={{0,64},{1,65},{4,68},{5,69},{8,72},{9,73},{12,76},{13,77},{16,80},... | collective-permute-start | bytes 49160 | tf_op jit(solution)/shard_map/ppermute | solution.py:250
  152.7 1.5 collective-permute-done.27
  154.3 5.2 %collective-permute-start.28 = (f32[4096]{0:T(1024)S(1)}, f32[4096]{0:T(1024)S(1)}, u32[]{:S(2)}, u32[]{:S(2)}) collective-permute-start(f32[4096]{0:T(1024)S(1)} %add.110), channel_id=1, source_target_pairs={{0,128},{1,129},{4,132},{5,133},{8,136},{9,137},{12,140},{13,141},... | collective-permute-start | bytes 49160 | tf_op jit(solution)/shard_map/ppermute | solution.py:250
  159.4 1.3 collective-permute-done.28
  160.8 10.1 %collective-permute-start.29 = (f32[4096]{0:T(1024)S(1)}, f32[4096]{0:T(1024)S(1)}, u32[]{:S(2)}, u32[]{:S(2)}) collective-permute-start(f32[4096]{0:T(1024)S(1)} %add.111), channel_id=1, source_target_pairs={{0,1},{1,0},{4,5},{5,4},{8,9},{9,8},{12,13},{13,12},{16,17},{17,16... | collective-permute-start | bytes 49160 | tf_op jit(solution)/shard_map/ppermute | solution.py:250
  171.7 3.0 %collective-permute-done.30 = f32[4096]{0:T(1024)S(1)} collective-permute-done((f32[4096]{0:T(1024)S(1)}, f32[4096]{0:T(1024)S(1)}, u32[]{:S(2)}, u32[]{:S(2)}) %collective-permute-start.30) | collective-permute-done | bytes 16416 | tf_op jit(solution)/shard_map/ppermute | solution.py:250
  175.3 3.5 %collective-permute-done.31 = f32[4096]{0:T(1024)S(1)} collective-permute-done((f32[4096]{0:T(1024)S(1)}, f32[4096]{0:T(1024)S(1)}, u32[]{:S(2)}, u32[]{:S(2)}) %collective-permute-start.31) | collective-permute-done | bytes 16416 | tf_op jit(solution)/shard_map/ppermute | solution.py:250
  178.8 3.0 %collective-permute-done.32 = f32[4096]{0:T(1024)S(1)} collective-permute-done((f32[4096]{0:T(1024)S(1)}, f32[4096]{0:T(1024)S(1)}, u32[]{:S(2)}, u32[]{:S(2)}) %collective-permute-start.32) | collective-permute-done | bytes 16416 | tf_op jit(solution)/shard_map/ppermute | solution.py:250
  182.6 3.3 %collective-permute-done.33 = f32[4096]{0:T(1024)S(1)} collective-permute-done((f32[4096]{0:T(1024)S(1)}, f32[4096]{0:T(1024)S(1)}, u32[]{:S(2)}, u32[]{:S(2)}) %collective-permute-start.33) | collective-permute-done | bytes 16416 | tf_op jit(solution)/shard_map/ppermute | solution.py:250
  186.5 11.7 %reduce-scatter.2.cloned.1.call-done = bf16[1,896,256]{2,1,0:T(8,128)(2,1)} async-done(((bf16[8,896,256]{2,1,0:T(8,128)(2,1)}), bf16[1,896,256]{2,1,0:T(8,128)(2,1)}) %reduce-scatter.2.cloned.1.call-update) | async-done | bytes 458768 | tf_op jit(solution)/shard_map/reduce_scatter | solution.py:231
  198.2 3.6 %collective-permute-start.41 = (bf16[896,256]{1,0:T(8,128)(2,1)}, bf16[896,256]{1,0:T(8,128)(2,1)S(1)}, u32[]{:S(2)}, u32[]{:S(2)}) collective-permute-start(bf16[896,256]{1,0:T(8,128)(2,1)} %bitcast.57), channel_id=1, source_target_pairs={{0,0},{1,16},{4,4},{5,20},{8,8},{9,24},{12,12},{13,28},{16,1},{17,... | collective-permute-start | bytes 1376264 | tf_op jit(solution)/shard_map/ppermute | solution.py:40
  201.9 2.1 add_convert_fusion.2
  205.6 2.4 collective-permute-start.35
  208.0 2.0 add_convert_fusion.1
  210.1 2.5 %collective-permute-start.37 = (bf16[2,16,4096]{2,1,0:T(8,128)(2,1)S(1)}, bf16[2,16,4096]{2,1,0:T(8,128)(2,1)S(1)}, u32[]{:S(2)}, u32[]{:S(2)}) collective-permute-start(bf16[2,16,4096]{2,1,0:T(8,128)(2,1)S(1)} %get-tuple-element.64), channel_id=1, source_target_pairs={{0,12},{1,13},{4,0},{5,1},{8,4},{9,5},{12,8},{13,9},{16,28},{17,29... | collective-permute-start | bytes 786440 | tf_op jit(solution)/shard_map/ppermute | solution.py:28
  212.6 1.1 collective-permute-start.39
  213.7 2.7 %collective-permute-start.38 = (bf16[2,16,4096]{2,1,0:T(8,128)(2,1)S(1)}, bf16[2,16,4096]{2,1,0:T(8,128)(2,1)S(1)}, u32[]{:S(2)}, u32[]{:S(2)}) collective-permute-start(bf16[2,16,4096]{2,1,0:T(8,128)(2,1)S(1)} %get-tuple-element.66), channel_id=1, source_target_pairs={{0,8},{1,9},{4,12},{5,13},{8,0},{9,1},{12,4},{13,5},{16,24},{17,25... | collective-permute-start | bytes 786440 | tf_op jit(solution)/shard_map/ppermute | solution.py:28
  216.4 5.2 %collective-permute-done.35 = bf16[2,16,4096]{2,1,0:T(8,128)(2,1)S(1)} collective-permute-done((bf16[2,16,4096]{2,1,0:T(8,128)(2,1)S(1)}, bf16[2,16,4096]{2,1,0:T(8,128)(2,1)S(1)}, u32[]{:S(2)}, u32[]{:S(2)}) %collective-permute-start.35) | collective-permute-done | bytes 262176 | tf_op jit(solution)/shard_map/ppermute | solution.py:28
  221.7 2.2 collective-permute-done.37
  224.5 9.1 %collective-permute-start.40 = (bf16[1,4096]{1,0:T(2,128)(2,1)S(1)}, bf16[1,4096]{1,0:T(2,128)(2,1)S(1)}, u32[]{:S(2)}, u32[]{:S(2)}) collective-permute-start(bf16[1,4096]{1,0:T(2,128)(2,1)S(1)} %slice.128), channel_id=1, source_target_pairs={{0,1},{1,2},{2,3},{3,4},{4,5},{5,6},{6,7},{7,8},{8,9},{9,10},{10,1... | collective-permute-start | bytes 24584 | tf_op jit(solution)/shard_map/ppermute | solution.py:46
  233.6 1.5 fusion.1
  235.1 1.4 fusion
  (112 shorter events, 16.1 us)
Async XLA Ops:
  7.2 15.6 %copy-start = (bf16[128,4096]{1,0:T(8,128)(2,1)S(1)}, bf16[128,4096]{1,0:T(8,128)(2,1)}, u32[]{:S(2)}) copy-start(bf16[128,4096]{1,0:T(8,128)(2,1)} %param.11) | copy-start | bytes 3145732
  7.2 17.8 %copy-start.1 = (bf16[128,4096]{1,0:T(8,128)(2,1)S(1)}, bf16[128,4096]{1,0:T(8,128)(2,1)}, u32[]{:S(2)}) copy-start(bf16[128,4096]{1,0:T(8,128)(2,1)} %param.6) | copy-start | bytes 3145732
  7.2 67.2 %all-gather.3.cloned.1.call-start = ((), (), s32[]{:S(2)}) async-start(), calls=%async_computation.2 | async-start | bytes 4128768 | tf_op jit(solution)/shard_map/all_gather | solution.py:267
  10.1 10.8 %collective-permute-start.15 = (bf16[896,256]{1,0:T(8,128)(2,1)S(1)}, bf16[896,256]{1,0:T(8,128)(2,1)S(1)}, u32[]{:S(2)}, u32[]{:S(2)}) collective-permute-start(bf16[896,256]{1,0:T(8,128)(2,1)S(1)} %pad_maximum_fusion.7), channel_id=1, source_target_pairs={{0,0},{1,16},{4,4},{5,20},{8,8},{9,24},{12,12},{13,28},{16,1},{17,... | collective-permute-start | bytes 1376264 | tf_op jit(solution)/shard_map/ppermute | solution.py:40
  20.8 0.8 copy-start.11
  21.6 176.6 %reduce-scatter.2.cloned.1.call-start = ((), (), s32[]{:S(2)}) async-start(), calls=%async_computation.1 | async-start | bytes 4128768 | tf_op jit(solution)/shard_map/reduce_scatter | solution.py:231
  23.1 6.6 %collective-permute-start = (bf16[1,4096]{1,0:T(2,128)(2,1)S(1)}, bf16[1,4096]{1,0:T(2,128)(2,1)S(1)}, u32[]{:S(2)}, u32[]{:S(2)}) collective-permute-start(bf16[1,4096]{1,0:T(2,128)(2,1)S(1)} %slice.113), channel_id=1, source_target_pairs={{1,0},{2,1},{3,2},{4,3},{5,4},{6,5},{7,6},{8,7},{9,8},{10,9},{11,1... | collective-permute-start | bytes 24584 | tf_op jit(solution)/shard_map/ppermute | solution.py:46
  25.4 4.3 %copy-start.3 = (bf16[31,4096]{1,0:T(8,128)(2,1)}, bf16[31,4096]{1,0:T(8,128)(2,1)S(1)}, u32[]{:S(2)}) copy-start(bf16[31,4096]{1,0:T(8,128)(2,1)S(1)} %slice.112) | copy-start | bytes 761860
  29.7 13.5 %collective-permute-start.6 = (bf16[2,16,4096]{2,1,0:T(8,128)(2,1)S(1)}, bf16[2,16,4096]{2,1,0:T(8,128)(2,1)S(1)}, u32[]{:S(2)}, u32[]{:S(2)}) collective-permute-start(bf16[2,16,4096]{2,1,0:T(8,128)(2,1)S(1)} %get-tuple-element.70), channel_id=1, source_target_pairs={{0,12},{1,13},{4,0},{5,1},{8,4},{9,5},{12,8},{13,9},{16,28},{17,29... | collective-permute-start | bytes 786440 | tf_op jit(solution)/shard_map/ppermute | solution.py:28
  32.3 11.3 %collective-permute-start.5 = (bf16[2,16,4096]{2,1,0:T(8,128)(2,1)S(1)}, bf16[2,16,4096]{2,1,0:T(8,128)(2,1)S(1)}, u32[]{:S(2)}, u32[]{:S(2)}) collective-permute-start(bf16[2,16,4096]{2,1,0:T(8,128)(2,1)S(1)} %get-tuple-element.70), channel_id=1, source_target_pairs={{0,8},{1,9},{4,12},{5,13},{8,0},{9,1},{12,4},{13,5},{16,24},{17,25... | collective-permute-start | bytes 786440 | tf_op jit(solution)/shard_map/ppermute | solution.py:28
  32.8 14.9 %collective-permute-start.4 = (bf16[2,16,4096]{2,1,0:T(8,128)(2,1)S(1)}, bf16[2,16,4096]{2,1,0:T(8,128)(2,1)S(1)}, u32[]{:S(2)}, u32[]{:S(2)}) collective-permute-start(bf16[2,16,4096]{2,1,0:T(8,128)(2,1)S(1)} %get-tuple-element.70), channel_id=1, source_target_pairs={{0,4},{1,5},{4,8},{5,9},{8,12},{9,13},{12,0},{13,1},{16,20},{17,21... | collective-permute-start | bytes 786440 | tf_op jit(solution)/shard_map/ppermute | solution.py:28
  33.4 14.4 %collective-permute-start.3 = (bf16[2,16,4096]{2,1,0:T(8,128)(2,1)S(1)}, bf16[2,16,4096]{2,1,0:T(8,128)(2,1)S(1)}, u32[]{:S(2)}, u32[]{:S(2)}) collective-permute-start(bf16[2,16,4096]{2,1,0:T(8,128)(2,1)S(1)} %get-tuple-element.71), channel_id=1, source_target_pairs={{0,18},{1,19},{4,22},{5,23},{8,26},{9,27},{12,30},{13,31},{16,0},{... | collective-permute-start | bytes 786440 | tf_op jit(solution)/shard_map/ppermute | solution.py:28
  34.9 12.9 %collective-permute-start.2 = (bf16[2,16,4096]{2,1,0:T(8,128)(2,1)S(1)}, bf16[2,16,4096]{2,1,0:T(8,128)(2,1)S(1)}, u32[]{:S(2)}, u32[]{:S(2)}) collective-permute-start(bf16[2,16,4096]{2,1,0:T(8,128)(2,1)S(1)} %get-tuple-element.71), channel_id=1, source_target_pairs={{0,2},{1,3},{4,6},{5,7},{8,10},{9,11},{12,14},{13,15},{16,18},{17,... | collective-permute-start | bytes 786440 | tf_op jit(solution)/shard_map/ppermute | solution.py:28
  43.2 7.9 %collective-permute-start.1 = (bf16[2,16,4096]{2,1,0:T(8,128)(2,1)S(1)}, bf16[2,16,4096]{2,1,0:T(8,128)(2,1)S(1)}, u32[]{:S(2)}, u32[]{:S(2)}) collective-permute-start(bf16[2,16,4096]{2,1,0:T(8,128)(2,1)S(1)} %get-tuple-element.71), channel_id=1, source_target_pairs={{0,16},{1,17},{4,20},{5,21},{8,24},{9,25},{12,28},{13,29},{16,2},{... | collective-permute-start | bytes 786440 | tf_op jit(solution)/shard_map/ppermute | solution.py:28
  47.8 35.0 %copy-start.9 = (bf16[2,64,4096]{2,1,0:T(8,128)(2,1)}, bf16[2,64,4096]{2,1,0:T(8,128)(2,1)S(1)}, u32[]{:S(2)}) copy-start(bf16[2,64,4096]{2,1,0:T(8,128)(2,1)S(1)} %pad_maximum_fusion.1.refs_5_) | copy-start | bytes 3145732
  52.2 24.9 %collective-permute-start.9 = (bf16[2,64,4096]{2,1,0:T(8,128)(2,1)}, bf16[2,64,4096]{2,1,0:T(8,128)(2,1)}, u32[]{:S(2)}, u32[]{:S(2)}) collective-permute-start(bf16[2,64,4096]{2,1,0:T(8,128)(2,1)} %pad_maximum_fusion.refs_0_), channel_id=1, source_target_pairs={{0,12},{1,13},{4,0},{5,1},{8,4},{9,5},{12,8},{13,9},{16,28},{17,29... | collective-permute-start | bytes 3145736 | tf_op jit(solution)/shard_map/ppermute | solution.py:28
  56.1 25.6 %collective-permute-start.7 = (bf16[2,64,4096]{2,1,0:T(8,128)(2,1)}, bf16[2,64,4096]{2,1,0:T(8,128)(2,1)}, u32[]{:S(2)}, u32[]{:S(2)}) collective-permute-start(bf16[2,64,4096]{2,1,0:T(8,128)(2,1)} %pad_maximum_fusion.refs_0_), channel_id=1, source_target_pairs={{0,4},{1,5},{4,8},{5,9},{8,12},{9,13},{12,0},{13,1},{16,20},{17,21... | collective-permute-start | bytes 3145736 | tf_op jit(solution)/shard_map/ppermute | solution.py:28
  56.1 26.8 %collective-permute-start.13 = (bf16[2,64,4096]{2,1,0:T(8,128)(2,1)S(1)}, bf16[2,64,4096]{2,1,0:T(8,128)(2,1)}, u32[]{:S(2)}, u32[]{:S(2)}) collective-permute-start(bf16[2,64,4096]{2,1,0:T(8,128)(2,1)S(1)} %pad_maximum_fusion.1.refs_5_), channel_id=1, source_target_pairs={{0,18},{1,19},{4,22},{5,23},{8,26},{9,27},{12,30},{13,31},{16,0},{... | collective-permute-start | bytes 3145736 | tf_op jit(solution)/shard_map/ppermute | solution.py:28
  56.1 28.0 %collective-permute-start.11 = (bf16[2,64,4096]{2,1,0:T(8,128)(2,1)S(1)}, bf16[2,64,4096]{2,1,0:T(8,128)(2,1)}, u32[]{:S(2)}, u32[]{:S(2)}) collective-permute-start(bf16[2,64,4096]{2,1,0:T(8,128)(2,1)S(1)} %pad_maximum_fusion.1.refs_5_), channel_id=1, source_target_pairs={{0,16},{1,17},{4,20},{5,21},{8,24},{9,25},{12,28},{13,29},{16,2},{... | collective-permute-start | bytes 3145736 | tf_op jit(solution)/shard_map/ppermute | solution.py:28
  74.4 22.7 %collective-permute-start.16 = (bf16[8,896,256]{2,1,0:T(8,128)(2,1)}, bf16[8,896,256]{2,1,0:T(8,128)(2,1)S(1)}, u32[]{:S(2)}, u32[]{:S(2)}) collective-permute-start(bf16[8,896,256]{2,1,0:T(8,128)(2,1)} %bitcast.55), channel_id=1, source_target_pairs={{0,1},{1,0},{4,5},{5,4},{8,9},{9,8},{12,13},{13,12},{16,17},{17,16... | collective-permute-start | bytes 11010056 | tf_op jit(solution)/shard_map/ppermute | solution.py:33
  78.2 12.0 %collective-permute-start.10 = (bf16[64,4096]{1,0:T(8,128)(2,1)S(1)}, bf16[64,4096]{1,0:T(8,128)(2,1)S(1)}, u32[]{:S(2)}, u32[]{:S(2)}) collective-permute-start(bf16[64,4096]{1,0:T(8,128)(2,1)S(1)} %slice_bitcast_fusion.2), channel_id=1, source_target_pairs={{0,12},{1,13},{4,0},{5,1},{8,4},{9,5},{12,8},{13,9},{16,28},{17,29... | collective-permute-start | bytes 1572872 | tf_op jit(solution)/shard_map/ppermute | solution.py:28
  82.8 11.8 %collective-permute-start.8 = (bf16[64,4096]{1,0:T(8,128)(2,1)S(1)}, bf16[64,4096]{1,0:T(8,128)(2,1)S(1)}, u32[]{:S(2)}, u32[]{:S(2)}) collective-permute-start(bf16[64,4096]{1,0:T(8,128)(2,1)S(1)} %slice_bitcast_fusion.3), channel_id=1, source_target_pairs={{0,4},{1,5},{4,8},{5,9},{8,12},{9,13},{12,0},{13,1},{16,20},{17,21... | collective-permute-start | bytes 1572872 | tf_op jit(solution)/shard_map/ppermute | solution.py:28
  84.0 10.6 %collective-permute-start.14 = (bf16[64,4096]{1,0:T(8,128)(2,1)S(1)}, bf16[64,4096]{1,0:T(8,128)(2,1)S(1)}, u32[]{:S(2)}, u32[]{:S(2)}) collective-permute-start(bf16[64,4096]{1,0:T(8,128)(2,1)S(1)} %slice_bitcast_fusion), channel_id=1, source_target_pairs={{0,18},{1,19},{4,22},{5,23},{8,26},{9,27},{12,30},{13,31},{16,0},{... | collective-permute-start | bytes 1572872 | tf_op jit(solution)/shard_map/ppermute | solution.py:28
  85.2 36.8 %copy-start.12 = (f32[4096]{0:T(1024)S(1)}, f32[4096]{0:T(1024)}, u32[]{:S(2)}) copy-start(f32[4096]{0:T(1024)} %param.8) | copy-start | bytes 49156
  85.2 11.9 %collective-permute-start.12 = (bf16[64,4096]{1,0:T(8,128)(2,1)S(1)}, bf16[64,4096]{1,0:T(8,128)(2,1)S(1)}, u32[]{:S(2)}, u32[]{:S(2)}) collective-permute-start(bf16[64,4096]{1,0:T(8,128)(2,1)S(1)} %slice_bitcast_fusion.1), channel_id=1, source_target_pairs={{0,16},{1,17},{4,20},{5,21},{8,24},{9,25},{12,28},{13,29},{16,2},{... | collective-permute-start | bytes 1572872 | tf_op jit(solution)/shard_map/ppermute | solution.py:28
  97.1 1.9 copy-start.13
  119.5 4.8 %copy-start.6 = (bf16[2,64,4096]{2,1,0:T(8,128)(2,1)S(1)}, bf16[2,64,4096]{2,1,0:T(8,128)(2,1)}, u32[]{:S(2)}) copy-start(bf16[2,64,4096]{2,1,0:T(8,128)(2,1)} %get-tuple-element.41) | copy-start | bytes 3145732
  119.5 4.8 %copy-start.5 = (bf16[2,64,4096]{2,1,0:T(8,128)(2,1)S(1)}, bf16[2,64,4096]{2,1,0:T(8,128)(2,1)}, u32[]{:S(2)}) copy-start(bf16[2,64,4096]{2,1,0:T(8,128)(2,1)} %get-tuple-element.43) | copy-start | bytes 3145732
  119.5 11.5 %collective-permute-start.17 = (bf16[64,4096]{1,0:T(8,128)(2,1)S(1)}, bf16[64,4096]{1,0:T(8,128)(2,1)S(1)}, u32[]{:S(2)}, u32[]{:S(2)}) collective-permute-start(bf16[64,4096]{1,0:T(8,128)(2,1)S(1)} %get-tuple-element.38), channel_id=1, source_target_pairs={{0,12},{1,13},{4,0},{5,1},{8,4},{9,5},{12,8},{13,9},{16,28},{17,29... | collective-permute-start | bytes 1572872 | tf_op jit(solution)/shard_map/ppermute | solution.py:28
  122.0 9.0 %copy-start.8 = (bf16[2,64,4096]{2,1,0:T(8,128)(2,1)S(1)}, bf16[2,64,4096]{2,1,0:T(8,128)(2,1)}, u32[]{:S(2)}) copy-start(bf16[2,64,4096]{2,1,0:T(8,128)(2,1)} %get-tuple-element.37) | copy-start | bytes 3145732
  124.3 10.4 %copy-start.7 = (bf16[2,64,4096]{2,1,0:T(8,128)(2,1)S(1)}, bf16[2,64,4096]{2,1,0:T(8,128)(2,1)}, u32[]{:S(2)}) copy-start(bf16[2,64,4096]{2,1,0:T(8,128)(2,1)} %get-tuple-element.39) | copy-start | bytes 3145732
  124.4 10.3 %collective-permute-start.18 = (bf16[64,4096]{1,0:T(8,128)(2,1)S(1)}, bf16[64,4096]{1,0:T(8,128)(2,1)S(1)}, u32[]{:S(2)}, u32[]{:S(2)}) collective-permute-start(bf16[64,4096]{1,0:T(8,128)(2,1)S(1)} %get-tuple-element.40), channel_id=1, source_target_pairs={{0,4},{1,5},{4,8},{5,9},{8,12},{9,13},{12,0},{13,1},{16,20},{17,21... | collective-permute-start | bytes 1572872 | tf_op jit(solution)/shard_map/ppermute | solution.py:28
  124.5 11.4 %collective-permute-start.19 = (bf16[64,4096]{1,0:T(8,128)(2,1)S(1)}, bf16[64,4096]{1,0:T(8,128)(2,1)S(1)}, u32[]{:S(2)}, u32[]{:S(2)}) collective-permute-start(bf16[64,4096]{1,0:T(8,128)(2,1)S(1)} %get-tuple-element.42), channel_id=1, source_target_pairs={{0,18},{1,19},{4,22},{5,23},{8,26},{9,27},{12,30},{13,31},{16,0},{... | collective-permute-start | bytes 1572872 | tf_op jit(solution)/shard_map/ppermute | solution.py:28
  124.6 13.6 %collective-permute-start.20 = (bf16[64,4096]{1,0:T(8,128)(2,1)S(1)}, bf16[64,4096]{1,0:T(8,128)(2,1)S(1)}, u32[]{:S(2)}, u32[]{:S(2)}) collective-permute-start(bf16[64,4096]{1,0:T(8,128)(2,1)S(1)} %get-tuple-element.44), channel_id=1, source_target_pairs={{0,16},{1,17},{4,20},{5,21},{8,24},{9,25},{12,28},{13,29},{16,2},{... | collective-permute-start | bytes 1572872 | tf_op jit(solution)/shard_map/ppermute | solution.py:28
  126.0 13.4 %collective-permute-start.21 = (bf16[8,896,256]{2,1,0:T(8,128)(2,1)}, bf16[8,896,256]{2,1,0:T(8,128)(2,1)S(1)}, u32[]{:S(2)}, u32[]{:S(2)}) collective-permute-start(bf16[8,896,256]{2,1,0:T(8,128)(2,1)} %get-tuple-element.47), channel_id=1, source_target_pairs={{0,1},{1,0},{4,5},{5,4},{8,9},{9,8},{12,13},{13,12},{16,17},{17,16... | collective-permute-start | bytes 11010056 | tf_op jit(solution)/shard_map/ppermute | solution.py:33
  138.2 2.4 copy-start.2
  143.3 43.3 %collective-permute-start.22 = (bf16[2,64,4096]{2,1,0:T(8,128)(2,1)}, bf16[2,64,4096]{2,1,0:T(8,128)(2,1)}, u32[]{:S(2)}, u32[]{:S(2)}) collective-permute-start(bf16[2,64,4096]{2,1,0:T(8,128)(2,1)} %pad_maximum_fusion.2), channel_id=1, source_target_pairs={{0,12},{1,13},{4,0},{5,1},{8,4},{9,5},{12,8},{13,9},{16,28},{17,29... | collective-permute-start | bytes 3145736 | tf_op jit(solution)/shard_map/ppermute | solution.py:28
  143.4 43.2 %collective-permute-start.23 = (bf16[2,64,4096]{2,1,0:T(8,128)(2,1)}, bf16[2,64,4096]{2,1,0:T(8,128)(2,1)}, u32[]{:S(2)}, u32[]{:S(2)}) collective-permute-start(bf16[2,64,4096]{2,1,0:T(8,128)(2,1)} %pad_maximum_fusion.3), channel_id=1, source_target_pairs={{0,4},{1,5},{4,8},{5,9},{8,12},{9,13},{12,0},{13,1},{16,20},{17,21... | collective-permute-start | bytes 3145736 | tf_op jit(solution)/shard_map/ppermute | solution.py:28
  144.8 41.7 %collective-permute-start.24 = (bf16[2,64,4096]{2,1,0:T(8,128)(2,1)}, bf16[2,64,4096]{2,1,0:T(8,128)(2,1)}, u32[]{:S(2)}, u32[]{:S(2)}) collective-permute-start(bf16[2,64,4096]{2,1,0:T(8,128)(2,1)} %pad_maximum_fusion.4), channel_id=1, source_target_pairs={{0,18},{1,19},{4,22},{5,23},{8,26},{9,27},{12,30},{13,31},{16,0},{... | collective-permute-start | bytes 3145736 | tf_op jit(solution)/shard_map/ppermute | solution.py:28
  145.3 41.2 %collective-permute-start.25 = (bf16[2,64,4096]{2,1,0:T(8,128)(2,1)}, bf16[2,64,4096]{2,1,0:T(8,128)(2,1)}, u32[]{:S(2)}, u32[]{:S(2)}) collective-permute-start(bf16[2,64,4096]{2,1,0:T(8,128)(2,1)} %pad_maximum_fusion.5), channel_id=1, source_target_pairs={{0,16},{1,17},{4,20},{5,21},{8,24},{9,25},{12,28},{13,29},{16,2},{... | collective-permute-start | bytes 3145736 | tf_op jit(solution)/shard_map/ppermute | solution.py:28
  146.3 3.6 %collective-permute-start.26 = (f32[4096]{0:T(1024)S(1)}, f32[4096]{0:T(1024)S(1)}, u32[]{:S(2)}, u32[]{:S(2)}) collective-permute-start(f32[4096]{0:T(1024)S(1)} %div.35), channel_id=1, source_target_pairs={{0,32},{1,33},{4,36},{5,37},{8,40},{9,41},{12,44},{13,45},{16,48},... | collective-permute-start | bytes 49160 | tf_op jit(solution)/shard_map/ppermute | solution.py:250
  149.9 4.3 %collective-permute-start.27 = (f32[4096]{0:T(1024)S(1)}, f32[4096]{0:T(1024)S(1)}, u32[]{:S(2)}, u32[]{:S(2)}) collective-permute-start(f32[4096]{0:T(1024)S(1)} %add.109), channel_id=1, source_target_pairs={{0,64},{1,65},{4,68},{5,69},{8,72},{9,73},{12,76},{13,77},{16,80},... | collective-permute-start | bytes 49160 | tf_op jit(solution)/shard_map/ppermute | solution.py:250
  154.3 6.5 %collective-permute-start.28 = (f32[4096]{0:T(1024)S(1)}, f32[4096]{0:T(1024)S(1)}, u32[]{:S(2)}, u32[]{:S(2)}) collective-permute-start(f32[4096]{0:T(1024)S(1)} %add.110), channel_id=1, source_target_pairs={{0,128},{1,129},{4,132},{5,133},{8,136},{9,137},{12,140},{13,141},... | collective-permute-start | bytes 49160 | tf_op jit(solution)/shard_map/ppermute | solution.py:250
  160.8 11.0 %collective-permute-start.29 = (f32[4096]{0:T(1024)S(1)}, f32[4096]{0:T(1024)S(1)}, u32[]{:S(2)}, u32[]{:S(2)}) collective-permute-start(f32[4096]{0:T(1024)S(1)} %add.111), channel_id=1, source_target_pairs={{0,1},{1,0},{4,5},{5,4},{8,9},{9,8},{12,13},{13,12},{16,17},{17,16... | collective-permute-start | bytes 49160 | tf_op jit(solution)/shard_map/ppermute | solution.py:250
  171.7 3.0 %collective-permute-start.30 = (f32[4096]{0:T(1024)S(1)}, f32[4096]{0:T(1024)S(1)}, u32[]{:S(2)}, u32[]{:S(2)}) collective-permute-start(f32[4096]{0:T(1024)S(1)} %add.112), channel_id=1, source_target_pairs={{0,16},{1,17},{4,20},{5,21},{8,24},{9,25},{12,28},{13,29},{16,0},{... | collective-permute-start | bytes 49160 | tf_op jit(solution)/shard_map/ppermute | solution.py:250
  174.7 4.1 %collective-permute-start.31 = (f32[4096]{0:T(1024)S(1)}, f32[4096]{0:T(1024)S(1)}, u32[]{:S(2)}, u32[]{:S(2)}) collective-permute-start(f32[4096]{0:T(1024)S(1)} %add.113), channel_id=1, source_target_pairs={{0,2},{1,3},{4,6},{5,7},{8,10},{9,11},{12,14},{13,15},{16,18},{17,... | collective-permute-start | bytes 49160 | tf_op jit(solution)/shard_map/ppermute | solution.py:250
  178.8 3.0 %collective-permute-start.32 = (f32[4096]{0:T(1024)S(1)}, f32[4096]{0:T(1024)S(1)}, u32[]{:S(2)}, u32[]{:S(2)}) collective-permute-start(f32[4096]{0:T(1024)S(1)} %add.114), channel_id=1, source_target_pairs={{0,4},{1,5},{4,0},{5,1},{8,12},{9,13},{12,8},{13,9},{16,20},{17,21... | collective-permute-start | bytes 49160 | tf_op jit(solution)/shard_map/ppermute | solution.py:250
  181.8 4.1 %collective-permute-start.33 = (f32[4096]{0:T(1024)S(1)}, f32[4096]{0:T(1024)S(1)}, u32[]{:S(2)}, u32[]{:S(2)}) collective-permute-start(f32[4096]{0:T(1024)S(1)} %add.115), channel_id=1, source_target_pairs={{0,8},{1,9},{4,12},{5,13},{8,0},{9,1},{12,4},{13,5},{16,24},{17,25... | collective-permute-start | bytes 49160 | tf_op jit(solution)/shard_map/ppermute | solution.py:250
  198.2 38.3 %collective-permute-start.41 = (bf16[896,256]{1,0:T(8,128)(2,1)}, bf16[896,256]{1,0:T(8,128)(2,1)S(1)}, u32[]{:S(2)}, u32[]{:S(2)}) collective-permute-start(bf16[896,256]{1,0:T(8,128)(2,1)} %bitcast.57), channel_id=1, source_target_pairs={{0,0},{1,16},{4,4},{5,20},{8,8},{9,24},{12,12},{13,28},{16,1},{17,... | collective-permute-start | bytes 1376264 | tf_op jit(solution)/shard_map/ppermute | solution.py:40
  201.9 6.2 %copy-start.10 = (bf16[2,64,4096]{2,1,0:T(8,128)(2,1)S(1)}, bf16[2,64,4096]{2,1,0:T(8,128)(2,1)}, u32[]{:S(2)}) copy-start(bf16[2,64,4096]{2,1,0:T(8,128)(2,1)} %get-tuple-element.56) | copy-start | bytes 3145732
  204.0 8.6 %collective-permute-start.34 = (bf16[2,16,4096]{2,1,0:T(8,128)(2,1)S(1)}, bf16[2,16,4096]{2,1,0:T(8,128)(2,1)S(1)}, u32[]{:S(2)}, u32[]{:S(2)}) collective-permute-start(bf16[2,16,4096]{2,1,0:T(8,128)(2,1)S(1)} %get-tuple-element.67), channel_id=1, source_target_pairs={{0,18},{1,19},{4,22},{5,23},{8,26},{9,27},{12,30},{13,31},{16,0},{... | collective-permute-start | bytes 786440 | tf_op jit(solution)/shard_map/ppermute | solution.py:28
  204.6 9.1 %collective-permute-start.36 = (bf16[2,16,4096]{2,1,0:T(8,128)(2,1)S(1)}, bf16[2,16,4096]{2,1,0:T(8,128)(2,1)S(1)}, u32[]{:S(2)}, u32[]{:S(2)}) collective-permute-start(bf16[2,16,4096]{2,1,0:T(8,128)(2,1)S(1)} %get-tuple-element.68), channel_id=1, source_target_pairs={{0,16},{1,17},{4,20},{5,21},{8,24},{9,25},{12,28},{13,29},{16,2},{... | collective-permute-start | bytes 786440 | tf_op jit(solution)/shard_map/ppermute | solution.py:28
  205.6 16.0 %collective-permute-start.35 = (bf16[2,16,4096]{2,1,0:T(8,128)(2,1)S(1)}, bf16[2,16,4096]{2,1,0:T(8,128)(2,1)S(1)}, u32[]{:S(2)}, u32[]{:S(2)}) collective-permute-start(bf16[2,16,4096]{2,1,0:T(8,128)(2,1)S(1)} %get-tuple-element.69), channel_id=1, source_target_pairs={{0,2},{1,3},{4,6},{5,7},{8,10},{9,11},{12,14},{13,15},{16,18},{17,... | collective-permute-start | bytes 786440 | tf_op jit(solution)/shard_map/ppermute | solution.py:28
  210.1 13.9 %collective-permute-start.37 = (bf16[2,16,4096]{2,1,0:T(8,128)(2,1)S(1)}, bf16[2,16,4096]{2,1,0:T(8,128)(2,1)S(1)}, u32[]{:S(2)}, u32[]{:S(2)}) collective-permute-start(bf16[2,16,4096]{2,1,0:T(8,128)(2,1)S(1)} %get-tuple-element.64), channel_id=1, source_target_pairs={{0,12},{1,13},{4,0},{5,1},{8,4},{9,5},{12,8},{13,9},{16,28},{17,29... | collective-permute-start | bytes 786440 | tf_op jit(solution)/shard_map/ppermute | solution.py:28
  212.6 11.4 %collective-permute-start.39 = (bf16[2,16,4096]{2,1,0:T(8,128)(2,1)S(1)}, bf16[2,16,4096]{2,1,0:T(8,128)(2,1)S(1)}, u32[]{:S(2)}, u32[]{:S(2)}) collective-permute-start(bf16[2,16,4096]{2,1,0:T(8,128)(2,1)S(1)} %get-tuple-element.65), channel_id=1, source_target_pairs={{0,4},{1,5},{4,8},{5,9},{8,12},{9,13},{12,0},{13,1},{16,20},{17,21... | collective-permute-start | bytes 786440 | tf_op jit(solution)/shard_map/ppermute | solution.py:28
  213.7 19.9 %copy-start.4 = (bf16[31,4096]{1,0:T(8,128)(2,1)S(1)}, bf16[31,4096]{1,0:T(8,128)(2,1)}, u32[]{:S(2)}) copy-start(bf16[31,4096]{1,0:T(8,128)(2,1)} %copy-done.3) | copy-start | bytes 761860
  213.7 10.4 %collective-permute-start.38 = (bf16[2,16,4096]{2,1,0:T(8,128)(2,1)S(1)}, bf16[2,16,4096]{2,1,0:T(8,128)(2,1)S(1)}, u32[]{:S(2)}, u32[]{:S(2)}) collective-permute-start(bf16[2,16,4096]{2,1,0:T(8,128)(2,1)S(1)} %get-tuple-element.66), channel_id=1, source_target_pairs={{0,8},{1,9},{4,12},{5,13},{8,0},{9,1},{12,4},{13,5},{16,24},{17,25... | collective-permute-start | bytes 786440 | tf_op jit(solution)/shard_map/ppermute | solution.py:28
  224.5 10.6 %collective-permute-start.40 = (bf16[1,4096]{1,0:T(2,128)(2,1)S(1)}, bf16[1,4096]{1,0:T(2,128)(2,1)S(1)}, u32[]{:S(2)}, u32[]{:S(2)}) collective-permute-start(bf16[1,4096]{1,0:T(2,128)(2,1)S(1)} %slice.128), channel_id=1, source_target_pairs={{0,1},{1,2},{2,3},{3,4},{4,5},{5,6},{6,7},{7,8},{8,9},{9,10},{10,1... | collective-permute-start | bytes 24584 | tf_op jit(solution)/shard_map/ppermute | solution.py:46
Sparse Core Ops, SparseCore 0:
  21.8 52.6 all-gather.2
  143.4 54.8 reduce-scatter.1

commit v3 on v2

--- a/solution.py
+++ b/solution.py
@@ -21,10 +21,11 @@
     ]
 
 
-def shift(value, dx=0, dy=0):
-    pairs = [
-        (linear(z, y, x, c), linear(z, (y + dy) % NY, (x + dx) % NX, c)) for z, y, x, c in places()
-    ]
+def shift(value, first=0, second=0):
+    pairs = []
+    for z, y, x, c in places():
+        dy, dx = (second, first) if c else (first, second)
+        pairs.append((linear(z, y, x, c), linear(z, (y + dy) % NY, (x + dx) % NX, c)))
     return lax.ppermute(value, AXES, pairs)
 
 
@@ -54,20 +55,15 @@
     return jnp.dot(a, b, preferred_element_type=jnp.float32)
 
 
-def slots(refs):
-    s0, s1, p2, g2, s3 = refs
-    return [(s0.at[0], s0.at[1]), (s1.at[0], s1.at[1]), (p2, g2), (s3.at[0], s3.at[1])]
-
-
 def block_kernel(chunks, *refs):
-    acts = slots(refs[:5]) + slots(refs[5:10])
-    w_own, w_oth = refs[10:12]
-    outs = slots(refs[12:17]) + slots(refs[17:22])
-    g_own, g_oth, gain = refs[22:25]
+    acts = list(zip(refs[:4], refs[4:8]))
+    w_own, w_oth = refs[8:10]
+    outs = list(zip(refs[10:14], refs[14:18]))
+    g_own, g_oth, gain = refs[18:21]
     (p_s, g_s, wi_s, wo_s, d_s, n_s, gi_s, go_s, h_s, ga_s, sq_s, act, gp, act_t, gp_t, in_sem,
-     out_sem) = refs[25:]
+     out_sem) = refs[21:]
     core = lax.axis_index("c")
-    rows = refs[0].shape[1]
+    rows = refs[0].shape[0]
     hidden = wi_s.shape[0]
     half = w_own.shape[2]
     width = 2 * half
@@ -162,10 +158,10 @@
 
 
 def block(acts, w_own, w_oth):
-    _, rows, feats = acts[0].shape
+    rows, feats = acts[0].shape
     chunks, hidden2, half = w_own.shape
     hidden = hidden2 // 2
-    total = 8 * rows
+    total = 4 * rows
     bf = jnp.bfloat16
     anywhere = pl.BlockSpec(memory_space=pl.ANY)
     flops = 12 * total * feats * hidden
@@ -174,8 +170,8 @@
         out_shape=[jax.ShapeDtypeStruct(act.shape, bf) for act in acts]
         + [jax.ShapeDtypeStruct(w_own.shape, bf)] * 2
         + [jax.ShapeDtypeStruct((1, feats), jnp.float32)],
-        in_specs=[anywhere] * 12,
-        out_specs=[anywhere] * 12 + [pl.BlockSpec(memory_space=pltpu.VMEM)],
+        in_specs=[anywhere] * 10,
+        out_specs=[anywhere] * 10 + [pl.BlockSpec(memory_space=pltpu.VMEM)],
         scratch_shapes=[pltpu.VMEM((total, feats), bf)] * 2
         + [pltpu.VMEM((hidden, feats), bf)] * 2
         + [pltpu.VMEM((total, feats), bf)] * 2
@@ -199,46 +195,35 @@
     return total
 
 
-def by_x(value, d):
-    return shift(value, dx=d)
-
-
-def by_y(value, d):
-    return shift(value, dy=d)
-
-
-def gather_plane(first, second):
-    a = jnp.concatenate([first] + [by_y(first, d) for d in (1, 2, 3)], axis=1)
-    b = jnp.concatenate([second] + [by_x(second, d) for d in (1, 2, 3)], axis=1)
-    a, b = lax.optimization_barrier((a, b))
-    a1, a3, b1, b3 = by_x(a, 1), by_x(a, -1), by_y(b, 1), by_y(b, -1)
-    a2, b2 = (by_x(a1[0], 1), by_x(a3[1], -1)), (by_y(b1[0], 1), by_y(b3[1], -1))
-    return [a, a1, *a2, a3, b, b1, *b2, b3], (a, b)
-
-
-def fold(half, move):
-    s0, s1, d2, n2, s3 = half
+def gather_plane(acts):
+    parts = [acts] + [shift(acts, first=d) for d in (1, 2, 3)]
+    p0 = jnp.concatenate([part[0] for part in parts], axis=0)
+    g0 = jnp.concatenate([part[1] for part in parts], axis=0)
+    p0, g0 = lax.optimization_barrier((p0, g0))
+    p1, g3 = shift(p0, second=1), shift(g0, second=-1)
+    g1, p3 = shift(g0, second=1), shift(p0, second=-1)
+    p1, g3, g1, p3 = lax.optimization_barrier((p1, g3, g1, p3))
+    p2, g2 = shift(p1, second=1), shift(g3, second=-1)
+    return [p0, p1, p2, p3, g0, g1, g2, g3]
+
+
+def scatter_plane(outs, gain_part, weight_part):
+    d0, d1, d2, d3, n0, n1, n2, n3 = outs
     bf = jnp.bfloat16
-    d2, n2 = move(d2, -1), move(n2, 1)
-    s1 = jnp.stack([add_all([s1[0], d2]).astype(bf), s1[1]])
-    s3 = jnp.stack([s3[0], add_all([s3[1], n2]).astype(bf)])
-    return s1, s3
-
-
-def scatter_plane(outs, rows, gain_part, weight_part):
-    sends = (*fold(outs[:5], by_x), *fold(outs[5:], by_y), gain_part, weight_part)
-    a1, a3, b1, b3, gain_part, weight_part = lax.optimization_barrier(sends)
+    d2, n2 = shift(d2, second=-1), shift(n2, second=1)
+    n1, d3 = shift(n1, second=-1), shift(d3, second=1)
+    d1, n3 = add_all([d1, d2]).astype(bf), add_all([n3, n2]).astype(bf)
+    d1, n3, weight_part = lax.optimization_barrier((d1, n3, weight_part))
     weight_sum = lax.psum_scatter(weight_part, "z", scatter_dimension=0, tiled=False)
-    a1, a3, b1, b3 = by_x(a1, -1), by_x(a3, 1), by_y(b1, -1), by_y(b3, 1)
-    arrived = (a1, a3, b1, b3, total_over_all(gain_part), weight_sum)
-    a1, a3, b1, b3, grad_gain, weight_sum = lax.optimization_barrier(arrived)
-    a = add_all([outs[0], a1, a3]).astype(jnp.bfloat16)
-    b = add_all([outs[5], b1, b3]).astype(jnp.bfloat16)
-    a = [a[:, d * rows : (d + 1) * rows] for d in range(4)]
-    b = [b[:, d * rows : (d + 1) * rows] for d in range(4)]
-    a = add_all([a[0]] + [by_y(a[d], -d) for d in (1, 2, 3)])
-    b = add_all([b[0]] + [by_x(b[d], -d) for d in (1, 2, 3)])
-    return jnp.concatenate([a, b], axis=1), grad_gain, weight_sum
+    d1, n3 = shift(d1, second=-1), shift(n3, second=1)
+    arrived = (d1, d3, n1, n3, total_over_all(gain_part))
+    d1, d3, n1, n3, grad_gain = lax.optimization_barrier(arrived)
+    both = jnp.stack([add_all([d0, d1, d3]).astype(bf), add_all([n0, n1, n3]).astype(bf)])
+    rows = both.shape[1] // 4
+    both = [both[:, d * rows : (d + 1) * rows] for d in range(4)]
+    arrived = [shift(both[d], first=-d) for d in (1, 2, 3)] + [weight_sum]
+    *arrived, weight_sum = lax.optimization_barrier(arrived)
+    return add_all([both[0], *arrived]), grad_gain, weight_sum
 
 
 def total_over_all(value):
@@ -278,15 +263,14 @@
     grad_coarse = jnp.concatenate([group_sums[1:], following], axis=0)
 
     acts = jnp.stack([pooled, grad_coarse], axis=0)
-    rows = groups // 2
-    blocks, begun = gather_plane(acts[:, :rows], acts[:, rows:])
-    w_own = lax.optimization_barrier((w_own, *begun))[0]
+    blocks = gather_plane(acts)
+    w_own = lax.optimization_barrier((w_own, blocks[1], blocks[3]))[0]
     w_oth = other_core(w_own)
     results = block(blocks, w_own, w_oth)
-    outs, (g_own, g_oth, gain_part) = results[:10], results[10:]
+    outs, (g_own, g_oth, gain_part) = results[:8], results[8:]
 
     mine = (g_own.astype(jnp.float32) + other_core(g_oth).astype(jnp.float32)).astype(bf)
-    (down_sum, scaled), grad_gain, grads = scatter_plane(outs, rows, gain_part[0] / norm_gain, mine)
+    (down_sum, scaled), grad_gain, grads = scatter_plane(outs, gain_part[0] / norm_gain, mine)
     grads = swap_low(grads)
     grad_weight_in = (grads[:hidden].astype(jnp.float32) * gain[None, :]).T
     grad_weight_out = grads[hidden:].astype(jnp.float32)

time: 246 us -> 222 us (0.902)
  starting transfers between devices: 82.8 us -> 49.8 us
  waiting for transfers between devices: 93.6 us -> 113 us
  other arithmetic: 18.3 us -> 13.3 us
  local copies, waits for them, and re-layouts: 11.8 us -> 7.22 us
    ppermute x28 -> x18, waiting for transfers between devices: 37 us -> 78.6 us  [shift(): return lax.ppermute(value, AXES, pairs)]
    all_gather x1, waiting for transfers between devices: 16.8 us -> 0.01 us  [shards(): w_own = lax.all_gather(both, 'z', axis=0, tiled=False)]
    ppermute x28 -> x18, starting transfers between devices: 35.8 us -> 19 us  [shift(): return lax.ppermute(value, AXES, pairs)]
    reduce_scatter x1, waiting for transfers between devices: 11.7 us -> 0.02 us  [scatter_plane(): lax.psum_scatter(weight_part, 'z', scatter_dimension=0, tiled=False)]
    ppermute x8, starting transfers between devices: 22 us -> 13.2 us  [total_over_all(): lax.ppermute(value, AXES, [(linear(*p), linear(*move(p))) for p in places...]
    squeeze x4 -> x3, local copies, waits for them, and re-layouts: 4.31 us -> 0.11 us  [gather_plane(): g0 = jnp.concatenate([part[1] for part in parts], axis=0)]
    another operation x8 -> x3, other arithmetic: 4.81 us -> 1.06 us  [scatter_plane(): jnp.stack([add_all([d0, d1, d3]).astype(bf), add_all([n0, n1, n3]).astype...]
    ppermute x2, starting transfers between devices: 5.67 us -> 2.24 us  [other_core(): return lax.ppermute(value, AXES, pairs)]
  transfers between devices with their start and end apart: 44 -> 34, of which waited for: 23 -> 21; matrix products, arithmetic and copies ran while one was open for 9% -> 4% of each run, Pallas kernels for 0% -> 0%
where the time goes in v3:
time: 222 us
  waiting for transfers between devices  113 us (51%)
  starting transfers between devices  49.8 us (22%)
  Pallas kernels  20.5 us (9%)
  between operations  14.5 us (7%)
  other arithmetic  13.3 us (6%)
  local copies, waits for them, and re-layouts  7.22 us (3%)
  matrix products  3.44 us (2%)
    ppermute x18, waiting for transfers between devices, shift(): return lax.ppermute(value, AXES, pairs)  78.6 us
    ppermute x8, waiting for transfers between devices, total_over_all(): lax.ppermute(value, AXES, [(linear(*p), linear(*move(p))) for p in places...  20.6 us
    pallas_call x1, Pallas kernels, block(): pl.pallas_call(functools.partial(block_kernel, chunks), out_shape=[jax.Sh...  20.5 us
    ppermute x18, starting transfers between devices, shift(): return lax.ppermute(value, AXES, pairs)  19 us
    ppermute x8, starting transfers between devices, total_over_all(): lax.ppermute(value, AXES, [(linear(*p), linear(*move(p))) for p in places...  13.2 us
    ppermute x2, waiting for transfers between devices, swap_low(): return lax.ppermute(value, AXES, pairs)  9.43 us
    ppermute x2, starting transfers between devices, from_behind(): return lax.ppermute(value, AXES, pairs)  8.05 us
    ppermute x2, starting transfers between devices, swap_low(): return lax.ppermute(value, AXES, pairs)  7.28 us
  transfers between devices with their start and end apart: 34, of which 21 were waited for; matrix products, arithmetic and copies ran while one was open for 4% of the time, Pallas kernels for 0%

profile of v3, /device:TPU:1, one launch (start us, length us, event | category | flops | bytes accessed | tf_op | source)
XLA Modules:
  0.0 221.8 jit_solution(14712646749377116429)
XLA Ops:
  7.2 0.9 dynamic_slice.3
  8.1 1.0 fusion.20
  9.1 1.0 pad_maximum_fusion.3
  10.1 4.6 %collective-permute-start.10 = (bf16[896,256]{1,0:T(8,128)(2,1)S(1)}, bf16[896,256]{1,0:T(8,128)(2,1)S(1)}, u32[]{:S(2)}, u32[]{:S(2)}) collective-permute-start(bf16[896,256]{1,0:T(8,128)(2,1)S(1)} %pad_maximum_fusion.3), channel_id=1, source_target_pairs={{0,0},{1,16},{4,4},{5,20},{8,8},{9,24},{12,12},{13,28},{16,1},{17,... | collective-permute-start | bytes 1376264 | tf_op jit(solution)/shard_map/ppermute | solution.py:41
  14.7 0.7 convert_subtract_fusion
  15.8 5.1 %collective-permute-done.10 = bf16[896,256]{1,0:T(8,128)(2,1)S(1)} collective-permute-done((bf16[896,256]{1,0:T(8,128)(2,1)S(1)}, bf16[896,256]{1,0:T(8,128)(2,1)S(1)}, u32[]{:S(2)}, u32[]{:S(2)}) %collective-permute-start.10) | collective-permute-done | bytes 458784 | tf_op jit(solution)/shard_map/ppermute | solution.py:41
  20.8 0.8 copy-done.12
  22.0 1.9 collective-permute-start
  24.3 4.3 %collective-permute-done = bf16[1,4096]{1,0:T(2,128)(2,1)S(1)} collective-permute-done((bf16[1,4096]{1,0:T(2,128)(2,1)S(1)}, bf16[1,4096]{1,0:T(2,128)(2,1)S(1)}, u32[]{:S(2)}, u32[]{:S(2)}) %collective-permute-start) | collective-permute-done | bytes 8224 | tf_op jit(solution)/shard_map/ppermute | solution.py:47
  28.7 2.6 %collective-permute-start.3 = (bf16[2,32,4096]{2,1,0:T(8,128)(2,1)S(1)}, bf16[2,32,4096]{2,1,0:T(8,128)(2,1)S(1)}, u32[]{:S(2)}, u32[]{:S(2)}) collective-permute-start(bf16[2,32,4096]{2,1,0:T(8,128)(2,1)S(1)} %pad_maximum_fusion.2), channel_id=1, source_target_pairs={{0,18},{1,13},{4,22},{5,1},{8,26},{9,5},{12,30},{13,9},{16,0},{17,... | collective-permute-start | bytes 1572872 | tf_op jit(solution)/shard_map/ppermute | solution.py:29
  31.2 0.5 collective-permute-start.2
  31.8 0.6 collective-permute-start.1
  32.4 10.6 %collective-permute-done.3 = bf16[2,32,4096]{2,1,0:T(8,128)(2,1)S(1)} collective-permute-done((bf16[2,32,4096]{2,1,0:T(8,128)(2,1)S(1)}, bf16[2,32,4096]{2,1,0:T(8,128)(2,1)S(1)}, u32[]{:S(2)}, u32[]{:S(2)}) %collective-permute-start.3) | collective-permute-done | bytes 524320 | tf_op jit(solution)/shard_map/ppermute | solution.py:29
  43.1 3.7 %collective-permute-done.1 = bf16[2,32,4096]{2,1,0:T(8,128)(2,1)S(1)} collective-permute-done((bf16[2,32,4096]{2,1,0:T(8,128)(2,1)S(1)}, bf16[2,32,4096]{2,1,0:T(8,128)(2,1)S(1)}, u32[]{:S(2)}, u32[]{:S(2)}) %collective-permute-start.1) | collective-permute-done | bytes 524320 | tf_op jit(solution)/shard_map/ppermute | solution.py:29
  47.5 1.5 collective-permute-start.4
  48.9 1.7 collective-permute-start.6
  50.6 1.0 collective-permute-start.5
  51.6 9.9 %collective-permute-done.7.refs_3_ = bf16[128,4096]{1,0:T(8,128)(2,1)S(1)} collective-permute-done((bf16[128,4096]{1,0:T(8,128)(2,1)S(1)}, bf16[128,4096]{1,0:T(8,128)(2,1)S(1)}, u32[]{:S(2)}, u32[]{:S(2)}) %collective-permute-start.7) | collective-permute-done | bytes 1048608 | tf_op jit(solution)/shard_map/ppermute | solution.py:29
  61.5 2.2 collective-permute-done.4.refs_1_
  63.7 11.1 %collective-permute-done.6.refs_5_ = bf16[128,4096]{1,0:T(8,128)(2,1)S(1)} collective-permute-done((bf16[128,4096]{1,0:T(8,128)(2,1)S(1)}, bf16[128,4096]{1,0:T(8,128)(2,1)S(1)}, u32[]{:S(2)}, u32[]{:S(2)}) %collective-permute-start.6) | collective-permute-done | bytes 1048608 | tf_op jit(solution)/shard_map/ppermute | solution.py:29
  74.8 1.0 copy-done.17
  75.8 1.2 collective-permute-start.11
  77.1 0.8 collective-permute-start.9
  77.9 0.7 collective-permute-start.8
  78.5 12.7 %collective-permute-done.9.refs_6_ = bf16[128,4096]{1,0:T(8,128)(2,1)S(1)} collective-permute-done((bf16[128,4096]{1,0:T(8,128)(2,1)}, bf16[128,4096]{1,0:T(8,128)(2,1)S(1)}, u32[]{:S(2)}, u32[]{:S(2)}) %collective-permute-start.9) | collective-permute-done | bytes 1048608 | tf_op jit(solution)/shard_map/ppermute | solution.py:29
  91.2 1.8 collective-permute-done.8.refs_2_
  93.1 1.0 copy-done.19
  94.0 1.8 copy-done.14
  95.8 20.5 %shard_map.101 = (bf16[128,4096]{1,0:T(8,128)(2,1)S(1)}, bf16[128,4096]{1,0:T(8,128)(2,1)S(1)}, bf16[128,4096]{1,0:T(8,128)(2,1)S(1)}, bf16[128,4096]{1,0:T(8,12...) custom-call(bf16[128,4096]{1,0:T(8,128)(2,1)} %copy-done.9, ...), custom_call_target="tpu_custom_call" | custom-call | flops 11274289152 | bytes 62914560 | tf_op jit(solution)/shard_map/pallas_call | solution.py:168
  116.4 1.0 collective-permute-start.14
  117.4 2.5 %collective-permute-start.12 = (bf16[128,4096]{1,0:T(8,128)(2,1)S(1)}, bf16[128,4096]{1,0:T(8,128)(2,1)S(1)}, u32[]{:S(2)}, u32[]{:S(2)}) collective-permute-start(bf16[128,4096]{1,0:T(8,128)(2,1)S(1)} %get-tuple-element.44), channel_id=1, source_target_pairs={{0,12},{1,19},{4,0},{5,23},{8,4},{9,27},{12,8},{13,31},{16,28},{17... | collective-permute-start | bytes 3145736 | tf_op jit(solution)/shard_map/ppermute | solution.py:29
  119.8 11.7 %collective-permute-done.12 = bf16[128,4096]{1,0:T(8,128)(2,1)S(1)} collective-permute-done((bf16[128,4096]{1,0:T(8,128)(2,1)S(1)}, bf16[128,4096]{1,0:T(8,128)(2,1)S(1)}, u32[]{:S(2)}, u32[]{:S(2)}) %collective-permute-start.12) | collective-permute-done | bytes 1048608 | tf_op jit(solution)/shard_map/ppermute | solution.py:29
  131.6 1.2 add_convert_fusion.4
  132.8 2.2 collective-permute-done.13
  135.0 1.2 add_convert_fusion.3
  136.2 2.7 %add_convert_fusion = bf16[8,896,256]{2,1,0:T(8,128)(2,1)} fusion(bf16[8,896,256]{2,1,0:T(8,128)(2,1)S(1)} %collective-permute-done.14, bf16[8,896,256]{2,1,0:T(8,128)(2,1)S(1)} %copy-done.6), kind=kLoop, calls=%fused_computation | loop fusion | flops 7340032 | bytes 11010048 | tf_op jit(solution)/shard_map/convert_element_type | solution.py:272
  139.0 2.7 %collective-permute-start.17 = (bf16[128,4096]{1,0:T(8,128)(2,1)}, bf16[128,4096]{1,0:T(8,128)(2,1)S(1)}, u32[]{:S(2)}, u32[]{:S(2)}) collective-permute-start(bf16[128,4096]{1,0:T(8,128)(2,1)} %get-tuple-element.51), channel_id=1, source_target_pairs={{0,12},{1,19},{4,0},{5,23},{8,4},{9,27},{12,8},{13,31},{16,28},{17... | collective-permute-start | bytes 3145736 | tf_op jit(solution)/shard_map/ppermute | solution.py:29
  141.7 1.4 collective-permute-start.18
  143.2 2.9 %collective-permute-done.19 = f32[4096]{0:T(1024)S(1)} collective-permute-done((f32[4096]{0:T(1024)S(1)}, f32[4096]{0:T(1024)S(1)}, u32[]{:S(2)}, u32[]{:S(2)}) %collective-permute-start.19) | collective-permute-done | bytes 16416 | tf_op jit(solution)/shard_map/ppermute | solution.py:235
  146.1 1.5 collective-permute-start.20
  147.6 2.3 %collective-permute-done.20 = f32[4096]{0:T(1024)S(1)} collective-permute-done((f32[4096]{0:T(1024)S(1)}, f32[4096]{0:T(1024)S(1)}, u32[]{:S(2)}, u32[]{:S(2)}) %collective-permute-start.20) | collective-permute-done | bytes 16416 | tf_op jit(solution)/shard_map/ppermute | solution.py:235
  149.9 5.1 %collective-permute-start.21 = (f32[4096]{0:T(1024)S(1)}, f32[4096]{0:T(1024)S(1)}, u32[]{:S(2)}, u32[]{:S(2)}) collective-permute-start(f32[4096]{0:T(1024)S(1)} %add.93), channel_id=1, source_target_pairs={{0,128},{1,129},{4,132},{5,133},{8,136},{9,137},{12,140},{13,141},... | collective-permute-start | bytes 49160 | tf_op jit(solution)/shard_map/ppermute | solution.py:235
  155.0 1.9 collective-permute-done.21
  156.9 5.1 %collective-permute-start.22 = (f32[4096]{0:T(1024)S(1)}, f32[4096]{0:T(1024)S(1)}, u32[]{:S(2)}, u32[]{:S(2)}) collective-permute-start(f32[4096]{0:T(1024)S(1)} %add.94), channel_id=1, source_target_pairs={{0,1},{1,0},{4,5},{5,4},{8,9},{9,8},{12,13},{13,12},{16,17},{17,16... | collective-permute-start | bytes 49160 | tf_op jit(solution)/shard_map/ppermute | solution.py:235
  162.0 0.8 collective-permute-done.22
  162.8 3.0 %collective-permute-done.23 = f32[4096]{0:T(1024)S(1)} collective-permute-done((f32[4096]{0:T(1024)S(1)}, f32[4096]{0:T(1024)S(1)}, u32[]{:S(2)}, u32[]{:S(2)}) %collective-permute-start.23) | collective-permute-done | bytes 16416 | tf_op jit(solution)/shard_map/ppermute | solution.py:235
  165.8 1.4 collective-permute-start.24
  167.1 2.7 %collective-permute-done.24 = f32[4096]{0:T(1024)S(1)} collective-permute-done((f32[4096]{0:T(1024)S(1)}, f32[4096]{0:T(1024)S(1)}, u32[]{:S(2)}, u32[]{:S(2)}) %collective-permute-start.24) | collective-permute-done | bytes 16416 | tf_op jit(solution)/shard_map/ppermute | solution.py:235
  169.9 3.0 %collective-permute-done.25 = f32[4096]{0:T(1024)S(1)} collective-permute-done((f32[4096]{0:T(1024)S(1)}, f32[4096]{0:T(1024)S(1)}, u32[]{:S(2)}, u32[]{:S(2)}) %collective-permute-start.25) | collective-permute-done | bytes 16416 | tf_op jit(solution)/shard_map/ppermute | solution.py:235
  172.9 4.1 %collective-permute-done.26 = f32[4096]{0:T(1024)S(1)} collective-permute-done((f32[4096]{0:T(1024)S(1)}, f32[4096]{0:T(1024)S(1)}, u32[]{:S(2)}, u32[]{:S(2)}) %collective-permute-start.26) | collective-permute-done | bytes 16416 | tf_op jit(solution)/shard_map/ppermute | solution.py:235
  177.0 0.6 add.99
  177.6 0.5 fusion.3
  178.7 0.7 collective-permute-start.29
  179.4 2.3 %collective-permute-start.27 = (bf16[2,32,4096]{2,1,0:T(8,128)(2,1)S(1)}, bf16[2,32,4096]{2,1,0:T(8,128)(2,1)S(1)}, u32[]{:S(2)}, u32[]{:S(2)}) collective-permute-start(bf16[2,32,4096]{2,1,0:T(8,128)(2,1)S(1)} %get-tuple-element.68), channel_id=1, source_target_pairs={{0,18},{1,13},{4,22},{5,1},{8,26},{9,5},{12,30},{13,9},{16,0},{17,... | collective-permute-start | bytes 1572872 | tf_op jit(solution)/shard_map/ppermute | solution.py:29
  181.7 12.6 %collective-permute-done.29 = bf16[2,32,4096]{2,1,0:T(8,128)(2,1)S(1)} collective-permute-done((bf16[2,32,4096]{2,1,0:T(8,128)(2,1)S(1)}, bf16[2,32,4096]{2,1,0:T(8,128)(2,1)S(1)}, u32[]{:S(2)}, u32[]{:S(2)}) %collective-permute-start.29) | collective-permute-done | bytes 524320 | tf_op jit(solution)/shard_map/ppermute | solution.py:29
  194.3 0.8 copy-done.10
  195.2 1.7 convert_add_fusion
  197.3 6.1 %collective-permute-start.30 = (bf16[1,4096]{1,0:T(2,128)(2,1)S(1)}, bf16[1,4096]{1,0:T(2,128)(2,1)S(1)}, u32[]{:S(2)}, u32[]{:S(2)}) collective-permute-start(bf16[1,4096]{1,0:T(2,128)(2,1)S(1)} %slice.78), channel_id=1, source_target_pairs={{0,1},{1,2},{2,3},{3,4},{4,5},{5,6},{6,7},{7,8},{8,9},{9,10},{10,1... | collective-permute-start | bytes 24584 | tf_op jit(solution)/shard_map/ppermute | solution.py:47
  203.4 2.7 %collective-permute-start.31 = (bf16[896,256]{1,0:T(8,128)(2,1)S(1)}, bf16[896,256]{1,0:T(8,128)(2,1)S(1)}, u32[]{:S(2)}, u32[]{:S(2)}) collective-permute-start(bf16[896,256]{1,0:T(8,128)(2,1)S(1)} %bitcast.45), channel_id=1, source_target_pairs={{0,0},{1,16},{4,4},{5,20},{8,8},{9,24},{12,12},{13,28},{16,1},{17,... | collective-permute-start | bytes 1376264 | tf_op jit(solution)/shard_map/ppermute | solution.py:41
  206.1 1.5 fusion.1
  207.6 1.4 fusion
  209.0 4.3 %collective-permute-done.31 = bf16[896,256]{1,0:T(8,128)(2,1)S(1)} collective-permute-done((bf16[896,256]{1,0:T(8,128)(2,1)S(1)}, bf16[896,256]{1,0:T(8,128)(2,1)S(1)}, u32[]{:S(2)}, u32[]{:S(2)}) %collective-permute-start.31) | collective-permute-done | bytes 458784 | tf_op jit(solution)/shard_map/ppermute | solution.py:41
  213.4 0.8 multiply_bitcast_fusion
  214.2 0.8 slice_convert_fusion
  (93 shorter events, 3.3 us)
Async XLA Ops:
  7.2 14.6 %copy-start = (bf16[128,4096]{1,0:T(8,128)(2,1)S(1)}, bf16[128,4096]{1,0:T(8,128)(2,1)}, u32[]{:S(2)}) copy-start(bf16[128,4096]{1,0:T(8,128)(2,1)} %param.11) | copy-start | bytes 3145732
  7.2 16.8 %copy-start.2 = (bf16[128,4096]{1,0:T(8,128)(2,1)S(1)}, bf16[128,4096]{1,0:T(8,128)(2,1)}, u32[]{:S(2)}) copy-start(bf16[128,4096]{1,0:T(8,128)(2,1)} %param.6) | copy-start | bytes 3145732
  7.2 68.6 %all-gather.3.cloned.1.call-start = ((), (), s32[]{:S(2)}) async-start(), calls=%async_computation.2 | async-start | bytes 4128768 | tf_op jit(solution)/shard_map/all_gather | solution.py:252
  10.1 10.8 %collective-permute-start.10 = (bf16[896,256]{1,0:T(8,128)(2,1)S(1)}, bf16[896,256]{1,0:T(8,128)(2,1)S(1)}, u32[]{:S(2)}, u32[]{:S(2)}) collective-permute-start(bf16[896,256]{1,0:T(8,128)(2,1)S(1)} %pad_maximum_fusion.3), channel_id=1, source_target_pairs={{0,0},{1,16},{4,4},{5,20},{8,8},{9,24},{12,12},{13,28},{16,1},{17,... | collective-permute-start | bytes 1376264 | tf_op jit(solution)/shard_map/ppermute | solution.py:41
  20.8 0.8 copy-start.12
  21.6 172.6 %reduce-scatter.2.cloned.1.call-start = ((), (), s32[]{:S(2)}) async-start(), calls=%async_computation.1 | async-start | bytes 4128768 | tf_op jit(solution)/shard_map/reduce_scatter | solution.py:217
  22.0 6.6 %collective-permute-start = (bf16[1,4096]{1,0:T(2,128)(2,1)S(1)}, bf16[1,4096]{1,0:T(2,128)(2,1)S(1)}, u32[]{:S(2)}, u32[]{:S(2)}) collective-permute-start(bf16[1,4096]{1,0:T(2,128)(2,1)S(1)} %slice.65), channel_id=1, source_target_pairs={{1,0},{2,1},{3,2},{4,3},{5,4},{6,5},{7,6},{8,7},{9,8},{10,9},{11,1... | collective-permute-start | bytes 24584 | tf_op jit(solution)/shard_map/ppermute | solution.py:47
  24.3 22.5 %copy-start.4 = (bf16[31,4096]{1,0:T(8,128)(2,1)}, bf16[31,4096]{1,0:T(8,128)(2,1)S(1)}, u32[]{:S(2)}) copy-start(bf16[31,4096]{1,0:T(8,128)(2,1)S(1)} %slice.64) | copy-start | bytes 761860
  28.7 14.3 %collective-permute-start.3 = (bf16[2,32,4096]{2,1,0:T(8,128)(2,1)S(1)}, bf16[2,32,4096]{2,1,0:T(8,128)(2,1)S(1)}, u32[]{:S(2)}, u32[]{:S(2)}) collective-permute-start(bf16[2,32,4096]{2,1,0:T(8,128)(2,1)S(1)} %pad_maximum_fusion.2), channel_id=1, source_target_pairs={{0,18},{1,13},{4,22},{5,1},{8,26},{9,5},{12,30},{13,9},{16,0},{17,... | collective-permute-start | bytes 1572872 | tf_op jit(solution)/shard_map/ppermute | solution.py:29
  31.2 11.8 %collective-permute-start.2 = (bf16[2,32,4096]{2,1,0:T(8,128)(2,1)S(1)}, bf16[2,32,4096]{2,1,0:T(8,128)(2,1)S(1)}, u32[]{:S(2)}, u32[]{:S(2)}) collective-permute-start(bf16[2,32,4096]{2,1,0:T(8,128)(2,1)S(1)} %pad_maximum_fusion.2), channel_id=1, source_target_pairs={{0,2},{1,9},{4,6},{5,13},{8,10},{9,1},{12,14},{13,5},{16,18},{17,2... | collective-permute-start | bytes 1572872 | tf_op jit(solution)/shard_map/ppermute | solution.py:29
  31.8 15.0 %collective-permute-start.1 = (bf16[2,32,4096]{2,1,0:T(8,128)(2,1)S(1)}, bf16[2,32,4096]{2,1,0:T(8,128)(2,1)S(1)}, u32[]{:S(2)}, u32[]{:S(2)}) collective-permute-start(bf16[2,32,4096]{2,1,0:T(8,128)(2,1)S(1)} %pad_maximum_fusion.2), channel_id=1, source_target_pairs={{0,16},{1,5},{4,20},{5,9},{8,24},{9,13},{12,28},{13,1},{16,2},{17,... | collective-permute-start | bytes 1572872 | tf_op jit(solution)/shard_map/ppermute | solution.py:29
  47.3 45.8 %copy-start.8 = (bf16[128,4096]{1,0:T(8,128)(2,1)}, bf16[128,4096]{1,0:T(8,128)(2,1)S(1)}, u32[]{:S(2)}) copy-start(bf16[128,4096]{1,0:T(8,128)(2,1)S(1)} %concatenate.18.refs_4_) | copy-start | bytes 3145732
  47.4 27.5 %copy-start.9 = (bf16[128,4096]{1,0:T(8,128)(2,1)}, bf16[128,4096]{1,0:T(8,128)(2,1)S(1)}, u32[]{:S(2)}) copy-start(bf16[128,4096]{1,0:T(8,128)(2,1)S(1)} %pad_maximum_fusion.refs_0_) | copy-start | bytes 3145732
  47.4 14.1 %collective-permute-start.7 = (bf16[128,4096]{1,0:T(8,128)(2,1)S(1)}, bf16[128,4096]{1,0:T(8,128)(2,1)S(1)}, u32[]{:S(2)}, u32[]{:S(2)}) collective-permute-start(bf16[128,4096]{1,0:T(8,128)(2,1)S(1)} %pad_maximum_fusion.refs_0_), channel_id=1, source_target_pairs={{0,12},{1,19},{4,0},{5,23},{8,4},{9,27},{12,8},{13,31},{16,28},{17... | collective-permute-start | bytes 3145736 | tf_op jit(solution)/shard_map/ppermute | solution.py:29
  47.5 16.3 %collective-permute-start.4 = (bf16[128,4096]{1,0:T(8,128)(2,1)S(1)}, bf16[128,4096]{1,0:T(8,128)(2,1)S(1)}, u32[]{:S(2)}, u32[]{:S(2)}) collective-permute-start(bf16[128,4096]{1,0:T(8,128)(2,1)S(1)} %pad_maximum_fusion.refs_0_), channel_id=1, source_target_pairs={{0,4},{1,17},{4,8},{5,21},{8,12},{9,25},{12,0},{13,29},{16,20},{17... | collective-permute-start | bytes 3145736 | tf_op jit(solution)/shard_map/ppermute | solution.py:29
  48.9 25.9 %collective-permute-start.6 = (bf16[128,4096]{1,0:T(8,128)(2,1)S(1)}, bf16[128,4096]{1,0:T(8,128)(2,1)S(1)}, u32[]{:S(2)}, u32[]{:S(2)}) collective-permute-start(bf16[128,4096]{1,0:T(8,128)(2,1)S(1)} %concatenate.18.refs_4_), channel_id=1, source_target_pairs={{0,4},{1,17},{4,8},{5,21},{8,12},{9,25},{12,0},{13,29},{16,20},{17... | collective-permute-start | bytes 3145736 | tf_op jit(solution)/shard_map/ppermute | solution.py:29
  50.6 25.2 %collective-permute-start.5 = (bf16[128,4096]{1,0:T(8,128)(2,1)S(1)}, bf16[128,4096]{1,0:T(8,128)(2,1)}, u32[]{:S(2)}, u32[]{:S(2)}) collective-permute-start(bf16[128,4096]{1,0:T(8,128)(2,1)S(1)} %concatenate.18.refs_4_), channel_id=1, source_target_pairs={{0,12},{1,19},{4,0},{5,23},{8,4},{9,27},{12,8},{13,31},{16,28},{17... | collective-permute-start | bytes 3145736 | tf_op jit(solution)/shard_map/ppermute | solution.py:29
  61.5 31.5 %copy-start.15 = (bf16[128,4096]{1,0:T(8,128)(2,1)}, bf16[128,4096]{1,0:T(8,128)(2,1)S(1)}, u32[]{:S(2)}) copy-start(bf16[128,4096]{1,0:T(8,128)(2,1)S(1)} %collective-permute-done.7.refs_3_) | copy-start | bytes 3145732
  63.7 29.3 %copy-start.16 = (bf16[128,4096]{1,0:T(8,128)(2,1)}, bf16[128,4096]{1,0:T(8,128)(2,1)S(1)}, u32[]{:S(2)}) copy-start(bf16[128,4096]{1,0:T(8,128)(2,1)S(1)} %collective-permute-done.4.refs_1_) | copy-start | bytes 3145732
  74.8 1.0 copy-start.17
  75.8 17.2 %collective-permute-start.11 = (bf16[8,896,256]{2,1,0:T(8,128)(2,1)}, bf16[8,896,256]{2,1,0:T(8,128)(2,1)S(1)}, u32[]{:S(2)}, u32[]{:S(2)}) collective-permute-start(bf16[8,896,256]{2,1,0:T(8,128)(2,1)} %bitcast.43), channel_id=1, source_target_pairs={{0,1},{1,0},{4,5},{5,4},{8,9},{9,8},{12,13},{13,12},{16,17},{17,16... | collective-permute-start | bytes 11010056 | tf_op jit(solution)/shard_map/ppermute | solution.py:34
  77.1 14.2 %collective-permute-start.9 = (bf16[128,4096]{1,0:T(8,128)(2,1)}, bf16[128,4096]{1,0:T(8,128)(2,1)S(1)}, u32[]{:S(2)}, u32[]{:S(2)}) collective-permute-start(bf16[128,4096]{1,0:T(8,128)(2,1)} %collective-permute-done.5.refs_7_), channel_id=1, source_target_pairs={{0,12},{1,19},{4,0},{5,23},{8,4},{9,27},{12,8},{13,31},{16,28},{17... | collective-permute-start | bytes 3145736 | tf_op jit(solution)/shard_map/ppermute | solution.py:29
  77.9 15.2 %collective-permute-start.8 = (bf16[128,4096]{1,0:T(8,128)(2,1)S(1)}, bf16[128,4096]{1,0:T(8,128)(2,1)S(1)}, u32[]{:S(2)}, u32[]{:S(2)}) collective-permute-start(bf16[128,4096]{1,0:T(8,128)(2,1)S(1)} %collective-permute-done.4.refs_1_), channel_id=1, source_target_pairs={{0,4},{1,17},{4,8},{5,21},{8,12},{9,25},{12,0},{13,29},{16,20},{17... | collective-permute-start | bytes 3145736 | tf_op jit(solution)/shard_map/ppermute | solution.py:29
  91.2 1.8 copy-start.18
  93.0 1.0 copy-start.19
  94.0 1.8 copy-start.14
  116.4 18.6 %copy-start.7 = (bf16[128,4096]{1,0:T(8,128)(2,1)S(1)}, bf16[128,4096]{1,0:T(8,128)(2,1)}, u32[]{:S(2)}) copy-start(bf16[128,4096]{1,0:T(8,128)(2,1)} %get-tuple-element.45) | copy-start | bytes 3145732
  116.4 19.9 %collective-permute-start.14 = (bf16[8,896,256]{2,1,0:T(8,128)(2,1)}, bf16[8,896,256]{2,1,0:T(8,128)(2,1)S(1)}, u32[]{:S(2)}, u32[]{:S(2)}) collective-permute-start(bf16[8,896,256]{2,1,0:T(8,128)(2,1)} %get-tuple-element.48), channel_id=1, source_target_pairs={{0,1},{1,0},{4,5},{5,4},{8,9},{9,8},{12,13},{13,12},{16,17},{17,16... | collective-permute-start | bytes 11010056 | tf_op jit(solution)/shard_map/ppermute | solution.py:34
  117.4 14.2 %collective-permute-start.12 = (bf16[128,4096]{1,0:T(8,128)(2,1)S(1)}, bf16[128,4096]{1,0:T(8,128)(2,1)S(1)}, u32[]{:S(2)}, u32[]{:S(2)}) collective-permute-start(bf16[128,4096]{1,0:T(8,128)(2,1)S(1)} %get-tuple-element.44), channel_id=1, source_target_pairs={{0,12},{1,19},{4,0},{5,23},{8,4},{9,27},{12,8},{13,31},{16,28},{17... | collective-permute-start | bytes 3145736 | tf_op jit(solution)/shard_map/ppermute | solution.py:29
  119.8 15.2 %collective-permute-start.13 = (bf16[128,4096]{1,0:T(8,128)(2,1)}, bf16[128,4096]{1,0:T(8,128)(2,1)S(1)}, u32[]{:S(2)}, u32[]{:S(2)}) collective-permute-start(bf16[128,4096]{1,0:T(8,128)(2,1)} %get-tuple-element.46), channel_id=1, source_target_pairs={{0,4},{1,17},{4,8},{5,21},{8,12},{9,25},{12,0},{13,29},{16,20},{17... | collective-permute-start | bytes 3145736 | tf_op jit(solution)/shard_map/ppermute | solution.py:29
  131.6 4.6 %copy-start.6 = (bf16[8,896,256]{2,1,0:T(8,128)(2,1)S(1)}, bf16[8,896,256]{2,1,0:T(8,128)(2,1)}, u32[]{:S(2)}) copy-start(bf16[8,896,256]{2,1,0:T(8,128)(2,1)} %get-tuple-element.47) | copy-start | bytes 11010052
  138.9 4.2 %copy-start.13 = (f32[4096]{0:T(1024)S(1)}, f32[4096]{0:T(1024)}, u32[]{:S(2)}) copy-start(f32[4096]{0:T(1024)} %param.8) | copy-start | bytes 49156
  138.9 38.7 %collective-permute-start.16 = (bf16[128,4096]{1,0:T(8,128)(2,1)S(1)}, bf16[128,4096]{1,0:T(8,128)(2,1)S(1)}, u32[]{:S(2)}, u32[]{:S(2)}) collective-permute-start(bf16[128,4096]{1,0:T(8,128)(2,1)S(1)} %get-tuple-element.50), channel_id=1, source_target_pairs={{0,4},{1,17},{4,8},{5,21},{8,12},{9,25},{12,0},{13,29},{16,20},{17... | collective-permute-start | bytes 3145736 | tf_op jit(solution)/shard_map/ppermute | solution.py:29
  139.0 38.6 %collective-permute-start.17 = (bf16[128,4096]{1,0:T(8,128)(2,1)}, bf16[128,4096]{1,0:T(8,128)(2,1)S(1)}, u32[]{:S(2)}, u32[]{:S(2)}) collective-permute-start(bf16[128,4096]{1,0:T(8,128)(2,1)} %get-tuple-element.51), channel_id=1, source_target_pairs={{0,12},{1,19},{4,0},{5,23},{8,4},{9,27},{12,8},{13,31},{16,28},{17... | collective-permute-start | bytes 3145736 | tf_op jit(solution)/shard_map/ppermute | solution.py:29
  141.7 35.9 %collective-permute-start.15 = (bf16[128,4096]{1,0:T(8,128)(2,1)}, bf16[128,4096]{1,0:T(8,128)(2,1)S(1)}, u32[]{:S(2)}, u32[]{:S(2)}) collective-permute-start(bf16[128,4096]{1,0:T(8,128)(2,1)} %add_convert_fusion.4), channel_id=1, source_target_pairs={{0,12},{1,19},{4,0},{5,23},{8,4},{9,27},{12,8},{13,31},{16,28},{17... | collective-permute-start | bytes 3145736 | tf_op jit(solution)/shard_map/ppermute | solution.py:29
  141.7 35.9 %collective-permute-start.18 = (bf16[128,4096]{1,0:T(8,128)(2,1)}, bf16[128,4096]{1,0:T(8,128)(2,1)S(1)}, u32[]{:S(2)}, u32[]{:S(2)}) collective-permute-start(bf16[128,4096]{1,0:T(8,128)(2,1)} %add_convert_fusion.3), channel_id=1, source_target_pairs={{0,4},{1,17},{4,8},{5,21},{8,12},{9,25},{12,0},{13,29},{16,20},{17... | collective-permute-start | bytes 3145736 | tf_op jit(solution)/shard_map/ppermute | solution.py:29
  143.1 3.0 %collective-permute-start.19 = (f32[4096]{0:T(1024)S(1)}, f32[4096]{0:T(1024)S(1)}, u32[]{:S(2)}, u32[]{:S(2)}) collective-permute-start(f32[4096]{0:T(1024)S(1)} %div.35), channel_id=1, source_target_pairs={{0,32},{1,33},{4,36},{5,37},{8,40},{9,41},{12,44},{13,45},{16,48},... | collective-permute-start | bytes 49160 | tf_op jit(solution)/shard_map/ppermute | solution.py:235
  146.1 3.8 %collective-permute-start.20 = (f32[4096]{0:T(1024)S(1)}, f32[4096]{0:T(1024)S(1)}, u32[]{:S(2)}, u32[]{:S(2)}) collective-permute-start(f32[4096]{0:T(1024)S(1)} %add.92), channel_id=1, source_target_pairs={{0,64},{1,65},{4,68},{5,69},{8,72},{9,73},{12,76},{13,77},{16,80},... | collective-permute-start | bytes 49160 | tf_op jit(solution)/shard_map/ppermute | solution.py:235
  149.9 7.0 %collective-permute-start.21 = (f32[4096]{0:T(1024)S(1)}, f32[4096]{0:T(1024)S(1)}, u32[]{:S(2)}, u32[]{:S(2)}) collective-permute-start(f32[4096]{0:T(1024)S(1)} %add.93), channel_id=1, source_target_pairs={{0,128},{1,129},{4,132},{5,133},{8,136},{9,137},{12,140},{13,141},... | collective-permute-start | bytes 49160 | tf_op jit(solution)/shard_map/ppermute | solution.py:235
  156.9 5.9 %collective-permute-start.22 = (f32[4096]{0:T(1024)S(1)}, f32[4096]{0:T(1024)S(1)}, u32[]{:S(2)}, u32[]{:S(2)}) collective-permute-start(f32[4096]{0:T(1024)S(1)} %add.94), channel_id=1, source_target_pairs={{0,1},{1,0},{4,5},{5,4},{8,9},{9,8},{12,13},{13,12},{16,17},{17,16... | collective-permute-start | bytes 49160 | tf_op jit(solution)/shard_map/ppermute | solution.py:235
  162.8 3.0 %collective-permute-start.23 = (f32[4096]{0:T(1024)S(1)}, f32[4096]{0:T(1024)S(1)}, u32[]{:S(2)}, u32[]{:S(2)}) collective-permute-start(f32[4096]{0:T(1024)S(1)} %add.95), channel_id=1, source_target_pairs={{0,16},{1,17},{4,20},{5,21},{8,24},{9,25},{12,28},{13,29},{16,0},{... | collective-permute-start | bytes 49160 | tf_op jit(solution)/shard_map/ppermute | solution.py:235
  165.8 4.1 %collective-permute-start.24 = (f32[4096]{0:T(1024)S(1)}, f32[4096]{0:T(1024)S(1)}, u32[]{:S(2)}, u32[]{:S(2)}) collective-permute-start(f32[4096]{0:T(1024)S(1)} %add.96), channel_id=1, source_target_pairs={{0,2},{1,3},{4,6},{5,7},{8,10},{9,11},{12,14},{13,15},{16,18},{17,... | collective-permute-start | bytes 49160 | tf_op jit(solution)/shard_map/ppermute | solution.py:235
  169.9 3.0 %collective-permute-start.25 = (f32[4096]{0:T(1024)S(1)}, f32[4096]{0:T(1024)S(1)}, u32[]{:S(2)}, u32[]{:S(2)}) collective-permute-start(f32[4096]{0:T(1024)S(1)} %add.97), channel_id=1, source_target_pairs={{0,4},{1,5},{4,0},{5,1},{8,12},{9,13},{12,8},{13,9},{16,20},{17,21... | collective-permute-start | bytes 49160 | tf_op jit(solution)/shard_map/ppermute | solution.py:235
  172.9 4.1 %collective-permute-start.26 = (f32[4096]{0:T(1024)S(1)}, f32[4096]{0:T(1024)S(1)}, u32[]{:S(2)}, u32[]{:S(2)}) collective-permute-start(f32[4096]{0:T(1024)S(1)} %add.98), channel_id=1, source_target_pairs={{0,8},{1,9},{4,12},{5,13},{8,0},{9,1},{12,4},{13,5},{16,24},{17,25... | collective-permute-start | bytes 49160 | tf_op jit(solution)/shard_map/ppermute | solution.py:235
  178.7 15.6 %collective-permute-start.29 = (bf16[2,32,4096]{2,1,0:T(8,128)(2,1)S(1)}, bf16[2,32,4096]{2,1,0:T(8,128)(2,1)S(1)}, u32[]{:S(2)}, u32[]{:S(2)}) collective-permute-start(bf16[2,32,4096]{2,1,0:T(8,128)(2,1)S(1)} %get-tuple-element.67), channel_id=1, source_target_pairs={{0,16},{1,5},{4,20},{5,9},{8,24},{9,13},{12,28},{13,1},{16,2},{17,... | collective-permute-start | bytes 1572872 | tf_op jit(solution)/shard_map/ppermute | solution.py:29
  179.4 14.9 %collective-permute-start.27 = (bf16[2,32,4096]{2,1,0:T(8,128)(2,1)S(1)}, bf16[2,32,4096]{2,1,0:T(8,128)(2,1)S(1)}, u32[]{:S(2)}, u32[]{:S(2)}) collective-permute-start(bf16[2,32,4096]{2,1,0:T(8,128)(2,1)S(1)} %get-tuple-element.68), channel_id=1, source_target_pairs={{0,18},{1,13},{4,22},{5,1},{8,26},{9,5},{12,30},{13,9},{16,0},{17,... | collective-permute-start | bytes 1572872 | tf_op jit(solution)/shard_map/ppermute | solution.py:29
  181.7 12.6 %collective-permute-start.28 = (bf16[2,32,4096]{2,1,0:T(8,128)(2,1)S(1)}, bf16[2,32,4096]{2,1,0:T(8,128)(2,1)}, u32[]{:S(2)}, u32[]{:S(2)}) collective-permute-start(bf16[2,32,4096]{2,1,0:T(8,128)(2,1)S(1)} %get-tuple-element.69), channel_id=1, source_target_pairs={{0,2},{1,9},{4,6},{5,13},{8,10},{9,1},{12,14},{13,5},{16,18},{17,2... | collective-permute-start | bytes 1572872 | tf_op jit(solution)/shard_map/ppermute | solution.py:29
  194.3 0.8 copy-start.10
  194.3 1.0 copy-start.11
  195.2 8.2 %copy-start.20 = (bf16[1,896,256]{2,1,0:T(8,128)(2,1)S(1)}, bf16[1,896,256]{2,1,0:T(8,128)(2,1)}, u32[]{:S(2)}) copy-start(bf16[1,896,256]{2,1,0:T(8,128)(2,1)} %reduce-scatter.2.cloned.1.call-done) | copy-start | bytes 1376260
  195.2 10.9 %copy-start.1 = (bf16[128,4096]{1,0:T(8,128)(2,1)S(1)}, bf16[128,4096]{1,0:T(8,128)(2,1)}, u32[]{:S(2)}) copy-start(bf16[128,4096]{1,0:T(8,128)(2,1)} %param.11) | copy-start | bytes 3145732
  195.2 10.9 %copy-start.5 = (bf16[31,4096]{1,0:T(8,128)(2,1)S(1)}, bf16[31,4096]{1,0:T(8,128)(2,1)}, u32[]{:S(2)}) copy-start(bf16[31,4096]{1,0:T(8,128)(2,1)} %copy-done.4) | copy-start | bytes 761860
  197.0 10.6 %copy-start.3 = (bf16[128,4096]{1,0:T(8,128)(2,1)S(1)}, bf16[128,4096]{1,0:T(8,128)(2,1)}, u32[]{:S(2)}) copy-start(bf16[128,4096]{1,0:T(8,128)(2,1)} %param.6) | copy-start | bytes 3145732
  197.3 10.3 %collective-permute-start.30 = (bf16[1,4096]{1,0:T(2,128)(2,1)S(1)}, bf16[1,4096]{1,0:T(2,128)(2,1)S(1)}, u32[]{:S(2)}, u32[]{:S(2)}) collective-permute-start(bf16[1,4096]{1,0:T(2,128)(2,1)S(1)} %slice.78), channel_id=1, source_target_pairs={{0,1},{1,2},{2,3},{3,4},{4,5},{5,6},{6,7},{7,8},{8,9},{9,10},{10,1... | collective-permute-start | bytes 24584 | tf_op jit(solution)/shard_map/ppermute | solution.py:47
  203.4 10.0 %collective-permute-start.31 = (bf16[896,256]{1,0:T(8,128)(2,1)S(1)}, bf16[896,256]{1,0:T(8,128)(2,1)S(1)}, u32[]{:S(2)}, u32[]{:S(2)}) collective-permute-start(bf16[896,256]{1,0:T(8,128)(2,1)S(1)} %bitcast.45), channel_id=1, source_target_pairs={{0,0},{1,16},{4,4},{5,20},{8,8},{9,24},{12,12},{13,28},{16,1},{17,... | collective-permute-start | bytes 1376264 | tf_op jit(solution)/shard_map/ppermute | solution.py:41
Sparse Core Ops, SparseCore 0:
  21.8 52.5 all-gather.2
  139.0 48.1 reduce-scatter.1

commit v4 on v3

--- a/solution.py
+++ b/solution.py
@@ -55,15 +55,30 @@
     return jnp.dot(a, b, preferred_element_type=jnp.float32)
 
 
-def block_kernel(chunks, *refs):
-    acts = list(zip(refs[:4], refs[4:8]))
-    w_own, w_oth = refs[8:10]
-    outs = list(zip(refs[10:14], refs[14:18]))
-    g_own, g_oth, gain = refs[18:21]
-    (p_s, g_s, wi_s, wo_s, d_s, n_s, gi_s, go_s, h_s, ga_s, sq_s, act, gp, act_t, gp_t, in_sem,
-     out_sem) = refs[21:]
+def block_kernel(chunks, blocks, kept, *refs):
+    refs = list(refs)
+
+    def take(count):
+        part = refs[:count]
+        del refs[:count]
+        return part
+
+    last = kept > 0
+    acts = list(zip(take(blocks), take(blocks)))
+    olds = list(zip(take(kept), take(kept)))
+    w_own, w_oth = take(2)
+    old_act, old_gp = take(2) if last else (None, None)
+    outs = list(zip(take(blocks), take(blocks)))
+    if last:
+        g_own, g_oth, gain = take(3)
+    else:
+        new_act, new_gp = take(2)
+    p_s, g_s, wi_s, wo_s, d_s, n_s, h_s, ga_s, sq_s, act, gp, in_sem, out_sem = take(13)
+    if last:
+        gi_s, go_s, act_t, gp_t, old_sem = take(5)
     core = lax.axis_index("c")
-    rows = refs[0].shape[0]
+    rows = acts[0][0].shape[0]
+    fresh = rows * blocks
     hidden = wi_s.shape[0]
     half = w_own.shape[2]
     width = 2 * half
@@ -93,18 +108,29 @@
             ).start()
         return carry
 
+    def fetch_old(z, carry):
+        for i, pair in enumerate(olds):
+            at = pl.ds(fresh + i * rows, rows)
+            for k, (source, buf) in enumerate(zip(pair, (p_s, g_s))):
+                pltpu.make_async_copy(
+                    source.at[:, cols(z)], buf.at[at, cols(z)], old_sem.at[k, z]
+                ).start()
+        return carry
+
     lax.fori_loop(0, chunks, fetch, 0)
+    if last:
+        lax.fori_loop(0, chunks, fetch_old, 0)
     h_s[...] = jnp.zeros_like(h_s)
     ga_s[...] = jnp.zeros_like(ga_s)
     sq_s[...] = jnp.zeros_like(sq_s)
 
     def first(z, carry):
-        for k, buf in enumerate((p_s, g_s, wi_s, wo_s)):
+        for k, buf in enumerate((p_s.at[pl.ds(0, fresh)], g_s.at[pl.ds(0, fresh)], wi_s, wo_s)):
             view = buf.at[:, cols(z)]
             pltpu.make_async_copy(view, view, in_sem.at[k, z]).wait()
-        p = p_s[:, cols(z)]
+        p = p_s[pl.ds(0, fresh), cols(z)]
         h_s[...] += nt(p, wi_s[:, cols(z)])
-        ga_s[...] += nt(g_s[:, cols(z)], wo_s[:, cols(z)])
+        ga_s[...] += nt(g_s[pl.ds(0, fresh), cols(z)], wo_s[:, cols(z)])
         pf = p.astype(jnp.float32)
         sq_s[...] += jnp.sum(pf * pf, axis=1, keepdims=True)
         return carry
@@ -120,23 +146,34 @@
     b = (ga_s[...] * slope * inv).astype(jnp.bfloat16)
     act[...] = a
     gp[...] = b
-    act_t[...] = a.T
-    gp_t[...] = b.T
+    if last:
+        act_t[:, pl.ds(0, fresh)] = a.T
+        gp_t[:, pl.ds(0, fresh)] = b.T
+        act_t[:, pl.ds(fresh, rows * kept)] = old_act[...].T
+        gp_t[:, pl.ds(fresh, rows * kept)] = old_gp[...].T
+    else:
+        new_act[...] = a
+        new_gp[...] = b
 
     def second(z, carry):
         wi = wi_s[:, cols(z)]
         d_s[:, cols(z)] = nn(act[...], wo_s[:, cols(z)]).astype(jnp.bfloat16)
         n_s[:, cols(z)] = nn(gp[...], wi).astype(jnp.bfloat16)
-        go_s[:, cols(z)] = nn(act_t[...], g_s[:, cols(z)]).astype(jnp.bfloat16)
-        gi = nn(gp_t[...], p_s[:, cols(z)])
-        gi_s[:, cols(z)] = gi.astype(jnp.bfloat16)
-        gain[:, cols(z)] = jnp.sum(gi * wi.astype(jnp.float32), axis=0, keepdims=True)
         for i, pair in enumerate(outs):
             at = pl.ds(i * rows, rows)
             for k, (dest, buf) in enumerate(zip(pair, (d_s, n_s))):
                 pltpu.make_async_copy(
                     buf.at[at, cols(z)], dest.at[:, cols(z)], out_sem.at[k, z]
                 ).start()
+        if not last:
+            return carry
+        for k, buf in enumerate((p_s, g_s)):
+            view = buf.at[pl.ds(fresh, rows * kept), cols(z)]
+            pltpu.make_async_copy(view, view, old_sem.at[k, z]).wait()
+        go_s[:, cols(z)] = nn(act_t[...], g_s[:, cols(z)]).astype(jnp.bfloat16)
+        gi = nn(gp_t[...], p_s[:, cols(z)])
+        gi_s[:, cols(z)] = gi.astype(jnp.bfloat16)
+        gain[:, cols(z)] = jnp.sum(gi * wi.astype(jnp.float32), axis=0, keepdims=True)
         for dest, which in ((g_own, core), (g_oth, 1 - core)):
             pltpu.make_async_copy(
                 gi_s.at[:, w_cols(z, which)], dest.at[z, pl.ds(0, hidden), :], out_sem.at[2, z]
@@ -149,7 +186,7 @@
     lax.fori_loop(0, chunks, second, 0)
 
     def drain(z, carry):
-        for k, buf in enumerate((d_s, n_s, gi_s, go_s)):
+        for k, buf in enumerate((d_s, n_s, gi_s, go_s) if last else (d_s, n_s)):
             view = buf.at[:, cols(z)]
             pltpu.make_async_copy(view, view, out_sem.at[k, z]).wait()
         return carry
@@ -157,35 +194,49 @@
     lax.fori_loop(0, chunks, drain, 0)
 
 
-def block(acts, w_own, w_oth):
-    rows, feats = acts[0].shape
+def block(pooled, cotangent, w_own, w_oth, old=None):
+    n = len(pooled)
+    rows, feats = pooled[0].shape
     chunks, hidden2, half = w_own.shape
     hidden = hidden2 // 2
-    total = 4 * rows
     bf = jnp.bfloat16
-    anywhere = pl.BlockSpec(memory_space=pl.ANY)
-    flops = 12 * total * feats * hidden
+    old_p, old_g, old_acts = old or ([], [], [])
+    kept = len(old_p)
+    fresh, total = n * rows, (n + kept) * rows
+    anywhere, inside = pl.BlockSpec(memory_space=pl.ANY), pl.BlockSpec(memory_space=pltpu.VMEM)
+    out_shape = [jax.ShapeDtypeStruct((rows, feats), bf)] * (2 * n)
+    out_specs = [anywhere] * (2 * n)
+    scratch = [pltpu.VMEM((total, feats), bf)] * 2
+    scratch += [pltpu.VMEM((hidden, feats), bf)] * 2
+    scratch += [pltpu.VMEM((fresh, feats), bf)] * 2
+    scratch += [pltpu.VMEM((fresh, hidden), jnp.float32)] * 2
+    scratch += [pltpu.VMEM((fresh, 1), jnp.float32)]
+    scratch += [pltpu.VMEM((fresh, hidden), bf)] * 2
+    scratch += [pltpu.SemaphoreType.DMA((4, chunks))] * 2
+    if kept:
+        out_shape += [jax.ShapeDtypeStruct(w_own.shape, bf)] * 2
+        out_shape += [jax.ShapeDtypeStruct((1, feats), jnp.float32)]
+        out_specs += [anywhere, anywhere, inside]
+        scratch += [pltpu.VMEM((hidden, feats), bf)] * 2
+        scratch += [pltpu.VMEM((hidden, total), bf)] * 2
+        scratch += [pltpu.SemaphoreType.DMA((2, chunks))]
+    else:
+        out_shape += [jax.ShapeDtypeStruct((fresh, hidden), bf)] * 2
+        out_specs += [inside, inside]
+    products = 4 * fresh + (2 * total if kept else 0)
     return pl.pallas_call(
-        functools.partial(block_kernel, chunks),
-        out_shape=[jax.ShapeDtypeStruct(act.shape, bf) for act in acts]
-        + [jax.ShapeDtypeStruct(w_own.shape, bf)] * 2
-        + [jax.ShapeDtypeStruct((1, feats), jnp.float32)],
-        in_specs=[anywhere] * 10,
-        out_specs=[anywhere] * 10 + [pl.BlockSpec(memory_space=pltpu.VMEM)],
-        scratch_shapes=[pltpu.VMEM((total, feats), bf)] * 2
-        + [pltpu.VMEM((hidden, feats), bf)] * 2
-        + [pltpu.VMEM((total, feats), bf)] * 2
-        + [pltpu.VMEM((hidden, feats), bf)] * 2
-        + [pltpu.VMEM((total, hidden), jnp.float32)] * 2
-        + [pltpu.VMEM((total, 1), jnp.float32)]
-        + [pltpu.VMEM((total, hidden), bf)] * 2
-        + [pltpu.VMEM((hidden, total), bf)] * 2
-        + [pltpu.SemaphoreType.DMA((4, chunks)), pltpu.SemaphoreType.DMA((4, chunks))],
+        functools.partial(block_kernel, chunks, n, kept),
+        out_shape=out_shape,
+        in_specs=[anywhere] * (2 * n + 2 * kept + 2) + [inside] * len(old_acts),
+        out_specs=out_specs,
+        scratch_shapes=scratch,
         compiler_params=pltpu.CompilerParams(vmem_limit_bytes=48 * 1024 * 1024),
         cost_estimate=pl.CostEstimate(
-            flops=flops, bytes_accessed=8 * (total + hidden) * feats * 2, transcendentals=0
+            flops=2 * products * feats * hidden,
+            bytes_accessed=2 * feats * (2 * total + 2 * fresh + (4 if kept else 2) * hidden),
+            transcendentals=0,
         ),
-    )(*acts, w_own, w_oth)
+    )(*pooled, *cotangent, *old_p, *old_g, w_own, w_oth, *old_acts)
 
 
 def add_all(parts):
@@ -204,38 +255,44 @@
     g1, p3 = shift(g0, second=1), shift(p0, second=-1)
     p1, g3, g1, p3 = lax.optimization_barrier((p1, g3, g1, p3))
     p2, g2 = shift(p1, second=1), shift(g3, second=-1)
-    return [p0, p1, p2, p3, g0, g1, g2, g3]
-
-
-def scatter_plane(outs, gain_part, weight_part):
-    d0, d1, d2, d3, n0, n1, n2, n3 = outs
-    bf = jnp.bfloat16
-    d2, n2 = shift(d2, second=-1), shift(n2, second=1)
-    n1, d3 = shift(n1, second=-1), shift(d3, second=1)
-    d1, n3 = add_all([d1, d2]).astype(bf), add_all([n3, n2]).astype(bf)
-    d1, n3, weight_part = lax.optimization_barrier((d1, n3, weight_part))
-    weight_sum = lax.psum_scatter(weight_part, "z", scatter_dimension=0, tiled=False)
-    d1, n3 = shift(d1, second=-1), shift(n3, second=1)
-    arrived = (d1, d3, n1, n3, total_over_all(gain_part))
-    d1, d3, n1, n3, grad_gain = lax.optimization_barrier(arrived)
-    both = jnp.stack([add_all([d0, d1, d3]).astype(bf), add_all([n0, n1, n3]).astype(bf)])
-    rows = both.shape[1] // 4
-    both = [both[:, d * rows : (d + 1) * rows] for d in range(4)]
-    arrived = [shift(both[d], first=-d) for d in (1, 2, 3)] + [weight_sum]
-    *arrived, weight_sum = lax.optimization_barrier(arrived)
-    return add_all([both[0], *arrived]), grad_gain, weight_sum
-
-
-def total_over_all(value):
-    moves = [lambda p, k=k: (p[0] ^ k, p[1], p[2], p[3]) for k in (1, 2, 4)]
-    moves += [lambda p: (p[0], p[1], p[2], 1 - p[3])]
-    moves += [lambda p, k=k: (p[0], p[1] ^ k, p[2], p[3]) for k in (1, 2)]
-    moves += [lambda p, k=k: (p[0], p[1], p[2] ^ k, p[3]) for k in (1, 2)]
+    return [p0, p1, p2, p3], [g0, g1, g2, g3]
+
+
+def swapped(value, moves):
     for move in moves:
         value = value + lax.ppermute(
             value, AXES, [(linear(*p), linear(*move(p))) for p in places()]
         )
     return value
+
+
+def all_moves():
+    moves = [lambda p, k=k: (p[0] ^ k, p[1], p[2], p[3]) for k in (1, 2, 4)]
+    moves += [lambda p: (p[0], p[1], p[2], 1 - p[3])]
+    moves += [lambda p, k=k: (p[0], p[1] ^ k, p[2], p[3]) for k in (1, 2)]
+    return moves + [lambda p, k=k: (p[0], p[1], p[2] ^ k, p[3]) for k in (1, 2)]
+
+
+def scatter_plane(d0, d1, d2, d3, n0, n1, n2, n3, g_own, g_oth, gain):
+    bf = jnp.bfloat16
+    tie = lax.optimization_barrier
+    moves = all_moves()
+    n1, d3 = shift(n1, second=-1), shift(d3, second=1)
+    mine = add_all([g_own, other_core(g_oth)]).astype(bf)
+    weight_sum = lax.psum_scatter(mine, "z", scatter_dimension=0, tiled=False)
+    d2, n2, n1, d3, gain = tie((d2, n2, n1, d3, swapped(gain, moves[:2])))
+    d2, n2 = shift(d2, second=-1), shift(n2, second=1)
+    gain = swapped(gain, moves[2:4])
+    d1, n3 = add_all([d1, d2]).astype(bf), add_all([n3, n2]).astype(bf)
+    d1, n3, gain = tie((d1, n3, gain))
+    d1, n3, gain = tie((shift(d1, second=-1), shift(n3, second=1), swapped(gain, moves[4:6])))
+    both = jnp.stack([add_all([d0, d1, d3]).astype(bf), add_all([n0, n1, n3]).astype(bf)])
+    rows = both.shape[1] // 4
+    both = [both[:, d * rows : (d + 1) * rows] for d in range(4)]
+    arrived = [shift(both[d], first=-d) for d in (1, 2, 3)] + [weight_sum]
+    gain = swapped(gain, moves[6:])
+    *arrived, weight_sum, gain = tie((*arrived, gain))
+    return add_all([both[0], *arrived]), gain, weight_sum
 
 
 def shards(stream, doc_start, norm_gain, weight_in, weight_out, upstream):
@@ -263,14 +320,15 @@
     grad_coarse = jnp.concatenate([group_sums[1:], following], axis=0)
 
     acts = jnp.stack([pooled, grad_coarse], axis=0)
-    blocks = gather_plane(acts)
-    w_own = lax.optimization_barrier((w_own, blocks[1], blocks[3]))[0]
+    p, g = gather_plane(acts)
+    w_own = lax.optimization_barrier((w_own, p[1], p[3]))[0]
     w_oth = other_core(w_own)
-    results = block(blocks, w_own, w_oth)
-    outs, (g_own, g_oth, gain_part) = results[:8], results[8:]
-
-    mine = (g_own.astype(jnp.float32) + other_core(g_oth).astype(jnp.float32)).astype(bf)
-    (down_sum, scaled), grad_gain, grads = scatter_plane(outs, gain_part[0] / norm_gain, mine)
+    early = [[part[0], part[1], part[3]] for part in (p, g)]
+    d0, d1, d3, n0, n1, n3, *kept = block(*early, w_own, w_oth)
+    d2, n2, g_own, g_oth, gain_part = block(p[2:3], g[2:3], w_own, w_oth, (*early, kept))
+    (down_sum, scaled), grad_gain, grads = scatter_plane(
+        d0, d1, d2, d3, n0, n1, n2, n3, g_own, g_oth, gain_part[0] / norm_gain
+    )
     grads = swap_low(grads)
     grad_weight_in = (grads[:hidden].astype(jnp.float32) * gain[None, :]).T
     grad_weight_out = grads[hidden:].astype(jnp.float32)

time: 222 us -> 220 us (level)
  waiting for transfers between devices: 113 us -> 97.4 us
  Pallas kernels: 20.5 us -> 28.3 us
  other arithmetic: 13.3 us -> 17.1 us
  local copies, waits for them, and re-layouts: 7.22 us -> 10.8 us
    ppermute x18, waiting for transfers between devices: 78.6 us -> 39.9 us  [shift(): return lax.ppermute(value, AXES, pairs)]
    ppermute x8, waiting for transfers between devices: 20.6 us -> 35.4 us  [swapped(): lax.ppermute(value, AXES, [(linear(*p), linear(*move(p))) for p in places...]
    ppermute x2, waiting for transfers between devices: 0.01 us -> 9.56 us  [other_core(): return lax.ppermute(value, AXES, pairs)]
    pallas_call x1 -> x2, Pallas kernels: 20.5 us -> 28.3 us  [block(): pl.pallas_call(functools.partial(block_kernel, chunks, n, kept), out_shap...]
    ppermute x8, starting transfers between devices: 13.2 us -> 17.3 us  [swapped(): lax.ppermute(value, AXES, [(linear(*p), linear(*move(p))) for p in places...]
    ppermute x2, starting transfers between devices: 8.05 us -> 3.97 us  [from_behind(): return lax.ppermute(value, AXES, pairs)]
    unnamed x42 -> x44, local copies, waits for them, and re-layouts: 5.49 us -> 8.36 us
    another operation x3, other arithmetic: 1.06 us -> 3.53 us  [scatter_plane(): jnp.stack([add_all([d0, d1, d3]).astype(bf), add_all([n0, n1, n3]).astype...]
  transfers between devices with their start and end apart: 34 -> 34, of which waited for: 21 -> 20; matrix products, arithmetic and copies ran while one was open for 4% -> 8% of each run, Pallas kernels for 0% -> 6%
where the time goes in v4:
time: 220 us; the launch traced here: 219 us
  waiting for transfers between devices  97.4 us (44%)
  starting transfers between devices  47.9 us (22%)
  Pallas kernels  28.3 us (13%)
  other arithmetic  17.1 us (8%)
  between operations  14.5 us (7%)
  local copies, waits for them, and re-layouts  10.8 us (5%)
  matrix products  3.44 us (2%)
    ppermute x18, waiting for transfers between devices, shift(): return lax.ppermute(value, AXES, pairs)  39.9 us
    ppermute x8, waiting for transfers between devices, swapped(): lax.ppermute(value, AXES, [(linear(*p), linear(*move(p))) for p in places...  35.4 us
    pallas_call x2, Pallas kernels, block(): pl.pallas_call(functools.partial(block_kernel, chunks, n, kept), out_shap...  28.3 us
    ppermute x8, starting transfers between devices, swapped(): lax.ppermute(value, AXES, [(linear(*p), linear(*move(p))) for p in places...  17.3 us
    ppermute x18, starting transfers between devices, shift(): return lax.ppermute(value, AXES, pairs)  16.7 us
    ppermute x2, waiting for transfers between devices, other_core(): return lax.ppermute(value, AXES, pairs)  9.56 us
    unnamed x44, local copies, waits for them, and re-layouts  8.36 us
    ppermute x2, starting transfers between devices, swap_low(): return lax.ppermute(value, AXES, pairs)  8.32 us
  transfers between devices with their start and end apart: 34, of which 20 were waited for; matrix products, arithmetic and copies ran while one was open for 8% of the time, Pallas kernels for 6%

profile of v4, /device:TPU:1, one launch (start us, length us, event | category | flops | bytes accessed | tf_op | source)
XLA Modules:
  0.0 219.5 jit_solution(9340761422476102348)
XLA Ops:
  7.2 0.9 dynamic_slice.3
  8.1 1.0 fusion.20
  9.1 1.0 pad_maximum_fusion.3
  10.1 4.6 %collective-permute-start.8 = (bf16[896,256]{1,0:T(8,128)(2,1)S(1)}, bf16[896,256]{1,0:T(8,128)(2,1)S(1)}, u32[]{:S(2)}, u32[]{:S(2)}) collective-permute-start(bf16[896,256]{1,0:T(8,128)(2,1)S(1)} %pad_maximum_fusion.3), channel_id=1, source_target_pairs={{0,0},{1,16},{4,4},{5,20},{8,8},{9,24},{12,12},{13,28},{16,1},{17,... | collective-permute-start | bytes 1376264 | tf_op jit(solution)/shard_map/ppermute | solution.py:41
  15.8 5.1 %collective-permute-done.8 = bf16[896,256]{1,0:T(8,128)(2,1)S(1)} collective-permute-done((bf16[896,256]{1,0:T(8,128)(2,1)S(1)}, bf16[896,256]{1,0:T(8,128)(2,1)S(1)}, u32[]{:S(2)}, u32[]{:S(2)}) %collective-permute-start.8) | collective-permute-done | bytes 458784 | tf_op jit(solution)/shard_map/ppermute | solution.py:41
  20.8 0.8 copy-done.15
  22.0 1.9 collective-permute-start
  24.3 4.3 %collective-permute-done = bf16[1,4096]{1,0:T(2,128)(2,1)S(1)} collective-permute-done((bf16[1,4096]{1,0:T(2,128)(2,1)S(1)}, bf16[1,4096]{1,0:T(2,128)(2,1)S(1)}, u32[]{:S(2)}, u32[]{:S(2)}) %collective-permute-start) | collective-permute-done | bytes 8224 | tf_op jit(solution)/shard_map/ppermute | solution.py:47
  28.7 2.6 %collective-permute-start.3 = (bf16[2,32,4096]{2,1,0:T(8,128)(2,1)S(1)}, bf16[2,32,4096]{2,1,0:T(8,128)(2,1)S(1)}, u32[]{:S(2)}, u32[]{:S(2)}) collective-permute-start(bf16[2,32,4096]{2,1,0:T(8,128)(2,1)S(1)} %pad_maximum_fusion.2), channel_id=1, source_target_pairs={{0,18},{1,13},{4,22},{5,1},{8,26},{9,5},{12,30},{13,9},{16,0},{17,... | collective-permute-start | bytes 1572872 | tf_op jit(solution)/shard_map/ppermute | solution.py:29
  32.4 10.6 %collective-permute-done.3 = bf16[2,32,4096]{2,1,0:T(8,128)(2,1)S(1)} collective-permute-done((bf16[2,32,4096]{2,1,0:T(8,128)(2,1)S(1)}, bf16[2,32,4096]{2,1,0:T(8,128)(2,1)S(1)}, u32[]{:S(2)}, u32[]{:S(2)}) %collective-permute-start.3) | collective-permute-done | bytes 524320 | tf_op jit(solution)/shard_map/ppermute | solution.py:29
  43.1 3.7 %collective-permute-done.1 = bf16[2,32,4096]{2,1,0:T(8,128)(2,1)S(1)} collective-permute-done((bf16[2,32,4096]{2,1,0:T(8,128)(2,1)S(1)}, bf16[2,32,4096]{2,1,0:T(8,128)(2,1)S(1)}, u32[]{:S(2)}, u32[]{:S(2)}) %collective-permute-start.1) | collective-permute-done | bytes 524320 | tf_op jit(solution)/shard_map/ppermute | solution.py:29
  46.8 0.7 slice_bitcast_fusion.4
  48.0 1.2 pad_maximum_fusion.refs_0_.refs_2_
  49.3 1.5 collective-permute-start.4
  50.7 1.7 collective-permute-start.6
  52.4 1.0 collective-permute-start.5
  53.4 9.9 %collective-permute-done.7.refs_2_.refs_4_ = bf16[128,4096]{1,0:T(8,128)(2,1)S(1)} collective-permute-done((bf16[128,4096]{1,0:T(8,128)(2,1)S(1)}, bf16[128,4096]{1,0:T(8,128)(2,1)S(1)}, u32[]{:S(2)}, u32[]{:S(2)}) %collective-permute-start.7) | collective-permute-done | bytes 1048608 | tf_op jit(solution)/shard_map/ppermute | solution.py:29
  63.3 2.2 %collective-permute-done.4.refs_1_.refs_3_ = bf16[128,4096]{1,0:T(8,128)(2,1)S(1)} collective-permute-done((bf16[128,4096]{1,0:T(8,128)(2,1)S(1)}, bf16[128,4096]{1,0:T(8,128)(2,1)S(1)}, u32[]{:S(2)}, u32[]{:S(2)}) %collective-permute-start.4) | collective-permute-done | bytes 1048608 | tf_op jit(solution)/shard_map/ppermute | solution.py:29
  65.6 11.1 %collective-permute-done.6.refs_4_.refs_6_ = bf16[128,4096]{1,0:T(8,128)(2,1)S(1)} collective-permute-done((bf16[128,4096]{1,0:T(8,128)(2,1)S(1)}, bf16[128,4096]{1,0:T(8,128)(2,1)S(1)}, u32[]{:S(2)}, u32[]{:S(2)}) %collective-permute-start.6) | collective-permute-done | bytes 1048608 | tf_op jit(solution)/shard_map/ppermute | solution.py:29
  76.7 1.0 copy-done.20
  77.7 1.2 collective-permute-start.9
  78.9 0.8 collective-permute-start.11
  79.7 0.7 collective-permute-start.10
  80.4 4.8 %collective-permute-done.9.refs_7_.refs_9_ = bf16[8,896,256]{2,1,0:T(8,128)(2,1)S(1)} collective-permute-done((bf16[8,896,256]{2,1,0:T(8,128)(2,1)}, bf16[8,896,256]{2,1,0:T(8,128)(2,1)S(1)}, u32[]{:S(2)}, u32[]{:S(2)}) %collective-permute-start.9) | collective-permute-done | bytes 3670048 | tf_op jit(solution)/shard_map/ppermute | solution.py:34
  85.2 1.8 copy-done.17
  86.9 13.5 %shard_map.101 = (bf16[128,4096]{1,0:T(8,128)(2,1)S(1)}, bf16[128,4096]{1,0:T(8,128)(2,1)S(1)}, bf16[128,4096]{1,0:T(8,128)(2,1)}, bf16[128,4096]{1,0:T(8,128)(2...) custom-call(bf16[128,4096]{1,0:T(8,128)(2,1)} %copy-done, ...), custom_call_target="tpu_custom_call" | custom-call | flops 5637144576 | bytes 19922944 | tf_op jit(solution)/shard_map/pallas_call | solution.py:227
  100.4 1.0 copy-done.2
  101.4 1.2 copy-done.1
  102.6 14.9 %shard_map.102 = (bf16[128,4096]{1,0:T(8,128)(2,1)S(1)}, bf16[128,4096]{1,0:T(8,128)(2,1)S(1)}, bf16[8,896,256]{2,1,0:T(8,128)(2,1)}, bf16[8,896,256]{2,1,0:T(8,128)(2,1)}, f32[1,4096]{1,0:T(1,128)S(1)}) custom-call(bf16[128,4096]{1,0:T(8,128)(2,1)S(1)} %collective-permute-done.10.refs_0_, bf16[128,4096]{1,0:T(8,128)(2,1)S(1)} %collective-permute-done.11.refs_1_, ...), custom_call_target="tpu_custom_call" | custom-call | flops 5637144576 | bytes 25165824 | tf_op jit(solution)/shard_map/pallas_call | solution.py:227
  117.5 1.0 copy-done.4
  118.9 0.8 collective-permute-start.12
  119.7 0.7 collective-permute-start.13
  120.3 4.8 %collective-permute-done.27 = bf16[8,896,256]{2,1,0:T(8,128)(2,1)S(1)} collective-permute-done((bf16[8,896,256]{2,1,0:T(8,128)(2,1)}, bf16[8,896,256]{2,1,0:T(8,128)(2,1)S(1)}, u32[]{:S(2)}, u32[]{:S(2)}) %collective-permute-start.27) | collective-permute-done | bytes 3670048 | tf_op jit(solution)/shard_map/ppermute | solution.py:34
  125.1 4.7 %add_convert_fusion = bf16[8,896,256]{2,1,0:T(8,128)(2,1)} fusion(bf16[8,896,256]{2,1,0:T(8,128)(2,1)S(1)} %collective-permute-done.27, bf16[8,896,256]{2,1,0:T(8,128)(2,1)} %get-tuple-element.69), kind=kLoop, calls=%fused_computation | loop fusion | flops 7340032 | bytes 11010048 | tf_op jit(solution)/shard_map/convert_element_type | solution.py:281
  129.9 0.7 copy-done.16
  130.5 1.6 collective-permute-start.14
  132.2 1.5 collective-permute-done.14
  133.7 3.0 %collective-permute-start.15 = (f32[4096]{0:T(1024)S(1)}, f32[4096]{0:T(1024)S(1)}, u32[]{:S(2)}, u32[]{:S(2)}) collective-permute-start(f32[4096]{0:T(1024)S(1)} %add.89), channel_id=1, source_target_pairs={{0,64},{1,65},{4,68},{5,69},{8,72},{9,73},{12,76},{13,77},{16,80},... | collective-permute-start | bytes 49160 | tf_op jit(solution)/shard_map/ppermute | solution.py:263
  136.7 1.1 collective-permute-done.15
  137.8 0.9 collective-permute-start.16
  139.4 6.1 %collective-permute-start.18 = (f32[4096]{0:T(1024)S(1)}, f32[4096]{0:T(1024)S(1)}, u32[]{:S(2)}, u32[]{:S(2)}) collective-permute-start(f32[4096]{0:T(1024)S(1)} %add.90), channel_id=1, source_target_pairs={{0,128},{1,129},{4,132},{5,133},{8,136},{9,137},{12,140},{13,141},... | collective-permute-start | bytes 49160 | tf_op jit(solution)/shard_map/ppermute | solution.py:263
  145.5 1.3 collective-permute-done.18
  146.8 3.9 %collective-permute-start.19 = (f32[4096]{0:T(1024)S(1)}, f32[4096]{0:T(1024)S(1)}, u32[]{:S(2)}, u32[]{:S(2)}) collective-permute-start(f32[4096]{0:T(1024)S(1)} %add.93), channel_id=1, source_target_pairs={{0,1},{1,0},{4,5},{5,4},{8,9},{9,8},{12,13},{13,12},{16,17},{17,16... | collective-permute-start | bytes 49160 | tf_op jit(solution)/shard_map/ppermute | solution.py:263
  150.7 0.8 collective-permute-done.19
  151.5 0.7 collective-permute-done.16
  152.4 1.6 collective-permute-done.17
  154.8 1.0 collective-permute-start.21
  155.8 13.1 %collective-permute-done.22 = f32[4096]{0:T(1024)S(1)} collective-permute-done((f32[4096]{0:T(1024)S(1)}, f32[4096]{0:T(1024)S(1)}, u32[]{:S(2)}, u32[]{:S(2)}) %collective-permute-start.22) | collective-permute-done | bytes 16416 | tf_op jit(solution)/shard_map/ppermute | solution.py:263
  169.1 3.9 %collective-permute-done.23 = f32[4096]{0:T(1024)S(1)} collective-permute-done((f32[4096]{0:T(1024)S(1)}, f32[4096]{0:T(1024)S(1)}, u32[]{:S(2)}, u32[]{:S(2)}) %collective-permute-start.23) | collective-permute-done | bytes 16416 | tf_op jit(solution)/shard_map/ppermute | solution.py:263
  173.0 1.7 fusion.3
  174.8 1.7 fusion.2
  176.7 2.7 %collective-permute-start.24 = (bf16[2,32,4096]{2,1,0:T(8,128)(2,1)S(1)}, bf16[2,32,4096]{2,1,0:T(8,128)(2,1)S(1)}, u32[]{:S(2)}, u32[]{:S(2)}) collective-permute-start(bf16[2,32,4096]{2,1,0:T(8,128)(2,1)S(1)} %get-tuple-element.80), channel_id=1, source_target_pairs={{0,18},{1,13},{4,22},{5,1},{8,26},{9,5},{12,30},{13,9},{16,0},{17,... | collective-permute-start | bytes 1572872 | tf_op jit(solution)/shard_map/ppermute | solution.py:29
  179.9 11.5 %collective-permute-done.28 = f32[4096]{0:T(1024)S(1)} collective-permute-done((f32[4096]{0:T(1024)S(1)}, f32[4096]{0:T(1024)S(1)}, u32[]{:S(2)}, u32[]{:S(2)}) %collective-permute-start.28) | collective-permute-done | bytes 16416 | tf_op jit(solution)/shard_map/ppermute | solution.py:263
  191.4 1.9 collective-permute-start.29
  193.2 2.2 %collective-permute-done.29 = f32[4096]{0:T(1024)S(1)} collective-permute-done((f32[4096]{0:T(1024)S(1)}, f32[4096]{0:T(1024)S(1)}, u32[]{:S(2)}, u32[]{:S(2)}) %collective-permute-start.29) | collective-permute-done | bytes 16416 | tf_op jit(solution)/shard_map/ppermute | solution.py:263
  196.2 0.7 copy-done.13
  197.1 1.7 convert_add_fusion
  199.1 2.1 collective-permute-start.30
  201.2 3.7 %collective-permute-start.31 = (bf16[896,256]{1,0:T(8,128)(2,1)S(1)}, bf16[896,256]{1,0:T(8,128)(2,1)S(1)}, u32[]{:S(2)}, u32[]{:S(2)}) collective-permute-start(bf16[896,256]{1,0:T(8,128)(2,1)S(1)} %bitcast.46), channel_id=1, source_target_pairs={{0,0},{1,16},{4,4},{5,20},{8,8},{9,24},{12,12},{13,28},{16,1},{17,... | collective-permute-start | bytes 1376264 | tf_op jit(solution)/shard_map/ppermute | solution.py:41
  204.9 1.5 fusion.1
  206.4 1.4 fusion
  207.8 3.2 %collective-permute-done.31 = bf16[896,256]{1,0:T(8,128)(2,1)S(1)} collective-permute-done((bf16[896,256]{1,0:T(8,128)(2,1)S(1)}, bf16[896,256]{1,0:T(8,128)(2,1)S(1)}, u32[]{:S(2)}, u32[]{:S(2)}) %collective-permute-start.31) | collective-permute-done | bytes 458784 | tf_op jit(solution)/shard_map/ppermute | solution.py:41
  211.0 0.8 multiply_bitcast_fusion
  211.9 0.8 slice_convert_fusion
  (96 shorter events, 7.9 us)
Async XLA Ops:
  7.2 14.6 %copy-start.5 = (bf16[128,4096]{1,0:T(8,128)(2,1)S(1)}, bf16[128,4096]{1,0:T(8,128)(2,1)}, u32[]{:S(2)}) copy-start(bf16[128,4096]{1,0:T(8,128)(2,1)} %param.11) | copy-start | bytes 3145732
  7.2 16.8 %copy-start.7 = (bf16[128,4096]{1,0:T(8,128)(2,1)S(1)}, bf16[128,4096]{1,0:T(8,128)(2,1)}, u32[]{:S(2)}) copy-start(bf16[128,4096]{1,0:T(8,128)(2,1)} %param.6) | copy-start | bytes 3145732
  7.2 70.5 %all-gather.3.cloned.1.call-start = ((), (), s32[]{:S(2)}) async-start(), calls=%async_computation.2 | async-start | bytes 4128768 | tf_op jit(solution)/shard_map/all_gather | solution.py:309
  10.1 10.8 %collective-permute-start.8 = (bf16[896,256]{1,0:T(8,128)(2,1)S(1)}, bf16[896,256]{1,0:T(8,128)(2,1)S(1)}, u32[]{:S(2)}, u32[]{:S(2)}) collective-permute-start(bf16[896,256]{1,0:T(8,128)(2,1)S(1)} %pad_maximum_fusion.3), channel_id=1, source_target_pairs={{0,0},{1,16},{4,4},{5,20},{8,8},{9,24},{12,12},{13,28},{16,1},{17,... | collective-permute-start | bytes 1376264 | tf_op jit(solution)/shard_map/ppermute | solution.py:41
  20.8 0.8 copy-start.15
  21.6 174.5 %reduce-scatter.2.cloned.1.call-start = ((), (), s32[]{:S(2)}) async-start(), calls=%async_computation.1 | async-start | bytes 4128768 | tf_op jit(solution)/shard_map/reduce_scatter | solution.py:282
  22.0 6.6 %collective-permute-start = (bf16[1,4096]{1,0:T(2,128)(2,1)S(1)}, bf16[1,4096]{1,0:T(2,128)(2,1)S(1)}, u32[]{:S(2)}, u32[]{:S(2)}) collective-permute-start(bf16[1,4096]{1,0:T(2,128)(2,1)S(1)} %slice.65), channel_id=1, source_target_pairs={{1,0},{2,1},{3,2},{4,3},{5,4},{6,5},{7,6},{8,7},{9,8},{10,9},{11,1... | collective-permute-start | bytes 24584 | tf_op jit(solution)/shard_map/ppermute | solution.py:47
  24.3 23.2 %copy-start.9 = (bf16[31,4096]{1,0:T(8,128)(2,1)}, bf16[31,4096]{1,0:T(8,128)(2,1)S(1)}, u32[]{:S(2)}) copy-start(bf16[31,4096]{1,0:T(8,128)(2,1)S(1)} %slice.64) | copy-start | bytes 761860
  28.7 14.3 %collective-permute-start.3 = (bf16[2,32,4096]{2,1,0:T(8,128)(2,1)S(1)}, bf16[2,32,4096]{2,1,0:T(8,128)(2,1)S(1)}, u32[]{:S(2)}, u32[]{:S(2)}) collective-permute-start(bf16[2,32,4096]{2,1,0:T(8,128)(2,1)S(1)} %pad_maximum_fusion.2), channel_id=1, source_target_pairs={{0,18},{1,13},{4,22},{5,1},{8,26},{9,5},{12,30},{13,9},{16,0},{17,... | collective-permute-start | bytes 1572872 | tf_op jit(solution)/shard_map/ppermute | solution.py:29
  31.2 11.8 %collective-permute-start.2 = (bf16[2,32,4096]{2,1,0:T(8,128)(2,1)S(1)}, bf16[2,32,4096]{2,1,0:T(8,128)(2,1)S(1)}, u32[]{:S(2)}, u32[]{:S(2)}) collective-permute-start(bf16[2,32,4096]{2,1,0:T(8,128)(2,1)S(1)} %pad_maximum_fusion.2), channel_id=1, source_target_pairs={{0,2},{1,9},{4,6},{5,13},{8,10},{9,1},{12,14},{13,5},{16,18},{17,2... | collective-permute-start | bytes 1572872 | tf_op jit(solution)/shard_map/ppermute | solution.py:29
  31.8 15.0 %collective-permute-start.1 = (bf16[2,32,4096]{2,1,0:T(8,128)(2,1)S(1)}, bf16[2,32,4096]{2,1,0:T(8,128)(2,1)S(1)}, u32[]{:S(2)}, u32[]{:S(2)}) collective-permute-start(bf16[2,32,4096]{2,1,0:T(8,128)(2,1)S(1)} %pad_maximum_fusion.2), channel_id=1, source_target_pairs={{0,16},{1,5},{4,20},{5,9},{8,24},{9,13},{12,28},{13,1},{16,2},{17,... | collective-permute-start | bytes 1572872 | tf_op jit(solution)/shard_map/ppermute | solution.py:29
  47.9 32.4 %copy-start.12 = (bf16[128,4096]{1,0:T(8,128)(2,1)}, bf16[128,4096]{1,0:T(8,128)(2,1)S(1)}, u32[]{:S(2)}) copy-start(bf16[128,4096]{1,0:T(8,128)(2,1)S(1)} %concatenate.18.refs_3_.refs_5_) | copy-start | bytes 3145732
  49.2 36.0 %copy-start = (bf16[128,4096]{1,0:T(8,128)(2,1)}, bf16[128,4096]{1,0:T(8,128)(2,1)S(1)}, u32[]{:S(2)}) copy-start(bf16[128,4096]{1,0:T(8,128)(2,1)S(1)} %pad_maximum_fusion.refs_0_.refs_2_) | copy-start | bytes 3145732
  49.2 14.1 %collective-permute-start.7 = (bf16[128,4096]{1,0:T(8,128)(2,1)S(1)}, bf16[128,4096]{1,0:T(8,128)(2,1)S(1)}, u32[]{:S(2)}, u32[]{:S(2)}) collective-permute-start(bf16[128,4096]{1,0:T(8,128)(2,1)S(1)} %pad_maximum_fusion.refs_0_.refs_2_), channel_id=1, source_target_pairs={{0,12},{1,19},{4,0},{5,23},{8,4},{9,27},{12,8},{13,31},{16,28},{17... | collective-permute-start | bytes 3145736 | tf_op jit(solution)/shard_map/ppermute | solution.py:29
  49.3 16.3 %collective-permute-start.4 = (bf16[128,4096]{1,0:T(8,128)(2,1)S(1)}, bf16[128,4096]{1,0:T(8,128)(2,1)S(1)}, u32[]{:S(2)}, u32[]{:S(2)}) collective-permute-start(bf16[128,4096]{1,0:T(8,128)(2,1)S(1)} %pad_maximum_fusion.refs_0_.refs_2_), channel_id=1, source_target_pairs={{0,4},{1,17},{4,8},{5,21},{8,12},{9,25},{12,0},{13,29},{16,20},{17... | collective-permute-start | bytes 3145736 | tf_op jit(solution)/shard_map/ppermute | solution.py:29
  50.7 25.9 %collective-permute-start.6 = (bf16[128,4096]{1,0:T(8,128)(2,1)S(1)}, bf16[128,4096]{1,0:T(8,128)(2,1)S(1)}, u32[]{:S(2)}, u32[]{:S(2)}) collective-permute-start(bf16[128,4096]{1,0:T(8,128)(2,1)S(1)} %concatenate.18.refs_3_.refs_5_), channel_id=1, source_target_pairs={{0,4},{1,17},{4,8},{5,21},{8,12},{9,25},{12,0},{13,29},{16,20},{17... | collective-permute-start | bytes 3145736 | tf_op jit(solution)/shard_map/ppermute | solution.py:29
  52.4 25.2 %collective-permute-start.5 = (bf16[128,4096]{1,0:T(8,128)(2,1)S(1)}, bf16[128,4096]{1,0:T(8,128)(2,1)}, u32[]{:S(2)}, u32[]{:S(2)}) collective-permute-start(bf16[128,4096]{1,0:T(8,128)(2,1)S(1)} %concatenate.18.refs_3_.refs_5_), channel_id=1, source_target_pairs={{0,12},{1,19},{4,0},{5,23},{8,4},{9,27},{12,8},{13,31},{16,28},{17... | collective-permute-start | bytes 3145736 | tf_op jit(solution)/shard_map/ppermute | solution.py:29
  63.3 17.0 %copy-start.18 = (bf16[128,4096]{1,0:T(8,128)(2,1)}, bf16[128,4096]{1,0:T(8,128)(2,1)S(1)}, u32[]{:S(2)}) copy-start(bf16[128,4096]{1,0:T(8,128)(2,1)S(1)} %collective-permute-done.7.refs_2_.refs_4_) | copy-start | bytes 3145732
  65.5 11.1 %copy-start.19 = (bf16[128,4096]{1,0:T(8,128)(2,1)}, bf16[128,4096]{1,0:T(8,128)(2,1)S(1)}, u32[]{:S(2)}) copy-start(bf16[128,4096]{1,0:T(8,128)(2,1)S(1)} %collective-permute-done.4.refs_1_.refs_3_) | copy-start | bytes 3145732
  76.7 1.0 copy-start.20
  77.7 7.5 %collective-permute-start.9 = (bf16[8,896,256]{2,1,0:T(8,128)(2,1)}, bf16[8,896,256]{2,1,0:T(8,128)(2,1)S(1)}, u32[]{:S(2)}, u32[]{:S(2)}) collective-permute-start(bf16[8,896,256]{2,1,0:T(8,128)(2,1)} %bitcast.43), channel_id=1, source_target_pairs={{0,1},{1,0},{4,5},{5,4},{8,9},{9,8},{12,13},{13,12},{16,17},{17,16... | collective-permute-start | bytes 11010056 | tf_op jit(solution)/shard_map/ppermute | solution.py:34
  78.9 22.5 %collective-permute-start.11 = (bf16[128,4096]{1,0:T(8,128)(2,1)}, bf16[128,4096]{1,0:T(8,128)(2,1)S(1)}, u32[]{:S(2)}, u32[]{:S(2)}) collective-permute-start(bf16[128,4096]{1,0:T(8,128)(2,1)} %collective-permute-done.5.refs_5_.refs_7_), channel_id=1, source_target_pairs={{0,12},{1,19},{4,0},{5,23},{8,4},{9,27},{12,8},{13,31},{16,28},{17... | collective-permute-start | bytes 3145736 | tf_op jit(solution)/shard_map/ppermute | solution.py:29
  79.7 21.7 %collective-permute-start.10 = (bf16[128,4096]{1,0:T(8,128)(2,1)}, bf16[128,4096]{1,0:T(8,128)(2,1)S(1)}, u32[]{:S(2)}, u32[]{:S(2)}) collective-permute-start(bf16[128,4096]{1,0:T(8,128)(2,1)} %copy-done.19), channel_id=1, source_target_pairs={{0,4},{1,17},{4,8},{5,21},{8,12},{9,25},{12,0},{13,29},{16,20},{17... | collective-permute-start | bytes 3145736 | tf_op jit(solution)/shard_map/ppermute | solution.py:29
  85.2 1.8 copy-start.17
  100.4 1.0 copy-start.2
  101.4 1.2 copy-start.1
  117.5 1.0 copy-start.4
  118.5 6.6 %collective-permute-start.27 = (bf16[8,896,256]{2,1,0:T(8,128)(2,1)}, bf16[8,896,256]{2,1,0:T(8,128)(2,1)S(1)}, u32[]{:S(2)}, u32[]{:S(2)}) collective-permute-start(bf16[8,896,256]{2,1,0:T(8,128)(2,1)} %get-tuple-element.70), channel_id=1, source_target_pairs={{0,1},{1,0},{4,5},{5,4},{8,9},{9,8},{12,13},{13,12},{16,17},{17,16... | collective-permute-start | bytes 11010056 | tf_op jit(solution)/shard_map/ppermute | solution.py:34
  118.9 19.0 %collective-permute-start.12 = (bf16[128,4096]{1,0:T(8,128)(2,1)}, bf16[128,4096]{1,0:T(8,128)(2,1)}, u32[]{:S(2)}, u32[]{:S(2)}) collective-permute-start(bf16[128,4096]{1,0:T(8,128)(2,1)} %get-tuple-element.54), channel_id=1, source_target_pairs={{0,12},{1,19},{4,0},{5,23},{8,4},{9,27},{12,8},{13,31},{16,28},{17... | collective-permute-start | bytes 3145736 | tf_op jit(solution)/shard_map/ppermute | solution.py:29
  119.7 18.2 %collective-permute-start.13 = (bf16[128,4096]{1,0:T(8,128)(2,1)}, bf16[128,4096]{1,0:T(8,128)(2,1)}, u32[]{:S(2)}, u32[]{:S(2)}) collective-permute-start(bf16[128,4096]{1,0:T(8,128)(2,1)} %get-tuple-element.55), channel_id=1, source_target_pairs={{0,4},{1,17},{4,8},{5,21},{8,12},{9,25},{12,0},{13,29},{16,20},{17... | collective-permute-start | bytes 3145736 | tf_op jit(solution)/shard_map/ppermute | solution.py:29
  129.8 0.7 copy-start.16
  129.8 24.2 %copy-start.11 = (bf16[128,4096]{1,0:T(8,128)(2,1)S(1)}, bf16[128,4096]{1,0:T(8,128)(2,1)}, u32[]{:S(2)}) copy-start(bf16[128,4096]{1,0:T(8,128)(2,1)} %get-tuple-element.58) | copy-start | bytes 3145732
  130.5 3.2 %collective-permute-start.14 = (f32[4096]{0:T(1024)S(1)}, f32[4096]{0:T(1024)S(1)}, u32[]{:S(2)}, u32[]{:S(2)}) collective-permute-start(f32[4096]{0:T(1024)S(1)} %div.35), channel_id=1, source_target_pairs={{0,32},{1,33},{4,36},{5,37},{8,40},{9,41},{12,44},{13,45},{16,48},... | collective-permute-start | bytes 49160 | tf_op jit(solution)/shard_map/ppermute | solution.py:263
  133.7 4.1 %collective-permute-start.15 = (f32[4096]{0:T(1024)S(1)}, f32[4096]{0:T(1024)S(1)}, u32[]{:S(2)}, u32[]{:S(2)}) collective-permute-start(f32[4096]{0:T(1024)S(1)} %add.89), channel_id=1, source_target_pairs={{0,64},{1,65},{4,68},{5,69},{8,72},{9,73},{12,76},{13,77},{16,80},... | collective-permute-start | bytes 49160 | tf_op jit(solution)/shard_map/ppermute | solution.py:263
  137.8 14.3 %collective-permute-start.16 = (bf16[128,4096]{1,0:T(8,128)(2,1)}, bf16[128,4096]{1,0:T(8,128)(2,1)S(1)}, u32[]{:S(2)}, u32[]{:S(2)}) collective-permute-start(bf16[128,4096]{1,0:T(8,128)(2,1)} %copy-done.4), channel_id=1, source_target_pairs={{0,12},{1,19},{4,0},{5,23},{8,4},{9,27},{12,8},{13,31},{16,28},{17... | collective-permute-start | bytes 3145736 | tf_op jit(solution)/shard_map/ppermute | solution.py:29
  138.7 15.3 %collective-permute-start.17 = (bf16[128,4096]{1,0:T(8,128)(2,1)S(1)}, bf16[128,4096]{1,0:T(8,128)(2,1)S(1)}, u32[]{:S(2)}, u32[]{:S(2)}) collective-permute-start(bf16[128,4096]{1,0:T(8,128)(2,1)S(1)} %get-tuple-element.59), channel_id=1, source_target_pairs={{0,4},{1,17},{4,8},{5,21},{8,12},{9,25},{12,0},{13,29},{16,20},{17... | collective-permute-start | bytes 3145736 | tf_op jit(solution)/shard_map/ppermute | solution.py:29
  139.4 7.4 %collective-permute-start.18 = (f32[4096]{0:T(1024)S(1)}, f32[4096]{0:T(1024)S(1)}, u32[]{:S(2)}, u32[]{:S(2)}) collective-permute-start(f32[4096]{0:T(1024)S(1)} %add.90), channel_id=1, source_target_pairs={{0,128},{1,129},{4,132},{5,133},{8,136},{9,137},{12,140},{13,141},... | collective-permute-start | bytes 49160 | tf_op jit(solution)/shard_map/ppermute | solution.py:263
  146.8 4.7 %collective-permute-start.19 = (f32[4096]{0:T(1024)S(1)}, f32[4096]{0:T(1024)S(1)}, u32[]{:S(2)}, u32[]{:S(2)}) collective-permute-start(f32[4096]{0:T(1024)S(1)} %add.93), channel_id=1, source_target_pairs={{0,1},{1,0},{4,5},{5,4},{8,9},{9,8},{12,13},{13,12},{16,17},{17,16... | collective-permute-start | bytes 49160 | tf_op jit(solution)/shard_map/ppermute | solution.py:263
  152.4 20.6 %copy-start.3 = (bf16[128,4096]{1,0:T(8,128)(2,1)S(1)}, bf16[128,4096]{1,0:T(8,128)(2,1)}, u32[]{:S(2)}) copy-start(bf16[128,4096]{1,0:T(8,128)(2,1)} %copy-done.2) | copy-start | bytes 3145732
  154.3 18.8 %collective-permute-start.20 = (bf16[128,4096]{1,0:T(8,128)(2,1)S(1)}, bf16[128,4096]{1,0:T(8,128)(2,1)S(1)}, u32[]{:S(2)}, u32[]{:S(2)}) collective-permute-start(bf16[128,4096]{1,0:T(8,128)(2,1)S(1)} %add_convert_fusion.4), channel_id=1, source_target_pairs={{0,12},{1,19},{4,0},{5,23},{8,4},{9,27},{12,8},{13,31},{16,28},{17... | collective-permute-start | bytes 3145736 | tf_op jit(solution)/shard_map/ppermute | solution.py:29
  154.8 18.2 %collective-permute-start.21 = (bf16[128,4096]{1,0:T(8,128)(2,1)S(1)}, bf16[128,4096]{1,0:T(8,128)(2,1)S(1)}, u32[]{:S(2)}, u32[]{:S(2)}) collective-permute-start(bf16[128,4096]{1,0:T(8,128)(2,1)S(1)} %add_convert_fusion.3), channel_id=1, source_target_pairs={{0,4},{1,17},{4,8},{5,21},{8,12},{9,25},{12,0},{13,29},{16,20},{17... | collective-permute-start | bytes 3145736 | tf_op jit(solution)/shard_map/ppermute | solution.py:29
  155.8 13.1 %collective-permute-start.22 = (f32[4096]{0:T(1024)S(1)}, f32[4096]{0:T(1024)S(1)}, u32[]{:S(2)}, u32[]{:S(2)}) collective-permute-start(f32[4096]{0:T(1024)S(1)} %add.94), channel_id=1, source_target_pairs={{0,16},{1,17},{4,20},{5,21},{8,24},{9,25},{12,28},{13,29},{16,0},{... | collective-permute-start | bytes 49160 | tf_op jit(solution)/shard_map/ppermute | solution.py:263
  168.9 4.1 %collective-permute-start.23 = (f32[4096]{0:T(1024)S(1)}, f32[4096]{0:T(1024)S(1)}, u32[]{:S(2)}, u32[]{:S(2)}) collective-permute-start(f32[4096]{0:T(1024)S(1)} %add.95), channel_id=1, source_target_pairs={{0,2},{1,3},{4,6},{5,7},{8,10},{9,11},{12,14},{13,15},{16,18},{17,... | collective-permute-start | bytes 49160 | tf_op jit(solution)/shard_map/ppermute | solution.py:263
  176.6 19.5 %collective-permute-start.26 = (bf16[2,32,4096]{2,1,0:T(8,128)(2,1)S(1)}, bf16[2,32,4096]{2,1,0:T(8,128)(2,1)S(1)}, u32[]{:S(2)}, u32[]{:S(2)}) collective-permute-start(bf16[2,32,4096]{2,1,0:T(8,128)(2,1)S(1)} %get-tuple-element.79), channel_id=1, source_target_pairs={{0,16},{1,5},{4,20},{5,9},{8,24},{9,13},{12,28},{13,1},{16,2},{17,... | collective-permute-start | bytes 1572872 | tf_op jit(solution)/shard_map/ppermute | solution.py:29
  176.7 19.4 %collective-permute-start.24 = (bf16[2,32,4096]{2,1,0:T(8,128)(2,1)S(1)}, bf16[2,32,4096]{2,1,0:T(8,128)(2,1)S(1)}, u32[]{:S(2)}, u32[]{:S(2)}) collective-permute-start(bf16[2,32,4096]{2,1,0:T(8,128)(2,1)S(1)} %get-tuple-element.80), channel_id=1, source_target_pairs={{0,18},{1,13},{4,22},{5,1},{8,26},{9,5},{12,30},{13,9},{16,0},{17,... | collective-permute-start | bytes 1572872 | tf_op jit(solution)/shard_map/ppermute | solution.py:29
  179.3 16.8 %collective-permute-start.25 = (bf16[2,32,4096]{2,1,0:T(8,128)(2,1)S(1)}, bf16[2,32,4096]{2,1,0:T(8,128)(2,1)}, u32[]{:S(2)}, u32[]{:S(2)}) collective-permute-start(bf16[2,32,4096]{2,1,0:T(8,128)(2,1)S(1)} %get-tuple-element.81), channel_id=1, source_target_pairs={{0,2},{1,9},{4,6},{5,13},{8,10},{9,1},{12,14},{13,5},{16,18},{17,2... | collective-permute-start | bytes 1572872 | tf_op jit(solution)/shard_map/ppermute | solution.py:29
  179.3 12.0 %collective-permute-start.28 = (f32[4096]{0:T(1024)S(1)}, f32[4096]{0:T(1024)S(1)}, u32[]{:S(2)}, u32[]{:S(2)}) collective-permute-start(f32[4096]{0:T(1024)S(1)} %add.96), channel_id=1, source_target_pairs={{0,4},{1,5},{4,0},{5,1},{8,12},{9,13},{12,8},{13,9},{16,20},{17,21... | collective-permute-start | bytes 49160 | tf_op jit(solution)/shard_map/ppermute | solution.py:263
  191.4 4.1 %collective-permute-start.29 = (f32[4096]{0:T(1024)S(1)}, f32[4096]{0:T(1024)S(1)}, u32[]{:S(2)}, u32[]{:S(2)}) collective-permute-start(f32[4096]{0:T(1024)S(1)} %add.102), channel_id=1, source_target_pairs={{0,8},{1,9},{4,12},{5,13},{8,0},{9,1},{12,4},{13,5},{16,24},{17,25... | collective-permute-start | bytes 49160 | tf_op jit(solution)/shard_map/ppermute | solution.py:263
  196.1 0.8 copy-start.13
  196.1 1.0 copy-start.14
  197.1 4.1 %copy-start.21 = (bf16[1,896,256]{2,1,0:T(8,128)(2,1)S(1)}, bf16[1,896,256]{2,1,0:T(8,128)(2,1)}, u32[]{:S(2)}) copy-start(bf16[1,896,256]{2,1,0:T(8,128)(2,1)} %reduce-scatter.2.cloned.1.call-done) | copy-start | bytes 1376260
  197.1 7.8 %copy-start.6 = (bf16[128,4096]{1,0:T(8,128)(2,1)S(1)}, bf16[128,4096]{1,0:T(8,128)(2,1)}, u32[]{:S(2)}) copy-start(bf16[128,4096]{1,0:T(8,128)(2,1)} %param.11) | copy-start | bytes 3145732
  197.1 7.8 %copy-start.10 = (bf16[31,4096]{1,0:T(8,128)(2,1)S(1)}, bf16[31,4096]{1,0:T(8,128)(2,1)}, u32[]{:S(2)}) copy-start(bf16[31,4096]{1,0:T(8,128)(2,1)} %copy-done.9) | copy-start | bytes 761860
  198.8 7.6 %copy-start.8 = (bf16[128,4096]{1,0:T(8,128)(2,1)S(1)}, bf16[128,4096]{1,0:T(8,128)(2,1)}, u32[]{:S(2)}) copy-start(bf16[128,4096]{1,0:T(8,128)(2,1)} %param.6) | copy-start | bytes 3145732
  199.1 7.3 %collective-permute-start.30 = (bf16[1,4096]{1,0:T(2,128)(2,1)S(1)}, bf16[1,4096]{1,0:T(2,128)(2,1)S(1)}, u32[]{:S(2)}, u32[]{:S(2)}) collective-permute-start(bf16[1,4096]{1,0:T(2,128)(2,1)S(1)} %slice.78), channel_id=1, source_target_pairs={{0,1},{1,2},{2,3},{3,4},{4,5},{5,6},{6,7},{7,8},{8,9},{9,10},{10,1... | collective-permute-start | bytes 24584 | tf_op jit(solution)/shard_map/ppermute | solution.py:47
  201.2 9.9 %collective-permute-start.31 = (bf16[896,256]{1,0:T(8,128)(2,1)S(1)}, bf16[896,256]{1,0:T(8,128)(2,1)S(1)}, u32[]{:S(2)}, u32[]{:S(2)}) collective-permute-start(bf16[896,256]{1,0:T(8,128)(2,1)S(1)} %bitcast.46), channel_id=1, source_target_pairs={{0,0},{1,16},{4,4},{5,20},{8,8},{9,24},{12,12},{13,28},{16,1},{17,... | collective-permute-start | bytes 1376264 | tf_op jit(solution)/shard_map/ppermute | solution.py:41
Sparse Core Ops, SparseCore 0:
  21.8 52.5 all-gather.2
  130.0 49.1 reduce-scatter.1

commit v5 on v3

--- a/solution.py
+++ b/solution.py
@@ -55,15 +55,27 @@
     return jnp.dot(a, b, preferred_element_type=jnp.float32)
 
 
+def pieces(refs):
+    o0, o1, o3, o2p, o2g = refs[:5]
+    own = [(o0.at[0], o0.at[1]), (o1.at[0], o1.at[1]), (o2p, o2g), (o3.at[0], o3.at[1])]
+    return own + list(zip(refs[5:9], refs[9:13]))
+
+
+def spans(pairs):
+    start = 0
+    for pair in pairs:
+        rows = pair[0].shape[0]
+        yield pl.ds(start, rows), pair
+        start += rows
+
+
 def block_kernel(chunks, *refs):
-    acts = list(zip(refs[:4], refs[4:8]))
-    w_own, w_oth = refs[8:10]
-    outs = list(zip(refs[10:14], refs[14:18]))
-    g_own, g_oth, gain = refs[18:21]
+    acts, outs = pieces(refs[:13]), pieces(refs[16:29])
+    w_own, w_oth, rgain = refs[13:16]
+    g_own, g_oth, gain = refs[29:32]
     (p_s, g_s, wi_s, wo_s, d_s, n_s, gi_s, go_s, h_s, ga_s, sq_s, act, gp, act_t, gp_t, in_sem,
-     out_sem) = refs[21:]
+     out_sem) = refs[32:]
     core = lax.axis_index("c")
-    rows = refs[0].shape[0]
     hidden = wi_s.shape[0]
     half = w_own.shape[2]
     width = 2 * half
@@ -76,8 +88,7 @@
         return pl.ds(pl.multiple_of(z * width + which * half, half), half)
 
     def fetch(z, carry):
-        for i, pair in enumerate(acts):
-            at = pl.ds(i * rows, rows)
+        for at, pair in spans(acts):
             for k, (source, buf) in enumerate(zip(pair, (p_s, g_s))):
                 pltpu.make_async_copy(
                     source.at[:, cols(z)], buf.at[at, cols(z)], in_sem.at[k, z]
@@ -105,7 +116,7 @@
         p = p_s[:, cols(z)]
         h_s[...] += nt(p, wi_s[:, cols(z)])
         ga_s[...] += nt(g_s[:, cols(z)], wo_s[:, cols(z)])
-        pf = p.astype(jnp.float32)
+        pf = p.astype(jnp.float32) * rgain[:, cols(z)]
         sq_s[...] += jnp.sum(pf * pf, axis=1, keepdims=True)
         return carry
 
@@ -130,9 +141,9 @@
         go_s[:, cols(z)] = nn(act_t[...], g_s[:, cols(z)]).astype(jnp.bfloat16)
         gi = nn(gp_t[...], p_s[:, cols(z)])
         gi_s[:, cols(z)] = gi.astype(jnp.bfloat16)
-        gain[:, cols(z)] = jnp.sum(gi * wi.astype(jnp.float32), axis=0, keepdims=True)
-        for i, pair in enumerate(outs):
-            at = pl.ds(i * rows, rows)
+        total = jnp.sum(gi * wi.astype(jnp.float32), axis=0, keepdims=True)
+        gain[:, cols(z)] = total * rgain[:, cols(z)]
+        for at, pair in spans(outs):
             for k, (dest, buf) in enumerate(zip(pair, (d_s, n_s))):
                 pltpu.make_async_copy(
                     buf.at[at, cols(z)], dest.at[:, cols(z)], out_sem.at[k, z]
@@ -157,21 +168,20 @@
     lax.fori_loop(0, chunks, drain, 0)
 
 
-def block(acts, w_own, w_oth):
-    rows, feats = acts[0].shape
+def block(acts, w_own, w_oth, rgain):
+    feats = acts[0].shape[-1]
     chunks, hidden2, half = w_own.shape
     hidden = hidden2 // 2
-    total = 4 * rows
+    total = 4 * (acts[0].shape[1] + acts[5].shape[0])
     bf = jnp.bfloat16
-    anywhere = pl.BlockSpec(memory_space=pl.ANY)
-    flops = 12 * total * feats * hidden
-    return pl.pallas_call(
+    anywhere, inside = pl.BlockSpec(memory_space=pl.ANY), pl.BlockSpec(memory_space=pltpu.VMEM)
+    results = pl.pallas_call(
         functools.partial(block_kernel, chunks),
         out_shape=[jax.ShapeDtypeStruct(act.shape, bf) for act in acts]
         + [jax.ShapeDtypeStruct(w_own.shape, bf)] * 2
         + [jax.ShapeDtypeStruct((1, feats), jnp.float32)],
-        in_specs=[anywhere] * 10,
-        out_specs=[anywhere] * 10 + [pl.BlockSpec(memory_space=pltpu.VMEM)],
+        in_specs=[anywhere] * 15 + [inside],
+        out_specs=[anywhere] * 15 + [inside],
         scratch_shapes=[pltpu.VMEM((total, feats), bf)] * 2
         + [pltpu.VMEM((hidden, feats), bf)] * 2
         + [pltpu.VMEM((total, feats), bf)] * 2
@@ -183,9 +193,12 @@
         + [pltpu.SemaphoreType.DMA((4, chunks)), pltpu.SemaphoreType.DMA((4, chunks))],
         compiler_params=pltpu.CompilerParams(vmem_limit_bytes=48 * 1024 * 1024),
         cost_estimate=pl.CostEstimate(
-            flops=flops, bytes_accessed=8 * (total + hidden) * feats * 2, transcendentals=0
+            flops=12 * total * feats * hidden,
+            bytes_accessed=8 * (total + hidden) * feats * 2,
+            transcendentals=0,
         ),
-    )(*acts, w_own, w_oth)
+    )(*acts, w_own, w_oth, rgain)
+    return results[:13], results[13:]
 
 
 def add_all(parts):
@@ -196,41 +209,21 @@
 
 
 def gather_plane(acts):
-    parts = [acts] + [shift(acts, first=d) for d in (1, 2, 3)]
+    tie = lax.optimization_barrier
+    parts = [shift(acts, first=d) for d in (1, 2, 3)]
+    o1, o3 = shift(acts, second=1), shift(acts, second=-1)
     p0 = jnp.concatenate([part[0] for part in parts], axis=0)
     g0 = jnp.concatenate([part[1] for part in parts], axis=0)
-    p0, g0 = lax.optimization_barrier((p0, g0))
+    p0, g0, o1, o3 = tie((p0, g0, o1, o3))
     p1, g3 = shift(p0, second=1), shift(g0, second=-1)
     g1, p3 = shift(g0, second=1), shift(p0, second=-1)
-    p1, g3, g1, p3 = lax.optimization_barrier((p1, g3, g1, p3))
+    o2p, o2g = shift(o1[0], second=1), shift(o3[1], second=-1)
+    p1, g3, g1, p3, o2p, o2g = tie((p1, g3, g1, p3, o2p, o2g))
     p2, g2 = shift(p1, second=1), shift(g3, second=-1)
-    return [p0, p1, p2, p3, g0, g1, g2, g3]
-
-
-def scatter_plane(outs, gain_part, weight_part):
-    d0, d1, d2, d3, n0, n1, n2, n3 = outs
-    bf = jnp.bfloat16
-    d2, n2 = shift(d2, second=-1), shift(n2, second=1)
-    n1, d3 = shift(n1, second=-1), shift(d3, second=1)
-    d1, n3 = add_all([d1, d2]).astype(bf), add_all([n3, n2]).astype(bf)
-    d1, n3, weight_part = lax.optimization_barrier((d1, n3, weight_part))
-    weight_sum = lax.psum_scatter(weight_part, "z", scatter_dimension=0, tiled=False)
-    d1, n3 = shift(d1, second=-1), shift(n3, second=1)
-    arrived = (d1, d3, n1, n3, total_over_all(gain_part))
-    d1, d3, n1, n3, grad_gain = lax.optimization_barrier(arrived)
-    both = jnp.stack([add_all([d0, d1, d3]).astype(bf), add_all([n0, n1, n3]).astype(bf)])
-    rows = both.shape[1] // 4
-    both = [both[:, d * rows : (d + 1) * rows] for d in range(4)]
-    arrived = [shift(both[d], first=-d) for d in (1, 2, 3)] + [weight_sum]
-    *arrived, weight_sum = lax.optimization_barrier(arrived)
-    return add_all([both[0], *arrived]), grad_gain, weight_sum
-
-
-def total_over_all(value):
-    moves = [lambda p, k=k: (p[0] ^ k, p[1], p[2], p[3]) for k in (1, 2, 4)]
-    moves += [lambda p: (p[0], p[1], p[2], 1 - p[3])]
-    moves += [lambda p, k=k: (p[0], p[1] ^ k, p[2], p[3]) for k in (1, 2)]
-    moves += [lambda p, k=k: (p[0], p[1], p[2] ^ k, p[3]) for k in (1, 2)]
+    return [acts, o1, o3, o2p, o2g, p0, p1, p2, p3, g0, g1, g2, g3]
+
+
+def swapped(value, moves):
     for move in moves:
         value = value + lax.ppermute(
             value, AXES, [(linear(*p), linear(*move(p))) for p in places()]
@@ -238,17 +231,47 @@
     return value
 
 
+def all_moves():
+    moves = [lambda p, k=k: (p[0] ^ k, p[1], p[2], p[3]) for k in (1, 2, 4)]
+    moves += [lambda p: (p[0], p[1], p[2], 1 - p[3])]
+    moves += [lambda p, k=k: (p[0], p[1] ^ k, p[2], p[3]) for k in (1, 2)]
+    return moves + [lambda p, k=k: (p[0], p[1], p[2] ^ k, p[3]) for k in (1, 2)]
+
+
+def rounded_sum(*parts):
+    return add_all(parts).astype(jnp.bfloat16)
+
+
+def scatter_plane(outs, g_own, g_oth, gain):
+    o0, o1, o3, od2, on2, d0, d1, d2, d3, n0, n1, n2, n3 = outs
+    tie = lax.optimization_barrier
+    moves = all_moves()
+    d2, n2 = shift(d2, second=-1), shift(n2, second=1)
+    n1, d3 = shift(n1, second=-1), shift(d3, second=1)
+    mine = rounded_sum(g_own, other_core(g_oth))
+    weight_sum = lax.psum_scatter(mine, "z", scatter_dimension=0, tiled=False)
+    d1, n3 = rounded_sum(d1, d2), rounded_sum(n3, n2)
+    d1, n3, n1, d3, od2, on2, gain, _ = tie((d1, n3, n1, d3, od2, on2, gain, mine))
+    od2, on2 = shift(od2, second=-1), shift(on2, second=1)
+    d1, n3 = shift(d1, second=-1), shift(n3, second=1)
+    o1 = jnp.stack([rounded_sum(o1[0], od2), o1[1]])
+    o3 = jnp.stack([o3[0], rounded_sum(o3[1], on2)])
+    both = jnp.stack([rounded_sum(d0, d1, d3), rounded_sum(n0, n1, n3)])
+    both, o1, o3 = tie((both, o1, o3))
+    rows = both.shape[1] // 3
+    arrived = [shift(both[:, d * rows - rows : d * rows], first=-d) for d in (1, 2, 3)]
+    gain, *ours = tie((gain, shift(o1, second=-1), shift(o3, second=1)))
+    gain = swapped(gain, moves)
+    *arrived, weight_sum = tie((*arrived, weight_sum))
+    return add_all([o0, *arrived, *ours]), gain, weight_sum
+
+
 def shards(stream, doc_start, norm_gain, weight_in, weight_out, upstream):
     tok_rows, feats = stream.shape
     groups = tok_rows // 4
     hidden = weight_out.shape[0]
-    k_rows = weight_in.shape[0]
     bf = jnp.bfloat16
-    seq = lax.axis_index("z") * 2 + lax.axis_index("yl")
-    gain = lax.dynamic_slice(norm_gain, (seq * k_rows,), (k_rows,))
-
-    scaled_in = (weight_in.T.astype(jnp.float32) * gain[None, :]).astype(bf)
-    both = swap_low(jnp.concatenate([scaled_in, weight_out], axis=0))
+    both = swap_low(jnp.concatenate([weight_in.T, weight_out], axis=0))
     w_own = lax.all_gather(both, "z", axis=0, tiled=False)
 
     starts = doc_start.reshape(groups, 4).astype(jnp.float32)
@@ -262,18 +285,18 @@
     following = from_behind(group_sums[:1], -1)
     grad_coarse = jnp.concatenate([group_sums[1:], following], axis=0)
 
-    acts = jnp.stack([pooled, grad_coarse], axis=0)
+    scaled = (pooled.astype(jnp.float32) * norm_gain[None, :]).astype(bf)
+    acts = jnp.stack([scaled, grad_coarse], axis=0)
     blocks = gather_plane(acts)
-    w_own = lax.optimization_barrier((w_own, blocks[1], blocks[3]))[0]
+    w_own = lax.optimization_barrier((w_own, blocks[6], blocks[8]))[0]
     w_oth = other_core(w_own)
-    results = block(blocks, w_own, w_oth)
-    outs, (g_own, g_oth, gain_part) = results[:8], results[8:]
-
-    mine = (g_own.astype(jnp.float32) + other_core(g_oth).astype(jnp.float32)).astype(bf)
-    (down_sum, scaled), grad_gain, grads = scatter_plane(outs, gain_part[0] / norm_gain, mine)
+    outs, (g_own, g_oth, gain_part) = block(blocks, w_own, w_oth, 1.0 / norm_gain[None, :])
+    (down_sum, grad_normed), grad_gain, grads = scatter_plane(outs, g_own, g_oth, gain_part[0])
     grads = swap_low(grads)
-    grad_weight_in = (grads[:hidden].astype(jnp.float32) * gain[None, :]).T
+    grad_weight_in = grads[:hidden].astype(jnp.float32).T
     grad_weight_out = grads[hidden:].astype(jnp.float32)
+
+    scaled = norm_gain * grad_normed
     pooled_f = pooled.astype(jnp.float32)
     inv_sq = 1.0 / (jnp.mean(pooled_f * pooled_f, axis=1, keepdims=True) + 1e-05)
     coarse = (pooled_f + down_sum).astype(bf)

time: 222 us -> 246 us (1.11); the launches traced: 222 us -> 243 us
  starting transfers between devices: 49.8 us -> 68.2 us
  waiting for transfers between devices: 113 us -> 107 us
  local copies, waits for them, and re-layouts: 7.22 us -> 11.7 us
    ppermute x8, starting transfers between devices: 13.2 us -> 23.2 us  [swapped(): lax.ppermute(value, AXES, [(linear(*p), linear(*move(p))) for p in places...]
    ppermute x18 -> x26, waiting for transfers between devices: 78.6 us -> 85.7 us  [shift(): return lax.ppermute(value, AXES, pairs)]
    unnamed x42 -> x58, local copies, waits for them, and re-layouts: 5.49 us -> 11.1 us
    ppermute x2, waiting for transfers between devices: 9.43 us -> 4.14 us  [swap_low(): return lax.ppermute(value, AXES, pairs)]
    ppermute x2, waiting for transfers between devices: 4.27 us -> 0.01 us  [from_behind(): return lax.ppermute(value, AXES, pairs)]
    ppermute x2, starting transfers between devices: 7.28 us -> 11.2 us  [swap_low(): return lax.ppermute(value, AXES, pairs)]
    ppermute x18 -> x26, starting transfers between devices: 19 us -> 22.3 us  [shift(): return lax.ppermute(value, AXES, pairs)]
    ppermute x8, waiting for transfers between devices: 20.6 us -> 17.4 us  [swapped(): lax.ppermute(value, AXES, [(linear(*p), linear(*move(p))) for p in places...]
  transfers between devices with their start and end apart: 34 -> 42, of which waited for: 21 -> 24; matrix products, arithmetic and copies ran while one was open for 4% -> 7% of each run, Pallas kernels for 0% -> 0%
where the time goes in v5:
time: 246 us; the launch traced here: 243 us
  waiting for transfers between devices  107 us (43%)
  starting transfers between devices  68.2 us (28%)
  Pallas kernels  21.1 us (9%)
  other arithmetic  15.3 us (6%)
  between operations  14.6 us (6%)
  local copies, waits for them, and re-layouts  11.7 us (5%)
  matrix products  4.69 us (2%)
    ppermute x26, waiting for transfers between devices, shift(): return lax.ppermute(value, AXES, pairs)  85.7 us
    ppermute x8, starting transfers between devices, swapped(): lax.ppermute(value, AXES, [(linear(*p), linear(*move(p))) for p in places...  23.2 us
    ppermute x26, starting transfers between devices, shift(): return lax.ppermute(value, AXES, pairs)  22.3 us
    pallas_call x1, Pallas kernels, block(): pl.pallas_call(functools.partial(block_kernel, chunks), out_shape=[jax.Sh...  21.1 us
    ppermute x8, waiting for transfers between devices, swapped(): lax.ppermute(value, AXES, [(linear(*p), linear(*move(p))) for p in places...  17.4 us
    ppermute x2, starting transfers between devices, swap_low(): return lax.ppermute(value, AXES, pairs)  11.2 us
    unnamed x58, local copies, waits for them, and re-layouts  11.1 us
    ppermute x2, starting transfers between devices, from_behind(): return lax.ppermute(value, AXES, pairs)  9.03 us
  transfers between devices with their start and end apart: 42, of which 24 were waited for; matrix products, arithmetic and copies ran while one was open for 7% of the time, Pallas kernels for 0%

profile of v5, /device:TPU:1, one launch (start us, length us, event | category | flops | bytes accessed | tf_op | source)
XLA Modules:
  0.0 242.9 jit_solution(6424428296616237076)
XLA Ops:
  8.4 1.5 convolution_convert_fusion
  9.9 5.2 %collective-permute-start = (bf16[1,4096]{1,0:T(2,128)(2,1)S(1)}, bf16[1,4096]{1,0:T(2,128)(2,1)S(1)}, u32[]{:S(2)}, u32[]{:S(2)}) collective-permute-start(bf16[1,4096]{1,0:T(2,128)(2,1)S(1)} %slice.85), channel_id=1, source_target_pairs={{1,0},{2,1},{3,2},{4,3},{5,4},{6,5},{7,6},{8,7},{9,8},{10,9},{11,1... | collective-permute-start | bytes 24584 | tf_op jit(solution)/shard_map/ppermute | solution.py:47
  15.1 1.1 pad_maximum_fusion.6
  16.2 4.6 %collective-permute-start.14 = (bf16[896,256]{1,0:T(8,128)(2,1)S(1)}, bf16[896,256]{1,0:T(8,128)(2,1)S(1)}, u32[]{:S(2)}, u32[]{:S(2)}) collective-permute-start(bf16[896,256]{1,0:T(8,128)(2,1)S(1)} %pad_maximum_fusion.6), channel_id=1, source_target_pairs={{0,0},{1,16},{4,4},{5,20},{8,8},{9,24},{12,12},{13,28},{16,1},{17,... | collective-permute-start | bytes 1376264 | tf_op jit(solution)/shard_map/ppermute | solution.py:41
  22.7 4.1 %collective-permute-done.14 = bf16[896,256]{1,0:T(8,128)(2,1)S(1)} collective-permute-done((bf16[896,256]{1,0:T(8,128)(2,1)S(1)}, bf16[896,256]{1,0:T(8,128)(2,1)S(1)}, u32[]{:S(2)}, u32[]{:S(2)}) %collective-permute-start.14) | collective-permute-done | bytes 458784 | tf_op jit(solution)/shard_map/ppermute | solution.py:41
  27.8 1.3 collective-permute-start.3
  29.1 1.5 collective-permute-start.4
  31.4 8.8 %collective-permute-done.3 = bf16[2,32,4096]{2,1,0:T(8,128)(2,1)S(1)} collective-permute-done((bf16[2,32,4096]{2,1,0:T(8,128)(2,1)S(1)}, bf16[2,32,4096]{2,1,0:T(8,128)(2,1)S(1)}, u32[]{:S(2)}, u32[]{:S(2)}) %collective-permute-start.3) | collective-permute-done | bytes 524320 | tf_op jit(solution)/shard_map/ppermute | solution.py:29
  40.3 5.2 %collective-permute-done.2 = bf16[2,32,4096]{2,1,0:T(8,128)(2,1)S(1)} collective-permute-done((bf16[2,32,4096]{2,1,0:T(8,128)(2,1)S(1)}, bf16[2,32,4096]{2,1,0:T(8,128)(2,1)S(1)}, u32[]{:S(2)}, u32[]{:S(2)}) %collective-permute-start.2) | collective-permute-done | bytes 524320 | tf_op jit(solution)/shard_map/ppermute | solution.py:29
  45.5 5.6 %collective-permute-done.1 = bf16[2,32,4096]{2,1,0:T(8,128)(2,1)S(1)} collective-permute-done((bf16[2,32,4096]{2,1,0:T(8,128)(2,1)S(1)}, bf16[2,32,4096]{2,1,0:T(8,128)(2,1)S(1)}, u32[]{:S(2)}, u32[]{:S(2)}) %collective-permute-start.1) | collective-permute-done | bytes 524320 | tf_op jit(solution)/shard_map/ppermute | solution.py:29
  51.3 1.8 collective-permute-start.9
  53.1 2.7 %collective-permute-start.7 = (bf16[96,4096]{1,0:T(8,128)(2,1)S(1)}, bf16[96,4096]{1,0:T(8,128)(2,1)}, u32[]{:S(2)}, u32[]{:S(2)}) collective-permute-start(bf16[96,4096]{1,0:T(8,128)(2,1)S(1)} %pad_maximum_fusion.2.refs_9_), channel_id=1, source_target_pairs={{0,12},{1,19},{4,0},{5,23},{8,4},{9,27},{12,8},{13,31},{16,28},{17... | collective-permute-start | bytes 2359304 | tf_op jit(solution)/shard_map/ppermute | solution.py:29
  55.8 1.5 collective-permute-start.11
  57.3 16.5 %collective-permute-done.11.refs_4_ = bf16[32,4096]{1,0:T(8,128)(2,1)S(1)} collective-permute-done((bf16[32,4096]{1,0:T(8,128)(2,1)S(1)}, bf16[32,4096]{1,0:T(8,128)(2,1)S(1)}, u32[]{:S(2)}, u32[]{:S(2)}) %collective-permute-start.11) | collective-permute-done | bytes 262176 | tf_op jit(solution)/shard_map/ppermute | solution.py:29
  74.6 6.9 %collective-permute-done.10.refs_3_ = bf16[32,4096]{1,0:T(8,128)(2,1)S(1)} collective-permute-done((bf16[32,4096]{1,0:T(8,128)(2,1)S(1)}, bf16[32,4096]{1,0:T(8,128)(2,1)S(1)}, u32[]{:S(2)}, u32[]{:S(2)}) %collective-permute-start.10) | collective-permute-done | bytes 262176 | tf_op jit(solution)/shard_map/ppermute | solution.py:29
  82.3 0.9 copy-done.24
  83.1 0.9 copy-done.26
  84.0 2.0 collective-permute-start.15
  86.0 1.0 collective-permute-start.13
  87.5 9.9 %collective-permute-done.13.refs_11_ = bf16[96,4096]{1,0:T(8,128)(2,1)S(1)} collective-permute-done((bf16[96,4096]{1,0:T(8,128)(2,1)}, bf16[96,4096]{1,0:T(8,128)(2,1)S(1)}, u32[]{:S(2)}, u32[]{:S(2)}) %collective-permute-start.13) | collective-permute-done | bytes 786464 | tf_op jit(solution)/shard_map/ppermute | solution.py:29
  97.3 1.8 collective-permute-done.12.refs_7_
  99.2 0.9 copy-done.28
  100.0 1.2 copy-done.23
  101.2 1.0 copy-done.1
  102.3 0.9 copy-done.7
  103.2 0.9 copy-done.9
  104.2 21.1 %shard_map.101 = (bf16[2,32,4096]{2,1,0:T(8,128)(2,1)S(1)}, bf16[2,32,4096]{2,1,0:T(8,128)(2,1)S(1)}, bf16[2,32,4096]{2,1,0:T(8,128)(2,1)S(1)}, bf16[32,4096]{1,...) custom-call(bf16[2,32,4096]{2,1,0:T(8,128)(2,1)S(1)} %pad_maximum_fu, ...), custom_call_target="tpu_custom_call" | custom-call | flops 11274289152 | bytes 62914560 | tf_op jit(solution)/shard_map/pallas_call | solution.py:178
  125.8 1.0 collective-permute-start.16
  127.2 2.2 collective-permute-start.18
  129.4 7.8 %collective-permute-done.16 = bf16[96,4096]{1,0:T(8,128)(2,1)S(1)} collective-permute-done((bf16[96,4096]{1,0:T(8,128)(2,1)}, bf16[96,4096]{1,0:T(8,128)(2,1)S(1)}, u32[]{:S(2)}, u32[]{:S(2)}) %collective-permute-start.16) | collective-permute-done | bytes 786464 | tf_op jit(solution)/shard_map/ppermute | solution.py:29
  137.2 1.1 add_convert_fusion.4
  138.3 4.7 %add_convert_fusion = bf16[8,896,256]{2,1,0:T(8,128)(2,1)} fusion(bf16[8,896,256]{2,1,0:T(8,128)(2,1)S(1)} %collective-permute-done.20, bf16[8,896,256]{2,1,0:T(8,128)(2,1)} %get-tuple-element.71), kind=kLoop, calls=%fused_computation | loop fusion | flops 7340032 | bytes 11010048 | tf_op jit(solution)/shard_map/convert_element_type | solution.py:242
  143.1 1.7 add_convert_fusion.3
  144.8 0.9 collective-permute-done.18
  145.7 2.0 collective-permute-done.19
  147.9 1.3 collective-permute-start.24
  149.2 1.4 collective-permute-start.21
  150.7 2.4 %collective-permute-done.23 = bf16[32,4096]{1,0:T(8,128)(2,1)S(1)} collective-permute-done((bf16[32,4096]{1,0:T(8,128)(2,1)S(1)}, bf16[32,4096]{1,0:T(8,128)(2,1)S(1)}, u32[]{:S(2)}, u32[]{:S(2)}) %collective-permute-start.23) | collective-permute-done | bytes 262176 | tf_op jit(solution)/shard_map/ppermute | solution.py:29
  153.2 1.5 collective-permute-done.24
  154.9 6.8 %collective-permute-done.21 = bf16[96,4096]{1,0:T(8,128)(2,1)S(1)} collective-permute-done((bf16[96,4096]{1,0:T(8,128)(2,1)S(1)}, bf16[96,4096]{1,0:T(8,128)(2,1)S(1)}, u32[]{:S(2)}, u32[]{:S(2)}) %collective-permute-start.21) | collective-permute-done | bytes 786464 | tf_op jit(solution)/shard_map/ppermute | solution.py:29
  161.7 1.5 fusion.3
  163.2 1.4 fusion.4
  164.8 1.7 collective-permute-start.28
  166.9 1.0 collective-permute-start.26
  167.9 1.6 collective-permute-start.25
  169.4 4.1 %collective-permute-done.28 = bf16[2,32,4096]{2,1,0:T(8,128)(2,1)S(1)} collective-permute-done((bf16[2,32,4096]{2,1,0:T(8,128)(2,1)S(1)}, bf16[2,32,4096]{2,1,0:T(8,128)(2,1)S(1)}, u32[]{:S(2)}, u32[]{:S(2)}) %collective-permute-start.28) | collective-permute-done | bytes 524320 | tf_op jit(solution)/shard_map/ppermute | solution.py:29
  173.5 5.5 %collective-permute-done.29 = bf16[2,32,4096]{2,1,0:T(8,128)(2,1)S(1)} collective-permute-done((bf16[2,32,4096]{2,1,0:T(8,128)(2,1)S(1)}, bf16[2,32,4096]{2,1,0:T(8,128)(2,1)S(1)}, u32[]{:S(2)}, u32[]{:S(2)}) %collective-permute-start.29) | collective-permute-done | bytes 524320 | tf_op jit(solution)/shard_map/ppermute | solution.py:29
  179.0 1.4 collective-permute-start.31
  180.4 2.1 collective-permute-done.31
  182.5 3.1 %collective-permute-start.32 = (f32[4096]{0:T(1024)S(1)}, f32[4096]{0:T(1024)S(1)}, u32[]{:S(2)}, u32[]{:S(2)}) collective-permute-start(f32[4096]{0:T(1024)S(1)} %add.113), channel_id=1, source_target_pairs={{0,64},{1,65},{4,68},{5,69},{8,72},{9,73},{12,76},{13,77},{16,80},... | collective-permute-start | bytes 49160 | tf_op jit(solution)/shard_map/ppermute | solution.py:228
  185.6 2.0 collective-permute-done.32
  187.7 6.4 %collective-permute-start.33 = (f32[4096]{0:T(1024)S(1)}, f32[4096]{0:T(1024)S(1)}, u32[]{:S(2)}, u32[]{:S(2)}) collective-permute-start(f32[4096]{0:T(1024)S(1)} %add.114), channel_id=1, source_target_pairs={{0,128},{1,129},{4,132},{5,133},{8,136},{9,137},{12,140},{13,141},... | collective-permute-start | bytes 49160 | tf_op jit(solution)/shard_map/ppermute | solution.py:228
  194.1 1.5 collective-permute-done.33
  195.6 9.9 %collective-permute-start.34 = (f32[4096]{0:T(1024)S(1)}, f32[4096]{0:T(1024)S(1)}, u32[]{:S(2)}, u32[]{:S(2)}) collective-permute-start(f32[4096]{0:T(1024)S(1)} %add.115), channel_id=1, source_target_pairs={{0,1},{1,0},{4,5},{5,4},{8,9},{9,8},{12,13},{13,12},{16,17},{17,16... | collective-permute-start | bytes 49160 | tf_op jit(solution)/shard_map/ppermute | solution.py:228
  206.3 2.6 %collective-permute-done.35 = f32[4096]{0:T(1024)S(1)} collective-permute-done((f32[4096]{0:T(1024)S(1)}, f32[4096]{0:T(1024)S(1)}, u32[]{:S(2)}, u32[]{:S(2)}) %collective-permute-start.35) | collective-permute-done | bytes 16416 | tf_op jit(solution)/shard_map/ppermute | solution.py:228
  208.9 2.2 collective-permute-start.36
  211.1 1.9 collective-permute-done.36
  213.0 2.6 %collective-permute-done.37 = f32[4096]{0:T(1024)S(1)} collective-permute-done((f32[4096]{0:T(1024)S(1)}, f32[4096]{0:T(1024)S(1)}, u32[]{:S(2)}, u32[]{:S(2)}) %collective-permute-start.37) | collective-permute-done | bytes 16416 | tf_op jit(solution)/shard_map/ppermute | solution.py:228
  215.7 3.9 %collective-permute-done.38 = f32[4096]{0:T(1024)S(1)} collective-permute-done((f32[4096]{0:T(1024)S(1)}, f32[4096]{0:T(1024)S(1)}, u32[]{:S(2)}, u32[]{:S(2)}) %collective-permute-start.38) | collective-permute-done | bytes 16416 | tf_op jit(solution)/shard_map/ppermute | solution.py:228
  220.3 6.6 %collective-permute-start.39 = (bf16[896,256]{1,0:T(8,128)(2,1)}, bf16[896,256]{1,0:T(8,128)(2,1)S(1)}, u32[]{:S(2)}, u32[]{:S(2)}) collective-permute-start(bf16[896,256]{1,0:T(8,128)(2,1)} %bitcast.66), channel_id=1, source_target_pairs={{0,0},{1,16},{4,4},{5,20},{8,8},{9,24},{12,12},{13,28},{16,1},{17,... | collective-permute-start | bytes 1376264 | tf_op jit(solution)/shard_map/ppermute | solution.py:41
  228.3 3.9 %collective-permute-start.30 = (bf16[1,4096]{1,0:T(2,128)(2,1)S(1)}, bf16[1,4096]{1,0:T(2,128)(2,1)S(1)}, u32[]{:S(2)}, u32[]{:S(2)}) collective-permute-start(bf16[1,4096]{1,0:T(2,128)(2,1)S(1)} %slice.92), channel_id=1, source_target_pairs={{0,1},{1,2},{2,3},{3,4},{4,5},{5,6},{6,7},{7,8},{8,9},{9,10},{10,1... | collective-permute-start | bytes 24584 | tf_op jit(solution)/shard_map/ppermute | solution.py:47
  232.2 1.5 fusion.1
  233.7 1.4 fusion
  235.1 1.0 slice_convert_fusion
  (132 shorter events, 12.4 us)
Async XLA Ops:
  7.2 13.6 %copy-start.13 = (bf16[128,4096]{1,0:T(8,128)(2,1)S(1)}, bf16[128,4096]{1,0:T(8,128)(2,1)}, u32[]{:S(2)}) copy-start(bf16[128,4096]{1,0:T(8,128)(2,1)} %param.6) | copy-start | bytes 3145732
  7.2 76.8 %all-gather.3.cloned.1.call-start = ((), (), s32[]{:S(2)}) async-start(), calls=%async_computation.2 | async-start | bytes 4128768 | tf_op jit(solution)/shard_map/all_gather | solution.py:275
  9.9 12.0 %copy-start.22 = (f32[4096]{0:T(1024)S(1)}, f32[4096]{0:T(1024)}, u32[]{:S(2)}) copy-start(f32[4096]{0:T(1024)} %param.8) | copy-start | bytes 49156
  9.9 12.1 %collective-permute-start = (bf16[1,4096]{1,0:T(2,128)(2,1)S(1)}, bf16[1,4096]{1,0:T(2,128)(2,1)S(1)}, u32[]{:S(2)}, u32[]{:S(2)}) collective-permute-start(bf16[1,4096]{1,0:T(2,128)(2,1)S(1)} %slice.85), channel_id=1, source_target_pairs={{1,0},{2,1},{3,2},{4,3},{5,4},{6,5},{7,6},{8,7},{9,8},{10,9},{11,1... | collective-permute-start | bytes 24584 | tf_op jit(solution)/shard_map/ppermute | solution.py:47
  16.2 10.7 %collective-permute-start.14 = (bf16[896,256]{1,0:T(8,128)(2,1)S(1)}, bf16[896,256]{1,0:T(8,128)(2,1)S(1)}, u32[]{:S(2)}, u32[]{:S(2)}) collective-permute-start(bf16[896,256]{1,0:T(8,128)(2,1)S(1)} %pad_maximum_fusion.6), channel_id=1, source_target_pairs={{0,0},{1,16},{4,4},{5,20},{8,8},{9,24},{12,12},{13,28},{16,1},{17,... | collective-permute-start | bytes 1376264 | tf_op jit(solution)/shard_map/ppermute | solution.py:41
  27.7 192.6 %reduce-scatter.2.cloned.1.call-start = ((), (), s32[]{:S(2)}) async-start(), calls=%async_computation.1 | async-start | bytes 4128768 | tf_op jit(solution)/shard_map/reduce_scatter | solution.py:252
  27.8 12.5 %collective-permute-start.3 = (bf16[2,32,4096]{2,1,0:T(8,128)(2,1)S(1)}, bf16[2,32,4096]{2,1,0:T(8,128)(2,1)S(1)}, u32[]{:S(2)}, u32[]{:S(2)}) collective-permute-start(bf16[2,32,4096]{2,1,0:T(8,128)(2,1)S(1)} %pad_maximum_fusion.3.refs_0_), channel_id=1, source_target_pairs={{0,18},{1,13},{4,22},{5,1},{8,26},{9,5},{12,30},{13,9},{16,0},{17,... | collective-permute-start | bytes 1572872 | tf_op jit(solution)/shard_map/ppermute | solution.py:29
  29.1 22.2 %collective-permute-start.5 = (bf16[2,32,4096]{2,1,0:T(8,128)(2,1)S(1)}, bf16[2,32,4096]{2,1,0:T(8,128)(2,1)S(1)}, u32[]{:S(2)}, u32[]{:S(2)}) collective-permute-start(bf16[2,32,4096]{2,1,0:T(8,128)(2,1)S(1)} %pad_maximum_fusion.3.refs_0_), channel_id=1, source_target_pairs={{0,12},{1,19},{4,0},{5,23},{8,4},{9,27},{12,8},{13,31},{16,28},{17... | collective-permute-start | bytes 1572872 | tf_op jit(solution)/shard_map/ppermute | solution.py:29
  29.1 22.2 %collective-permute-start.4 = (bf16[2,32,4096]{2,1,0:T(8,128)(2,1)S(1)}, bf16[2,32,4096]{2,1,0:T(8,128)(2,1)S(1)}, u32[]{:S(2)}, u32[]{:S(2)}) collective-permute-start(bf16[2,32,4096]{2,1,0:T(8,128)(2,1)S(1)} %pad_maximum_fusion.3.refs_0_), channel_id=1, source_target_pairs={{0,4},{1,17},{4,8},{5,21},{8,12},{9,25},{12,0},{13,29},{16,20},{17... | collective-permute-start | bytes 1572872 | tf_op jit(solution)/shard_map/ppermute | solution.py:29
  30.6 14.9 %collective-permute-start.2 = (bf16[2,32,4096]{2,1,0:T(8,128)(2,1)S(1)}, bf16[2,32,4096]{2,1,0:T(8,128)(2,1)S(1)}, u32[]{:S(2)}, u32[]{:S(2)}) collective-permute-start(bf16[2,32,4096]{2,1,0:T(8,128)(2,1)S(1)} %pad_maximum_fusion.3.refs_0_), channel_id=1, source_target_pairs={{0,2},{1,9},{4,6},{5,13},{8,10},{9,1},{12,14},{13,5},{16,18},{17,2... | collective-permute-start | bytes 1572872 | tf_op jit(solution)/shard_map/ppermute | solution.py:29
  30.8 20.3 %collective-permute-start.1 = (bf16[2,32,4096]{2,1,0:T(8,128)(2,1)S(1)}, bf16[2,32,4096]{2,1,0:T(8,128)(2,1)S(1)}, u32[]{:S(2)}, u32[]{:S(2)}) collective-permute-start(bf16[2,32,4096]{2,1,0:T(8,128)(2,1)S(1)} %pad_maximum_fusion.3.refs_0_), channel_id=1, source_target_pairs={{0,16},{1,5},{4,20},{5,9},{8,24},{9,13},{12,28},{13,1},{16,2},{17,... | collective-permute-start | bytes 1572872 | tf_op jit(solution)/shard_map/ppermute | solution.py:29
  51.2 30.3 %copy-start.17 = (bf16[96,4096]{1,0:T(8,128)(2,1)}, bf16[96,4096]{1,0:T(8,128)(2,1)S(1)}, u32[]{:S(2)}) copy-start(bf16[96,4096]{1,0:T(8,128)(2,1)S(1)} %pad_maximum_fusion.2.refs_9_) | copy-start | bytes 2359300
  51.3 31.0 %copy-start.18 = (bf16[96,4096]{1,0:T(8,128)(2,1)}, bf16[96,4096]{1,0:T(8,128)(2,1)S(1)}, u32[]{:S(2)}) copy-start(bf16[96,4096]{1,0:T(8,128)(2,1)S(1)} %pad_maximum_fusion.1.refs_5_) | copy-start | bytes 2359300
  51.3 47.8 %copy-start = (bf16[2,32,4096]{2,1,0:T(8,128)(2,1)}, bf16[2,32,4096]{2,1,0:T(8,128)(2,1)S(1)}, u32[]{:S(2)}) copy-start(bf16[2,32,4096]{2,1,0:T(8,128)(2,1)S(1)} %collective-permute-done.4.refs_1_) | copy-start | bytes 1572868
  51.3 30.9 %collective-permute-start.9 = (bf16[96,4096]{1,0:T(8,128)(2,1)S(1)}, bf16[96,4096]{1,0:T(8,128)(2,1)S(1)}, u32[]{:S(2)}, u32[]{:S(2)}) collective-permute-start(bf16[96,4096]{1,0:T(8,128)(2,1)S(1)} %pad_maximum_fusion.1.refs_5_), channel_id=1, source_target_pairs={{0,12},{1,19},{4,0},{5,23},{8,4},{9,27},{12,8},{13,31},{16,28},{17... | collective-permute-start | bytes 2359304 | tf_op jit(solution)/shard_map/ppermute | solution.py:29
  53.1 29.2 %collective-permute-start.6 = (bf16[96,4096]{1,0:T(8,128)(2,1)S(1)}, bf16[96,4096]{1,0:T(8,128)(2,1)S(1)}, u32[]{:S(2)}, u32[]{:S(2)}) collective-permute-start(bf16[96,4096]{1,0:T(8,128)(2,1)S(1)} %pad_maximum_fusion.1.refs_5_), channel_id=1, source_target_pairs={{0,4},{1,17},{4,8},{5,21},{8,12},{9,25},{12,0},{13,29},{16,20},{17... | collective-permute-start | bytes 2359304 | tf_op jit(solution)/shard_map/ppermute | solution.py:29
  53.1 29.2 %collective-permute-start.8 = (bf16[96,4096]{1,0:T(8,128)(2,1)S(1)}, bf16[96,4096]{1,0:T(8,128)(2,1)S(1)}, u32[]{:S(2)}, u32[]{:S(2)}) collective-permute-start(bf16[96,4096]{1,0:T(8,128)(2,1)S(1)} %pad_maximum_fusion.2.refs_9_), channel_id=1, source_target_pairs={{0,4},{1,17},{4,8},{5,21},{8,12},{9,25},{12,0},{13,29},{16,20},{17... | collective-permute-start | bytes 2359304 | tf_op jit(solution)/shard_map/ppermute | solution.py:29
  53.1 30.9 %collective-permute-start.7 = (bf16[96,4096]{1,0:T(8,128)(2,1)S(1)}, bf16[96,4096]{1,0:T(8,128)(2,1)}, u32[]{:S(2)}, u32[]{:S(2)}) collective-permute-start(bf16[96,4096]{1,0:T(8,128)(2,1)S(1)} %pad_maximum_fusion.2.refs_9_), channel_id=1, source_target_pairs={{0,12},{1,19},{4,0},{5,23},{8,4},{9,27},{12,8},{13,31},{16,28},{17... | collective-permute-start | bytes 2359304 | tf_op jit(solution)/shard_map/ppermute | solution.py:29
  55.8 18.1 %collective-permute-start.11 = (bf16[32,4096]{1,0:T(8,128)(2,1)S(1)}, bf16[32,4096]{1,0:T(8,128)(2,1)S(1)}, u32[]{:S(2)}, u32[]{:S(2)}) collective-permute-start(bf16[32,4096]{1,0:T(8,128)(2,1)S(1)} %slice_bitcast_fusion.8), channel_id=1, source_target_pairs={{0,12},{1,19},{4,0},{5,23},{8,4},{9,27},{12,8},{13,31},{16,28},{17... | collective-permute-start | bytes 786440 | tf_op jit(solution)/shard_map/ppermute | solution.py:29
  74.6 6.9 %collective-permute-start.10 = (bf16[32,4096]{1,0:T(8,128)(2,1)S(1)}, bf16[32,4096]{1,0:T(8,128)(2,1)S(1)}, u32[]{:S(2)}, u32[]{:S(2)}) collective-permute-start(bf16[32,4096]{1,0:T(8,128)(2,1)S(1)} %slice_bitcast_fusion.9), channel_id=1, source_target_pairs={{0,4},{1,17},{4,8},{5,21},{8,12},{9,25},{12,0},{13,29},{16,20},{17... | collective-permute-start | bytes 786440 | tf_op jit(solution)/shard_map/ppermute | solution.py:29
  82.2 16.9 %copy-start.25 = (bf16[96,4096]{1,0:T(8,128)(2,1)}, bf16[96,4096]{1,0:T(8,128)(2,1)S(1)}, u32[]{:S(2)}) copy-start(bf16[96,4096]{1,0:T(8,128)(2,1)S(1)} %collective-permute-done.6.refs_6_) | copy-start | bytes 2359300
  84.0 15.1 %collective-permute-start.15 = (bf16[8,896,256]{2,1,0:T(8,128)(2,1)}, bf16[8,896,256]{2,1,0:T(8,128)(2,1)S(1)}, u32[]{:S(2)}, u32[]{:S(2)}) collective-permute-start(bf16[8,896,256]{2,1,0:T(8,128)(2,1)} %bitcast.64), channel_id=1, source_target_pairs={{0,1},{1,0},{4,5},{5,4},{8,9},{9,8},{12,13},{13,12},{16,17},{17,16... | collective-permute-start | bytes 11010056 | tf_op jit(solution)/shard_map/ppermute | solution.py:34
  86.0 11.3 %collective-permute-start.13 = (bf16[96,4096]{1,0:T(8,128)(2,1)}, bf16[96,4096]{1,0:T(8,128)(2,1)S(1)}, u32[]{:S(2)}, u32[]{:S(2)}) collective-permute-start(bf16[96,4096]{1,0:T(8,128)(2,1)} %collective-permute-done.7.refs_12_), channel_id=1, source_target_pairs={{0,12},{1,19},{4,0},{5,23},{8,4},{9,27},{12,8},{13,31},{16,28},{17... | collective-permute-start | bytes 2359304 | tf_op jit(solution)/shard_map/ppermute | solution.py:29
  87.0 12.2 %collective-permute-start.12 = (bf16[96,4096]{1,0:T(8,128)(2,1)S(1)}, bf16[96,4096]{1,0:T(8,128)(2,1)S(1)}, u32[]{:S(2)}, u32[]{:S(2)}) collective-permute-start(bf16[96,4096]{1,0:T(8,128)(2,1)S(1)} %collective-permute-done.6.refs_6_), channel_id=1, source_target_pairs={{0,4},{1,17},{4,8},{5,21},{8,12},{9,25},{12,0},{13,29},{16,20},{17... | collective-permute-start | bytes 2359304 | tf_op jit(solution)/shard_map/ppermute | solution.py:29
  97.3 1.8 copy-start.27
  99.1 0.9 copy-start.28
  99.2 2.1 copy-start.23
  101.2 1.0 copy-start.1
  102.3 0.9 copy-start.7
  103.2 0.9 copy-start.9
  125.2 13.1 %copy-start.2 = (bf16[32,4096]{1,0:T(8,128)(2,1)}, bf16[32,4096]{1,0:T(8,128)(2,1)S(1)}, u32[]{:S(2)}) copy-start(bf16[32,4096]{1,0:T(8,128)(2,1)S(1)} %get-tuple-element.81) | copy-start | bytes 786436
  125.2 13.1 %copy-start.4 = (bf16[32,4096]{1,0:T(8,128)(2,1)}, bf16[32,4096]{1,0:T(8,128)(2,1)S(1)}, u32[]{:S(2)}) copy-start(bf16[32,4096]{1,0:T(8,128)(2,1)S(1)} %get-tuple-element.79) | copy-start | bytes 786436
  125.3 13.0 %collective-permute-start.20 = (bf16[8,896,256]{2,1,0:T(8,128)(2,1)}, bf16[8,896,256]{2,1,0:T(8,128)(2,1)S(1)}, u32[]{:S(2)}, u32[]{:S(2)}) collective-permute-start(bf16[8,896,256]{2,1,0:T(8,128)(2,1)} %get-tuple-element.72), channel_id=1, source_target_pairs={{0,1},{1,0},{4,5},{5,4},{8,9},{9,8},{12,13},{13,12},{16,17},{17,16... | collective-permute-start | bytes 11010056 | tf_op jit(solution)/shard_map/ppermute | solution.py:34
  125.8 11.5 %collective-permute-start.16 = (bf16[96,4096]{1,0:T(8,128)(2,1)}, bf16[96,4096]{1,0:T(8,128)(2,1)S(1)}, u32[]{:S(2)}, u32[]{:S(2)}) collective-permute-start(bf16[96,4096]{1,0:T(8,128)(2,1)} %get-tuple-element.63), channel_id=1, source_target_pairs={{0,12},{1,19},{4,0},{5,23},{8,4},{9,27},{12,8},{13,31},{16,28},{17... | collective-permute-start | bytes 2359304 | tf_op jit(solution)/shard_map/ppermute | solution.py:29
  126.7 16.3 %collective-permute-start.17 = (bf16[96,4096]{1,0:T(8,128)(2,1)}, bf16[96,4096]{1,0:T(8,128)(2,1)}, u32[]{:S(2)}, u32[]{:S(2)}) collective-permute-start(bf16[96,4096]{1,0:T(8,128)(2,1)} %get-tuple-element.65), channel_id=1, source_target_pairs={{0,4},{1,17},{4,8},{5,21},{8,12},{9,25},{12,0},{13,29},{16,20},{17... | collective-permute-start | bytes 2359304 | tf_op jit(solution)/shard_map/ppermute | solution.py:29
  127.2 18.4 %collective-permute-start.18 = (bf16[96,4096]{1,0:T(8,128)(2,1)}, bf16[96,4096]{1,0:T(8,128)(2,1)}, u32[]{:S(2)}, u32[]{:S(2)}) collective-permute-start(bf16[96,4096]{1,0:T(8,128)(2,1)} %get-tuple-element.66), channel_id=1, source_target_pairs={{0,12},{1,19},{4,0},{5,23},{8,4},{9,27},{12,8},{13,31},{16,28},{17... | collective-permute-start | bytes 2359304 | tf_op jit(solution)/shard_map/ppermute | solution.py:29
  129.4 18.2 %collective-permute-start.19 = (bf16[96,4096]{1,0:T(8,128)(2,1)}, bf16[96,4096]{1,0:T(8,128)(2,1)}, u32[]{:S(2)}, u32[]{:S(2)}) collective-permute-start(bf16[96,4096]{1,0:T(8,128)(2,1)} %get-tuple-element.67), channel_id=1, source_target_pairs={{0,4},{1,17},{4,8},{5,21},{8,12},{9,25},{12,0},{13,29},{16,20},{17... | collective-permute-start | bytes 2359304 | tf_op jit(solution)/shard_map/ppermute | solution.py:29
  143.1 4.6 %copy-start.5 = (bf16[32,4096]{1,0:T(8,128)(2,1)S(1)}, bf16[32,4096]{1,0:T(8,128)(2,1)}, u32[]{:S(2)}) copy-start(bf16[32,4096]{1,0:T(8,128)(2,1)} %copy-done.4) | copy-start | bytes 786436
  143.1 4.8 %copy-start.3 = (bf16[32,4096]{1,0:T(8,128)(2,1)S(1)}, bf16[32,4096]{1,0:T(8,128)(2,1)}, u32[]{:S(2)}) copy-start(bf16[32,4096]{1,0:T(8,128)(2,1)} %copy-done.2) | copy-start | bytes 786436
  143.1 6.1 %copy-start.20 = (bf16[96,4096]{1,0:T(8,128)(2,1)S(1)}, bf16[96,4096]{1,0:T(8,128)(2,1)}, u32[]{:S(2)}) copy-start(bf16[96,4096]{1,0:T(8,128)(2,1)} %add_convert_fusion.4) | copy-start | bytes 2359300
  147.6 5.5 %collective-permute-start.23 = (bf16[32,4096]{1,0:T(8,128)(2,1)S(1)}, bf16[32,4096]{1,0:T(8,128)(2,1)S(1)}, u32[]{:S(2)}, u32[]{:S(2)}) collective-permute-start(bf16[32,4096]{1,0:T(8,128)(2,1)S(1)} %copy-done.5), channel_id=1, source_target_pairs={{0,12},{1,19},{4,0},{5,23},{8,4},{9,27},{12,8},{13,31},{16,28},{17... | collective-permute-start | bytes 786440 | tf_op jit(solution)/shard_map/ppermute | solution.py:29
  147.9 6.8 %collective-permute-start.24 = (bf16[32,4096]{1,0:T(8,128)(2,1)S(1)}, bf16[32,4096]{1,0:T(8,128)(2,1)S(1)}, u32[]{:S(2)}, u32[]{:S(2)}) collective-permute-start(bf16[32,4096]{1,0:T(8,128)(2,1)S(1)} %copy-done.3), channel_id=1, source_target_pairs={{0,4},{1,17},{4,8},{5,21},{8,12},{9,25},{12,0},{13,29},{16,20},{17... | collective-permute-start | bytes 786440 | tf_op jit(solution)/shard_map/ppermute | solution.py:29
  149.2 12.4 %collective-permute-start.21 = (bf16[96,4096]{1,0:T(8,128)(2,1)S(1)}, bf16[96,4096]{1,0:T(8,128)(2,1)S(1)}, u32[]{:S(2)}, u32[]{:S(2)}) collective-permute-start(bf16[96,4096]{1,0:T(8,128)(2,1)S(1)} %copy-done.20), channel_id=1, source_target_pairs={{0,12},{1,19},{4,0},{5,23},{8,4},{9,27},{12,8},{13,31},{16,28},{17... | collective-permute-start | bytes 2359304 | tf_op jit(solution)/shard_map/ppermute | solution.py:29
  150.6 12.6 %collective-permute-start.22 = (bf16[96,4096]{1,0:T(8,128)(2,1)S(1)}, bf16[96,4096]{1,0:T(8,128)(2,1)S(1)}, u32[]{:S(2)}, u32[]{:S(2)}) collective-permute-start(bf16[96,4096]{1,0:T(8,128)(2,1)S(1)} %add_convert_fusion.3), channel_id=1, source_target_pairs={{0,4},{1,17},{4,8},{5,21},{8,12},{9,25},{12,0},{13,29},{16,20},{17... | collective-permute-start | bytes 2359304 | tf_op jit(solution)/shard_map/ppermute | solution.py:29
  161.7 1.6 copy-start.19
  164.8 8.7 %collective-permute-start.28 = (bf16[2,32,4096]{2,1,0:T(8,128)(2,1)S(1)}, bf16[2,32,4096]{2,1,0:T(8,128)(2,1)S(1)}, u32[]{:S(2)}, u32[]{:S(2)}) collective-permute-start(bf16[2,32,4096]{2,1,0:T(8,128)(2,1)S(1)} %pad_maximum_fusion.4), channel_id=1, source_target_pairs={{0,12},{1,19},{4,0},{5,23},{8,4},{9,27},{12,8},{13,31},{16,28},{17... | collective-permute-start | bytes 1572872 | tf_op jit(solution)/shard_map/ppermute | solution.py:29
  166.5 12.5 %collective-permute-start.29 = (bf16[2,32,4096]{2,1,0:T(8,128)(2,1)S(1)}, bf16[2,32,4096]{2,1,0:T(8,128)(2,1)S(1)}, u32[]{:S(2)}, u32[]{:S(2)}) collective-permute-start(bf16[2,32,4096]{2,1,0:T(8,128)(2,1)S(1)} %pad_maximum_fusion.5), channel_id=1, source_target_pairs={{0,4},{1,17},{4,8},{5,21},{8,12},{9,25},{12,0},{13,29},{16,20},{17... | collective-permute-start | bytes 1572872 | tf_op jit(solution)/shard_map/ppermute | solution.py:29
  166.7 53.6 %collective-permute-start.27 = (bf16[2,32,4096]{2,1,0:T(8,128)(2,1)S(1)}, bf16[2,32,4096]{2,1,0:T(8,128)(2,1)S(1)}, u32[]{:S(2)}, u32[]{:S(2)}) collective-permute-start(bf16[2,32,4096]{2,1,0:T(8,128)(2,1)S(1)} %get-tuple-element.96), channel_id=1, source_target_pairs={{0,16},{1,5},{4,20},{5,9},{8,24},{9,13},{12,28},{13,1},{16,2},{17,... | collective-permute-start | bytes 1572872 | tf_op jit(solution)/shard_map/ppermute | solution.py:29
  166.9 53.3 %collective-permute-start.26 = (bf16[2,32,4096]{2,1,0:T(8,128)(2,1)S(1)}, bf16[2,32,4096]{2,1,0:T(8,128)(2,1)S(1)}, u32[]{:S(2)}, u32[]{:S(2)}) collective-permute-start(bf16[2,32,4096]{2,1,0:T(8,128)(2,1)S(1)} %get-tuple-element.97), channel_id=1, source_target_pairs={{0,2},{1,9},{4,6},{5,13},{8,10},{9,1},{12,14},{13,5},{16,18},{17,2... | collective-permute-start | bytes 1572872 | tf_op jit(solution)/shard_map/ppermute | solution.py:29
  167.9 52.4 %collective-permute-start.25 = (bf16[2,32,4096]{2,1,0:T(8,128)(2,1)S(1)}, bf16[2,32,4096]{2,1,0:T(8,128)(2,1)S(1)}, u32[]{:S(2)}, u32[]{:S(2)}) collective-permute-start(bf16[2,32,4096]{2,1,0:T(8,128)(2,1)S(1)} %get-tuple-element.98), channel_id=1, source_target_pairs={{0,18},{1,13},{4,22},{5,1},{8,26},{9,5},{12,30},{13,9},{16,0},{17,... | collective-permute-start | bytes 1572872 | tf_op jit(solution)/shard_map/ppermute | solution.py:29
  179.0 3.5 %collective-permute-start.31 = (f32[4096]{0:T(1024)S(1)}, f32[4096]{0:T(1024)S(1)}, u32[]{:S(2)}, u32[]{:S(2)}) collective-permute-start(f32[4096]{0:T(1024)S(1)} %bitcast.59), channel_id=1, source_target_pairs={{0,32},{1,33},{4,36},{5,37},{8,40},{9,41},{12,44},{13,45},{16,48},... | collective-permute-start | bytes 49160 | tf_op jit(solution)/shard_map/ppermute | solution.py:228
  182.5 5.1 %collective-permute-start.32 = (f32[4096]{0:T(1024)S(1)}, f32[4096]{0:T(1024)S(1)}, u32[]{:S(2)}, u32[]{:S(2)}) collective-permute-start(f32[4096]{0:T(1024)S(1)} %add.113), channel_id=1, source_target_pairs={{0,64},{1,65},{4,68},{5,69},{8,72},{9,73},{12,76},{13,77},{16,80},... | collective-permute-start | bytes 49160 | tf_op jit(solution)/shard_map/ppermute | solution.py:228
  187.7 7.9 %collective-permute-start.33 = (f32[4096]{0:T(1024)S(1)}, f32[4096]{0:T(1024)S(1)}, u32[]{:S(2)}, u32[]{:S(2)}) collective-permute-start(f32[4096]{0:T(1024)S(1)} %add.114), channel_id=1, source_target_pairs={{0,128},{1,129},{4,132},{5,133},{8,136},{9,137},{12,140},{13,141},... | collective-permute-start | bytes 49160 | tf_op jit(solution)/shard_map/ppermute | solution.py:228
  195.6 10.7 %collective-permute-start.34 = (f32[4096]{0:T(1024)S(1)}, f32[4096]{0:T(1024)S(1)}, u32[]{:S(2)}, u32[]{:S(2)}) collective-permute-start(f32[4096]{0:T(1024)S(1)} %add.115), channel_id=1, source_target_pairs={{0,1},{1,0},{4,5},{5,4},{8,9},{9,8},{12,13},{13,12},{16,17},{17,16... | collective-permute-start | bytes 49160 | tf_op jit(solution)/shard_map/ppermute | solution.py:228
  206.3 2.6 %collective-permute-start.35 = (f32[4096]{0:T(1024)S(1)}, f32[4096]{0:T(1024)S(1)}, u32[]{:S(2)}, u32[]{:S(2)}) collective-permute-start(f32[4096]{0:T(1024)S(1)} %add.116), channel_id=1, source_target_pairs={{0,16},{1,17},{4,20},{5,21},{8,24},{9,25},{12,28},{13,29},{16,0},{... | collective-permute-start | bytes 49160 | tf_op jit(solution)/shard_map/ppermute | solution.py:228
  208.9 4.1 %collective-permute-start.36 = (f32[4096]{0:T(1024)S(1)}, f32[4096]{0:T(1024)S(1)}, u32[]{:S(2)}, u32[]{:S(2)}) collective-permute-start(f32[4096]{0:T(1024)S(1)} %add.117), channel_id=1, source_target_pairs={{0,2},{1,3},{4,6},{5,7},{8,10},{9,11},{12,14},{13,15},{16,18},{17,... | collective-permute-start | bytes 49160 | tf_op jit(solution)/shard_map/ppermute | solution.py:228
  213.0 2.6 %collective-permute-start.37 = (f32[4096]{0:T(1024)S(1)}, f32[4096]{0:T(1024)S(1)}, u32[]{:S(2)}, u32[]{:S(2)}) collective-permute-start(f32[4096]{0:T(1024)S(1)} %add.118), channel_id=1, source_target_pairs={{0,4},{1,5},{4,0},{5,1},{8,12},{9,13},{12,8},{13,9},{16,20},{17,21... | collective-permute-start | bytes 49160 | tf_op jit(solution)/shard_map/ppermute | solution.py:228
  215.6 4.1 %collective-permute-start.38 = (f32[4096]{0:T(1024)S(1)}, f32[4096]{0:T(1024)S(1)}, u32[]{:S(2)}, u32[]{:S(2)}) collective-permute-start(f32[4096]{0:T(1024)S(1)} %add.119), channel_id=1, source_target_pairs={{0,8},{1,9},{4,12},{5,13},{8,0},{9,1},{12,4},{13,5},{16,24},{17,25... | collective-permute-start | bytes 49160 | tf_op jit(solution)/shard_map/ppermute | solution.py:228
  220.3 14.8 %collective-permute-start.39 = (bf16[896,256]{1,0:T(8,128)(2,1)}, bf16[896,256]{1,0:T(8,128)(2,1)S(1)}, u32[]{:S(2)}, u32[]{:S(2)}) collective-permute-start(bf16[896,256]{1,0:T(8,128)(2,1)} %bitcast.66), channel_id=1, source_target_pairs={{0,0},{1,16},{4,4},{5,20},{8,8},{9,24},{12,12},{13,28},{16,1},{17,... | collective-permute-start | bytes 1376264 | tf_op jit(solution)/shard_map/ppermute | solution.py:41
  226.9 1.0 copy-start.11
  227.9 4.2 %copy-start.12 = (bf16[128,4096]{1,0:T(8,128)(2,1)S(1)}, bf16[128,4096]{1,0:T(8,128)(2,1)}, u32[]{:S(2)}) copy-start(bf16[128,4096]{1,0:T(8,128)(2,1)} %param.11) | copy-start | bytes 3145732
  227.9 4.2 %copy-start.16 = (bf16[31,4096]{1,0:T(8,128)(2,1)S(1)}, bf16[31,4096]{1,0:T(8,128)(2,1)}, u32[]{:S(2)}) copy-start(bf16[31,4096]{1,0:T(8,128)(2,1)} %copy-done.15) | copy-start | bytes 761860
  228.2 5.4 %copy-start.14 = (bf16[128,4096]{1,0:T(8,128)(2,1)S(1)}, bf16[128,4096]{1,0:T(8,128)(2,1)}, u32[]{:S(2)}) copy-start(bf16[128,4096]{1,0:T(8,128)(2,1)} %param.6) | copy-start | bytes 3145732
  228.3 5.4 %collective-permute-start.30 = (bf16[1,4096]{1,0:T(2,128)(2,1)S(1)}, bf16[1,4096]{1,0:T(2,128)(2,1)S(1)}, u32[]{:S(2)}, u32[]{:S(2)}) collective-permute-start(bf16[1,4096]{1,0:T(2,128)(2,1)S(1)} %slice.92), channel_id=1, source_target_pairs={{0,1},{1,2},{2,3},{3,4},{4,5},{5,6},{6,7},{7,8},{8,9},{9,10},{10,1... | collective-permute-start | bytes 24584 | tf_op jit(solution)/shard_map/ppermute | solution.py:47
  (7 other events, 5.5 us)
Sparse Core Ops, SparseCore 0:
  27.8 50.0 all-gather.2
  143.2 50.5 reduce-scatter.1

commit v6 on v3

--- a/solution.py
+++ b/solution.py
@@ -70,12 +70,13 @@
     feats = chunks * width
 
     def cols(z):
-        return pl.ds(pl.multiple_of(z * width, width), width)
+        start = z * width
+        return pl.ds(start if isinstance(z, int) else pl.multiple_of(start, width), width)
 
     def w_cols(z, which):
         return pl.ds(pl.multiple_of(z * width + which * half, half), half)
 
-    def fetch(z, carry):
+    def fetch(z):
         for i, pair in enumerate(acts):
             at = pl.ds(i * rows, rows)
             for k, (source, buf) in enumerate(zip(pair, (p_s, g_s))):
@@ -91,14 +92,19 @@
                 wo_s.at[:, w_cols(z, which)],
                 in_sem.at[3, z],
             ).start()
-        return carry
-
-    lax.fori_loop(0, chunks, fetch, 0)
+
+    ahead = 3
+    for z in range(ahead):
+        fetch(z)
     h_s[...] = jnp.zeros_like(h_s)
     ga_s[...] = jnp.zeros_like(ga_s)
     sq_s[...] = jnp.zeros_like(sq_s)
 
     def first(z, carry):
+        @pl.when(z + ahead < chunks)
+        def _():
+            fetch(z + ahead)
+
         for k, buf in enumerate((p_s, g_s, wi_s, wo_s)):
             view = buf.at[:, cols(z)]
             pltpu.make_async_copy(view, view, in_sem.at[k, z]).wait()
@@ -110,18 +116,22 @@
         return carry
 
     lax.fori_loop(0, chunks, first, 0)
-    inv = lax.rsqrt(sq_s[...] * (1.0 / feats) + 1e-05)
-    v = h_s[...] * inv
-    v2 = v * v
-    t = jnp.tanh(0.7978845608 * v * (1.0 + 0.044715 * v2))
-    up = 0.5 * (1.0 + t)
-    a = (v * up).astype(jnp.bfloat16)
-    slope = up + 0.5 * v * (1.0 - t * t) * (0.7978845608 * (1.0 + 0.134145 * v2))
-    b = (ga_s[...] * slope * inv).astype(jnp.bfloat16)
-    act[...] = a
-    gp[...] = b
-    act_t[...] = a.T
-    gp_t[...] = b.T
+
+    def middle(i, carry):
+        at = pl.ds(pl.multiple_of(i * 32, 32), 32)
+        inv = lax.rsqrt(sq_s[at, :] * (1.0 / feats) + 1e-05)
+        v = h_s[at, :] * inv
+        v2 = v * v
+        t = jnp.tanh(0.7978845608 * v * (1.0 + 0.044715 * v2))
+        up = 0.5 * (1.0 + t)
+        act[at, :] = (v * up).astype(jnp.bfloat16)
+        slope = up + 0.5 * v * (1.0 - t * t) * (0.7978845608 * (1.0 + 0.134145 * v2))
+        gp[at, :] = (ga_s[at, :] * slope * inv).astype(jnp.bfloat16)
+        return carry
+
+    lax.fori_loop(0, act.shape[0] // 32, middle, 0)
+    act_t[...] = act[...].T
+    gp_t[...] = gp[...].T
 
     def second(z, carry):
         wi = wi_s[:, cols(z)]
@@ -181,7 +191,7 @@
         + [pltpu.VMEM((total, hidden), bf)] * 2
         + [pltpu.VMEM((hidden, total), bf)] * 2
         + [pltpu.SemaphoreType.DMA((4, chunks)), pltpu.SemaphoreType.DMA((4, chunks))],
-        compiler_params=pltpu.CompilerParams(vmem_limit_bytes=48 * 1024 * 1024),
+        compiler_params=pltpu.CompilerParams(vmem_limit_bytes=40 * 1024 * 1024),
         cost_estimate=pl.CostEstimate(
             flops=flops, bytes_accessed=8 * (total + hidden) * feats * 2, transcendentals=0
         ),
@@ -207,35 +217,42 @@
     return [p0, p1, p2, p3, g0, g1, g2, g3]
 
 
-def scatter_plane(outs, gain_part, weight_part):
-    d0, d1, d2, d3, n0, n1, n2, n3 = outs
-    bf = jnp.bfloat16
-    d2, n2 = shift(d2, second=-1), shift(n2, second=1)
-    n1, d3 = shift(n1, second=-1), shift(d3, second=1)
-    d1, n3 = add_all([d1, d2]).astype(bf), add_all([n3, n2]).astype(bf)
-    d1, n3, weight_part = lax.optimization_barrier((d1, n3, weight_part))
-    weight_sum = lax.psum_scatter(weight_part, "z", scatter_dimension=0, tiled=False)
-    d1, n3 = shift(d1, second=-1), shift(n3, second=1)
-    arrived = (d1, d3, n1, n3, total_over_all(gain_part))
-    d1, d3, n1, n3, grad_gain = lax.optimization_barrier(arrived)
-    both = jnp.stack([add_all([d0, d1, d3]).astype(bf), add_all([n0, n1, n3]).astype(bf)])
-    rows = both.shape[1] // 4
-    both = [both[:, d * rows : (d + 1) * rows] for d in range(4)]
-    arrived = [shift(both[d], first=-d) for d in (1, 2, 3)] + [weight_sum]
-    *arrived, weight_sum = lax.optimization_barrier(arrived)
-    return add_all([both[0], *arrived]), grad_gain, weight_sum
-
-
-def total_over_all(value):
-    moves = [lambda p, k=k: (p[0] ^ k, p[1], p[2], p[3]) for k in (1, 2, 4)]
-    moves += [lambda p: (p[0], p[1], p[2], 1 - p[3])]
-    moves += [lambda p, k=k: (p[0], p[1] ^ k, p[2], p[3]) for k in (1, 2)]
-    moves += [lambda p, k=k: (p[0], p[1], p[2] ^ k, p[3]) for k in (1, 2)]
+def swapped(value, moves):
     for move in moves:
         value = value + lax.ppermute(
             value, AXES, [(linear(*p), linear(*move(p))) for p in places()]
         )
     return value
+
+
+def all_moves():
+    moves = [lambda p, k=k: (p[0] ^ k, p[1], p[2], p[3]) for k in (1, 2, 4)]
+    moves += [lambda p: (p[0], p[1], p[2], 1 - p[3])]
+    moves += [lambda p, k=k: (p[0], p[1] ^ k, p[2], p[3]) for k in (1, 2)]
+    return moves + [lambda p, k=k: (p[0], p[1], p[2] ^ k, p[3]) for k in (1, 2)]
+
+
+def rounded_sum(*parts):
+    return add_all(parts).astype(jnp.bfloat16)
+
+
+def scatter_plane(outs, g_own, g_oth, gain):
+    d0, d1, d2, d3, n0, n1, n2, n3 = outs
+    tie = lax.optimization_barrier
+    moves = all_moves()
+    d2, n2 = shift(d2, second=-1), shift(n2, second=1)
+    n1, d3 = shift(n1, second=-1), shift(d3, second=1)
+    mine = rounded_sum(g_own, other_core(g_oth))
+    weight_sum = lax.psum_scatter(mine, "z", scatter_dimension=0, tiled=False)
+    d1, n3 = rounded_sum(d1, d2), rounded_sum(n3, n2)
+    d1, n3, n1, d3, gain, _ = tie((d1, n3, n1, d3, gain, mine))
+    d1, n3, gain = tie((shift(d1, second=-1), shift(n3, second=1), swapped(gain, moves[:3])))
+    both = jnp.stack([rounded_sum(d0, d1, d3), rounded_sum(n0, n1, n3)])
+    rows = both.shape[1] // 4
+    both = [both[:, d * rows : (d + 1) * rows] for d in range(4)]
+    arrived = [shift(both[d], first=-d) for d in (1, 2, 3)]
+    *arrived, gain, weight_sum = tie((*arrived, swapped(gain, moves[3:6]), weight_sum))
+    return add_all([both[0], *arrived]), swapped(gain, moves[6:]), weight_sum
 
 
 def shards(stream, doc_start, norm_gain, weight_in, weight_out, upstream):
@@ -268,9 +285,9 @@
     w_oth = other_core(w_own)
     results = block(blocks, w_own, w_oth)
     outs, (g_own, g_oth, gain_part) = results[:8], results[8:]
-
-    mine = (g_own.astype(jnp.float32) + other_core(g_oth).astype(jnp.float32)).astype(bf)
-    (down_sum, scaled), grad_gain, grads = scatter_plane(outs, gain_part[0] / norm_gain, mine)
+    (down_sum, scaled), grad_gain, grads = scatter_plane(
+        outs, g_own, g_oth, gain_part[0] / norm_gain
+    )
     grads = swap_low(grads)
     grad_weight_in = (grads[:hidden].astype(jnp.float32) * gain[None, :]).T
     grad_weight_out = grads[hidden:].astype(jnp.float32)

time: 222 us -> 238 us (1.072)
  waiting for transfers between devices: 113 us -> 100 us
  starting transfers between devices: 49.8 us -> 62.5 us
  local copies, waits for them, and re-layouts: 7.22 us -> 19.3 us
  Pallas kernels: 20.5 us -> 23 us
    unnamed x42 -> x54, local copies, waits for them, and re-layouts: 5.49 us -> 16.9 us
    ppermute x8, waiting for transfers between devices: 20.6 us -> 10.8 us  [swapped(): lax.ppermute(value, AXES, [(linear(*p), linear(*move(p))) for p in places...]
    ppermute x8, starting transfers between devices: 13.2 us -> 22 us  [swapped(): lax.ppermute(value, AXES, [(linear(*p), linear(*move(p))) for p in places...]
    ppermute x2, starting transfers between devices: 8.05 us -> 14.6 us  [from_behind(): return lax.ppermute(value, AXES, pairs)]
    ppermute x2, waiting for transfers between devices: 0.01 us -> 6.25 us  [other_core(): return lax.ppermute(value, AXES, pairs)]
    ppermute x18, waiting for transfers between devices: 78.6 us -> 72.4 us  [shift(): return lax.ppermute(value, AXES, pairs)]
    ppermute x2, waiting for transfers between devices: 9.43 us -> 6.67 us  [swap_low(): return lax.ppermute(value, AXES, pairs)]
    pallas_call x1, Pallas kernels: 20.5 us -> 23 us  [block(): pl.pallas_call(functools.partial(block_kernel, chunks), out_shape=[jax.Sh...]
  transfers between devices with their start and end apart: 34 -> 34, of which waited for: 21 -> 22; matrix products, arithmetic and copies ran while one was open for 4% -> 5% of each run, Pallas kernels for 0% -> 0%
where the time goes in v6:
time: 238 us; the launch traced here: 237 us
  waiting for transfers between devices  100 us (42%)
  starting transfers between devices  62.5 us (26%)
  Pallas kernels  23 us (10%)
  local copies, waits for them, and re-layouts  19.3 us (8%)
  between operations  14.5 us (6%)
  other arithmetic  14.1 us (6%)
  matrix products  3.44 us (1%)
    ppermute x18, waiting for transfers between devices, shift(): return lax.ppermute(value, AXES, pairs)  72.4 us
    pallas_call x1, Pallas kernels, block(): pl.pallas_call(functools.partial(block_kernel, chunks), out_shape=[jax.Sh...  23 us
    ppermute x8, starting transfers between devices, swapped(): lax.ppermute(value, AXES, [(linear(*p), linear(*move(p))) for p in places...  22 us
    ppermute x18, starting transfers between devices, shift(): return lax.ppermute(value, AXES, pairs)  17.8 us
    unnamed x54, local copies, waits for them, and re-layouts  16.9 us
    ppermute x2, starting transfers between devices, from_behind(): return lax.ppermute(value, AXES, pairs)  14.6 us
    ppermute x8, waiting for transfers between devices, swapped(): lax.ppermute(value, AXES, [(linear(*p), linear(*move(p))) for p in places...  10.8 us
    ppermute x2, waiting for transfers between devices, swap_low(): return lax.ppermute(value, AXES, pairs)  6.67 us
  transfers between devices with their start and end apart: 34, of which 22 were waited for; matrix products, arithmetic and copies ran while one was open for 5% of the time, Pallas kernels for 0%

profile of v6, /device:TPU:1, one launch (start us, length us, event | category | flops | bytes accessed | tf_op | source)
XLA Modules:
  0.0 237.3 jit_solution(13036581619648466355)
XLA Ops:
  7.2 0.9 dynamic_slice.3
  8.1 1.0 fusion.20
  9.1 1.0 pad_maximum_fusion.3
  10.1 4.6 %collective-permute-start.10 = (bf16[896,256]{1,0:T(8,128)(2,1)S(1)}, bf16[896,256]{1,0:T(8,128)(2,1)S(1)}, u32[]{:S(2)}, u32[]{:S(2)}) collective-permute-start(bf16[896,256]{1,0:T(8,128)(2,1)S(1)} %pad_maximum_fusion.3), channel_id=1, source_target_pairs={{0,0},{1,16},{4,4},{5,20},{8,8},{9,24},{12,12},{13,28},{16,1},{17,... | collective-permute-start | bytes 1376264 | tf_op jit(solution)/shard_map/ppermute | solution.py:41
  15.8 5.1 %collective-permute-done.10 = bf16[896,256]{1,0:T(8,128)(2,1)S(1)} collective-permute-done((bf16[896,256]{1,0:T(8,128)(2,1)S(1)}, bf16[896,256]{1,0:T(8,128)(2,1)S(1)}, u32[]{:S(2)}, u32[]{:S(2)}) %collective-permute-start.10) | collective-permute-done | bytes 458784 | tf_op jit(solution)/shard_map/ppermute | solution.py:41
  22.0 1.9 collective-permute-start
  24.3 4.3 %collective-permute-done = bf16[1,4096]{1,0:T(2,128)(2,1)S(1)} collective-permute-done((bf16[1,4096]{1,0:T(2,128)(2,1)S(1)}, bf16[1,4096]{1,0:T(2,128)(2,1)S(1)}, u32[]{:S(2)}, u32[]{:S(2)}) %collective-permute-start) | collective-permute-done | bytes 8224 | tf_op jit(solution)/shard_map/ppermute | solution.py:47
  28.7 2.6 %collective-permute-start.3 = (bf16[2,32,4096]{2,1,0:T(8,128)(2,1)S(1)}, bf16[2,32,4096]{2,1,0:T(8,128)(2,1)S(1)}, u32[]{:S(2)}, u32[]{:S(2)}) collective-permute-start(bf16[2,32,4096]{2,1,0:T(8,128)(2,1)S(1)} %pad_maximum_fusion.2), channel_id=1, source_target_pairs={{0,18},{1,13},{4,22},{5,1},{8,26},{9,5},{12,30},{13,9},{16,0},{17,... | collective-permute-start | bytes 1572872 | tf_op jit(solution)/shard_map/ppermute | solution.py:29
  32.4 10.6 %collective-permute-done.3 = bf16[2,32,4096]{2,1,0:T(8,128)(2,1)S(1)} collective-permute-done((bf16[2,32,4096]{2,1,0:T(8,128)(2,1)S(1)}, bf16[2,32,4096]{2,1,0:T(8,128)(2,1)S(1)}, u32[]{:S(2)}, u32[]{:S(2)}) %collective-permute-start.3) | collective-permute-done | bytes 524320 | tf_op jit(solution)/shard_map/ppermute | solution.py:29
  43.1 3.7 %collective-permute-done.1 = bf16[2,32,4096]{2,1,0:T(8,128)(2,1)S(1)} collective-permute-done((bf16[2,32,4096]{2,1,0:T(8,128)(2,1)S(1)}, bf16[2,32,4096]{2,1,0:T(8,128)(2,1)S(1)}, u32[]{:S(2)}, u32[]{:S(2)}) %collective-permute-start.1) | collective-permute-done | bytes 524320 | tf_op jit(solution)/shard_map/ppermute | solution.py:29
  47.9 1.0 pad_maximum_fusion.refs_0_
  49.1 1.5 collective-permute-start.4
  50.5 1.0 copy-done
  51.5 1.7 collective-permute-start.6
  53.2 1.0 collective-permute-start.5
  54.2 8.9 %collective-permute-done.7.refs_3_ = bf16[128,4096]{1,0:T(8,128)(2,1)S(1)} collective-permute-done((bf16[128,4096]{1,0:T(8,128)(2,1)S(1)}, bf16[128,4096]{1,0:T(8,128)(2,1)S(1)}, u32[]{:S(2)}, u32[]{:S(2)}) %collective-permute-start.7) | collective-permute-done | bytes 1048608 | tf_op jit(solution)/shard_map/ppermute | solution.py:29
  63.1 1.0 copy-done.9
  64.1 1.2 collective-permute-done.4.refs_1_
  65.3 11.1 %collective-permute-done.6.refs_5_ = bf16[128,4096]{1,0:T(8,128)(2,1)S(1)} collective-permute-done((bf16[128,4096]{1,0:T(8,128)(2,1)S(1)}, bf16[128,4096]{1,0:T(8,128)(2,1)S(1)}, u32[]{:S(2)}, u32[]{:S(2)}) %collective-permute-start.6) | collective-permute-done | bytes 1048608 | tf_op jit(solution)/shard_map/ppermute | solution.py:29
  76.5 1.0 copy-done.24
  77.5 1.2 collective-permute-start.11
  78.7 0.8 collective-permute-start.9
  80.2 1.0 copy-done.11
  81.1 11.7 %collective-permute-done.9.refs_6_ = bf16[128,4096]{1,0:T(8,128)(2,1)S(1)} collective-permute-done((bf16[128,4096]{1,0:T(8,128)(2,1)}, bf16[128,4096]{1,0:T(8,128)(2,1)S(1)}, u32[]{:S(2)}, u32[]{:S(2)}) %collective-permute-start.9) | collective-permute-done | bytes 1048608 | tf_op jit(solution)/shard_map/ppermute | solution.py:29
  92.8 1.6 collective-permute-done.8.refs_2_
  94.5 1.9 copy-done.23
  96.3 1.2 copy-done.1
  97.6 1.2 copy-done.10
  98.8 1.2 copy-done.12
  100.0 23.0 %shard_map.101 = (bf16[128,4096]{1,0:T(8,128)(2,1)S(1)}, bf16[128,4096]{1,0:T(8,128)(2,1)S(1)}, bf16[128,4096]{1,0:T(8,128)(2,1)S(1)}, bf16[128,4096]{1,0:T(8,12...) custom-call(bf16[128,4096]{1,0:T(8,128)(2,1)S(1)} %copy-done.1, ...), custom_call_target="tpu_custom_call" | custom-call | flops 11274289152 | bytes 62914560 | tf_op jit(solution)/shard_map/pallas_call | solution.py:178
  123.0 1.0 copy-done.2
  124.1 1.0 copy-done.4
  125.0 1.0 copy-done.6
  126.0 1.0 copy-done.8
  127.0 1.0 copy-done.13
  127.9 1.0 copy-done.14
  129.3 6.2 %collective-permute-done.16 = bf16[8,896,256]{2,1,0:T(8,128)(2,1)S(1)} collective-permute-done((bf16[8,896,256]{2,1,0:T(8,128)(2,1)}, bf16[8,896,256]{2,1,0:T(8,128)(2,1)S(1)}, u32[]{:S(2)}, u32[]{:S(2)}) %collective-permute-start.16) | collective-permute-done | bytes 3670048 | tf_op jit(solution)/shard_map/ppermute | solution.py:34
  135.5 4.7 %add_convert_fusion = bf16[8,896,256]{2,1,0:T(8,128)(2,1)} fusion(bf16[8,896,256]{2,1,0:T(8,128)(2,1)S(1)} %collective-permute-done.16, bf16[8,896,256]{2,1,0:T(8,128)(2,1)} %get-tuple-element.51), kind=kLoop, calls=%fused_computation | loop fusion | flops 7340032 | bytes 11010048 | tf_op jit(solution)/shard_map/convert_element_type | solution.py:236
  140.3 1.4 collective-permute-start.12
  141.9 2.7 %collective-permute-start.14 = (bf16[128,4096]{1,0:T(8,128)(2,1)}, bf16[128,4096]{1,0:T(8,128)(2,1)S(1)}, u32[]{:S(2)}, u32[]{:S(2)}) collective-permute-start(bf16[128,4096]{1,0:T(8,128)(2,1)} %copy-done.8), channel_id=1, source_target_pairs={{0,12},{1,19},{4,0},{5,23},{8,4},{9,27},{12,8},{13,31},{16,28},{17... | collective-permute-start | bytes 3145736 | tf_op jit(solution)/shard_map/ppermute | solution.py:29
  144.5 10.1 %collective-permute-done.12 = bf16[128,4096]{1,0:T(8,128)(2,1)S(1)} collective-permute-done((bf16[128,4096]{1,0:T(8,128)(2,1)}, bf16[128,4096]{1,0:T(8,128)(2,1)S(1)}, u32[]{:S(2)}, u32[]{:S(2)}) %collective-permute-start.12) | collective-permute-done | bytes 1048608 | tf_op jit(solution)/shard_map/ppermute | solution.py:29
  154.9 2.3 collective-permute-done.13
  157.5 8.4 %collective-permute-done.14 = bf16[128,4096]{1,0:T(8,128)(2,1)S(1)} collective-permute-done((bf16[128,4096]{1,0:T(8,128)(2,1)}, bf16[128,4096]{1,0:T(8,128)(2,1)S(1)}, u32[]{:S(2)}, u32[]{:S(2)}) %collective-permute-start.14) | collective-permute-done | bytes 1048608 | tf_op jit(solution)/shard_map/ppermute | solution.py:29
  165.9 2.6 %collective-permute-done.15 = bf16[128,4096]{1,0:T(8,128)(2,1)S(1)} collective-permute-done((bf16[128,4096]{1,0:T(8,128)(2,1)S(1)}, bf16[128,4096]{1,0:T(8,128)(2,1)S(1)}, u32[]{:S(2)}, u32[]{:S(2)}) %collective-permute-start.15) | collective-permute-done | bytes 1048608 | tf_op jit(solution)/shard_map/ppermute | solution.py:29
  168.4 1.5 collective-permute-start.18
  169.9 1.5 collective-permute-start.19
  171.5 2.0 collective-permute-done.19
  173.5 2.8 %collective-permute-start.20 = (f32[4096]{0:T(1024)S(1)}, f32[4096]{0:T(1024)S(1)}, u32[]{:S(2)}, u32[]{:S(2)}) collective-permute-start(f32[4096]{0:T(1024)S(1)} %add.92), channel_id=1, source_target_pairs={{0,64},{1,65},{4,68},{5,69},{8,72},{9,73},{12,76},{13,77},{16,80},... | collective-permute-start | bytes 49160 | tf_op jit(solution)/shard_map/ppermute | solution.py:222
  176.3 1.8 collective-permute-done.20
  178.2 6.7 %collective-permute-start.21 = (f32[4096]{0:T(1024)S(1)}, f32[4096]{0:T(1024)S(1)}, u32[]{:S(2)}, u32[]{:S(2)}) collective-permute-start(f32[4096]{0:T(1024)S(1)} %add.93), channel_id=1, source_target_pairs={{0,128},{1,129},{4,132},{5,133},{8,136},{9,137},{12,140},{13,141},... | collective-permute-start | bytes 49160 | tf_op jit(solution)/shard_map/ppermute | solution.py:222
  184.8 1.5 collective-permute-done.21
  188.4 2.6 %collective-permute-start.22 = (bf16[2,32,4096]{2,1,0:T(8,128)(2,1)S(1)}, bf16[2,32,4096]{2,1,0:T(8,128)(2,1)S(1)}, u32[]{:S(2)}, u32[]{:S(2)}) collective-permute-start(bf16[2,32,4096]{2,1,0:T(8,128)(2,1)S(1)} %get-tuple-element.70), channel_id=1, source_target_pairs={{0,18},{1,13},{4,22},{5,1},{8,26},{9,5},{12,30},{13,9},{16,0},{17,... | collective-permute-start | bytes 1572872 | tf_op jit(solution)/shard_map/ppermute | solution.py:29
  191.0 4.5 %collective-permute-start.25 = (f32[4096]{0:T(1024)S(1)}, f32[4096]{0:T(1024)S(1)}, u32[]{:S(2)}, u32[]{:S(2)}) collective-permute-start(f32[4096]{0:T(1024)S(1)} %add.94), channel_id=1, source_target_pairs={{0,1},{1,0},{4,5},{5,4},{8,9},{9,8},{12,13},{13,12},{16,17},{17,16... | collective-permute-start | bytes 49160 | tf_op jit(solution)/shard_map/ppermute | solution.py:222
  195.4 0.8 collective-permute-done.25
  196.9 2.5 %collective-permute-done.26 = f32[4096]{0:T(1024)S(1)} collective-permute-done((f32[4096]{0:T(1024)S(1)}, f32[4096]{0:T(1024)S(1)}, u32[]{:S(2)}, u32[]{:S(2)}) %collective-permute-start.26) | collective-permute-done | bytes 16416 | tf_op jit(solution)/shard_map/ppermute | solution.py:222
  199.4 3.4 %collective-permute-start.27 = (f32[4096]{0:T(1024)S(1)}, f32[4096]{0:T(1024)S(1)}, u32[]{:S(2)}, u32[]{:S(2)}) collective-permute-start(f32[4096]{0:T(1024)S(1)} %add.100), channel_id=1, source_target_pairs={{0,2},{1,3},{4,6},{5,7},{8,10},{9,11},{12,14},{13,15},{16,18},{17,... | collective-permute-start | bytes 49160 | tf_op jit(solution)/shard_map/ppermute | solution.py:222
  202.7 1.8 collective-permute-done.27
  204.7 1.4 convert_add_fusion
  206.4 12.6 %collective-permute-start.28 = (bf16[1,4096]{1,0:T(2,128)(2,1)S(1)}, bf16[1,4096]{1,0:T(2,128)(2,1)S(1)}, u32[]{:S(2)}, u32[]{:S(2)}) collective-permute-start(bf16[1,4096]{1,0:T(2,128)(2,1)S(1)} %slice.78), channel_id=1, source_target_pairs={{0,1},{1,2},{2,3},{3,4},{4,5},{5,6},{6,7},{7,8},{8,9},{9,10},{10,1... | collective-permute-start | bytes 24584 | tf_op jit(solution)/shard_map/ppermute | solution.py:47
  219.0 1.9 collective-permute-start.31
  221.0 1.5 fusion.1
  222.5 2.4 %collective-permute-start.30 = (f32[4096]{0:T(1024)S(1)}, f32[4096]{0:T(1024)S(1)}, u32[]{:S(2)}, u32[]{:S(2)}) collective-permute-start(f32[4096]{0:T(1024)S(1)} %add.111), channel_id=1, source_target_pairs={{0,8},{1,9},{4,12},{5,13},{8,0},{9,1},{12,4},{13,5},{16,24},{17,25... | collective-permute-start | bytes 49160 | tf_op jit(solution)/shard_map/ppermute | solution.py:222
  224.9 1.4 fusion
  227.3 1.6 collective-permute-done.31
  (105 shorter events, 12.3 us)
Async XLA Ops:
  7.2 14.6 %copy-start.15 = (bf16[128,4096]{1,0:T(8,128)(2,1)S(1)}, bf16[128,4096]{1,0:T(8,128)(2,1)}, u32[]{:S(2)}) copy-start(bf16[128,4096]{1,0:T(8,128)(2,1)} %param.11) | copy-start | bytes 3145732
  7.2 16.8 %copy-start.17 = (bf16[128,4096]{1,0:T(8,128)(2,1)S(1)}, bf16[128,4096]{1,0:T(8,128)(2,1)}, u32[]{:S(2)}) copy-start(bf16[128,4096]{1,0:T(8,128)(2,1)} %param.6) | copy-start | bytes 3145732
  7.2 70.3 %all-gather.3.cloned.1.call-start = ((), (), s32[]{:S(2)}) async-start(), calls=%async_computation.2 | async-start | bytes 4128768 | tf_op jit(solution)/shard_map/all_gather | solution.py:269
  10.1 10.8 %collective-permute-start.10 = (bf16[896,256]{1,0:T(8,128)(2,1)S(1)}, bf16[896,256]{1,0:T(8,128)(2,1)S(1)}, u32[]{:S(2)}, u32[]{:S(2)}) collective-permute-start(bf16[896,256]{1,0:T(8,128)(2,1)S(1)} %pad_maximum_fusion.3), channel_id=1, source_target_pairs={{0,0},{1,16},{4,4},{5,20},{8,8},{9,24},{12,12},{13,28},{16,1},{17,... | collective-permute-start | bytes 1376264 | tf_op jit(solution)/shard_map/ppermute | solution.py:41
  20.8 0.8 copy-start.21
  21.6 182.9 %reduce-scatter.2.cloned.1.call-start = ((), (), s32[]{:S(2)}) async-start(), calls=%async_computation.1 | async-start | bytes 4128768 | tf_op jit(solution)/shard_map/reduce_scatter | solution.py:246
  22.0 6.6 %collective-permute-start = (bf16[1,4096]{1,0:T(2,128)(2,1)S(1)}, bf16[1,4096]{1,0:T(2,128)(2,1)S(1)}, u32[]{:S(2)}, u32[]{:S(2)}) collective-permute-start(bf16[1,4096]{1,0:T(2,128)(2,1)S(1)} %slice.65), channel_id=1, source_target_pairs={{1,0},{2,1},{3,2},{4,3},{5,4},{6,5},{7,6},{8,7},{9,8},{10,9},{11,1... | collective-permute-start | bytes 24584 | tf_op jit(solution)/shard_map/ppermute | solution.py:47
  24.3 23.2 %copy-start.19 = (bf16[31,4096]{1,0:T(8,128)(2,1)}, bf16[31,4096]{1,0:T(8,128)(2,1)S(1)}, u32[]{:S(2)}) copy-start(bf16[31,4096]{1,0:T(8,128)(2,1)S(1)} %slice.64) | copy-start | bytes 761860
  28.7 14.3 %collective-permute-start.3 = (bf16[2,32,4096]{2,1,0:T(8,128)(2,1)S(1)}, bf16[2,32,4096]{2,1,0:T(8,128)(2,1)S(1)}, u32[]{:S(2)}, u32[]{:S(2)}) collective-permute-start(bf16[2,32,4096]{2,1,0:T(8,128)(2,1)S(1)} %pad_maximum_fusion.2), channel_id=1, source_target_pairs={{0,18},{1,13},{4,22},{5,1},{8,26},{9,5},{12,30},{13,9},{16,0},{17,... | collective-permute-start | bytes 1572872 | tf_op jit(solution)/shard_map/ppermute | solution.py:29
  31.2 11.8 %collective-permute-start.2 = (bf16[2,32,4096]{2,1,0:T(8,128)(2,1)S(1)}, bf16[2,32,4096]{2,1,0:T(8,128)(2,1)S(1)}, u32[]{:S(2)}, u32[]{:S(2)}) collective-permute-start(bf16[2,32,4096]{2,1,0:T(8,128)(2,1)S(1)} %pad_maximum_fusion.2), channel_id=1, source_target_pairs={{0,2},{1,9},{4,6},{5,13},{8,10},{9,1},{12,14},{13,5},{16,18},{17,2... | collective-permute-start | bytes 1572872 | tf_op jit(solution)/shard_map/ppermute | solution.py:29
  31.8 15.0 %collective-permute-start.1 = (bf16[2,32,4096]{2,1,0:T(8,128)(2,1)S(1)}, bf16[2,32,4096]{2,1,0:T(8,128)(2,1)S(1)}, u32[]{:S(2)}, u32[]{:S(2)}) collective-permute-start(bf16[2,32,4096]{2,1,0:T(8,128)(2,1)S(1)} %pad_maximum_fusion.2), channel_id=1, source_target_pairs={{0,16},{1,5},{4,20},{5,9},{8,24},{9,13},{12,28},{13,1},{16,2},{17,... | collective-permute-start | bytes 1572872 | tf_op jit(solution)/shard_map/ppermute | solution.py:29
  49.0 14.1 %collective-permute-start.7 = (bf16[128,4096]{1,0:T(8,128)(2,1)S(1)}, bf16[128,4096]{1,0:T(8,128)(2,1)S(1)}, u32[]{:S(2)}, u32[]{:S(2)}) collective-permute-start(bf16[128,4096]{1,0:T(8,128)(2,1)S(1)} %pad_maximum_fusion.refs_0_), channel_id=1, source_target_pairs={{0,12},{1,19},{4,0},{5,23},{8,4},{9,27},{12,8},{13,31},{16,28},{17... | collective-permute-start | bytes 3145736 | tf_op jit(solution)/shard_map/ppermute | solution.py:29
  49.1 16.3 %collective-permute-start.4 = (bf16[128,4096]{1,0:T(8,128)(2,1)S(1)}, bf16[128,4096]{1,0:T(8,128)(2,1)S(1)}, u32[]{:S(2)}, u32[]{:S(2)}) collective-permute-start(bf16[128,4096]{1,0:T(8,128)(2,1)S(1)} %pad_maximum_fusion.refs_0_), channel_id=1, source_target_pairs={{0,4},{1,17},{4,8},{5,21},{8,12},{9,25},{12,0},{13,29},{16,20},{17... | collective-permute-start | bytes 3145736 | tf_op jit(solution)/shard_map/ppermute | solution.py:29
  50.5 1.0 copy-start
  51.5 25.0 %collective-permute-start.6 = (bf16[128,4096]{1,0:T(8,128)(2,1)S(1)}, bf16[128,4096]{1,0:T(8,128)(2,1)S(1)}, u32[]{:S(2)}, u32[]{:S(2)}) collective-permute-start(bf16[128,4096]{1,0:T(8,128)(2,1)S(1)} %concatenate.18.refs_4_), channel_id=1, source_target_pairs={{0,4},{1,17},{4,8},{5,21},{8,12},{9,25},{12,0},{13,29},{16,20},{17... | collective-permute-start | bytes 3145736 | tf_op jit(solution)/shard_map/ppermute | solution.py:29
  53.2 24.2 %collective-permute-start.5 = (bf16[128,4096]{1,0:T(8,128)(2,1)S(1)}, bf16[128,4096]{1,0:T(8,128)(2,1)}, u32[]{:S(2)}, u32[]{:S(2)}) collective-permute-start(bf16[128,4096]{1,0:T(8,128)(2,1)S(1)} %concatenate.18.refs_4_), channel_id=1, source_target_pairs={{0,12},{1,19},{4,0},{5,23},{8,4},{9,27},{12,8},{13,31},{16,28},{17... | collective-permute-start | bytes 3145736 | tf_op jit(solution)/shard_map/ppermute | solution.py:29
  63.1 1.0 copy-start.9
  76.5 1.0 copy-start.24
  77.5 17.0 %collective-permute-start.11 = (bf16[8,896,256]{2,1,0:T(8,128)(2,1)}, bf16[8,896,256]{2,1,0:T(8,128)(2,1)S(1)}, u32[]{:S(2)}, u32[]{:S(2)}) collective-permute-start(bf16[8,896,256]{2,1,0:T(8,128)(2,1)} %bitcast.43), channel_id=1, source_target_pairs={{0,1},{1,0},{4,5},{5,4},{8,9},{9,8},{12,13},{13,12},{16,17},{17,16... | collective-permute-start | bytes 11010056 | tf_op jit(solution)/shard_map/ppermute | solution.py:34
  78.7 14.2 %collective-permute-start.9 = (bf16[128,4096]{1,0:T(8,128)(2,1)}, bf16[128,4096]{1,0:T(8,128)(2,1)S(1)}, u32[]{:S(2)}, u32[]{:S(2)}) collective-permute-start(bf16[128,4096]{1,0:T(8,128)(2,1)} %collective-permute-done.5.refs_7_), channel_id=1, source_target_pairs={{0,12},{1,19},{4,0},{5,23},{8,4},{9,27},{12,8},{13,31},{16,28},{17... | collective-permute-start | bytes 3145736 | tf_op jit(solution)/shard_map/ppermute | solution.py:29
  79.5 15.0 %collective-permute-start.8 = (bf16[128,4096]{1,0:T(8,128)(2,1)S(1)}, bf16[128,4096]{1,0:T(8,128)(2,1)S(1)}, u32[]{:S(2)}, u32[]{:S(2)}) collective-permute-start(bf16[128,4096]{1,0:T(8,128)(2,1)S(1)} %collective-permute-done.4.refs_1_), channel_id=1, source_target_pairs={{0,4},{1,17},{4,8},{5,21},{8,12},{9,25},{12,0},{13,29},{16,20},{17... | collective-permute-start | bytes 3145736 | tf_op jit(solution)/shard_map/ppermute | solution.py:29
  80.1 1.0 copy-start.11
  92.8 1.6 copy-start.25
  94.5 1.9 copy-start.23
  96.3 1.2 copy-start.1
  97.6 1.2 copy-start.10
  98.8 1.2 copy-start.12
  123.0 1.1 copy-start.2
  124.1 1.0 copy-start.4
  125.0 1.0 copy-start.6
  126.0 1.0 copy-start.8
  127.0 1.0 copy-start.13
  127.9 1.0 copy-start.14
  128.9 6.6 %collective-permute-start.16 = (bf16[8,896,256]{2,1,0:T(8,128)(2,1)}, bf16[8,896,256]{2,1,0:T(8,128)(2,1)S(1)}, u32[]{:S(2)}, u32[]{:S(2)}) collective-permute-start(bf16[8,896,256]{2,1,0:T(8,128)(2,1)} %get-tuple-element.52), channel_id=1, source_target_pairs={{0,1},{1,0},{4,5},{5,4},{8,9},{9,8},{12,13},{13,12},{16,17},{17,16... | collective-permute-start | bytes 11010056 | tf_op jit(solution)/shard_map/ppermute | solution.py:34
  140.3 1.6 copy-start.22
  140.3 4.2 %copy-start.7 = (bf16[128,4096]{1,0:T(8,128)(2,1)S(1)}, bf16[128,4096]{1,0:T(8,128)(2,1)}, u32[]{:S(2)}) copy-start(bf16[128,4096]{1,0:T(8,128)(2,1)} %copy-done.6) | copy-start | bytes 3145732
  140.3 14.3 %collective-permute-start.12 = (bf16[128,4096]{1,0:T(8,128)(2,1)}, bf16[128,4096]{1,0:T(8,128)(2,1)S(1)}, u32[]{:S(2)}, u32[]{:S(2)}) collective-permute-start(bf16[128,4096]{1,0:T(8,128)(2,1)} %copy-done.14), channel_id=1, source_target_pairs={{0,12},{1,19},{4,0},{5,23},{8,4},{9,27},{12,8},{13,31},{16,28},{17... | collective-permute-start | bytes 3145736 | tf_op jit(solution)/shard_map/ppermute | solution.py:29
  141.7 15.5 %collective-permute-start.13 = (bf16[128,4096]{1,0:T(8,128)(2,1)}, bf16[128,4096]{1,0:T(8,128)(2,1)S(1)}, u32[]{:S(2)}, u32[]{:S(2)}) collective-permute-start(bf16[128,4096]{1,0:T(8,128)(2,1)} %copy-done.13), channel_id=1, source_target_pairs={{0,4},{1,17},{4,8},{5,21},{8,12},{9,25},{12,0},{13,29},{16,20},{17... | collective-permute-start | bytes 3145736 | tf_op jit(solution)/shard_map/ppermute | solution.py:29
  141.9 24.0 %collective-permute-start.14 = (bf16[128,4096]{1,0:T(8,128)(2,1)}, bf16[128,4096]{1,0:T(8,128)(2,1)S(1)}, u32[]{:S(2)}, u32[]{:S(2)}) collective-permute-start(bf16[128,4096]{1,0:T(8,128)(2,1)} %copy-done.8), channel_id=1, source_target_pairs={{0,12},{1,19},{4,0},{5,23},{8,4},{9,27},{12,8},{13,31},{16,28},{17... | collective-permute-start | bytes 3145736 | tf_op jit(solution)/shard_map/ppermute | solution.py:29
  144.5 23.9 %collective-permute-start.15 = (bf16[128,4096]{1,0:T(8,128)(2,1)S(1)}, bf16[128,4096]{1,0:T(8,128)(2,1)S(1)}, u32[]{:S(2)}, u32[]{:S(2)}) collective-permute-start(bf16[128,4096]{1,0:T(8,128)(2,1)S(1)} %copy-done.7), channel_id=1, source_target_pairs={{0,4},{1,17},{4,8},{5,21},{8,12},{9,25},{12,0},{13,29},{16,20},{17... | collective-permute-start | bytes 3145736 | tf_op jit(solution)/shard_map/ppermute | solution.py:29
  154.9 31.5 %copy-start.5 = (bf16[128,4096]{1,0:T(8,128)(2,1)S(1)}, bf16[128,4096]{1,0:T(8,128)(2,1)}, u32[]{:S(2)}) copy-start(bf16[128,4096]{1,0:T(8,128)(2,1)} %copy-done.4) | copy-start | bytes 3145732
  168.4 17.9 %collective-permute-start.17 = (bf16[128,4096]{1,0:T(8,128)(2,1)S(1)}, bf16[128,4096]{1,0:T(8,128)(2,1)S(1)}, u32[]{:S(2)}, u32[]{:S(2)}) collective-permute-start(bf16[128,4096]{1,0:T(8,128)(2,1)S(1)} %add_convert_fusion.4), channel_id=1, source_target_pairs={{0,12},{1,19},{4,0},{5,23},{8,4},{9,27},{12,8},{13,31},{16,28},{17... | collective-permute-start | bytes 3145736 | tf_op jit(solution)/shard_map/ppermute | solution.py:29
  168.4 17.9 %collective-permute-start.18 = (bf16[128,4096]{1,0:T(8,128)(2,1)S(1)}, bf16[128,4096]{1,0:T(8,128)(2,1)S(1)}, u32[]{:S(2)}, u32[]{:S(2)}) collective-permute-start(bf16[128,4096]{1,0:T(8,128)(2,1)S(1)} %add_convert_fusion.3), channel_id=1, source_target_pairs={{0,4},{1,17},{4,8},{5,21},{8,12},{9,25},{12,0},{13,29},{16,20},{17... | collective-permute-start | bytes 3145736 | tf_op jit(solution)/shard_map/ppermute | solution.py:29
  169.9 3.6 %collective-permute-start.19 = (f32[4096]{0:T(1024)S(1)}, f32[4096]{0:T(1024)S(1)}, u32[]{:S(2)}, u32[]{:S(2)}) collective-permute-start(f32[4096]{0:T(1024)S(1)} %div.35), channel_id=1, source_target_pairs={{0,32},{1,33},{4,36},{5,37},{8,40},{9,41},{12,44},{13,45},{16,48},... | collective-permute-start | bytes 49160 | tf_op jit(solution)/shard_map/ppermute | solution.py:222
  173.5 4.7 %collective-permute-start.20 = (f32[4096]{0:T(1024)S(1)}, f32[4096]{0:T(1024)S(1)}, u32[]{:S(2)}, u32[]{:S(2)}) collective-permute-start(f32[4096]{0:T(1024)S(1)} %add.92), channel_id=1, source_target_pairs={{0,64},{1,65},{4,68},{5,69},{8,72},{9,73},{12,76},{13,77},{16,80},... | collective-permute-start | bytes 49160 | tf_op jit(solution)/shard_map/ppermute | solution.py:222
  178.2 8.2 %collective-permute-start.21 = (f32[4096]{0:T(1024)S(1)}, f32[4096]{0:T(1024)S(1)}, u32[]{:S(2)}, u32[]{:S(2)}) collective-permute-start(f32[4096]{0:T(1024)S(1)} %add.93), channel_id=1, source_target_pairs={{0,128},{1,129},{4,132},{5,133},{8,136},{9,137},{12,140},{13,141},... | collective-permute-start | bytes 49160 | tf_op jit(solution)/shard_map/ppermute | solution.py:222
  186.4 1.2 copy-start.3
  188.2 16.3 %collective-permute-start.24 = (bf16[2,32,4096]{2,1,0:T(8,128)(2,1)S(1)}, bf16[2,32,4096]{2,1,0:T(8,128)(2,1)S(1)}, u32[]{:S(2)}, u32[]{:S(2)}) collective-permute-start(bf16[2,32,4096]{2,1,0:T(8,128)(2,1)S(1)} %get-tuple-element.69), channel_id=1, source_target_pairs={{0,16},{1,5},{4,20},{5,9},{8,24},{9,13},{12,28},{13,1},{16,2},{17,... | collective-permute-start | bytes 1572872 | tf_op jit(solution)/shard_map/ppermute | solution.py:29
  188.4 16.1 %collective-permute-start.22 = (bf16[2,32,4096]{2,1,0:T(8,128)(2,1)S(1)}, bf16[2,32,4096]{2,1,0:T(8,128)(2,1)S(1)}, u32[]{:S(2)}, u32[]{:S(2)}) collective-permute-start(bf16[2,32,4096]{2,1,0:T(8,128)(2,1)S(1)} %get-tuple-element.70), channel_id=1, source_target_pairs={{0,18},{1,13},{4,22},{5,1},{8,26},{9,5},{12,30},{13,9},{16,0},{17,... | collective-permute-start | bytes 1572872 | tf_op jit(solution)/shard_map/ppermute | solution.py:29
  191.0 13.6 %collective-permute-start.23 = (bf16[2,32,4096]{2,1,0:T(8,128)(2,1)S(1)}, bf16[2,32,4096]{2,1,0:T(8,128)(2,1)}, u32[]{:S(2)}, u32[]{:S(2)}) collective-permute-start(bf16[2,32,4096]{2,1,0:T(8,128)(2,1)S(1)} %get-tuple-element.71), channel_id=1, source_target_pairs={{0,2},{1,9},{4,6},{5,13},{8,10},{9,1},{12,14},{13,5},{16,18},{17,2... | collective-permute-start | bytes 1572872 | tf_op jit(solution)/shard_map/ppermute | solution.py:29
  191.0 5.3 %collective-permute-start.25 = (f32[4096]{0:T(1024)S(1)}, f32[4096]{0:T(1024)S(1)}, u32[]{:S(2)}, u32[]{:S(2)}) collective-permute-start(f32[4096]{0:T(1024)S(1)} %add.94), channel_id=1, source_target_pairs={{0,1},{1,0},{4,5},{5,4},{8,9},{9,8},{12,13},{13,12},{16,17},{17,16... | collective-permute-start | bytes 49160 | tf_op jit(solution)/shard_map/ppermute | solution.py:222
  196.3 3.1 %collective-permute-start.26 = (f32[4096]{0:T(1024)S(1)}, f32[4096]{0:T(1024)S(1)}, u32[]{:S(2)}, u32[]{:S(2)}) collective-permute-start(f32[4096]{0:T(1024)S(1)} %add.99), channel_id=1, source_target_pairs={{0,16},{1,17},{4,20},{5,21},{8,24},{9,25},{12,28},{13,29},{16,0},{... | collective-permute-start | bytes 49160 | tf_op jit(solution)/shard_map/ppermute | solution.py:222
  199.4 5.1 %collective-permute-start.27 = (f32[4096]{0:T(1024)S(1)}, f32[4096]{0:T(1024)S(1)}, u32[]{:S(2)}, u32[]{:S(2)}) collective-permute-start(f32[4096]{0:T(1024)S(1)} %add.100), channel_id=1, source_target_pairs={{0,2},{1,3},{4,6},{5,7},{8,10},{9,11},{12,14},{13,15},{16,18},{17,... | collective-permute-start | bytes 49160 | tf_op jit(solution)/shard_map/ppermute | solution.py:222
  204.6 14.5 %copy-start.26 = (bf16[1,896,256]{2,1,0:T(8,128)(2,1)S(1)}, bf16[1,896,256]{2,1,0:T(8,128)(2,1)}, u32[]{:S(2)}) copy-start(bf16[1,896,256]{2,1,0:T(8,128)(2,1)} %reduce-scatter.2.cloned.1.call-done) | copy-start | bytes 1376260
  204.6 16.4 %copy-start.16 = (bf16[128,4096]{1,0:T(8,128)(2,1)S(1)}, bf16[128,4096]{1,0:T(8,128)(2,1)}, u32[]{:S(2)}) copy-start(bf16[128,4096]{1,0:T(8,128)(2,1)} %param.11) | copy-start | bytes 3145732
  204.6 16.4 %copy-start.20 = (bf16[31,4096]{1,0:T(8,128)(2,1)S(1)}, bf16[31,4096]{1,0:T(8,128)(2,1)}, u32[]{:S(2)}) copy-start(bf16[31,4096]{1,0:T(8,128)(2,1)} %copy-done.19) | copy-start | bytes 761860
  204.6 17.9 %collective-permute-start.29 = (f32[4096]{0:T(1024)S(1)}, f32[4096]{0:T(1024)S(1)}, u32[]{:S(2)}, u32[]{:S(2)}) collective-permute-start(f32[4096]{0:T(1024)S(1)} %add.101), channel_id=1, source_target_pairs={{0,4},{1,5},{4,0},{5,1},{8,12},{9,13},{12,8},{13,9},{16,20},{17,21... | collective-permute-start | bytes 49160 | tf_op jit(solution)/shard_map/ppermute | solution.py:222
  206.1 18.8 %copy-start.18 = (bf16[128,4096]{1,0:T(8,128)(2,1)S(1)}, bf16[128,4096]{1,0:T(8,128)(2,1)}, u32[]{:S(2)}) copy-start(bf16[128,4096]{1,0:T(8,128)(2,1)} %param.6) | copy-start | bytes 3145732
  206.4 18.5 %collective-permute-start.28 = (bf16[1,4096]{1,0:T(2,128)(2,1)S(1)}, bf16[1,4096]{1,0:T(2,128)(2,1)S(1)}, u32[]{:S(2)}, u32[]{:S(2)}) collective-permute-start(bf16[1,4096]{1,0:T(2,128)(2,1)S(1)} %slice.78), channel_id=1, source_target_pairs={{0,1},{1,2},{2,3},{3,4},{4,5},{5,6},{6,7},{7,8},{8,9},{9,10},{10,1... | collective-permute-start | bytes 24584 | tf_op jit(solution)/shard_map/ppermute | solution.py:47
  219.0 9.8 %collective-permute-start.31 = (bf16[896,256]{1,0:T(8,128)(2,1)S(1)}, bf16[896,256]{1,0:T(8,128)(2,1)S(1)}, u32[]{:S(2)}, u32[]{:S(2)}) collective-permute-start(bf16[896,256]{1,0:T(8,128)(2,1)S(1)} %bitcast.45), channel_id=1, source_target_pairs={{0,0},{1,16},{4,4},{5,20},{8,8},{9,24},{12,12},{13,28},{16,1},{17,... | collective-permute-start | bytes 1376264 | tf_op jit(solution)/shard_map/ppermute | solution.py:41
  222.5 4.2 %collective-permute-start.30 = (f32[4096]{0:T(1024)S(1)}, f32[4096]{0:T(1024)S(1)}, u32[]{:S(2)}, u32[]{:S(2)}) collective-permute-start(f32[4096]{0:T(1024)S(1)} %add.111), channel_id=1, source_target_pairs={{0,8},{1,9},{4,12},{5,13},{8,0},{9,1},{12,4},{13,5},{16,24},{17,25... | collective-permute-start | bytes 49160 | tf_op jit(solution)/shard_map/ppermute | solution.py:222
Sparse Core Ops, SparseCore 0:
  21.8 52.5 all-gather.2
  140.4 49.5 reduce-scatter.1

commit v7 on v3

--- a/solution.py
+++ b/solution.py
@@ -207,35 +207,43 @@
     return [p0, p1, p2, p3, g0, g1, g2, g3]
 
 
-def scatter_plane(outs, gain_part, weight_part):
-    d0, d1, d2, d3, n0, n1, n2, n3 = outs
-    bf = jnp.bfloat16
-    d2, n2 = shift(d2, second=-1), shift(n2, second=1)
-    n1, d3 = shift(n1, second=-1), shift(d3, second=1)
-    d1, n3 = add_all([d1, d2]).astype(bf), add_all([n3, n2]).astype(bf)
-    d1, n3, weight_part = lax.optimization_barrier((d1, n3, weight_part))
-    weight_sum = lax.psum_scatter(weight_part, "z", scatter_dimension=0, tiled=False)
-    d1, n3 = shift(d1, second=-1), shift(n3, second=1)
-    arrived = (d1, d3, n1, n3, total_over_all(gain_part))
-    d1, d3, n1, n3, grad_gain = lax.optimization_barrier(arrived)
-    both = jnp.stack([add_all([d0, d1, d3]).astype(bf), add_all([n0, n1, n3]).astype(bf)])
-    rows = both.shape[1] // 4
-    both = [both[:, d * rows : (d + 1) * rows] for d in range(4)]
-    arrived = [shift(both[d], first=-d) for d in (1, 2, 3)] + [weight_sum]
-    *arrived, weight_sum = lax.optimization_barrier(arrived)
-    return add_all([both[0], *arrived]), grad_gain, weight_sum
-
-
-def total_over_all(value):
-    moves = [lambda p, k=k: (p[0] ^ k, p[1], p[2], p[3]) for k in (1, 2, 4)]
-    moves += [lambda p: (p[0], p[1], p[2], 1 - p[3])]
-    moves += [lambda p, k=k: (p[0], p[1] ^ k, p[2], p[3]) for k in (1, 2)]
-    moves += [lambda p, k=k: (p[0], p[1], p[2] ^ k, p[3]) for k in (1, 2)]
+def swapped(value, moves):
     for move in moves:
         value = value + lax.ppermute(
             value, AXES, [(linear(*p), linear(*move(p))) for p in places()]
         )
     return value
+
+
+def all_moves():
+    moves = [lambda p, k=k: (p[0], p[1] ^ k, p[2], p[3]) for k in (1, 2)]
+    moves += [lambda p, k=k: (p[0], p[1], p[2] ^ k, p[3]) for k in (1, 2)]
+    moves += [lambda p, k=k: (p[0] ^ k, p[1], p[2], p[3]) for k in (1, 2, 4)]
+    return moves + [lambda p: (p[0], p[1], p[2], 1 - p[3])]
+
+
+def rounded_sum(*parts):
+    return add_all(parts).astype(jnp.bfloat16)
+
+
+def scatter_plane(outs, g_own, g_oth, gain):
+    d0, d1, d2, d3, n0, n1, n2, n3 = outs
+    tie = lax.optimization_barrier
+    moves = all_moves()
+    d2, n2 = shift(d2, second=-1), shift(n2, second=1)
+    n1, d3 = shift(n1, second=-1), shift(d3, second=1)
+    d2, n2, g_oth = tie((d2, n2, other_core(g_oth)))
+    mine = rounded_sum(g_own, g_oth)
+    weight_sum = lax.psum_scatter(mine, "z", scatter_dimension=0, tiled=False)
+    d1, n3 = rounded_sum(d1, d2), rounded_sum(n3, n2)
+    d1, n3, n1, d3, gain, _ = tie((d1, n3, n1, d3, gain, mine))
+    d1, n3, gain = tie((shift(d1, second=-1), shift(n3, second=1), swapped(gain, moves[:2])))
+    both = jnp.stack([rounded_sum(d0, d1, d3), rounded_sum(n0, n1, n3)])
+    rows = both.shape[1] // 4
+    both = [both[:, d * rows : (d + 1) * rows] for d in range(4)]
+    arrived = [shift(both[d], first=-d) for d in (1, 2, 3)]
+    *arrived, gain, weight_sum = tie((*arrived, swapped(gain, moves[2:4]), weight_sum))
+    return add_all([both[0], *arrived]), swapped(gain, moves[4:]), weight_sum
 
 
 def shards(stream, doc_start, norm_gain, weight_in, weight_out, upstream):
@@ -268,9 +276,9 @@
     w_oth = other_core(w_own)
     results = block(blocks, w_own, w_oth)
     outs, (g_own, g_oth, gain_part) = results[:8], results[8:]
-
-    mine = (g_own.astype(jnp.float32) + other_core(g_oth).astype(jnp.float32)).astype(bf)
-    (down_sum, scaled), grad_gain, grads = scatter_plane(outs, gain_part[0] / norm_gain, mine)
+    (down_sum, scaled), grad_gain, grads = scatter_plane(
+        outs, g_own, g_oth, gain_part[0] / norm_gain
+    )
     grads = swap_low(grads)
     grad_weight_in = (grads[:hidden].astype(jnp.float32) * gain[None, :]).T
     grad_weight_out = grads[hidden:].astype(jnp.float32)

time: 222 us -> 226 us (1.018)
  starting transfers between devices: 49.8 us -> 41.6 us
  waiting for transfers between devices: 113 us -> 121 us
  local copies, waits for them, and re-layouts: 7.22 us -> 9.89 us
    ppermute x8, waiting for transfers between devices: 20.6 us -> 31.7 us  [swapped(): lax.ppermute(value, AXES, [(linear(*p), linear(*move(p))) for p in places...]
    ppermute x2, waiting for transfers between devices: 9.43 us -> 5.09 us  [swap_low(): return lax.ppermute(value, AXES, pairs)]
    ppermute x2, starting transfers between devices: 8.05 us -> 3.84 us  [from_behind(): return lax.ppermute(value, AXES, pairs)]
    ppermute x8, starting transfers between devices: 13.2 us -> 9.51 us  [swapped(): lax.ppermute(value, AXES, [(linear(*p), linear(*move(p))) for p in places...]
    unnamed x42 -> x48, local copies, waits for them, and re-layouts: 5.49 us -> 8.15 us
  transfers between devices with their start and end apart: 34 -> 34, of which waited for: 21 -> 19; matrix products, arithmetic and copies ran while one was open for 4% -> 5% of each run, Pallas kernels for 0% -> 0%
where the time goes in v7:
time: 226 us
  waiting for transfers between devices  121 us (54%)
  starting transfers between devices  41.6 us (18%)
  Pallas kernels  20.6 us (9%)
  other arithmetic  14.6 us (6%)
  between operations  14.5 us (6%)
  local copies, waits for them, and re-layouts  9.89 us (4%)
  matrix products  3.44 us (2%)
    ppermute x18, waiting for transfers between devices, shift(): return lax.ppermute(value, AXES, pairs)  79.8 us
    ppermute x8, waiting for transfers between devices, swapped(): lax.ppermute(value, AXES, [(linear(*p), linear(*move(p))) for p in places...  31.7 us
    pallas_call x1, Pallas kernels, block(): pl.pallas_call(functools.partial(block_kernel, chunks), out_shape=[jax.Sh...  20.6 us
    ppermute x18, starting transfers between devices, shift(): return lax.ppermute(value, AXES, pairs)  17.5 us
    ppermute x8, starting transfers between devices, swapped(): lax.ppermute(value, AXES, [(linear(*p), linear(*move(p))) for p in places...  9.51 us
    ppermute x2, starting transfers between devices, swap_low(): return lax.ppermute(value, AXES, pairs)  8.75 us
    unnamed x48, local copies, waits for them, and re-layouts  8.15 us
    convert_element_type x3, other arithmetic, rounded_sum(): return add_all(parts).astype(jnp.bfloat16)  6.43 us
  transfers between devices with their start and end apart: 34, of which 19 were waited for; matrix products, arithmetic and copies ran while one was open for 5% of the time, Pallas kernels for 0%

profile of v7, /device:TPU:1, one launch (start us, length us, event | category | flops | bytes accessed | tf_op | source)
XLA Modules:
  0.0 225.7 jit_solution(10180198315228017508)
XLA Ops:
  7.2 0.9 dynamic_slice.3
  8.1 1.0 fusion.20
  9.1 1.0 pad_maximum_fusion.3
  10.1 4.6 %collective-permute-start.10 = (bf16[896,256]{1,0:T(8,128)(2,1)S(1)}, bf16[896,256]{1,0:T(8,128)(2,1)S(1)}, u32[]{:S(2)}, u32[]{:S(2)}) collective-permute-start(bf16[896,256]{1,0:T(8,128)(2,1)S(1)} %pad_maximum_fusion.3), channel_id=1, source_target_pairs={{0,0},{1,16},{4,4},{5,20},{8,8},{9,24},{12,12},{13,28},{16,1},{17,... | collective-permute-start | bytes 1376264 | tf_op jit(solution)/shard_map/ppermute | solution.py:41
  14.7 0.7 convert_subtract_fusion
  15.8 5.1 %collective-permute-done.10 = bf16[896,256]{1,0:T(8,128)(2,1)S(1)} collective-permute-done((bf16[896,256]{1,0:T(8,128)(2,1)S(1)}, bf16[896,256]{1,0:T(8,128)(2,1)S(1)}, u32[]{:S(2)}, u32[]{:S(2)}) %collective-permute-start.10) | collective-permute-done | bytes 458784 | tf_op jit(solution)/shard_map/ppermute | solution.py:41
  20.8 0.8 copy-done.15
  22.0 1.9 collective-permute-start
  24.3 4.3 %collective-permute-done = bf16[1,4096]{1,0:T(2,128)(2,1)S(1)} collective-permute-done((bf16[1,4096]{1,0:T(2,128)(2,1)S(1)}, bf16[1,4096]{1,0:T(2,128)(2,1)S(1)}, u32[]{:S(2)}, u32[]{:S(2)}) %collective-permute-start) | collective-permute-done | bytes 8224 | tf_op jit(solution)/shard_map/ppermute | solution.py:47
  28.7 2.6 %collective-permute-start.3 = (bf16[2,32,4096]{2,1,0:T(8,128)(2,1)S(1)}, bf16[2,32,4096]{2,1,0:T(8,128)(2,1)S(1)}, u32[]{:S(2)}, u32[]{:S(2)}) collective-permute-start(bf16[2,32,4096]{2,1,0:T(8,128)(2,1)S(1)} %pad_maximum_fusion.2), channel_id=1, source_target_pairs={{0,18},{1,13},{4,22},{5,1},{8,26},{9,5},{12,30},{13,9},{16,0},{17,... | collective-permute-start | bytes 1572872 | tf_op jit(solution)/shard_map/ppermute | solution.py:29
  31.2 0.5 collective-permute-start.2
  31.8 0.6 collective-permute-start.1
  32.4 10.6 %collective-permute-done.3 = bf16[2,32,4096]{2,1,0:T(8,128)(2,1)S(1)} collective-permute-done((bf16[2,32,4096]{2,1,0:T(8,128)(2,1)S(1)}, bf16[2,32,4096]{2,1,0:T(8,128)(2,1)S(1)}, u32[]{:S(2)}, u32[]{:S(2)}) %collective-permute-start.3) | collective-permute-done | bytes 524320 | tf_op jit(solution)/shard_map/ppermute | solution.py:29
  43.1 3.7 %collective-permute-done.1 = bf16[2,32,4096]{2,1,0:T(8,128)(2,1)S(1)} collective-permute-done((bf16[2,32,4096]{2,1,0:T(8,128)(2,1)S(1)}, bf16[2,32,4096]{2,1,0:T(8,128)(2,1)S(1)}, u32[]{:S(2)}, u32[]{:S(2)}) %collective-permute-start.1) | collective-permute-done | bytes 524320 | tf_op jit(solution)/shard_map/ppermute | solution.py:29
  47.5 1.5 collective-permute-start.4
  48.9 1.7 collective-permute-start.6
  50.6 1.0 collective-permute-start.5
  51.6 9.9 %collective-permute-done.7.refs_3_ = bf16[128,4096]{1,0:T(8,128)(2,1)S(1)} collective-permute-done((bf16[128,4096]{1,0:T(8,128)(2,1)S(1)}, bf16[128,4096]{1,0:T(8,128)(2,1)S(1)}, u32[]{:S(2)}, u32[]{:S(2)}) %collective-permute-start.7) | collective-permute-done | bytes 1048608 | tf_op jit(solution)/shard_map/ppermute | solution.py:29
  61.5 2.2 collective-permute-done.4.refs_1_
  63.7 11.1 %collective-permute-done.6.refs_5_ = bf16[128,4096]{1,0:T(8,128)(2,1)S(1)} collective-permute-done((bf16[128,4096]{1,0:T(8,128)(2,1)S(1)}, bf16[128,4096]{1,0:T(8,128)(2,1)S(1)}, u32[]{:S(2)}, u32[]{:S(2)}) %collective-permute-start.6) | collective-permute-done | bytes 1048608 | tf_op jit(solution)/shard_map/ppermute | solution.py:29
  74.8 1.0 copy-done.20
  75.8 1.2 collective-permute-start.11
  77.1 0.8 collective-permute-start.9
  77.9 0.7 collective-permute-start.8
  78.5 12.7 %collective-permute-done.9.refs_6_ = bf16[128,4096]{1,0:T(8,128)(2,1)S(1)} collective-permute-done((bf16[128,4096]{1,0:T(8,128)(2,1)}, bf16[128,4096]{1,0:T(8,128)(2,1)S(1)}, u32[]{:S(2)}, u32[]{:S(2)}) %collective-permute-start.9) | collective-permute-done | bytes 1048608 | tf_op jit(solution)/shard_map/ppermute | solution.py:29
  91.2 1.8 collective-permute-done.8.refs_2_
  93.1 0.9 copy-done.22
  94.0 1.9 copy-done.17
  95.9 20.6 %shard_map.101 = (bf16[128,4096]{1,0:T(8,128)(2,1)S(1)}, bf16[128,4096]{1,0:T(8,128)(2,1)S(1)}, bf16[128,4096]{1,0:T(8,128)(2,1)S(1)}, bf16[128,4096]{1,0:T(8,12...) custom-call(bf16[128,4096]{1,0:T(8,128)(2,1)} %copy-done.12, ...), custom_call_target="tpu_custom_call" | custom-call | flops 11274289152 | bytes 62914560 | tf_op jit(solution)/shard_map/pallas_call | solution.py:168
  116.5 1.0 copy-done
  117.5 0.7 collective-permute-start.14
  118.2 2.5 %collective-permute-start.12 = (bf16[128,4096]{1,0:T(8,128)(2,1)S(1)}, bf16[128,4096]{1,0:T(8,128)(2,1)S(1)}, u32[]{:S(2)}, u32[]{:S(2)}) collective-permute-start(bf16[128,4096]{1,0:T(8,128)(2,1)S(1)} %get-tuple-element.48), channel_id=1, source_target_pairs={{0,12},{1,19},{4,0},{5,23},{8,4},{9,27},{12,8},{13,31},{16,28},{17... | collective-permute-start | bytes 3145736 | tf_op jit(solution)/shard_map/ppermute | solution.py:29
  120.7 11.7 %collective-permute-done.12 = bf16[128,4096]{1,0:T(8,128)(2,1)S(1)} collective-permute-done((bf16[128,4096]{1,0:T(8,128)(2,1)S(1)}, bf16[128,4096]{1,0:T(8,128)(2,1)S(1)}, u32[]{:S(2)}, u32[]{:S(2)}) %collective-permute-start.12) | collective-permute-done | bytes 1048608 | tf_op jit(solution)/shard_map/ppermute | solution.py:29
  132.4 3.4 %collective-permute-done.13 = bf16[128,4096]{1,0:T(8,128)(2,1)S(1)} collective-permute-done((bf16[128,4096]{1,0:T(8,128)(2,1)}, bf16[128,4096]{1,0:T(8,128)(2,1)S(1)}, u32[]{:S(2)}, u32[]{:S(2)}) %collective-permute-start.13) | collective-permute-done | bytes 1048608 | tf_op jit(solution)/shard_map/ppermute | solution.py:29
  135.8 1.0 copy-done.9
  136.8 4.7 %add_convert_fusion = bf16[8,896,256]{2,1,0:T(8,128)(2,1)} fusion(bf16[8,896,256]{2,1,0:T(8,128)(2,1)S(1)} %collective-permute-done.14, bf16[8,896,256]{2,1,0:T(8,128)(2,1)} %get-tuple-element.57), kind=kLoop, calls=%fused_computation | loop fusion | flops 7340032 | bytes 11010048 | tf_op jit(solution)/shard_map/convert_element_type | solution.py:226
  141.6 0.7 copy-done.16
  142.6 1.1 collective-permute-start.16
  143.7 1.5 add_convert_fusion.4
  145.5 11.0 %collective-permute-done.15 = bf16[128,4096]{1,0:T(8,128)(2,1)S(1)} collective-permute-done((bf16[128,4096]{1,0:T(8,128)(2,1)}, bf16[128,4096]{1,0:T(8,128)(2,1)S(1)}, u32[]{:S(2)}, u32[]{:S(2)}) %collective-permute-start.15) | collective-permute-done | bytes 1048608 | tf_op jit(solution)/shard_map/ppermute | solution.py:29
  156.5 1.5 collective-permute-done.16
  158.0 1.5 collective-permute-start.18
  159.5 13.1 %collective-permute-done.19 = f32[4096]{0:T(1024)S(1)} collective-permute-done((f32[4096]{0:T(1024)S(1)}, f32[4096]{0:T(1024)S(1)}, u32[]{:S(2)}, u32[]{:S(2)}) %collective-permute-start.19) | collective-permute-done | bytes 16416 | tf_op jit(solution)/shard_map/ppermute | solution.py:212
  172.9 3.8 %collective-permute-done.20 = f32[4096]{0:T(1024)S(1)} collective-permute-done((f32[4096]{0:T(1024)S(1)}, f32[4096]{0:T(1024)S(1)}, u32[]{:S(2)}, u32[]{:S(2)}) %collective-permute-start.20) | collective-permute-done | bytes 16416 | tf_op jit(solution)/shard_map/ppermute | solution.py:212
  176.7 0.5 fusion.3
  177.2 0.5 fusion.2
  177.9 2.7 %collective-permute-start.21 = (bf16[2,32,4096]{2,1,0:T(8,128)(2,1)S(1)}, bf16[2,32,4096]{2,1,0:T(8,128)(2,1)S(1)}, u32[]{:S(2)}, u32[]{:S(2)}) collective-permute-start(bf16[2,32,4096]{2,1,0:T(8,128)(2,1)S(1)} %get-tuple-element.76), channel_id=1, source_target_pairs={{0,18},{1,13},{4,22},{5,1},{8,26},{9,5},{12,30},{13,9},{16,0},{17,... | collective-permute-start | bytes 1572872 | tf_op jit(solution)/shard_map/ppermute | solution.py:29
  180.6 0.6 collective-permute-start.24
  181.2 11.1 %collective-permute-done.24 = f32[4096]{0:T(1024)S(1)} collective-permute-done((f32[4096]{0:T(1024)S(1)}, f32[4096]{0:T(1024)S(1)}, u32[]{:S(2)}, u32[]{:S(2)}) %collective-permute-start.24) | collective-permute-done | bytes 16416 | tf_op jit(solution)/shard_map/ppermute | solution.py:212
  192.2 2.3 %collective-permute-start.25 = (f32[4096]{0:T(1024)S(1)}, f32[4096]{0:T(1024)S(1)}, u32[]{:S(2)}, u32[]{:S(2)}) collective-permute-start(f32[4096]{0:T(1024)S(1)} %add.98), channel_id=1, source_target_pairs={{0,8},{1,9},{4,12},{5,13},{8,0},{9,1},{12,4},{13,5},{16,24},{17,25... | collective-permute-start | bytes 49160 | tf_op jit(solution)/shard_map/ppermute | solution.py:212
  194.5 1.8 collective-permute-done.25
  196.4 0.7 copy-done.13
  197.5 1.7 convert_add_fusion
  199.4 0.6 collective-permute-done.27
  200.1 2.3 %collective-permute-start.28 = (f32[4096]{0:T(1024)S(1)}, f32[4096]{0:T(1024)S(1)}, u32[]{:S(2)}, u32[]{:S(2)}) collective-permute-start(f32[4096]{0:T(1024)S(1)} %add.109), channel_id=1, source_target_pairs={{0,64},{1,65},{4,68},{5,69},{8,72},{9,73},{12,76},{13,77},{16,80},... | collective-permute-start | bytes 49160 | tf_op jit(solution)/shard_map/ppermute | solution.py:212
  202.4 1.9 collective-permute-start.26
  204.4 4.2 %collective-permute-start.31 = (bf16[896,256]{1,0:T(8,128)(2,1)S(1)}, bf16[896,256]{1,0:T(8,128)(2,1)S(1)}, u32[]{:S(2)}, u32[]{:S(2)}) collective-permute-start(bf16[896,256]{1,0:T(8,128)(2,1)S(1)} %bitcast.45), channel_id=1, source_target_pairs={{0,0},{1,16},{4,4},{5,20},{8,8},{9,24},{12,12},{13,28},{16,1},{17,... | collective-permute-start | bytes 1376264 | tf_op jit(solution)/shard_map/ppermute | solution.py:41
  208.6 3.9 %collective-permute-start.29 = (f32[4096]{0:T(1024)S(1)}, f32[4096]{0:T(1024)S(1)}, u32[]{:S(2)}, u32[]{:S(2)}) collective-permute-start(f32[4096]{0:T(1024)S(1)} %add.110), channel_id=1, source_target_pairs={{0,128},{1,129},{4,132},{5,133},{8,136},{9,137},{12,140},{13,141},... | collective-permute-start | bytes 49160 | tf_op jit(solution)/shard_map/ppermute | solution.py:212
  212.4 1.5 fusion.1
  213.9 1.2 collective-permute-done.29
  215.2 1.4 fusion
  216.6 0.6 add.112
  217.2 0.8 multiply_bitcast_fusion
  218.0 0.8 slice_convert_fusion
  (99 shorter events, 3.8 us)
Async XLA Ops:
  7.2 14.6 %copy-start.1 = (bf16[128,4096]{1,0:T(8,128)(2,1)S(1)}, bf16[128,4096]{1,0:T(8,128)(2,1)}, u32[]{:S(2)}) copy-start(bf16[128,4096]{1,0:T(8,128)(2,1)} %param.11) | copy-start | bytes 3145732
  7.2 16.8 %copy-start.3 = (bf16[128,4096]{1,0:T(8,128)(2,1)S(1)}, bf16[128,4096]{1,0:T(8,128)(2,1)}, u32[]{:S(2)}) copy-start(bf16[128,4096]{1,0:T(8,128)(2,1)} %param.6) | copy-start | bytes 3145732
  7.2 68.7 %all-gather.3.cloned.1.call-start = ((), (), s32[]{:S(2)}) async-start(), calls=%async_computation.2 | async-start | bytes 4128768 | tf_op jit(solution)/shard_map/all_gather | solution.py:260
  10.1 10.8 %collective-permute-start.10 = (bf16[896,256]{1,0:T(8,128)(2,1)S(1)}, bf16[896,256]{1,0:T(8,128)(2,1)S(1)}, u32[]{:S(2)}, u32[]{:S(2)}) collective-permute-start(bf16[896,256]{1,0:T(8,128)(2,1)S(1)} %pad_maximum_fusion.3), channel_id=1, source_target_pairs={{0,0},{1,16},{4,4},{5,20},{8,8},{9,24},{12,12},{13,28},{16,1},{17,... | collective-permute-start | bytes 1376264 | tf_op jit(solution)/shard_map/ppermute | solution.py:41
  20.8 0.8 copy-start.15
  21.6 174.7 %reduce-scatter.2.cloned.1.call-start = ((), (), s32[]{:S(2)}) async-start(), calls=%async_computation.1 | async-start | bytes 4128768 | tf_op jit(solution)/shard_map/reduce_scatter | solution.py:237
  22.0 6.6 %collective-permute-start = (bf16[1,4096]{1,0:T(2,128)(2,1)S(1)}, bf16[1,4096]{1,0:T(2,128)(2,1)S(1)}, u32[]{:S(2)}, u32[]{:S(2)}) collective-permute-start(bf16[1,4096]{1,0:T(2,128)(2,1)S(1)} %slice.65), channel_id=1, source_target_pairs={{1,0},{2,1},{3,2},{4,3},{5,4},{6,5},{7,6},{8,7},{9,8},{10,9},{11,1... | collective-permute-start | bytes 24584 | tf_op jit(solution)/shard_map/ppermute | solution.py:47
  24.3 22.5 %copy-start.5 = (bf16[31,4096]{1,0:T(8,128)(2,1)}, bf16[31,4096]{1,0:T(8,128)(2,1)S(1)}, u32[]{:S(2)}) copy-start(bf16[31,4096]{1,0:T(8,128)(2,1)S(1)} %slice.64) | copy-start | bytes 761860
  28.7 14.3 %collective-permute-start.3 = (bf16[2,32,4096]{2,1,0:T(8,128)(2,1)S(1)}, bf16[2,32,4096]{2,1,0:T(8,128)(2,1)S(1)}, u32[]{:S(2)}, u32[]{:S(2)}) collective-permute-start(bf16[2,32,4096]{2,1,0:T(8,128)(2,1)S(1)} %pad_maximum_fusion.2), channel_id=1, source_target_pairs={{0,18},{1,13},{4,22},{5,1},{8,26},{9,5},{12,30},{13,9},{16,0},{17,... | collective-permute-start | bytes 1572872 | tf_op jit(solution)/shard_map/ppermute | solution.py:29
  31.2 11.8 %collective-permute-start.2 = (bf16[2,32,4096]{2,1,0:T(8,128)(2,1)S(1)}, bf16[2,32,4096]{2,1,0:T(8,128)(2,1)S(1)}, u32[]{:S(2)}, u32[]{:S(2)}) collective-permute-start(bf16[2,32,4096]{2,1,0:T(8,128)(2,1)S(1)} %pad_maximum_fusion.2), channel_id=1, source_target_pairs={{0,2},{1,9},{4,6},{5,13},{8,10},{9,1},{12,14},{13,5},{16,18},{17,2... | collective-permute-start | bytes 1572872 | tf_op jit(solution)/shard_map/ppermute | solution.py:29
  31.8 15.0 %collective-permute-start.1 = (bf16[2,32,4096]{2,1,0:T(8,128)(2,1)S(1)}, bf16[2,32,4096]{2,1,0:T(8,128)(2,1)S(1)}, u32[]{:S(2)}, u32[]{:S(2)}) collective-permute-start(bf16[2,32,4096]{2,1,0:T(8,128)(2,1)S(1)} %pad_maximum_fusion.2), channel_id=1, source_target_pairs={{0,16},{1,5},{4,20},{5,9},{8,24},{9,13},{12,28},{13,1},{16,2},{17,... | collective-permute-start | bytes 1572872 | tf_op jit(solution)/shard_map/ppermute | solution.py:29
  47.3 45.8 %copy-start.11 = (bf16[128,4096]{1,0:T(8,128)(2,1)}, bf16[128,4096]{1,0:T(8,128)(2,1)S(1)}, u32[]{:S(2)}) copy-start(bf16[128,4096]{1,0:T(8,128)(2,1)S(1)} %concatenate.18.refs_4_) | copy-start | bytes 3145732
  47.4 27.5 %copy-start.12 = (bf16[128,4096]{1,0:T(8,128)(2,1)}, bf16[128,4096]{1,0:T(8,128)(2,1)S(1)}, u32[]{:S(2)}) copy-start(bf16[128,4096]{1,0:T(8,128)(2,1)S(1)} %pad_maximum_fusion.refs_0_) | copy-start | bytes 3145732
  47.4 14.1 %collective-permute-start.7 = (bf16[128,4096]{1,0:T(8,128)(2,1)S(1)}, bf16[128,4096]{1,0:T(8,128)(2,1)S(1)}, u32[]{:S(2)}, u32[]{:S(2)}) collective-permute-start(bf16[128,4096]{1,0:T(8,128)(2,1)S(1)} %pad_maximum_fusion.refs_0_), channel_id=1, source_target_pairs={{0,12},{1,19},{4,0},{5,23},{8,4},{9,27},{12,8},{13,31},{16,28},{17... | collective-permute-start | bytes 3145736 | tf_op jit(solution)/shard_map/ppermute | solution.py:29
  47.5 16.3 %collective-permute-start.4 = (bf16[128,4096]{1,0:T(8,128)(2,1)S(1)}, bf16[128,4096]{1,0:T(8,128)(2,1)S(1)}, u32[]{:S(2)}, u32[]{:S(2)}) collective-permute-start(bf16[128,4096]{1,0:T(8,128)(2,1)S(1)} %pad_maximum_fusion.refs_0_), channel_id=1, source_target_pairs={{0,4},{1,17},{4,8},{5,21},{8,12},{9,25},{12,0},{13,29},{16,20},{17... | collective-permute-start | bytes 3145736 | tf_op jit(solution)/shard_map/ppermute | solution.py:29
  48.9 25.9 %collective-permute-start.6 = (bf16[128,4096]{1,0:T(8,128)(2,1)S(1)}, bf16[128,4096]{1,0:T(8,128)(2,1)S(1)}, u32[]{:S(2)}, u32[]{:S(2)}) collective-permute-start(bf16[128,4096]{1,0:T(8,128)(2,1)S(1)} %concatenate.18.refs_4_), channel_id=1, source_target_pairs={{0,4},{1,17},{4,8},{5,21},{8,12},{9,25},{12,0},{13,29},{16,20},{17... | collective-permute-start | bytes 3145736 | tf_op jit(solution)/shard_map/ppermute | solution.py:29
  50.6 25.2 %collective-permute-start.5 = (bf16[128,4096]{1,0:T(8,128)(2,1)S(1)}, bf16[128,4096]{1,0:T(8,128)(2,1)}, u32[]{:S(2)}, u32[]{:S(2)}) collective-permute-start(bf16[128,4096]{1,0:T(8,128)(2,1)S(1)} %concatenate.18.refs_4_), channel_id=1, source_target_pairs={{0,12},{1,19},{4,0},{5,23},{8,4},{9,27},{12,8},{13,31},{16,28},{17... | collective-permute-start | bytes 3145736 | tf_op jit(solution)/shard_map/ppermute | solution.py:29
  61.5 31.6 %copy-start.18 = (bf16[128,4096]{1,0:T(8,128)(2,1)}, bf16[128,4096]{1,0:T(8,128)(2,1)S(1)}, u32[]{:S(2)}) copy-start(bf16[128,4096]{1,0:T(8,128)(2,1)S(1)} %collective-permute-done.7.refs_3_) | copy-start | bytes 3145732
  63.7 29.3 %copy-start.19 = (bf16[128,4096]{1,0:T(8,128)(2,1)}, bf16[128,4096]{1,0:T(8,128)(2,1)S(1)}, u32[]{:S(2)}) copy-start(bf16[128,4096]{1,0:T(8,128)(2,1)S(1)} %collective-permute-done.4.refs_1_) | copy-start | bytes 3145732
  74.8 1.0 copy-start.20
  75.8 17.2 %collective-permute-start.11 = (bf16[8,896,256]{2,1,0:T(8,128)(2,1)}, bf16[8,896,256]{2,1,0:T(8,128)(2,1)S(1)}, u32[]{:S(2)}, u32[]{:S(2)}) collective-permute-start(bf16[8,896,256]{2,1,0:T(8,128)(2,1)} %bitcast.43), channel_id=1, source_target_pairs={{0,1},{1,0},{4,5},{5,4},{8,9},{9,8},{12,13},{13,12},{16,17},{17,16... | collective-permute-start | bytes 11010056 | tf_op jit(solution)/shard_map/ppermute | solution.py:34
  77.1 14.2 %collective-permute-start.9 = (bf16[128,4096]{1,0:T(8,128)(2,1)}, bf16[128,4096]{1,0:T(8,128)(2,1)S(1)}, u32[]{:S(2)}, u32[]{:S(2)}) collective-permute-start(bf16[128,4096]{1,0:T(8,128)(2,1)} %collective-permute-done.5.refs_7_), channel_id=1, source_target_pairs={{0,12},{1,19},{4,0},{5,23},{8,4},{9,27},{12,8},{13,31},{16,28},{17... | collective-permute-start | bytes 3145736 | tf_op jit(solution)/shard_map/ppermute | solution.py:29
  77.9 15.2 %collective-permute-start.8 = (bf16[128,4096]{1,0:T(8,128)(2,1)S(1)}, bf16[128,4096]{1,0:T(8,128)(2,1)S(1)}, u32[]{:S(2)}, u32[]{:S(2)}) collective-permute-start(bf16[128,4096]{1,0:T(8,128)(2,1)S(1)} %collective-permute-done.4.refs_1_), channel_id=1, source_target_pairs={{0,4},{1,17},{4,8},{5,21},{8,12},{9,25},{12,0},{13,29},{16,20},{17... | collective-permute-start | bytes 3145736 | tf_op jit(solution)/shard_map/ppermute | solution.py:29
  91.2 1.8 copy-start.21
  93.1 1.0 copy-start.22
  94.0 1.9 copy-start.17
  116.5 1.0 copy-start
  117.5 18.4 %collective-permute-start.14 = (bf16[8,896,256]{2,1,0:T(8,128)(2,1)}, bf16[8,896,256]{2,1,0:T(8,128)(2,1)S(1)}, u32[]{:S(2)}, u32[]{:S(2)}) collective-permute-start(bf16[8,896,256]{2,1,0:T(8,128)(2,1)} %get-tuple-element.50), channel_id=1, source_target_pairs={{0,1},{1,0},{4,5},{5,4},{8,9},{9,8},{12,13},{13,12},{16,17},{17,16... | collective-permute-start | bytes 11010056 | tf_op jit(solution)/shard_map/ppermute | solution.py:34
  118.2 14.2 %collective-permute-start.12 = (bf16[128,4096]{1,0:T(8,128)(2,1)S(1)}, bf16[128,4096]{1,0:T(8,128)(2,1)S(1)}, u32[]{:S(2)}, u32[]{:S(2)}) collective-permute-start(bf16[128,4096]{1,0:T(8,128)(2,1)S(1)} %get-tuple-element.48), channel_id=1, source_target_pairs={{0,12},{1,19},{4,0},{5,23},{8,4},{9,27},{12,8},{13,31},{16,28},{17... | collective-permute-start | bytes 3145736 | tf_op jit(solution)/shard_map/ppermute | solution.py:29
  120.7 15.2 %collective-permute-start.13 = (bf16[128,4096]{1,0:T(8,128)(2,1)}, bf16[128,4096]{1,0:T(8,128)(2,1)S(1)}, u32[]{:S(2)}, u32[]{:S(2)}) collective-permute-start(bf16[128,4096]{1,0:T(8,128)(2,1)} %get-tuple-element.49), channel_id=1, source_target_pairs={{0,4},{1,17},{4,8},{5,21},{8,12},{9,25},{12,0},{13,29},{16,20},{17... | collective-permute-start | bytes 3145736 | tf_op jit(solution)/shard_map/ppermute | solution.py:29
  132.4 3.4 %copy-start.8 = (bf16[128,4096]{1,0:T(8,128)(2,1)}, bf16[128,4096]{1,0:T(8,128)(2,1)S(1)}, u32[]{:S(2)}) copy-start(bf16[128,4096]{1,0:T(8,128)(2,1)S(1)} %collective-permute-done.12) | copy-start | bytes 3145732
  135.8 1.0 copy-start.9
  141.5 0.7 copy-start.16
  141.5 3.6 %copy-start.7 = (bf16[128,4096]{1,0:T(8,128)(2,1)S(1)}, bf16[128,4096]{1,0:T(8,128)(2,1)}, u32[]{:S(2)}) copy-start(bf16[128,4096]{1,0:T(8,128)(2,1)} %get-tuple-element.52) | copy-start | bytes 3145732
  141.6 3.6 %copy-start.10 = (bf16[128,4096]{1,0:T(8,128)(2,1)S(1)}, bf16[128,4096]{1,0:T(8,128)(2,1)}, u32[]{:S(2)}) copy-start(bf16[128,4096]{1,0:T(8,128)(2,1)} %copy-done.9) | copy-start | bytes 3145732
  142.2 14.3 %collective-permute-start.15 = (bf16[128,4096]{1,0:T(8,128)(2,1)}, bf16[128,4096]{1,0:T(8,128)(2,1)S(1)}, u32[]{:S(2)}, u32[]{:S(2)}) collective-permute-start(bf16[128,4096]{1,0:T(8,128)(2,1)} %get-tuple-element.54), channel_id=1, source_target_pairs={{0,12},{1,19},{4,0},{5,23},{8,4},{9,27},{12,8},{13,31},{16,28},{17... | collective-permute-start | bytes 3145736 | tf_op jit(solution)/shard_map/ppermute | solution.py:29
  142.6 15.5 %collective-permute-start.16 = (bf16[128,4096]{1,0:T(8,128)(2,1)}, bf16[128,4096]{1,0:T(8,128)(2,1)S(1)}, u32[]{:S(2)}, u32[]{:S(2)}) collective-permute-start(bf16[128,4096]{1,0:T(8,128)(2,1)} %copy-done), channel_id=1, source_target_pairs={{0,4},{1,17},{4,8},{5,21},{8,12},{9,25},{12,0},{13,29},{16,20},{17... | collective-permute-start | bytes 3145736 | tf_op jit(solution)/shard_map/ppermute | solution.py:29
  158.0 18.7 %collective-permute-start.17 = (bf16[128,4096]{1,0:T(8,128)(2,1)S(1)}, bf16[128,4096]{1,0:T(8,128)(2,1)S(1)}, u32[]{:S(2)}, u32[]{:S(2)}) collective-permute-start(bf16[128,4096]{1,0:T(8,128)(2,1)S(1)} %add_convert_fusion.4), channel_id=1, source_target_pairs={{0,12},{1,19},{4,0},{5,23},{8,4},{9,27},{12,8},{13,31},{16,28},{17... | collective-permute-start | bytes 3145736 | tf_op jit(solution)/shard_map/ppermute | solution.py:29
  158.0 18.7 %collective-permute-start.18 = (bf16[128,4096]{1,0:T(8,128)(2,1)S(1)}, bf16[128,4096]{1,0:T(8,128)(2,1)S(1)}, u32[]{:S(2)}, u32[]{:S(2)}) collective-permute-start(bf16[128,4096]{1,0:T(8,128)(2,1)S(1)} %add_convert_fusion.3), channel_id=1, source_target_pairs={{0,4},{1,17},{4,8},{5,21},{8,12},{9,25},{12,0},{13,29},{16,20},{17... | collective-permute-start | bytes 3145736 | tf_op jit(solution)/shard_map/ppermute | solution.py:29
  159.5 13.1 %collective-permute-start.19 = (f32[4096]{0:T(1024)S(1)}, f32[4096]{0:T(1024)S(1)}, u32[]{:S(2)}, u32[]{:S(2)}) collective-permute-start(f32[4096]{0:T(1024)S(1)} %div.35), channel_id=1, source_target_pairs={{0,16},{1,17},{4,20},{5,21},{8,24},{9,25},{12,28},{13,29},{16,0},{... | collective-permute-start | bytes 49160 | tf_op jit(solution)/shard_map/ppermute | solution.py:212
  172.6 4.1 %collective-permute-start.20 = (f32[4096]{0:T(1024)S(1)}, f32[4096]{0:T(1024)S(1)}, u32[]{:S(2)}, u32[]{:S(2)}) collective-permute-start(f32[4096]{0:T(1024)S(1)} %add.92), channel_id=1, source_target_pairs={{0,2},{1,3},{4,6},{5,7},{8,10},{9,11},{12,14},{13,15},{16,18},{17,... | collective-permute-start | bytes 49160 | tf_op jit(solution)/shard_map/ppermute | solution.py:212
  177.8 18.5 %collective-permute-start.23 = (bf16[2,32,4096]{2,1,0:T(8,128)(2,1)S(1)}, bf16[2,32,4096]{2,1,0:T(8,128)(2,1)S(1)}, u32[]{:S(2)}, u32[]{:S(2)}) collective-permute-start(bf16[2,32,4096]{2,1,0:T(8,128)(2,1)S(1)} %get-tuple-element.75), channel_id=1, source_target_pairs={{0,16},{1,5},{4,20},{5,9},{8,24},{9,13},{12,28},{13,1},{16,2},{17,... | collective-permute-start | bytes 1572872 | tf_op jit(solution)/shard_map/ppermute | solution.py:29
  177.9 18.4 %collective-permute-start.21 = (bf16[2,32,4096]{2,1,0:T(8,128)(2,1)S(1)}, bf16[2,32,4096]{2,1,0:T(8,128)(2,1)S(1)}, u32[]{:S(2)}, u32[]{:S(2)}) collective-permute-start(bf16[2,32,4096]{2,1,0:T(8,128)(2,1)S(1)} %get-tuple-element.76), channel_id=1, source_target_pairs={{0,18},{1,13},{4,22},{5,1},{8,26},{9,5},{12,30},{13,9},{16,0},{17,... | collective-permute-start | bytes 1572872 | tf_op jit(solution)/shard_map/ppermute | solution.py:29
  180.6 15.8 %collective-permute-start.22 = (bf16[2,32,4096]{2,1,0:T(8,128)(2,1)S(1)}, bf16[2,32,4096]{2,1,0:T(8,128)(2,1)}, u32[]{:S(2)}, u32[]{:S(2)}) collective-permute-start(bf16[2,32,4096]{2,1,0:T(8,128)(2,1)S(1)} %get-tuple-element.77), channel_id=1, source_target_pairs={{0,2},{1,9},{4,6},{5,13},{8,10},{9,1},{12,14},{13,5},{16,18},{17,2... | collective-permute-start | bytes 1572872 | tf_op jit(solution)/shard_map/ppermute | solution.py:29
  180.6 11.6 %collective-permute-start.24 = (f32[4096]{0:T(1024)S(1)}, f32[4096]{0:T(1024)S(1)}, u32[]{:S(2)}, u32[]{:S(2)}) collective-permute-start(f32[4096]{0:T(1024)S(1)} %add.93), channel_id=1, source_target_pairs={{0,4},{1,5},{4,0},{5,1},{8,12},{9,13},{12,8},{13,9},{16,20},{17,21... | collective-permute-start | bytes 49160 | tf_op jit(solution)/shard_map/ppermute | solution.py:212
  192.2 4.1 %collective-permute-start.25 = (f32[4096]{0:T(1024)S(1)}, f32[4096]{0:T(1024)S(1)}, u32[]{:S(2)}, u32[]{:S(2)}) collective-permute-start(f32[4096]{0:T(1024)S(1)} %add.98), channel_id=1, source_target_pairs={{0,8},{1,9},{4,12},{5,13},{8,0},{9,1},{12,4},{13,5},{16,24},{17,25... | collective-permute-start | bytes 49160 | tf_op jit(solution)/shard_map/ppermute | solution.py:212
  196.3 0.8 copy-start.13
  196.3 0.9 copy-start.14
  197.3 7.1 %copy-start.23 = (bf16[1,896,256]{2,1,0:T(8,128)(2,1)S(1)}, bf16[1,896,256]{2,1,0:T(8,128)(2,1)}, u32[]{:S(2)}) copy-start(bf16[1,896,256]{2,1,0:T(8,128)(2,1)} %reduce-scatter.2.cloned.1.call-done) | copy-start | bytes 1376260
  197.3 15.1 %copy-start.2 = (bf16[128,4096]{1,0:T(8,128)(2,1)S(1)}, bf16[128,4096]{1,0:T(8,128)(2,1)}, u32[]{:S(2)}) copy-start(bf16[128,4096]{1,0:T(8,128)(2,1)} %param.11) | copy-start | bytes 3145732
  197.3 15.1 %copy-start.6 = (bf16[31,4096]{1,0:T(8,128)(2,1)S(1)}, bf16[31,4096]{1,0:T(8,128)(2,1)}, u32[]{:S(2)}) copy-start(bf16[31,4096]{1,0:T(8,128)(2,1)} %copy-done.5) | copy-start | bytes 761860
  197.3 2.8 %collective-permute-start.27 = (f32[4096]{0:T(1024)S(1)}, f32[4096]{0:T(1024)S(1)}, u32[]{:S(2)}, u32[]{:S(2)}) collective-permute-start(f32[4096]{0:T(1024)S(1)} %add.99), channel_id=1, source_target_pairs={{0,32},{1,33},{4,36},{5,37},{8,40},{9,41},{12,44},{13,45},{16,48},... | collective-permute-start | bytes 49160 | tf_op jit(solution)/shard_map/ppermute | solution.py:212
  199.2 16.0 %copy-start.4 = (bf16[128,4096]{1,0:T(8,128)(2,1)S(1)}, bf16[128,4096]{1,0:T(8,128)(2,1)}, u32[]{:S(2)}) copy-start(bf16[128,4096]{1,0:T(8,128)(2,1)} %param.6) | copy-start | bytes 3145732
  200.1 8.5 %collective-permute-start.28 = (f32[4096]{0:T(1024)S(1)}, f32[4096]{0:T(1024)S(1)}, u32[]{:S(2)}, u32[]{:S(2)}) collective-permute-start(f32[4096]{0:T(1024)S(1)} %add.109), channel_id=1, source_target_pairs={{0,64},{1,65},{4,68},{5,69},{8,72},{9,73},{12,76},{13,77},{16,80},... | collective-permute-start | bytes 49160 | tf_op jit(solution)/shard_map/ppermute | solution.py:212
  202.4 12.7 %collective-permute-start.26 = (bf16[1,4096]{1,0:T(2,128)(2,1)S(1)}, bf16[1,4096]{1,0:T(2,128)(2,1)S(1)}, u32[]{:S(2)}, u32[]{:S(2)}) collective-permute-start(bf16[1,4096]{1,0:T(2,128)(2,1)S(1)} %slice.78), channel_id=1, source_target_pairs={{0,1},{1,2},{2,3},{3,4},{4,5},{5,6},{6,7},{7,8},{8,9},{9,10},{10,1... | collective-permute-start | bytes 24584 | tf_op jit(solution)/shard_map/ppermute | solution.py:47
  204.4 12.9 %collective-permute-start.31 = (bf16[896,256]{1,0:T(8,128)(2,1)S(1)}, bf16[896,256]{1,0:T(8,128)(2,1)S(1)}, u32[]{:S(2)}, u32[]{:S(2)}) collective-permute-start(bf16[896,256]{1,0:T(8,128)(2,1)S(1)} %bitcast.45), channel_id=1, source_target_pairs={{0,0},{1,16},{4,4},{5,20},{8,8},{9,24},{12,12},{13,28},{16,1},{17,... | collective-permute-start | bytes 1376264 | tf_op jit(solution)/shard_map/ppermute | solution.py:41
  208.6 6.6 %collective-permute-start.29 = (f32[4096]{0:T(1024)S(1)}, f32[4096]{0:T(1024)S(1)}, u32[]{:S(2)}, u32[]{:S(2)}) collective-permute-start(f32[4096]{0:T(1024)S(1)} %add.110), channel_id=1, source_target_pairs={{0,128},{1,129},{4,132},{5,133},{8,136},{9,137},{12,140},{13,141},... | collective-permute-start | bytes 49160 | tf_op jit(solution)/shard_map/ppermute | solution.py:212
  215.2 1.5 collective-permute-start.30
Sparse Core Ops, SparseCore 0:
  21.8 52.5 all-gather.2
  141.7 47.2 reduce-scatter.1

commit v8 on v3

--- a/solution.py
+++ b/solution.py
@@ -216,26 +216,20 @@
     d1, n3, weight_part = lax.optimization_barrier((d1, n3, weight_part))
     weight_sum = lax.psum_scatter(weight_part, "z", scatter_dimension=0, tiled=False)
     d1, n3 = shift(d1, second=-1), shift(n3, second=1)
-    arrived = (d1, d3, n1, n3, total_over_all(gain_part))
-    d1, d3, n1, n3, grad_gain = lax.optimization_barrier(arrived)
+    gain = pair(pair(pair(pair(pair(gain_part, z=1), z=2), c=1), y=1), y=2)
+    d1, d3, n1, n3, gain = lax.optimization_barrier((d1, d3, n1, n3, gain))
     both = jnp.stack([add_all([d0, d1, d3]).astype(bf), add_all([n0, n1, n3]).astype(bf)])
     rows = both.shape[1] // 4
     both = [both[:, d * rows : (d + 1) * rows] for d in range(4)]
     arrived = [shift(both[d], first=-d) for d in (1, 2, 3)] + [weight_sum]
-    *arrived, weight_sum = lax.optimization_barrier(arrived)
-    return add_all([both[0], *arrived]), grad_gain, weight_sum
-
-
-def total_over_all(value):
-    moves = [lambda p, k=k: (p[0] ^ k, p[1], p[2], p[3]) for k in (1, 2, 4)]
-    moves += [lambda p: (p[0], p[1], p[2], 1 - p[3])]
-    moves += [lambda p, k=k: (p[0], p[1] ^ k, p[2], p[3]) for k in (1, 2)]
-    moves += [lambda p, k=k: (p[0], p[1], p[2] ^ k, p[3]) for k in (1, 2)]
-    for move in moves:
-        value = value + lax.ppermute(
-            value, AXES, [(linear(*p), linear(*move(p))) for p in places()]
-        )
-    return value
+    gain = pair(pair(pair(gain, x=1), x=2), z=4)
+    *arrived, weight_sum, gain = lax.optimization_barrier([*arrived, gain])
+    return add_all([both[0], *arrived]), gain, weight_sum
+
+
+def pair(value, z=0, y=0, x=0, c=0):
+    pairs = [(linear(*p), linear(p[0] ^ z, p[1] ^ y, p[2] ^ x, p[3] ^ c)) for p in places()]
+    return value + lax.ppermute(value, AXES, pairs)
 
 
 def shards(stream, doc_start, norm_gain, weight_in, weight_out, upstream):

time: 222 us -> 220 us (level)
  starting transfers between devices: 49.8 us -> 47.2 us
    ppermute x8, waiting for transfers between devices: 20.6 us -> 33.6 us  [pair(): return value + lax.ppermute(value, AXES, pairs)]
    ppermute x18, waiting for transfers between devices: 78.6 us -> 66 us  [shift(): return lax.ppermute(value, AXES, pairs)]
    ppermute x2, starting transfers between devices: 8.05 us -> 3.97 us  [from_behind(): return lax.ppermute(value, AXES, pairs)]
  transfers between devices with their start and end apart: 34 -> 34, of which waited for: 21 -> 20; matrix products, arithmetic and copies ran while one was open for 4% -> 4% of each run, Pallas kernels for 0% -> 0%
where the time goes in v8:
time: 220 us
  waiting for transfers between devices  113 us (51%)
  starting transfers between devices  47.2 us (21%)
  Pallas kernels  20.5 us (9%)
  between operations  14.5 us (7%)
  other arithmetic  13.3 us (6%)
  local copies, waits for them, and re-layouts  7.21 us (3%)
  matrix products  3.44 us (2%)
    ppermute x18, waiting for transfers between devices, shift(): return lax.ppermute(value, AXES, pairs)  66 us
    ppermute x8, waiting for transfers between devices, pair(): return value + lax.ppermute(value, AXES, pairs)  33.6 us
    pallas_call x1, Pallas kernels, block(): pl.pallas_call(functools.partial(block_kernel, chunks), out_shape=[jax.Sh...  20.5 us
    ppermute x18, starting transfers between devices, shift(): return lax.ppermute(value, AXES, pairs)  18.8 us
    ppermute x8, starting transfers between devices, pair(): return value + lax.ppermute(value, AXES, pairs)  15.1 us
    ppermute x2, waiting for transfers between devices, swap_low(): return lax.ppermute(value, AXES, pairs)  9.54 us
    ppermute x2, starting transfers between devices, swap_low(): return lax.ppermute(value, AXES, pairs)  7.01 us
    unnamed x42, local copies, waits for them, and re-layouts  5.47 us
  transfers between devices with their start and end apart: 34, of which 20 were waited for; matrix products, arithmetic and copies ran while one was open for 4% of the time, Pallas kernels for 0%

profile of v8, /device:TPU:1, one launch (start us, length us, event | category | flops | bytes accessed | tf_op | source)
XLA Modules:
  0.0 219.6 jit_solution(6458433814030161851)
XLA Ops:
  7.2 0.9 dynamic_slice.3
  8.1 1.0 fusion.20
  9.1 1.0 pad_maximum_fusion.3
  10.1 4.6 %collective-permute-start.10 = (bf16[896,256]{1,0:T(8,128)(2,1)S(1)}, bf16[896,256]{1,0:T(8,128)(2,1)S(1)}, u32[]{:S(2)}, u32[]{:S(2)}) collective-permute-start(bf16[896,256]{1,0:T(8,128)(2,1)S(1)} %pad_maximum_fusion.3), channel_id=1, source_target_pairs={{0,0},{1,16},{4,4},{5,20},{8,8},{9,24},{12,12},{13,28},{16,1},{17,... | collective-permute-start | bytes 1376264 | tf_op jit(solution)/shard_map/ppermute | solution.py:41
  14.7 0.7 convert_subtract_fusion
  15.8 5.1 %collective-permute-done.10 = bf16[896,256]{1,0:T(8,128)(2,1)S(1)} collective-permute-done((bf16[896,256]{1,0:T(8,128)(2,1)S(1)}, bf16[896,256]{1,0:T(8,128)(2,1)S(1)}, u32[]{:S(2)}, u32[]{:S(2)}) %collective-permute-start.10) | collective-permute-done | bytes 458784 | tf_op jit(solution)/shard_map/ppermute | solution.py:41
  20.8 0.8 copy-done.12
  22.0 1.9 collective-permute-start
  24.3 4.3 %collective-permute-done = bf16[1,4096]{1,0:T(2,128)(2,1)S(1)} collective-permute-done((bf16[1,4096]{1,0:T(2,128)(2,1)S(1)}, bf16[1,4096]{1,0:T(2,128)(2,1)S(1)}, u32[]{:S(2)}, u32[]{:S(2)}) %collective-permute-start) | collective-permute-done | bytes 8224 | tf_op jit(solution)/shard_map/ppermute | solution.py:47
  28.7 2.6 %collective-permute-start.3 = (bf16[2,32,4096]{2,1,0:T(8,128)(2,1)S(1)}, bf16[2,32,4096]{2,1,0:T(8,128)(2,1)S(1)}, u32[]{:S(2)}, u32[]{:S(2)}) collective-permute-start(bf16[2,32,4096]{2,1,0:T(8,128)(2,1)S(1)} %pad_maximum_fusion.2), channel_id=1, source_target_pairs={{0,18},{1,13},{4,22},{5,1},{8,26},{9,5},{12,30},{13,9},{16,0},{17,... | collective-permute-start | bytes 1572872 | tf_op jit(solution)/shard_map/ppermute | solution.py:29
  31.2 0.5 collective-permute-start.2
  31.8 0.6 collective-permute-start.1
  32.4 10.6 %collective-permute-done.3 = bf16[2,32,4096]{2,1,0:T(8,128)(2,1)S(1)} collective-permute-done((bf16[2,32,4096]{2,1,0:T(8,128)(2,1)S(1)}, bf16[2,32,4096]{2,1,0:T(8,128)(2,1)S(1)}, u32[]{:S(2)}, u32[]{:S(2)}) %collective-permute-start.3) | collective-permute-done | bytes 524320 | tf_op jit(solution)/shard_map/ppermute | solution.py:29
  43.1 3.7 %collective-permute-done.1 = bf16[2,32,4096]{2,1,0:T(8,128)(2,1)S(1)} collective-permute-done((bf16[2,32,4096]{2,1,0:T(8,128)(2,1)S(1)}, bf16[2,32,4096]{2,1,0:T(8,128)(2,1)S(1)}, u32[]{:S(2)}, u32[]{:S(2)}) %collective-permute-start.1) | collective-permute-done | bytes 524320 | tf_op jit(solution)/shard_map/ppermute | solution.py:29
  47.5 1.5 collective-permute-start.4
  48.9 1.7 collective-permute-start.6
  50.6 1.0 collective-permute-start.5
  51.6 9.9 %collective-permute-done.7.refs_3_ = bf16[128,4096]{1,0:T(8,128)(2,1)S(1)} collective-permute-done((bf16[128,4096]{1,0:T(8,128)(2,1)S(1)}, bf16[128,4096]{1,0:T(8,128)(2,1)S(1)}, u32[]{:S(2)}, u32[]{:S(2)}) %collective-permute-start.7) | collective-permute-done | bytes 1048608 | tf_op jit(solution)/shard_map/ppermute | solution.py:29
  61.5 2.2 %collective-permute-done.4.refs_1_ = bf16[128,4096]{1,0:T(8,128)(2,1)S(1)} collective-permute-done((bf16[128,4096]{1,0:T(8,128)(2,1)S(1)}, bf16[128,4096]{1,0:T(8,128)(2,1)S(1)}, u32[]{:S(2)}, u32[]{:S(2)}) %collective-permute-start.4) | collective-permute-done | bytes 1048608 | tf_op jit(solution)/shard_map/ppermute | solution.py:29
  63.7 11.1 %collective-permute-done.6.refs_5_ = bf16[128,4096]{1,0:T(8,128)(2,1)S(1)} collective-permute-done((bf16[128,4096]{1,0:T(8,128)(2,1)S(1)}, bf16[128,4096]{1,0:T(8,128)(2,1)S(1)}, u32[]{:S(2)}, u32[]{:S(2)}) %collective-permute-start.6) | collective-permute-done | bytes 1048608 | tf_op jit(solution)/shard_map/ppermute | solution.py:29
  74.8 1.0 copy-done.17
  75.8 1.2 collective-permute-start.11
  77.1 0.8 collective-permute-start.9
  77.9 0.7 collective-permute-start.8
  78.5 12.7 %collective-permute-done.9.refs_6_ = bf16[128,4096]{1,0:T(8,128)(2,1)S(1)} collective-permute-done((bf16[128,4096]{1,0:T(8,128)(2,1)}, bf16[128,4096]{1,0:T(8,128)(2,1)S(1)}, u32[]{:S(2)}, u32[]{:S(2)}) %collective-permute-start.9) | collective-permute-done | bytes 1048608 | tf_op jit(solution)/shard_map/ppermute | solution.py:29
  91.2 1.8 collective-permute-done.8.refs_2_
  93.1 1.0 copy-done.19
  94.0 1.8 copy-done.14
  95.8 20.5 %shard_map.101 = (bf16[128,4096]{1,0:T(8,128)(2,1)S(1)}, bf16[128,4096]{1,0:T(8,128)(2,1)S(1)}, bf16[128,4096]{1,0:T(8,128)(2,1)S(1)}, bf16[128,4096]{1,0:T(8,12...) custom-call(bf16[128,4096]{1,0:T(8,128)(2,1)} %copy-done.9, ...), custom_call_target="tpu_custom_call" | custom-call | flops 11274289152 | bytes 62914560 | tf_op jit(solution)/shard_map/pallas_call | solution.py:168
  116.4 1.0 collective-permute-start.14
  117.4 2.5 %collective-permute-start.12 = (bf16[128,4096]{1,0:T(8,128)(2,1)S(1)}, bf16[128,4096]{1,0:T(8,128)(2,1)S(1)}, u32[]{:S(2)}, u32[]{:S(2)}) collective-permute-start(bf16[128,4096]{1,0:T(8,128)(2,1)S(1)} %get-tuple-element.45), channel_id=1, source_target_pairs={{0,12},{1,19},{4,0},{5,23},{8,4},{9,27},{12,8},{13,31},{16,28},{17... | collective-permute-start | bytes 3145736 | tf_op jit(solution)/shard_map/ppermute | solution.py:29
  119.8 11.7 %collective-permute-done.12 = bf16[128,4096]{1,0:T(8,128)(2,1)S(1)} collective-permute-done((bf16[128,4096]{1,0:T(8,128)(2,1)S(1)}, bf16[128,4096]{1,0:T(8,128)(2,1)S(1)}, u32[]{:S(2)}, u32[]{:S(2)}) %collective-permute-start.12) | collective-permute-done | bytes 1048608 | tf_op jit(solution)/shard_map/ppermute | solution.py:29
  131.6 1.2 add_convert_fusion.4
  132.8 2.2 collective-permute-done.13
  135.0 1.2 add_convert_fusion.3
  136.2 2.7 %add_convert_fusion = bf16[8,896,256]{2,1,0:T(8,128)(2,1)} fusion(bf16[8,896,256]{2,1,0:T(8,128)(2,1)S(1)} %collective-permute-done.14, bf16[8,896,256]{2,1,0:T(8,128)(2,1)S(1)} %copy-done.6), kind=kLoop, calls=%fused_computation | loop fusion | flops 7340032 | bytes 11010048 | tf_op jit(solution)/shard_map/convert_element_type | solution.py:266
  139.0 2.7 %collective-permute-start.17 = (bf16[128,4096]{1,0:T(8,128)(2,1)}, bf16[128,4096]{1,0:T(8,128)(2,1)S(1)}, u32[]{:S(2)}, u32[]{:S(2)}) collective-permute-start(bf16[128,4096]{1,0:T(8,128)(2,1)} %get-tuple-element.52), channel_id=1, source_target_pairs={{0,12},{1,19},{4,0},{5,23},{8,4},{9,27},{12,8},{13,31},{16,28},{17... | collective-permute-start | bytes 3145736 | tf_op jit(solution)/shard_map/ppermute | solution.py:29
  141.7 1.4 collective-permute-start.18
  143.2 2.9 %collective-permute-done.19 = f32[4096]{0:T(1024)S(1)} collective-permute-done((f32[4096]{0:T(1024)S(1)}, f32[4096]{0:T(1024)S(1)}, u32[]{:S(2)}, u32[]{:S(2)}) %collective-permute-start.19) | collective-permute-done | bytes 16416 | tf_op jit(solution)/shard_map/ppermute | solution.py:232
  146.1 1.5 collective-permute-start.20
  147.6 2.3 %collective-permute-done.20 = f32[4096]{0:T(1024)S(1)} collective-permute-done((f32[4096]{0:T(1024)S(1)}, f32[4096]{0:T(1024)S(1)}, u32[]{:S(2)}, u32[]{:S(2)}) %collective-permute-start.20) | collective-permute-done | bytes 16416 | tf_op jit(solution)/shard_map/ppermute | solution.py:232
  149.9 3.7 %collective-permute-start.21 = (f32[4096]{0:T(1024)S(1)}, f32[4096]{0:T(1024)S(1)}, u32[]{:S(2)}, u32[]{:S(2)}) collective-permute-start(f32[4096]{0:T(1024)S(1)} %add.93), channel_id=1, source_target_pairs={{0,1},{1,0},{4,5},{5,4},{8,9},{9,8},{12,13},{13,12},{16,17},{17,16... | collective-permute-start | bytes 49160 | tf_op jit(solution)/shard_map/ppermute | solution.py:232
  153.6 0.8 collective-permute-done.21
  154.5 10.6 %collective-permute-done.22 = f32[4096]{0:T(1024)S(1)} collective-permute-done((f32[4096]{0:T(1024)S(1)}, f32[4096]{0:T(1024)S(1)}, u32[]{:S(2)}, u32[]{:S(2)}) %collective-permute-start.22) | collective-permute-done | bytes 16416 | tf_op jit(solution)/shard_map/ppermute | solution.py:232
  165.1 2.3 %collective-permute-start.23 = (f32[4096]{0:T(1024)S(1)}, f32[4096]{0:T(1024)S(1)}, u32[]{:S(2)}, u32[]{:S(2)}) collective-permute-start(f32[4096]{0:T(1024)S(1)} %add.95), channel_id=1, source_target_pairs={{0,2},{1,3},{4,6},{5,7},{8,10},{9,11},{12,14},{13,15},{16,18},{17,... | collective-permute-start | bytes 49160 | tf_op jit(solution)/shard_map/ppermute | solution.py:232
  167.4 1.8 collective-permute-done.23
  169.2 0.5 fusion.3
  170.4 2.7 %collective-permute-start.24 = (bf16[2,32,4096]{2,1,0:T(8,128)(2,1)S(1)}, bf16[2,32,4096]{2,1,0:T(8,128)(2,1)S(1)}, u32[]{:S(2)}, u32[]{:S(2)}) collective-permute-start(bf16[2,32,4096]{2,1,0:T(8,128)(2,1)S(1)} %get-tuple-element.70), channel_id=1, source_target_pairs={{0,18},{1,13},{4,22},{5,1},{8,26},{9,5},{12,30},{13,9},{16,0},{17,... | collective-permute-start | bytes 1572872 | tf_op jit(solution)/shard_map/ppermute | solution.py:29
  173.1 0.6 collective-permute-start.27
  173.7 11.5 %collective-permute-done.27 = f32[4096]{0:T(1024)S(1)} collective-permute-done((f32[4096]{0:T(1024)S(1)}, f32[4096]{0:T(1024)S(1)}, u32[]{:S(2)}, u32[]{:S(2)}) %collective-permute-start.27) | collective-permute-done | bytes 16416 | tf_op jit(solution)/shard_map/ppermute | solution.py:232
  185.1 2.3 %collective-permute-start.28 = (f32[4096]{0:T(1024)S(1)}, f32[4096]{0:T(1024)S(1)}, u32[]{:S(2)}, u32[]{:S(2)}) collective-permute-start(f32[4096]{0:T(1024)S(1)} %add.101), channel_id=1, source_target_pairs={{0,8},{1,9},{4,12},{5,13},{8,0},{9,1},{12,4},{13,5},{16,24},{17,25... | collective-permute-start | bytes 49160 | tf_op jit(solution)/shard_map/ppermute | solution.py:232
  187.4 1.8 collective-permute-done.28
  189.2 4.6 %collective-permute-start.29 = (f32[4096]{0:T(1024)S(1)}, f32[4096]{0:T(1024)S(1)}, u32[]{:S(2)}, u32[]{:S(2)}) collective-permute-start(f32[4096]{0:T(1024)S(1)} %add.102), channel_id=1, source_target_pairs={{0,128},{1,129},{4,132},{5,133},{8,136},{9,137},{12,140},{13,141},... | collective-permute-start | bytes 49160 | tf_op jit(solution)/shard_map/ppermute | solution.py:232
  193.8 1.9 collective-permute-done.29
  195.7 0.6 add.103
  196.4 0.7 copy-done.10
  197.3 1.7 convert_add_fusion
  199.3 2.1 collective-permute-start.30
  201.4 2.4 %collective-permute-start.31 = (bf16[896,256]{1,0:T(8,128)(2,1)S(1)}, bf16[896,256]{1,0:T(8,128)(2,1)S(1)}, u32[]{:S(2)}, u32[]{:S(2)}) collective-permute-start(bf16[896,256]{1,0:T(8,128)(2,1)S(1)} %bitcast.45), channel_id=1, source_target_pairs={{0,0},{1,16},{4,4},{5,20},{8,8},{9,24},{12,12},{13,28},{16,1},{17,... | collective-permute-start | bytes 1376264 | tf_op jit(solution)/shard_map/ppermute | solution.py:41
  203.8 1.5 fusion.1
  205.3 1.4 fusion
  206.8 4.4 %collective-permute-done.31 = bf16[896,256]{1,0:T(8,128)(2,1)S(1)} collective-permute-done((bf16[896,256]{1,0:T(8,128)(2,1)S(1)}, bf16[896,256]{1,0:T(8,128)(2,1)S(1)}, u32[]{:S(2)}, u32[]{:S(2)}) %collective-permute-start.31) | collective-permute-done | bytes 458784 | tf_op jit(solution)/shard_map/ppermute | solution.py:41
  211.2 0.8 multiply_bitcast_fusion
  212.0 0.8 slice_convert_fusion
  (93 shorter events, 3.4 us)
Async XLA Ops:
  7.2 14.6 %copy-start = (bf16[128,4096]{1,0:T(8,128)(2,1)S(1)}, bf16[128,4096]{1,0:T(8,128)(2,1)}, u32[]{:S(2)}) copy-start(bf16[128,4096]{1,0:T(8,128)(2,1)} %param.11) | copy-start | bytes 3145732
  7.2 16.8 %copy-start.2 = (bf16[128,4096]{1,0:T(8,128)(2,1)S(1)}, bf16[128,4096]{1,0:T(8,128)(2,1)}, u32[]{:S(2)}) copy-start(bf16[128,4096]{1,0:T(8,128)(2,1)} %param.6) | copy-start | bytes 3145732
  7.2 68.6 %all-gather.3.cloned.1.call-start = ((), (), s32[]{:S(2)}) async-start(), calls=%async_computation.2 | async-start | bytes 4128768 | tf_op jit(solution)/shard_map/all_gather | solution.py:246
  10.1 10.8 %collective-permute-start.10 = (bf16[896,256]{1,0:T(8,128)(2,1)S(1)}, bf16[896,256]{1,0:T(8,128)(2,1)S(1)}, u32[]{:S(2)}, u32[]{:S(2)}) collective-permute-start(bf16[896,256]{1,0:T(8,128)(2,1)S(1)} %pad_maximum_fusion.3), channel_id=1, source_target_pairs={{0,0},{1,16},{4,4},{5,20},{8,8},{9,24},{12,12},{13,28},{16,1},{17,... | collective-permute-start | bytes 1376264 | tf_op jit(solution)/shard_map/ppermute | solution.py:41
  20.8 0.8 copy-start.12
  21.6 174.7 %reduce-scatter.2.cloned.1.call-start = ((), (), s32[]{:S(2)}) async-start(), calls=%async_computation.1 | async-start | bytes 4128768 | tf_op jit(solution)/shard_map/reduce_scatter | solution.py:217
  22.0 6.6 %collective-permute-start = (bf16[1,4096]{1,0:T(2,128)(2,1)S(1)}, bf16[1,4096]{1,0:T(2,128)(2,1)S(1)}, u32[]{:S(2)}, u32[]{:S(2)}) collective-permute-start(bf16[1,4096]{1,0:T(2,128)(2,1)S(1)} %slice.65), channel_id=1, source_target_pairs={{1,0},{2,1},{3,2},{4,3},{5,4},{6,5},{7,6},{8,7},{9,8},{10,9},{11,1... | collective-permute-start | bytes 24584 | tf_op jit(solution)/shard_map/ppermute | solution.py:47
  24.3 22.5 %copy-start.4 = (bf16[31,4096]{1,0:T(8,128)(2,1)}, bf16[31,4096]{1,0:T(8,128)(2,1)S(1)}, u32[]{:S(2)}) copy-start(bf16[31,4096]{1,0:T(8,128)(2,1)S(1)} %slice.64) | copy-start | bytes 761860
  28.7 14.3 %collective-permute-start.3 = (bf16[2,32,4096]{2,1,0:T(8,128)(2,1)S(1)}, bf16[2,32,4096]{2,1,0:T(8,128)(2,1)S(1)}, u32[]{:S(2)}, u32[]{:S(2)}) collective-permute-start(bf16[2,32,4096]{2,1,0:T(8,128)(2,1)S(1)} %pad_maximum_fusion.2), channel_id=1, source_target_pairs={{0,18},{1,13},{4,22},{5,1},{8,26},{9,5},{12,30},{13,9},{16,0},{17,... | collective-permute-start | bytes 1572872 | tf_op jit(solution)/shard_map/ppermute | solution.py:29
  31.2 11.8 %collective-permute-start.2 = (bf16[2,32,4096]{2,1,0:T(8,128)(2,1)S(1)}, bf16[2,32,4096]{2,1,0:T(8,128)(2,1)S(1)}, u32[]{:S(2)}, u32[]{:S(2)}) collective-permute-start(bf16[2,32,4096]{2,1,0:T(8,128)(2,1)S(1)} %pad_maximum_fusion.2), channel_id=1, source_target_pairs={{0,2},{1,9},{4,6},{5,13},{8,10},{9,1},{12,14},{13,5},{16,18},{17,2... | collective-permute-start | bytes 1572872 | tf_op jit(solution)/shard_map/ppermute | solution.py:29
  31.8 15.0 %collective-permute-start.1 = (bf16[2,32,4096]{2,1,0:T(8,128)(2,1)S(1)}, bf16[2,32,4096]{2,1,0:T(8,128)(2,1)S(1)}, u32[]{:S(2)}, u32[]{:S(2)}) collective-permute-start(bf16[2,32,4096]{2,1,0:T(8,128)(2,1)S(1)} %pad_maximum_fusion.2), channel_id=1, source_target_pairs={{0,16},{1,5},{4,20},{5,9},{8,24},{9,13},{12,28},{13,1},{16,2},{17,... | collective-permute-start | bytes 1572872 | tf_op jit(solution)/shard_map/ppermute | solution.py:29
  47.3 45.8 %copy-start.8 = (bf16[128,4096]{1,0:T(8,128)(2,1)}, bf16[128,4096]{1,0:T(8,128)(2,1)S(1)}, u32[]{:S(2)}) copy-start(bf16[128,4096]{1,0:T(8,128)(2,1)S(1)} %concatenate.18.refs_4_) | copy-start | bytes 3145732
  47.4 27.5 %copy-start.9 = (bf16[128,4096]{1,0:T(8,128)(2,1)}, bf16[128,4096]{1,0:T(8,128)(2,1)S(1)}, u32[]{:S(2)}) copy-start(bf16[128,4096]{1,0:T(8,128)(2,1)S(1)} %pad_maximum_fusion.refs_0_) | copy-start | bytes 3145732
  47.4 14.1 %collective-permute-start.7 = (bf16[128,4096]{1,0:T(8,128)(2,1)S(1)}, bf16[128,4096]{1,0:T(8,128)(2,1)S(1)}, u32[]{:S(2)}, u32[]{:S(2)}) collective-permute-start(bf16[128,4096]{1,0:T(8,128)(2,1)S(1)} %pad_maximum_fusion.refs_0_), channel_id=1, source_target_pairs={{0,12},{1,19},{4,0},{5,23},{8,4},{9,27},{12,8},{13,31},{16,28},{17... | collective-permute-start | bytes 3145736 | tf_op jit(solution)/shard_map/ppermute | solution.py:29
  47.5 16.3 %collective-permute-start.4 = (bf16[128,4096]{1,0:T(8,128)(2,1)S(1)}, bf16[128,4096]{1,0:T(8,128)(2,1)S(1)}, u32[]{:S(2)}, u32[]{:S(2)}) collective-permute-start(bf16[128,4096]{1,0:T(8,128)(2,1)S(1)} %pad_maximum_fusion.refs_0_), channel_id=1, source_target_pairs={{0,4},{1,17},{4,8},{5,21},{8,12},{9,25},{12,0},{13,29},{16,20},{17... | collective-permute-start | bytes 3145736 | tf_op jit(solution)/shard_map/ppermute | solution.py:29
  48.9 25.9 %collective-permute-start.6 = (bf16[128,4096]{1,0:T(8,128)(2,1)S(1)}, bf16[128,4096]{1,0:T(8,128)(2,1)S(1)}, u32[]{:S(2)}, u32[]{:S(2)}) collective-permute-start(bf16[128,4096]{1,0:T(8,128)(2,1)S(1)} %concatenate.18.refs_4_), channel_id=1, source_target_pairs={{0,4},{1,17},{4,8},{5,21},{8,12},{9,25},{12,0},{13,29},{16,20},{17... | collective-permute-start | bytes 3145736 | tf_op jit(solution)/shard_map/ppermute | solution.py:29
  50.6 25.2 %collective-permute-start.5 = (bf16[128,4096]{1,0:T(8,128)(2,1)S(1)}, bf16[128,4096]{1,0:T(8,128)(2,1)}, u32[]{:S(2)}, u32[]{:S(2)}) collective-permute-start(bf16[128,4096]{1,0:T(8,128)(2,1)S(1)} %concatenate.18.refs_4_), channel_id=1, source_target_pairs={{0,12},{1,19},{4,0},{5,23},{8,4},{9,27},{12,8},{13,31},{16,28},{17... | collective-permute-start | bytes 3145736 | tf_op jit(solution)/shard_map/ppermute | solution.py:29
  61.5 31.5 %copy-start.15 = (bf16[128,4096]{1,0:T(8,128)(2,1)}, bf16[128,4096]{1,0:T(8,128)(2,1)S(1)}, u32[]{:S(2)}) copy-start(bf16[128,4096]{1,0:T(8,128)(2,1)S(1)} %collective-permute-done.7.refs_3_) | copy-start | bytes 3145732
  63.7 29.3 %copy-start.16 = (bf16[128,4096]{1,0:T(8,128)(2,1)}, bf16[128,4096]{1,0:T(8,128)(2,1)S(1)}, u32[]{:S(2)}) copy-start(bf16[128,4096]{1,0:T(8,128)(2,1)S(1)} %collective-permute-done.4.refs_1_) | copy-start | bytes 3145732
  74.8 1.0 copy-start.17
  75.8 17.2 %collective-permute-start.11 = (bf16[8,896,256]{2,1,0:T(8,128)(2,1)}, bf16[8,896,256]{2,1,0:T(8,128)(2,1)S(1)}, u32[]{:S(2)}, u32[]{:S(2)}) collective-permute-start(bf16[8,896,256]{2,1,0:T(8,128)(2,1)} %bitcast.43), channel_id=1, source_target_pairs={{0,1},{1,0},{4,5},{5,4},{8,9},{9,8},{12,13},{13,12},{16,17},{17,16... | collective-permute-start | bytes 11010056 | tf_op jit(solution)/shard_map/ppermute | solution.py:34
  77.1 14.2 %collective-permute-start.9 = (bf16[128,4096]{1,0:T(8,128)(2,1)}, bf16[128,4096]{1,0:T(8,128)(2,1)S(1)}, u32[]{:S(2)}, u32[]{:S(2)}) collective-permute-start(bf16[128,4096]{1,0:T(8,128)(2,1)} %collective-permute-done.5.refs_7_), channel_id=1, source_target_pairs={{0,12},{1,19},{4,0},{5,23},{8,4},{9,27},{12,8},{13,31},{16,28},{17... | collective-permute-start | bytes 3145736 | tf_op jit(solution)/shard_map/ppermute | solution.py:29
  77.9 15.2 %collective-permute-start.8 = (bf16[128,4096]{1,0:T(8,128)(2,1)S(1)}, bf16[128,4096]{1,0:T(8,128)(2,1)S(1)}, u32[]{:S(2)}, u32[]{:S(2)}) collective-permute-start(bf16[128,4096]{1,0:T(8,128)(2,1)S(1)} %collective-permute-done.4.refs_1_), channel_id=1, source_target_pairs={{0,4},{1,17},{4,8},{5,21},{8,12},{9,25},{12,0},{13,29},{16,20},{17... | collective-permute-start | bytes 3145736 | tf_op jit(solution)/shard_map/ppermute | solution.py:29
  91.2 1.8 copy-start.18
  93.0 1.0 copy-start.19
  94.0 1.8 copy-start.14
  116.4 18.6 %copy-start.7 = (bf16[128,4096]{1,0:T(8,128)(2,1)S(1)}, bf16[128,4096]{1,0:T(8,128)(2,1)}, u32[]{:S(2)}) copy-start(bf16[128,4096]{1,0:T(8,128)(2,1)} %get-tuple-element.46) | copy-start | bytes 3145732
  116.4 19.9 %collective-permute-start.14 = (bf16[8,896,256]{2,1,0:T(8,128)(2,1)}, bf16[8,896,256]{2,1,0:T(8,128)(2,1)S(1)}, u32[]{:S(2)}, u32[]{:S(2)}) collective-permute-start(bf16[8,896,256]{2,1,0:T(8,128)(2,1)} %get-tuple-element.49), channel_id=1, source_target_pairs={{0,1},{1,0},{4,5},{5,4},{8,9},{9,8},{12,13},{13,12},{16,17},{17,16... | collective-permute-start | bytes 11010056 | tf_op jit(solution)/shard_map/ppermute | solution.py:34
  117.4 14.2 %collective-permute-start.12 = (bf16[128,4096]{1,0:T(8,128)(2,1)S(1)}, bf16[128,4096]{1,0:T(8,128)(2,1)S(1)}, u32[]{:S(2)}, u32[]{:S(2)}) collective-permute-start(bf16[128,4096]{1,0:T(8,128)(2,1)S(1)} %get-tuple-element.45), channel_id=1, source_target_pairs={{0,12},{1,19},{4,0},{5,23},{8,4},{9,27},{12,8},{13,31},{16,28},{17... | collective-permute-start | bytes 3145736 | tf_op jit(solution)/shard_map/ppermute | solution.py:29
  119.8 15.2 %collective-permute-start.13 = (bf16[128,4096]{1,0:T(8,128)(2,1)}, bf16[128,4096]{1,0:T(8,128)(2,1)S(1)}, u32[]{:S(2)}, u32[]{:S(2)}) collective-permute-start(bf16[128,4096]{1,0:T(8,128)(2,1)} %get-tuple-element.47), channel_id=1, source_target_pairs={{0,4},{1,17},{4,8},{5,21},{8,12},{9,25},{12,0},{13,29},{16,20},{17... | collective-permute-start | bytes 3145736 | tf_op jit(solution)/shard_map/ppermute | solution.py:29
  131.6 4.6 %copy-start.6 = (bf16[8,896,256]{2,1,0:T(8,128)(2,1)S(1)}, bf16[8,896,256]{2,1,0:T(8,128)(2,1)}, u32[]{:S(2)}) copy-start(bf16[8,896,256]{2,1,0:T(8,128)(2,1)} %get-tuple-element.48) | copy-start | bytes 11010052
  138.9 4.2 %copy-start.13 = (f32[4096]{0:T(1024)S(1)}, f32[4096]{0:T(1024)}, u32[]{:S(2)}) copy-start(f32[4096]{0:T(1024)} %param.8) | copy-start | bytes 49156
  138.9 30.3 %collective-permute-start.16 = (bf16[128,4096]{1,0:T(8,128)(2,1)S(1)}, bf16[128,4096]{1,0:T(8,128)(2,1)S(1)}, u32[]{:S(2)}, u32[]{:S(2)}) collective-permute-start(bf16[128,4096]{1,0:T(8,128)(2,1)S(1)} %get-tuple-element.51), channel_id=1, source_target_pairs={{0,4},{1,17},{4,8},{5,21},{8,12},{9,25},{12,0},{13,29},{16,20},{17... | collective-permute-start | bytes 3145736 | tf_op jit(solution)/shard_map/ppermute | solution.py:29
  139.0 30.2 %collective-permute-start.17 = (bf16[128,4096]{1,0:T(8,128)(2,1)}, bf16[128,4096]{1,0:T(8,128)(2,1)S(1)}, u32[]{:S(2)}, u32[]{:S(2)}) collective-permute-start(bf16[128,4096]{1,0:T(8,128)(2,1)} %get-tuple-element.52), channel_id=1, source_target_pairs={{0,12},{1,19},{4,0},{5,23},{8,4},{9,27},{12,8},{13,31},{16,28},{17... | collective-permute-start | bytes 3145736 | tf_op jit(solution)/shard_map/ppermute | solution.py:29
  141.7 27.6 %collective-permute-start.15 = (bf16[128,4096]{1,0:T(8,128)(2,1)}, bf16[128,4096]{1,0:T(8,128)(2,1)S(1)}, u32[]{:S(2)}, u32[]{:S(2)}) collective-permute-start(bf16[128,4096]{1,0:T(8,128)(2,1)} %add_convert_fusion.4), channel_id=1, source_target_pairs={{0,12},{1,19},{4,0},{5,23},{8,4},{9,27},{12,8},{13,31},{16,28},{17... | collective-permute-start | bytes 3145736 | tf_op jit(solution)/shard_map/ppermute | solution.py:29
  141.7 27.5 %collective-permute-start.18 = (bf16[128,4096]{1,0:T(8,128)(2,1)}, bf16[128,4096]{1,0:T(8,128)(2,1)S(1)}, u32[]{:S(2)}, u32[]{:S(2)}) collective-permute-start(bf16[128,4096]{1,0:T(8,128)(2,1)} %add_convert_fusion.3), channel_id=1, source_target_pairs={{0,4},{1,17},{4,8},{5,21},{8,12},{9,25},{12,0},{13,29},{16,20},{17... | collective-permute-start | bytes 3145736 | tf_op jit(solution)/shard_map/ppermute | solution.py:29
  143.1 3.0 %collective-permute-start.19 = (f32[4096]{0:T(1024)S(1)}, f32[4096]{0:T(1024)S(1)}, u32[]{:S(2)}, u32[]{:S(2)}) collective-permute-start(f32[4096]{0:T(1024)S(1)} %div.35), channel_id=1, source_target_pairs={{0,32},{1,33},{4,36},{5,37},{8,40},{9,41},{12,44},{13,45},{16,48},... | collective-permute-start | bytes 49160 | tf_op jit(solution)/shard_map/ppermute | solution.py:232
  146.1 3.8 %collective-permute-start.20 = (f32[4096]{0:T(1024)S(1)}, f32[4096]{0:T(1024)S(1)}, u32[]{:S(2)}, u32[]{:S(2)}) collective-permute-start(f32[4096]{0:T(1024)S(1)} %add.92), channel_id=1, source_target_pairs={{0,64},{1,65},{4,68},{5,69},{8,72},{9,73},{12,76},{13,77},{16,80},... | collective-permute-start | bytes 49160 | tf_op jit(solution)/shard_map/ppermute | solution.py:232
  149.9 4.6 %collective-permute-start.21 = (f32[4096]{0:T(1024)S(1)}, f32[4096]{0:T(1024)S(1)}, u32[]{:S(2)}, u32[]{:S(2)}) collective-permute-start(f32[4096]{0:T(1024)S(1)} %add.93), channel_id=1, source_target_pairs={{0,1},{1,0},{4,5},{5,4},{8,9},{9,8},{12,13},{13,12},{16,17},{17,16... | collective-permute-start | bytes 49160 | tf_op jit(solution)/shard_map/ppermute | solution.py:232
  154.5 10.6 %collective-permute-start.22 = (f32[4096]{0:T(1024)S(1)}, f32[4096]{0:T(1024)S(1)}, u32[]{:S(2)}, u32[]{:S(2)}) collective-permute-start(f32[4096]{0:T(1024)S(1)} %add.94), channel_id=1, source_target_pairs={{0,16},{1,17},{4,20},{5,21},{8,24},{9,25},{12,28},{13,29},{16,0},{... | collective-permute-start | bytes 49160 | tf_op jit(solution)/shard_map/ppermute | solution.py:232
  165.1 4.1 %collective-permute-start.23 = (f32[4096]{0:T(1024)S(1)}, f32[4096]{0:T(1024)S(1)}, u32[]{:S(2)}, u32[]{:S(2)}) collective-permute-start(f32[4096]{0:T(1024)S(1)} %add.95), channel_id=1, source_target_pairs={{0,2},{1,3},{4,6},{5,7},{8,10},{9,11},{12,14},{13,15},{16,18},{17,... | collective-permute-start | bytes 49160 | tf_op jit(solution)/shard_map/ppermute | solution.py:232
  170.3 26.0 %collective-permute-start.26 = (bf16[2,32,4096]{2,1,0:T(8,128)(2,1)S(1)}, bf16[2,32,4096]{2,1,0:T(8,128)(2,1)S(1)}, u32[]{:S(2)}, u32[]{:S(2)}) collective-permute-start(bf16[2,32,4096]{2,1,0:T(8,128)(2,1)S(1)} %get-tuple-element.69), channel_id=1, source_target_pairs={{0,16},{1,5},{4,20},{5,9},{8,24},{9,13},{12,28},{13,1},{16,2},{17,... | collective-permute-start | bytes 1572872 | tf_op jit(solution)/shard_map/ppermute | solution.py:29
  170.4 25.9 %collective-permute-start.24 = (bf16[2,32,4096]{2,1,0:T(8,128)(2,1)S(1)}, bf16[2,32,4096]{2,1,0:T(8,128)(2,1)S(1)}, u32[]{:S(2)}, u32[]{:S(2)}) collective-permute-start(bf16[2,32,4096]{2,1,0:T(8,128)(2,1)S(1)} %get-tuple-element.70), channel_id=1, source_target_pairs={{0,18},{1,13},{4,22},{5,1},{8,26},{9,5},{12,30},{13,9},{16,0},{17,... | collective-permute-start | bytes 1572872 | tf_op jit(solution)/shard_map/ppermute | solution.py:29
  173.1 23.3 %collective-permute-start.25 = (bf16[2,32,4096]{2,1,0:T(8,128)(2,1)S(1)}, bf16[2,32,4096]{2,1,0:T(8,128)(2,1)}, u32[]{:S(2)}, u32[]{:S(2)}) collective-permute-start(bf16[2,32,4096]{2,1,0:T(8,128)(2,1)S(1)} %get-tuple-element.71), channel_id=1, source_target_pairs={{0,2},{1,9},{4,6},{5,13},{8,10},{9,1},{12,14},{13,5},{16,18},{17,2... | collective-permute-start | bytes 1572872 | tf_op jit(solution)/shard_map/ppermute | solution.py:29
  173.1 12.0 %collective-permute-start.27 = (f32[4096]{0:T(1024)S(1)}, f32[4096]{0:T(1024)S(1)}, u32[]{:S(2)}, u32[]{:S(2)}) collective-permute-start(f32[4096]{0:T(1024)S(1)} %add.96), channel_id=1, source_target_pairs={{0,4},{1,5},{4,0},{5,1},{8,12},{9,13},{12,8},{13,9},{16,20},{17,21... | collective-permute-start | bytes 49160 | tf_op jit(solution)/shard_map/ppermute | solution.py:232
  185.1 4.1 %collective-permute-start.28 = (f32[4096]{0:T(1024)S(1)}, f32[4096]{0:T(1024)S(1)}, u32[]{:S(2)}, u32[]{:S(2)}) collective-permute-start(f32[4096]{0:T(1024)S(1)} %add.101), channel_id=1, source_target_pairs={{0,8},{1,9},{4,12},{5,13},{8,0},{9,1},{12,4},{13,5},{16,24},{17,25... | collective-permute-start | bytes 49160 | tf_op jit(solution)/shard_map/ppermute | solution.py:232
  189.2 6.5 %collective-permute-start.29 = (f32[4096]{0:T(1024)S(1)}, f32[4096]{0:T(1024)S(1)}, u32[]{:S(2)}, u32[]{:S(2)}) collective-permute-start(f32[4096]{0:T(1024)S(1)} %add.102), channel_id=1, source_target_pairs={{0,128},{1,129},{4,132},{5,133},{8,136},{9,137},{12,140},{13,141},... | collective-permute-start | bytes 49160 | tf_op jit(solution)/shard_map/ppermute | solution.py:232
  196.3 0.8 copy-start.10
  196.3 1.0 copy-start.11
  197.3 4.1 %copy-start.20 = (bf16[1,896,256]{2,1,0:T(8,128)(2,1)S(1)}, bf16[1,896,256]{2,1,0:T(8,128)(2,1)}, u32[]{:S(2)}) copy-start(bf16[1,896,256]{2,1,0:T(8,128)(2,1)} %reduce-scatter.2.cloned.1.call-done) | copy-start | bytes 1376260
  197.3 6.5 %copy-start.1 = (bf16[128,4096]{1,0:T(8,128)(2,1)S(1)}, bf16[128,4096]{1,0:T(8,128)(2,1)}, u32[]{:S(2)}) copy-start(bf16[128,4096]{1,0:T(8,128)(2,1)} %param.11) | copy-start | bytes 3145732
  197.3 6.5 %copy-start.5 = (bf16[31,4096]{1,0:T(8,128)(2,1)S(1)}, bf16[31,4096]{1,0:T(8,128)(2,1)}, u32[]{:S(2)}) copy-start(bf16[31,4096]{1,0:T(8,128)(2,1)} %copy-done.4) | copy-start | bytes 761860
  199.0 6.3 %copy-start.3 = (bf16[128,4096]{1,0:T(8,128)(2,1)S(1)}, bf16[128,4096]{1,0:T(8,128)(2,1)}, u32[]{:S(2)}) copy-start(bf16[128,4096]{1,0:T(8,128)(2,1)} %param.6) | copy-start | bytes 3145732
  199.3 6.0 %collective-permute-start.30 = (bf16[1,4096]{1,0:T(2,128)(2,1)S(1)}, bf16[1,4096]{1,0:T(2,128)(2,1)S(1)}, u32[]{:S(2)}, u32[]{:S(2)}) collective-permute-start(bf16[1,4096]{1,0:T(2,128)(2,1)S(1)} %slice.78), channel_id=1, source_target_pairs={{0,1},{1,2},{2,3},{3,4},{4,5},{5,6},{6,7},{7,8},{8,9},{9,10},{10,1... | collective-permute-start | bytes 24584 | tf_op jit(solution)/shard_map/ppermute | solution.py:47
  201.4 9.8 %collective-permute-start.31 = (bf16[896,256]{1,0:T(8,128)(2,1)S(1)}, bf16[896,256]{1,0:T(8,128)(2,1)S(1)}, u32[]{:S(2)}, u32[]{:S(2)}) collective-permute-start(bf16[896,256]{1,0:T(8,128)(2,1)S(1)} %bitcast.45), channel_id=1, source_target_pairs={{0,0},{1,16},{4,4},{5,20},{8,8},{9,24},{12,12},{13,28},{16,1},{17,... | collective-permute-start | bytes 1376264 | tf_op jit(solution)/shard_map/ppermute | solution.py:41
Sparse Core Ops, SparseCore 0:
  21.8 52.5 all-gather.2
  139.0 47.4 reduce-scatter.1

commit v9 on v8

--- a/solution.py
+++ b/solution.py
@@ -213,17 +213,17 @@
     d2, n2 = shift(d2, second=-1), shift(n2, second=1)
     n1, d3 = shift(n1, second=-1), shift(d3, second=1)
     d1, n3 = add_all([d1, d2]).astype(bf), add_all([n3, n2]).astype(bf)
-    d1, n3, weight_part = lax.optimization_barrier((d1, n3, weight_part))
+    gain = pair(pair(pair(gain_part, z=1), z=2), z=4)
+    d1, n3, weight_part, gain = lax.optimization_barrier((d1, n3, weight_part, gain))
     weight_sum = lax.psum_scatter(weight_part, "z", scatter_dimension=0, tiled=False)
     d1, n3 = shift(d1, second=-1), shift(n3, second=1)
-    gain = pair(pair(pair(pair(pair(gain_part, z=1), z=2), c=1), y=1), y=2)
+    gain = pair(pair(pair(pair(pair(gain, c=1), y=1), y=2), x=1), x=2)
     d1, d3, n1, n3, gain = lax.optimization_barrier((d1, d3, n1, n3, gain))
     both = jnp.stack([add_all([d0, d1, d3]).astype(bf), add_all([n0, n1, n3]).astype(bf)])
     rows = both.shape[1] // 4
     both = [both[:, d * rows : (d + 1) * rows] for d in range(4)]
     arrived = [shift(both[d], first=-d) for d in (1, 2, 3)] + [weight_sum]
-    gain = pair(pair(pair(gain, x=1), x=2), z=4)
-    *arrived, weight_sum, gain = lax.optimization_barrier([*arrived, gain])
+    *arrived, weight_sum = lax.optimization_barrier(arrived)
     return add_all([both[0], *arrived]), gain, weight_sum
 
 

time: 220 us -> 217 us (0.986)
  no operation moved by 1% of the time
where the time goes in v9:
time: 217 us
  waiting for transfers between devices  111 us (51%)
  starting transfers between devices  46.6 us (21%)
  Pallas kernels  20.5 us (9%)
  between operations  14.5 us (7%)
  other arithmetic  13.3 us (6%)
  local copies, waits for them, and re-layouts  7.22 us (3%)
  matrix products  3.44 us (2%)
    ppermute x18, waiting for transfers between devices, shift(): return lax.ppermute(value, AXES, pairs)  65.1 us
    ppermute x8, waiting for transfers between devices, pair(): return value + lax.ppermute(value, AXES, pairs)  32.3 us
    pallas_call x1, Pallas kernels, block(): pl.pallas_call(functools.partial(block_kernel, chunks), out_shape=[jax.Sh...  20.5 us
    ppermute x18, starting transfers between devices, shift(): return lax.ppermute(value, AXES, pairs)  19 us
    ppermute x8, starting transfers between devices, pair(): return value + lax.ppermute(value, AXES, pairs)  14.3 us
    ppermute x2, waiting for transfers between devices, swap_low(): return lax.ppermute(value, AXES, pairs)  9.61 us
    ppermute x2, starting transfers between devices, swap_low(): return lax.ppermute(value, AXES, pairs)  6.93 us
    unnamed x42, local copies, waits for them, and re-layouts  5.49 us
  transfers between devices with their start and end apart: 34, of which 20 were waited for; matrix products, arithmetic and copies ran while one was open for 4% of the time, Pallas kernels for 0%

profile of v9, /device:TPU:1, one launch (start us, length us, event | category | flops | bytes accessed | tf_op | source)
XLA Modules:
  0.0 216.9 jit_solution(13903170947245722207)
XLA Ops:
  7.2 0.9 dynamic_slice.3
  8.1 1.0 fusion.20
  9.1 1.0 pad_maximum_fusion.3
  10.1 4.6 %collective-permute-start.10 = (bf16[896,256]{1,0:T(8,128)(2,1)S(1)}, bf16[896,256]{1,0:T(8,128)(2,1)S(1)}, u32[]{:S(2)}, u32[]{:S(2)}) collective-permute-start(bf16[896,256]{1,0:T(8,128)(2,1)S(1)} %pad_maximum_fusion.3), channel_id=1, source_target_pairs={{0,0},{1,16},{4,4},{5,20},{8,8},{9,24},{12,12},{13,28},{16,1},{17,... | collective-permute-start | bytes 1376264 | tf_op jit(solution)/shard_map/ppermute | solution.py:41
  14.7 0.7 convert_subtract_fusion
  15.8 5.1 %collective-permute-done.10 = bf16[896,256]{1,0:T(8,128)(2,1)S(1)} collective-permute-done((bf16[896,256]{1,0:T(8,128)(2,1)S(1)}, bf16[896,256]{1,0:T(8,128)(2,1)S(1)}, u32[]{:S(2)}, u32[]{:S(2)}) %collective-permute-start.10) | collective-permute-done | bytes 458784 | tf_op jit(solution)/shard_map/ppermute | solution.py:41
  20.8 0.8 copy-done.12
  22.0 1.9 collective-permute-start
  24.3 4.3 %collective-permute-done = bf16[1,4096]{1,0:T(2,128)(2,1)S(1)} collective-permute-done((bf16[1,4096]{1,0:T(2,128)(2,1)S(1)}, bf16[1,4096]{1,0:T(2,128)(2,1)S(1)}, u32[]{:S(2)}, u32[]{:S(2)}) %collective-permute-start) | collective-permute-done | bytes 8224 | tf_op jit(solution)/shard_map/ppermute | solution.py:47
  28.7 2.6 %collective-permute-start.3 = (bf16[2,32,4096]{2,1,0:T(8,128)(2,1)S(1)}, bf16[2,32,4096]{2,1,0:T(8,128)(2,1)S(1)}, u32[]{:S(2)}, u32[]{:S(2)}) collective-permute-start(bf16[2,32,4096]{2,1,0:T(8,128)(2,1)S(1)} %pad_maximum_fusion.2), channel_id=1, source_target_pairs={{0,18},{1,13},{4,22},{5,1},{8,26},{9,5},{12,30},{13,9},{16,0},{17,... | collective-permute-start | bytes 1572872 | tf_op jit(solution)/shard_map/ppermute | solution.py:29
  31.2 0.5 collective-permute-start.2
  31.8 0.6 collective-permute-start.1
  32.4 10.6 %collective-permute-done.3 = bf16[2,32,4096]{2,1,0:T(8,128)(2,1)S(1)} collective-permute-done((bf16[2,32,4096]{2,1,0:T(8,128)(2,1)S(1)}, bf16[2,32,4096]{2,1,0:T(8,128)(2,1)S(1)}, u32[]{:S(2)}, u32[]{:S(2)}) %collective-permute-start.3) | collective-permute-done | bytes 524320 | tf_op jit(solution)/shard_map/ppermute | solution.py:29
  43.1 3.7 %collective-permute-done.1 = bf16[2,32,4096]{2,1,0:T(8,128)(2,1)S(1)} collective-permute-done((bf16[2,32,4096]{2,1,0:T(8,128)(2,1)S(1)}, bf16[2,32,4096]{2,1,0:T(8,128)(2,1)S(1)}, u32[]{:S(2)}, u32[]{:S(2)}) %collective-permute-start.1) | collective-permute-done | bytes 524320 | tf_op jit(solution)/shard_map/ppermute | solution.py:29
  47.5 1.5 collective-permute-start.4
  48.9 1.7 collective-permute-start.6
  50.6 1.0 collective-permute-start.5
  51.6 9.9 %collective-permute-done.7.refs_3_ = bf16[128,4096]{1,0:T(8,128)(2,1)S(1)} collective-permute-done((bf16[128,4096]{1,0:T(8,128)(2,1)S(1)}, bf16[128,4096]{1,0:T(8,128)(2,1)S(1)}, u32[]{:S(2)}, u32[]{:S(2)}) %collective-permute-start.7) | collective-permute-done | bytes 1048608 | tf_op jit(solution)/shard_map/ppermute | solution.py:29
  61.5 2.2 %collective-permute-done.4.refs_1_ = bf16[128,4096]{1,0:T(8,128)(2,1)S(1)} collective-permute-done((bf16[128,4096]{1,0:T(8,128)(2,1)S(1)}, bf16[128,4096]{1,0:T(8,128)(2,1)S(1)}, u32[]{:S(2)}, u32[]{:S(2)}) %collective-permute-start.4) | collective-permute-done | bytes 1048608 | tf_op jit(solution)/shard_map/ppermute | solution.py:29
  63.7 11.1 %collective-permute-done.6.refs_5_ = bf16[128,4096]{1,0:T(8,128)(2,1)S(1)} collective-permute-done((bf16[128,4096]{1,0:T(8,128)(2,1)S(1)}, bf16[128,4096]{1,0:T(8,128)(2,1)S(1)}, u32[]{:S(2)}, u32[]{:S(2)}) %collective-permute-start.6) | collective-permute-done | bytes 1048608 | tf_op jit(solution)/shard_map/ppermute | solution.py:29
  74.8 1.0 copy-done.17
  75.8 1.2 collective-permute-start.11
  77.1 0.8 collective-permute-start.9
  77.9 0.7 collective-permute-start.8
  78.5 12.7 %collective-permute-done.9.refs_6_ = bf16[128,4096]{1,0:T(8,128)(2,1)S(1)} collective-permute-done((bf16[128,4096]{1,0:T(8,128)(2,1)}, bf16[128,4096]{1,0:T(8,128)(2,1)S(1)}, u32[]{:S(2)}, u32[]{:S(2)}) %collective-permute-start.9) | collective-permute-done | bytes 1048608 | tf_op jit(solution)/shard_map/ppermute | solution.py:29
  91.2 1.8 collective-permute-done.8.refs_2_
  93.1 1.0 copy-done.19
  94.0 1.8 copy-done.14
  95.8 20.5 %shard_map.101 = (bf16[128,4096]{1,0:T(8,128)(2,1)S(1)}, bf16[128,4096]{1,0:T(8,128)(2,1)S(1)}, bf16[128,4096]{1,0:T(8,128)(2,1)S(1)}, bf16[128,4096]{1,0:T(8,12...) custom-call(bf16[128,4096]{1,0:T(8,128)(2,1)} %copy-done.9, ...), custom_call_target="tpu_custom_call" | custom-call | flops 11274289152 | bytes 62914560 | tf_op jit(solution)/shard_map/pallas_call | solution.py:168
  116.4 1.0 collective-permute-start.14
  117.4 2.5 %collective-permute-start.12 = (bf16[128,4096]{1,0:T(8,128)(2,1)S(1)}, bf16[128,4096]{1,0:T(8,128)(2,1)S(1)}, u32[]{:S(2)}, u32[]{:S(2)}) collective-permute-start(bf16[128,4096]{1,0:T(8,128)(2,1)S(1)} %get-tuple-element.45), channel_id=1, source_target_pairs={{0,12},{1,19},{4,0},{5,23},{8,4},{9,27},{12,8},{13,31},{16,28},{17... | collective-permute-start | bytes 3145736 | tf_op jit(solution)/shard_map/ppermute | solution.py:29
  120.1 2.8 %collective-permute-done.15 = f32[4096]{0:T(1024)S(1)} collective-permute-done((f32[4096]{0:T(1024)S(1)}, f32[4096]{0:T(1024)S(1)}, u32[]{:S(2)}, u32[]{:S(2)}) %collective-permute-start.15) | collective-permute-done | bytes 16416 | tf_op jit(solution)/shard_map/ppermute | solution.py:232
  122.9 1.6 collective-permute-start.16
  124.5 2.2 %collective-permute-done.16 = f32[4096]{0:T(1024)S(1)} collective-permute-done((f32[4096]{0:T(1024)S(1)}, f32[4096]{0:T(1024)S(1)}, u32[]{:S(2)}, u32[]{:S(2)}) %collective-permute-start.16) | collective-permute-done | bytes 16416 | tf_op jit(solution)/shard_map/ppermute | solution.py:232
  126.7 5.4 %collective-permute-start.17 = (f32[4096]{0:T(1024)S(1)}, f32[4096]{0:T(1024)S(1)}, u32[]{:S(2)}, u32[]{:S(2)}) collective-permute-start(f32[4096]{0:T(1024)S(1)} %add.93), channel_id=1, source_target_pairs={{0,128},{1,129},{4,132},{5,133},{8,136},{9,137},{12,140},{13,141},... | collective-permute-start | bytes 49160 | tf_op jit(solution)/shard_map/ppermute | solution.py:232
  132.0 1.1 collective-permute-done.17
  133.2 1.2 add_convert_fusion.4
  134.4 0.8 collective-permute-done.13
  135.2 1.2 add_convert_fusion.3
  136.4 2.7 %add_convert_fusion = bf16[8,896,256]{2,1,0:T(8,128)(2,1)} fusion(bf16[8,896,256]{2,1,0:T(8,128)(2,1)S(1)} %collective-permute-done.14, bf16[8,896,256]{2,1,0:T(8,128)(2,1)S(1)} %copy-done.6), kind=kLoop, calls=%fused_computation | loop fusion | flops 7340032 | bytes 11010048 | tf_op jit(solution)/shard_map/convert_element_type | solution.py:266
  139.2 2.7 %collective-permute-start.20 = (bf16[128,4096]{1,0:T(8,128)(2,1)}, bf16[128,4096]{1,0:T(8,128)(2,1)S(1)}, u32[]{:S(2)}, u32[]{:S(2)}) collective-permute-start(bf16[128,4096]{1,0:T(8,128)(2,1)} %get-tuple-element.53), channel_id=1, source_target_pairs={{0,12},{1,19},{4,0},{5,23},{8,4},{9,27},{12,8},{13,31},{16,28},{17... | collective-permute-start | bytes 3145736 | tf_op jit(solution)/shard_map/ppermute | solution.py:29
  141.9 0.7 collective-permute-start.18
  142.6 0.8 collective-permute-start.21
  143.3 3.6 %collective-permute-start.22 = (f32[4096]{0:T(1024)S(1)}, f32[4096]{0:T(1024)S(1)}, u32[]{:S(2)}, u32[]{:S(2)}) collective-permute-start(f32[4096]{0:T(1024)S(1)} %add.94), channel_id=1, source_target_pairs={{0,1},{1,0},{4,5},{5,4},{8,9},{9,8},{12,13},{13,12},{16,17},{17,16... | collective-permute-start | bytes 49160 | tf_op jit(solution)/shard_map/ppermute | solution.py:232
  146.9 0.8 collective-permute-done.22
  147.7 0.6 collective-permute-start.23
  148.4 16.9 %collective-permute-done.23 = f32[4096]{0:T(1024)S(1)} collective-permute-done((f32[4096]{0:T(1024)S(1)}, f32[4096]{0:T(1024)S(1)}, u32[]{:S(2)}, u32[]{:S(2)}) %collective-permute-start.23) | collective-permute-done | bytes 16416 | tf_op jit(solution)/shard_map/ppermute | solution.py:232
  165.3 3.0 %collective-permute-start.24 = (f32[4096]{0:T(1024)S(1)}, f32[4096]{0:T(1024)S(1)}, u32[]{:S(2)}, u32[]{:S(2)}) collective-permute-start(f32[4096]{0:T(1024)S(1)} %add.96), channel_id=1, source_target_pairs={{0,2},{1,3},{4,6},{5,7},{8,10},{9,11},{12,14},{13,15},{16,18},{17,... | collective-permute-start | bytes 49160 | tf_op jit(solution)/shard_map/ppermute | solution.py:232
  168.3 1.1 collective-permute-done.24
  169.5 3.1 %collective-permute-done.25 = f32[4096]{0:T(1024)S(1)} collective-permute-done((f32[4096]{0:T(1024)S(1)}, f32[4096]{0:T(1024)S(1)}, u32[]{:S(2)}, u32[]{:S(2)}) %collective-permute-start.25) | collective-permute-done | bytes 16416 | tf_op jit(solution)/shard_map/ppermute | solution.py:232
  172.6 4.1 %collective-permute-done.26 = f32[4096]{0:T(1024)S(1)} collective-permute-done((f32[4096]{0:T(1024)S(1)}, f32[4096]{0:T(1024)S(1)}, u32[]{:S(2)}, u32[]{:S(2)}) %collective-permute-start.26) | collective-permute-done | bytes 16416 | tf_op jit(solution)/shard_map/ppermute | solution.py:232
  176.7 0.6 add.99
  178.4 0.6 collective-permute-start.29
  179.0 2.4 %collective-permute-start.27 = (bf16[2,32,4096]{2,1,0:T(8,128)(2,1)S(1)}, bf16[2,32,4096]{2,1,0:T(8,128)(2,1)S(1)}, u32[]{:S(2)}, u32[]{:S(2)}) collective-permute-start(bf16[2,32,4096]{2,1,0:T(8,128)(2,1)S(1)} %get-tuple-element.70), channel_id=1, source_target_pairs={{0,18},{1,13},{4,22},{5,1},{8,26},{9,5},{12,30},{13,9},{16,0},{17,... | collective-permute-start | bytes 1572872 | tf_op jit(solution)/shard_map/ppermute | solution.py:29
  181.4 12.2 %collective-permute-done.29 = bf16[2,32,4096]{2,1,0:T(8,128)(2,1)S(1)} collective-permute-done((bf16[2,32,4096]{2,1,0:T(8,128)(2,1)S(1)}, bf16[2,32,4096]{2,1,0:T(8,128)(2,1)S(1)}, u32[]{:S(2)}, u32[]{:S(2)}) %collective-permute-start.29) | collective-permute-done | bytes 524320 | tf_op jit(solution)/shard_map/ppermute | solution.py:29
  193.6 0.8 copy-done.10
  194.5 1.7 convert_add_fusion
  196.6 2.1 collective-permute-start.30
  198.6 2.3 %collective-permute-start.31 = (bf16[896,256]{1,0:T(8,128)(2,1)S(1)}, bf16[896,256]{1,0:T(8,128)(2,1)S(1)}, u32[]{:S(2)}, u32[]{:S(2)}) collective-permute-start(bf16[896,256]{1,0:T(8,128)(2,1)S(1)} %bitcast.45), channel_id=1, source_target_pairs={{0,0},{1,16},{4,4},{5,20},{8,8},{9,24},{12,12},{13,28},{16,1},{17,... | collective-permute-start | bytes 1376264 | tf_op jit(solution)/shard_map/ppermute | solution.py:41
  201.0 1.5 fusion.1
  202.5 1.4 fusion
  203.9 4.5 %collective-permute-done.31 = bf16[896,256]{1,0:T(8,128)(2,1)S(1)} collective-permute-done((bf16[896,256]{1,0:T(8,128)(2,1)S(1)}, bf16[896,256]{1,0:T(8,128)(2,1)S(1)}, u32[]{:S(2)}, u32[]{:S(2)}) %collective-permute-start.31) | collective-permute-done | bytes 458784 | tf_op jit(solution)/shard_map/ppermute | solution.py:41
  208.4 0.8 multiply_bitcast_fusion
  209.2 0.8 slice_convert_fusion
  (93 shorter events, 3.9 us)
Async XLA Ops:
  7.2 14.6 %copy-start = (bf16[128,4096]{1,0:T(8,128)(2,1)S(1)}, bf16[128,4096]{1,0:T(8,128)(2,1)}, u32[]{:S(2)}) copy-start(bf16[128,4096]{1,0:T(8,128)(2,1)} %param.11) | copy-start | bytes 3145732
  7.2 16.8 %copy-start.2 = (bf16[128,4096]{1,0:T(8,128)(2,1)S(1)}, bf16[128,4096]{1,0:T(8,128)(2,1)}, u32[]{:S(2)}) copy-start(bf16[128,4096]{1,0:T(8,128)(2,1)} %param.6) | copy-start | bytes 3145732
  7.2 68.6 %all-gather.3.cloned.1.call-start = ((), (), s32[]{:S(2)}) async-start(), calls=%async_computation.2 | async-start | bytes 4128768 | tf_op jit(solution)/shard_map/all_gather | solution.py:246
  10.1 10.8 %collective-permute-start.10 = (bf16[896,256]{1,0:T(8,128)(2,1)S(1)}, bf16[896,256]{1,0:T(8,128)(2,1)S(1)}, u32[]{:S(2)}, u32[]{:S(2)}) collective-permute-start(bf16[896,256]{1,0:T(8,128)(2,1)S(1)} %pad_maximum_fusion.3), channel_id=1, source_target_pairs={{0,0},{1,16},{4,4},{5,20},{8,8},{9,24},{12,12},{13,28},{16,1},{17,... | collective-permute-start | bytes 1376264 | tf_op jit(solution)/shard_map/ppermute | solution.py:41
  20.8 0.8 copy-start.12
  21.6 172.0 %reduce-scatter.2.cloned.1.call-start = ((), (), s32[]{:S(2)}) async-start(), calls=%async_computation.1 | async-start | bytes 4128768 | tf_op jit(solution)/shard_map/reduce_scatter | solution.py:218
  22.0 6.6 %collective-permute-start = (bf16[1,4096]{1,0:T(2,128)(2,1)S(1)}, bf16[1,4096]{1,0:T(2,128)(2,1)S(1)}, u32[]{:S(2)}, u32[]{:S(2)}) collective-permute-start(bf16[1,4096]{1,0:T(2,128)(2,1)S(1)} %slice.65), channel_id=1, source_target_pairs={{1,0},{2,1},{3,2},{4,3},{5,4},{6,5},{7,6},{8,7},{9,8},{10,9},{11,1... | collective-permute-start | bytes 24584 | tf_op jit(solution)/shard_map/ppermute | solution.py:47
  24.3 22.5 %copy-start.4 = (bf16[31,4096]{1,0:T(8,128)(2,1)}, bf16[31,4096]{1,0:T(8,128)(2,1)S(1)}, u32[]{:S(2)}) copy-start(bf16[31,4096]{1,0:T(8,128)(2,1)S(1)} %slice.64) | copy-start | bytes 761860
  28.7 14.3 %collective-permute-start.3 = (bf16[2,32,4096]{2,1,0:T(8,128)(2,1)S(1)}, bf16[2,32,4096]{2,1,0:T(8,128)(2,1)S(1)}, u32[]{:S(2)}, u32[]{:S(2)}) collective-permute-start(bf16[2,32,4096]{2,1,0:T(8,128)(2,1)S(1)} %pad_maximum_fusion.2), channel_id=1, source_target_pairs={{0,18},{1,13},{4,22},{5,1},{8,26},{9,5},{12,30},{13,9},{16,0},{17,... | collective-permute-start | bytes 1572872 | tf_op jit(solution)/shard_map/ppermute | solution.py:29
  31.2 11.8 %collective-permute-start.2 = (bf16[2,32,4096]{2,1,0:T(8,128)(2,1)S(1)}, bf16[2,32,4096]{2,1,0:T(8,128)(2,1)S(1)}, u32[]{:S(2)}, u32[]{:S(2)}) collective-permute-start(bf16[2,32,4096]{2,1,0:T(8,128)(2,1)S(1)} %pad_maximum_fusion.2), channel_id=1, source_target_pairs={{0,2},{1,9},{4,6},{5,13},{8,10},{9,1},{12,14},{13,5},{16,18},{17,2... | collective-permute-start | bytes 1572872 | tf_op jit(solution)/shard_map/ppermute | solution.py:29
  31.8 15.0 %collective-permute-start.1 = (bf16[2,32,4096]{2,1,0:T(8,128)(2,1)S(1)}, bf16[2,32,4096]{2,1,0:T(8,128)(2,1)S(1)}, u32[]{:S(2)}, u32[]{:S(2)}) collective-permute-start(bf16[2,32,4096]{2,1,0:T(8,128)(2,1)S(1)} %pad_maximum_fusion.2), channel_id=1, source_target_pairs={{0,16},{1,5},{4,20},{5,9},{8,24},{9,13},{12,28},{13,1},{16,2},{17,... | collective-permute-start | bytes 1572872 | tf_op jit(solution)/shard_map/ppermute | solution.py:29
  47.3 45.8 %copy-start.8 = (bf16[128,4096]{1,0:T(8,128)(2,1)}, bf16[128,4096]{1,0:T(8,128)(2,1)S(1)}, u32[]{:S(2)}) copy-start(bf16[128,4096]{1,0:T(8,128)(2,1)S(1)} %concatenate.18.refs_4_) | copy-start | bytes 3145732
  47.4 27.5 %copy-start.9 = (bf16[128,4096]{1,0:T(8,128)(2,1)}, bf16[128,4096]{1,0:T(8,128)(2,1)S(1)}, u32[]{:S(2)}) copy-start(bf16[128,4096]{1,0:T(8,128)(2,1)S(1)} %pad_maximum_fusion.refs_0_) | copy-start | bytes 3145732
  47.4 14.1 %collective-permute-start.7 = (bf16[128,4096]{1,0:T(8,128)(2,1)S(1)}, bf16[128,4096]{1,0:T(8,128)(2,1)S(1)}, u32[]{:S(2)}, u32[]{:S(2)}) collective-permute-start(bf16[128,4096]{1,0:T(8,128)(2,1)S(1)} %pad_maximum_fusion.refs_0_), channel_id=1, source_target_pairs={{0,12},{1,19},{4,0},{5,23},{8,4},{9,27},{12,8},{13,31},{16,28},{17... | collective-permute-start | bytes 3145736 | tf_op jit(solution)/shard_map/ppermute | solution.py:29
  47.5 16.3 %collective-permute-start.4 = (bf16[128,4096]{1,0:T(8,128)(2,1)S(1)}, bf16[128,4096]{1,0:T(8,128)(2,1)S(1)}, u32[]{:S(2)}, u32[]{:S(2)}) collective-permute-start(bf16[128,4096]{1,0:T(8,128)(2,1)S(1)} %pad_maximum_fusion.refs_0_), channel_id=1, source_target_pairs={{0,4},{1,17},{4,8},{5,21},{8,12},{9,25},{12,0},{13,29},{16,20},{17... | collective-permute-start | bytes 3145736 | tf_op jit(solution)/shard_map/ppermute | solution.py:29
  48.9 25.9 %collective-permute-start.6 = (bf16[128,4096]{1,0:T(8,128)(2,1)S(1)}, bf16[128,4096]{1,0:T(8,128)(2,1)S(1)}, u32[]{:S(2)}, u32[]{:S(2)}) collective-permute-start(bf16[128,4096]{1,0:T(8,128)(2,1)S(1)} %concatenate.18.refs_4_), channel_id=1, source_target_pairs={{0,4},{1,17},{4,8},{5,21},{8,12},{9,25},{12,0},{13,29},{16,20},{17... | collective-permute-start | bytes 3145736 | tf_op jit(solution)/shard_map/ppermute | solution.py:29
  50.6 25.2 %collective-permute-start.5 = (bf16[128,4096]{1,0:T(8,128)(2,1)S(1)}, bf16[128,4096]{1,0:T(8,128)(2,1)}, u32[]{:S(2)}, u32[]{:S(2)}) collective-permute-start(bf16[128,4096]{1,0:T(8,128)(2,1)S(1)} %concatenate.18.refs_4_), channel_id=1, source_target_pairs={{0,12},{1,19},{4,0},{5,23},{8,4},{9,27},{12,8},{13,31},{16,28},{17... | collective-permute-start | bytes 3145736 | tf_op jit(solution)/shard_map/ppermute | solution.py:29
  61.5 31.5 %copy-start.15 = (bf16[128,4096]{1,0:T(8,128)(2,1)}, bf16[128,4096]{1,0:T(8,128)(2,1)S(1)}, u32[]{:S(2)}) copy-start(bf16[128,4096]{1,0:T(8,128)(2,1)S(1)} %collective-permute-done.7.refs_3_) | copy-start | bytes 3145732
  63.7 29.3 %copy-start.16 = (bf16[128,4096]{1,0:T(8,128)(2,1)}, bf16[128,4096]{1,0:T(8,128)(2,1)S(1)}, u32[]{:S(2)}) copy-start(bf16[128,4096]{1,0:T(8,128)(2,1)S(1)} %collective-permute-done.4.refs_1_) | copy-start | bytes 3145732
  74.8 1.0 copy-start.17
  75.8 44.0 %copy-start.13 = (f32[4096]{0:T(1024)S(1)}, f32[4096]{0:T(1024)}, u32[]{:S(2)}) copy-start(f32[4096]{0:T(1024)} %param.8) | copy-start | bytes 49156
  75.8 17.2 %collective-permute-start.11 = (bf16[8,896,256]{2,1,0:T(8,128)(2,1)}, bf16[8,896,256]{2,1,0:T(8,128)(2,1)S(1)}, u32[]{:S(2)}, u32[]{:S(2)}) collective-permute-start(bf16[8,896,256]{2,1,0:T(8,128)(2,1)} %bitcast.43), channel_id=1, source_target_pairs={{0,1},{1,0},{4,5},{5,4},{8,9},{9,8},{12,13},{13,12},{16,17},{17,16... | collective-permute-start | bytes 11010056 | tf_op jit(solution)/shard_map/ppermute | solution.py:34
  77.1 14.2 %collective-permute-start.9 = (bf16[128,4096]{1,0:T(8,128)(2,1)}, bf16[128,4096]{1,0:T(8,128)(2,1)S(1)}, u32[]{:S(2)}, u32[]{:S(2)}) collective-permute-start(bf16[128,4096]{1,0:T(8,128)(2,1)} %collective-permute-done.5.refs_7_), channel_id=1, source_target_pairs={{0,12},{1,19},{4,0},{5,23},{8,4},{9,27},{12,8},{13,31},{16,28},{17... | collective-permute-start | bytes 3145736 | tf_op jit(solution)/shard_map/ppermute | solution.py:29
  77.9 15.2 %collective-permute-start.8 = (bf16[128,4096]{1,0:T(8,128)(2,1)S(1)}, bf16[128,4096]{1,0:T(8,128)(2,1)S(1)}, u32[]{:S(2)}, u32[]{:S(2)}) collective-permute-start(bf16[128,4096]{1,0:T(8,128)(2,1)S(1)} %collective-permute-done.4.refs_1_), channel_id=1, source_target_pairs={{0,4},{1,17},{4,8},{5,21},{8,12},{9,25},{12,0},{13,29},{16,20},{17... | collective-permute-start | bytes 3145736 | tf_op jit(solution)/shard_map/ppermute | solution.py:29
  91.2 1.8 copy-start.18
  93.0 1.0 copy-start.19
  94.0 1.8 copy-start.14
  116.4 18.8 %copy-start.7 = (bf16[128,4096]{1,0:T(8,128)(2,1)S(1)}, bf16[128,4096]{1,0:T(8,128)(2,1)}, u32[]{:S(2)}) copy-start(bf16[128,4096]{1,0:T(8,128)(2,1)} %get-tuple-element.46) | copy-start | bytes 3145732
  116.4 20.1 %collective-permute-start.14 = (bf16[8,896,256]{2,1,0:T(8,128)(2,1)}, bf16[8,896,256]{2,1,0:T(8,128)(2,1)S(1)}, u32[]{:S(2)}, u32[]{:S(2)}) collective-permute-start(bf16[8,896,256]{2,1,0:T(8,128)(2,1)} %get-tuple-element.49), channel_id=1, source_target_pairs={{0,1},{1,0},{4,5},{5,4},{8,9},{9,8},{12,13},{13,12},{16,17},{17,16... | collective-permute-start | bytes 11010056 | tf_op jit(solution)/shard_map/ppermute | solution.py:34
  117.4 15.8 %collective-permute-start.12 = (bf16[128,4096]{1,0:T(8,128)(2,1)S(1)}, bf16[128,4096]{1,0:T(8,128)(2,1)S(1)}, u32[]{:S(2)}, u32[]{:S(2)}) collective-permute-start(bf16[128,4096]{1,0:T(8,128)(2,1)S(1)} %get-tuple-element.45), channel_id=1, source_target_pairs={{0,12},{1,19},{4,0},{5,23},{8,4},{9,27},{12,8},{13,31},{16,28},{17... | collective-permute-start | bytes 3145736 | tf_op jit(solution)/shard_map/ppermute | solution.py:29
  119.8 15.4 %collective-permute-start.13 = (bf16[128,4096]{1,0:T(8,128)(2,1)}, bf16[128,4096]{1,0:T(8,128)(2,1)S(1)}, u32[]{:S(2)}, u32[]{:S(2)}) collective-permute-start(bf16[128,4096]{1,0:T(8,128)(2,1)} %get-tuple-element.47), channel_id=1, source_target_pairs={{0,4},{1,17},{4,8},{5,21},{8,12},{9,25},{12,0},{13,29},{16,20},{17... | collective-permute-start | bytes 3145736 | tf_op jit(solution)/shard_map/ppermute | solution.py:29
  119.9 3.0 %collective-permute-start.15 = (f32[4096]{0:T(1024)S(1)}, f32[4096]{0:T(1024)S(1)}, u32[]{:S(2)}, u32[]{:S(2)}) collective-permute-start(f32[4096]{0:T(1024)S(1)} %div.35), channel_id=1, source_target_pairs={{0,32},{1,33},{4,36},{5,37},{8,40},{9,41},{12,44},{13,45},{16,48},... | collective-permute-start | bytes 49160 | tf_op jit(solution)/shard_map/ppermute | solution.py:232
  122.9 3.8 %collective-permute-start.16 = (f32[4096]{0:T(1024)S(1)}, f32[4096]{0:T(1024)S(1)}, u32[]{:S(2)}, u32[]{:S(2)}) collective-permute-start(f32[4096]{0:T(1024)S(1)} %add.92), channel_id=1, source_target_pairs={{0,64},{1,65},{4,68},{5,69},{8,72},{9,73},{12,76},{13,77},{16,80},... | collective-permute-start | bytes 49160 | tf_op jit(solution)/shard_map/ppermute | solution.py:232
  126.7 6.5 %collective-permute-start.17 = (f32[4096]{0:T(1024)S(1)}, f32[4096]{0:T(1024)S(1)}, u32[]{:S(2)}, u32[]{:S(2)}) collective-permute-start(f32[4096]{0:T(1024)S(1)} %add.93), channel_id=1, source_target_pairs={{0,128},{1,129},{4,132},{5,133},{8,136},{9,137},{12,140},{13,141},... | collective-permute-start | bytes 49160 | tf_op jit(solution)/shard_map/ppermute | solution.py:232
  133.2 3.2 %copy-start.6 = (bf16[8,896,256]{2,1,0:T(8,128)(2,1)S(1)}, bf16[8,896,256]{2,1,0:T(8,128)(2,1)}, u32[]{:S(2)}) copy-start(bf16[8,896,256]{2,1,0:T(8,128)(2,1)} %get-tuple-element.48) | copy-start | bytes 11010052
  139.1 38.2 %collective-permute-start.19 = (bf16[128,4096]{1,0:T(8,128)(2,1)S(1)}, bf16[128,4096]{1,0:T(8,128)(2,1)S(1)}, u32[]{:S(2)}, u32[]{:S(2)}) collective-permute-start(bf16[128,4096]{1,0:T(8,128)(2,1)S(1)} %get-tuple-element.52), channel_id=1, source_target_pairs={{0,4},{1,17},{4,8},{5,21},{8,12},{9,25},{12,0},{13,29},{16,20},{17... | collective-permute-start | bytes 3145736 | tf_op jit(solution)/shard_map/ppermute | solution.py:29
  139.2 38.1 %collective-permute-start.20 = (bf16[128,4096]{1,0:T(8,128)(2,1)}, bf16[128,4096]{1,0:T(8,128)(2,1)S(1)}, u32[]{:S(2)}, u32[]{:S(2)}) collective-permute-start(bf16[128,4096]{1,0:T(8,128)(2,1)} %get-tuple-element.53), channel_id=1, source_target_pairs={{0,12},{1,19},{4,0},{5,23},{8,4},{9,27},{12,8},{13,31},{16,28},{17... | collective-permute-start | bytes 3145736 | tf_op jit(solution)/shard_map/ppermute | solution.py:29
  141.9 35.4 %collective-permute-start.18 = (bf16[128,4096]{1,0:T(8,128)(2,1)}, bf16[128,4096]{1,0:T(8,128)(2,1)S(1)}, u32[]{:S(2)}, u32[]{:S(2)}) collective-permute-start(bf16[128,4096]{1,0:T(8,128)(2,1)} %add_convert_fusion.4), channel_id=1, source_target_pairs={{0,12},{1,19},{4,0},{5,23},{8,4},{9,27},{12,8},{13,31},{16,28},{17... | collective-permute-start | bytes 3145736 | tf_op jit(solution)/shard_map/ppermute | solution.py:29
  142.6 34.7 %collective-permute-start.21 = (bf16[128,4096]{1,0:T(8,128)(2,1)}, bf16[128,4096]{1,0:T(8,128)(2,1)S(1)}, u32[]{:S(2)}, u32[]{:S(2)}) collective-permute-start(bf16[128,4096]{1,0:T(8,128)(2,1)} %add_convert_fusion.3), channel_id=1, source_target_pairs={{0,4},{1,17},{4,8},{5,21},{8,12},{9,25},{12,0},{13,29},{16,20},{17... | collective-permute-start | bytes 3145736 | tf_op jit(solution)/shard_map/ppermute | solution.py:29
  143.3 4.4 %collective-permute-start.22 = (f32[4096]{0:T(1024)S(1)}, f32[4096]{0:T(1024)S(1)}, u32[]{:S(2)}, u32[]{:S(2)}) collective-permute-start(f32[4096]{0:T(1024)S(1)} %add.94), channel_id=1, source_target_pairs={{0,1},{1,0},{4,5},{5,4},{8,9},{9,8},{12,13},{13,12},{16,17},{17,16... | collective-permute-start | bytes 49160 | tf_op jit(solution)/shard_map/ppermute | solution.py:232
  147.7 17.6 %collective-permute-start.23 = (f32[4096]{0:T(1024)S(1)}, f32[4096]{0:T(1024)S(1)}, u32[]{:S(2)}, u32[]{:S(2)}) collective-permute-start(f32[4096]{0:T(1024)S(1)} %add.95), channel_id=1, source_target_pairs={{0,16},{1,17},{4,20},{5,21},{8,24},{9,25},{12,28},{13,29},{16,0},{... | collective-permute-start | bytes 49160 | tf_op jit(solution)/shard_map/ppermute | solution.py:232
  165.3 4.1 %collective-permute-start.24 = (f32[4096]{0:T(1024)S(1)}, f32[4096]{0:T(1024)S(1)}, u32[]{:S(2)}, u32[]{:S(2)}) collective-permute-start(f32[4096]{0:T(1024)S(1)} %add.96), channel_id=1, source_target_pairs={{0,2},{1,3},{4,6},{5,7},{8,10},{9,11},{12,14},{13,15},{16,18},{17,... | collective-permute-start | bytes 49160 | tf_op jit(solution)/shard_map/ppermute | solution.py:232
  169.5 3.1 %collective-permute-start.25 = (f32[4096]{0:T(1024)S(1)}, f32[4096]{0:T(1024)S(1)}, u32[]{:S(2)}, u32[]{:S(2)}) collective-permute-start(f32[4096]{0:T(1024)S(1)} %add.97), channel_id=1, source_target_pairs={{0,4},{1,5},{4,0},{5,1},{8,12},{9,13},{12,8},{13,9},{16,20},{17,21... | collective-permute-start | bytes 49160 | tf_op jit(solution)/shard_map/ppermute | solution.py:232
  172.6 4.1 %collective-permute-start.26 = (f32[4096]{0:T(1024)S(1)}, f32[4096]{0:T(1024)S(1)}, u32[]{:S(2)}, u32[]{:S(2)}) collective-permute-start(f32[4096]{0:T(1024)S(1)} %add.98), channel_id=1, source_target_pairs={{0,8},{1,9},{4,12},{5,13},{8,0},{9,1},{12,4},{13,5},{16,24},{17,25... | collective-permute-start | bytes 49160 | tf_op jit(solution)/shard_map/ppermute | solution.py:232
  178.4 15.2 %collective-permute-start.29 = (bf16[2,32,4096]{2,1,0:T(8,128)(2,1)S(1)}, bf16[2,32,4096]{2,1,0:T(8,128)(2,1)S(1)}, u32[]{:S(2)}, u32[]{:S(2)}) collective-permute-start(bf16[2,32,4096]{2,1,0:T(8,128)(2,1)S(1)} %get-tuple-element.69), channel_id=1, source_target_pairs={{0,16},{1,5},{4,20},{5,9},{8,24},{9,13},{12,28},{13,1},{16,2},{17,... | collective-permute-start | bytes 1572872 | tf_op jit(solution)/shard_map/ppermute | solution.py:29
  179.0 14.6 %collective-permute-start.27 = (bf16[2,32,4096]{2,1,0:T(8,128)(2,1)S(1)}, bf16[2,32,4096]{2,1,0:T(8,128)(2,1)S(1)}, u32[]{:S(2)}, u32[]{:S(2)}) collective-permute-start(bf16[2,32,4096]{2,1,0:T(8,128)(2,1)S(1)} %get-tuple-element.70), channel_id=1, source_target_pairs={{0,18},{1,13},{4,22},{5,1},{8,26},{9,5},{12,30},{13,9},{16,0},{17,... | collective-permute-start | bytes 1572872 | tf_op jit(solution)/shard_map/ppermute | solution.py:29
  181.4 12.2 %collective-permute-start.28 = (bf16[2,32,4096]{2,1,0:T(8,128)(2,1)S(1)}, bf16[2,32,4096]{2,1,0:T(8,128)(2,1)}, u32[]{:S(2)}, u32[]{:S(2)}) collective-permute-start(bf16[2,32,4096]{2,1,0:T(8,128)(2,1)S(1)} %get-tuple-element.71), channel_id=1, source_target_pairs={{0,2},{1,9},{4,6},{5,13},{8,10},{9,1},{12,14},{13,5},{16,18},{17,2... | collective-permute-start | bytes 1572872 | tf_op jit(solution)/shard_map/ppermute | solution.py:29
  193.6 0.8 copy-start.10
  193.6 1.0 copy-start.11
  194.5 4.1 %copy-start.20 = (bf16[1,896,256]{2,1,0:T(8,128)(2,1)S(1)}, bf16[1,896,256]{2,1,0:T(8,128)(2,1)}, u32[]{:S(2)}) copy-start(bf16[1,896,256]{2,1,0:T(8,128)(2,1)} %reduce-scatter.2.cloned.1.call-done) | copy-start | bytes 1376260
  194.5 6.4 %copy-start.1 = (bf16[128,4096]{1,0:T(8,128)(2,1)S(1)}, bf16[128,4096]{1,0:T(8,128)(2,1)}, u32[]{:S(2)}) copy-start(bf16[128,4096]{1,0:T(8,128)(2,1)} %param.11) | copy-start | bytes 3145732
  194.5 6.5 %copy-start.5 = (bf16[31,4096]{1,0:T(8,128)(2,1)S(1)}, bf16[31,4096]{1,0:T(8,128)(2,1)}, u32[]{:S(2)}) copy-start(bf16[31,4096]{1,0:T(8,128)(2,1)} %copy-done.4) | copy-start | bytes 761860
  196.3 6.2 %copy-start.3 = (bf16[128,4096]{1,0:T(8,128)(2,1)S(1)}, bf16[128,4096]{1,0:T(8,128)(2,1)}, u32[]{:S(2)}) copy-start(bf16[128,4096]{1,0:T(8,128)(2,1)} %param.6) | copy-start | bytes 3145732
  196.6 5.9 %collective-permute-start.30 = (bf16[1,4096]{1,0:T(2,128)(2,1)S(1)}, bf16[1,4096]{1,0:T(2,128)(2,1)S(1)}, u32[]{:S(2)}, u32[]{:S(2)}) collective-permute-start(bf16[1,4096]{1,0:T(2,128)(2,1)S(1)} %slice.78), channel_id=1, source_target_pairs={{0,1},{1,2},{2,3},{3,4},{4,5},{5,6},{6,7},{7,8},{8,9},{9,10},{10,1... | collective-permute-start | bytes 24584 | tf_op jit(solution)/shard_map/ppermute | solution.py:47
  198.6 9.8 %collective-permute-start.31 = (bf16[896,256]{1,0:T(8,128)(2,1)S(1)}, bf16[896,256]{1,0:T(8,128)(2,1)S(1)}, u32[]{:S(2)}, u32[]{:S(2)}) collective-permute-start(bf16[896,256]{1,0:T(8,128)(2,1)S(1)} %bitcast.45), channel_id=1, source_target_pairs={{0,0},{1,16},{4,4},{5,20},{8,8},{9,24},{12,12},{13,28},{16,1},{17,... | collective-permute-start | bytes 1376264 | tf_op jit(solution)/shard_map/ppermute | solution.py:41
Sparse Core Ops, SparseCore 0:
  21.8 52.5 all-gather.2
  139.2 50.5 reduce-scatter.1

commit v10 on v9

--- a/solution.py
+++ b/solution.py
@@ -217,18 +217,22 @@
     d1, n3, weight_part, gain = lax.optimization_barrier((d1, n3, weight_part, gain))
     weight_sum = lax.psum_scatter(weight_part, "z", scatter_dimension=0, tiled=False)
     d1, n3 = shift(d1, second=-1), shift(n3, second=1)
-    gain = pair(pair(pair(pair(pair(gain, c=1), y=1), y=2), x=1), x=2)
+    gain = pair(pair(gain, first=1), first=2)
     d1, d3, n1, n3, gain = lax.optimization_barrier((d1, d3, n1, n3, gain))
     both = jnp.stack([add_all([d0, d1, d3]).astype(bf), add_all([n0, n1, n3]).astype(bf)])
     rows = both.shape[1] // 4
     both = [both[:, d * rows : (d + 1) * rows] for d in range(4)]
     arrived = [shift(both[d], first=-d) for d in (1, 2, 3)] + [weight_sum]
-    *arrived, weight_sum = lax.optimization_barrier(arrived)
+    gain = pair(pair(pair(gain, second=1), second=2), c=1)
+    *arrived, weight_sum, gain = lax.optimization_barrier([*arrived, gain])
     return add_all([both[0], *arrived]), gain, weight_sum
 
 
-def pair(value, z=0, y=0, x=0, c=0):
-    pairs = [(linear(*p), linear(p[0] ^ z, p[1] ^ y, p[2] ^ x, p[3] ^ c)) for p in places()]
+def pair(value, z=0, first=0, second=0, c=0):
+    pairs = []
+    for p in places():
+        y, x = (second, first) if p[3] else (first, second)
+        pairs.append((linear(*p), linear(p[0] ^ z, p[1] ^ y, p[2] ^ x, p[3] ^ c)))
     return value + lax.ppermute(value, AXES, pairs)
 
 

time: 217 us -> 216 us (level)
  starting transfers between devices: 46.6 us -> 51.8 us
  waiting for transfers between devices: 111 us -> 106 us
    ppermute x8, waiting for transfers between devices: 32.3 us -> 18.8 us  [pair(): return value + lax.ppermute(value, AXES, pairs)]
    reduce_scatter x1, waiting for transfers between devices: 0.02 us -> 4.5 us  [scatter_plane(): lax.psum_scatter(weight_part, 'z', scatter_dimension=0, tiled=False)]
    ppermute x2, starting transfers between devices: 3.97 us -> 7.21 us  [from_behind(): return lax.ppermute(value, AXES, pairs)]
    ppermute x18, waiting for transfers between devices: 65.1 us -> 68 us  [shift(): return lax.ppermute(value, AXES, pairs)]
    ppermute x8, starting transfers between devices: 14.3 us -> 16.9 us  [pair(): return value + lax.ppermute(value, AXES, pairs)]
  transfers between devices with their start and end apart: 34 -> 34, of which waited for: 20 -> 23; matrix products, arithmetic and copies ran while one was open for 4% -> 4% of each run, Pallas kernels for 0% -> 0%
where the time goes in v10:
time: 216 us; the launch traced here: 215 us
  waiting for transfers between devices  106 us (49%)
  starting transfers between devices  51.8 us (24%)
  Pallas kernels  20.5 us (9%)
  between operations  14.5 us (7%)
  other arithmetic  13.3 us (6%)
  local copies, waits for them, and re-layouts  6.31 us (3%)
  matrix products  3.44 us (2%)
    ppermute x18, waiting for transfers between devices, shift(): return lax.ppermute(value, AXES, pairs)  68 us
    pallas_call x1, Pallas kernels, block(): pl.pallas_call(functools.partial(block_kernel, chunks), out_shape=[jax.Sh...  20.5 us
    ppermute x8, waiting for transfers between devices, pair(): return value + lax.ppermute(value, AXES, pairs)  18.8 us
    ppermute x18, starting transfers between devices, shift(): return lax.ppermute(value, AXES, pairs)  18.8 us
    ppermute x8, starting transfers between devices, pair(): return value + lax.ppermute(value, AXES, pairs)  16.9 us
    ppermute x2, waiting for transfers between devices, swap_low(): return lax.ppermute(value, AXES, pairs)  10 us
    ppermute x2, starting transfers between devices, from_behind(): return lax.ppermute(value, AXES, pairs)  7.21 us
    ppermute x2, starting transfers between devices, swap_low(): return lax.ppermute(value, AXES, pairs)  6.52 us
  transfers between devices with their start and end apart: 34, of which 23 were waited for; matrix products, arithmetic and copies ran while one was open for 4% of the time, Pallas kernels for 0%

profile of v10, /device:TPU:1, one launch (start us, length us, event | category | flops | bytes accessed | tf_op | source)
XLA Modules:
  0.0 215.5 jit_solution(17797118965572997220)
XLA Ops:
  7.2 0.9 dynamic_slice.3
  8.1 1.0 fusion.20
  9.1 1.0 pad_maximum_fusion.3
  10.1 4.6 %collective-permute-start.10 = (bf16[896,256]{1,0:T(8,128)(2,1)S(1)}, bf16[896,256]{1,0:T(8,128)(2,1)S(1)}, u32[]{:S(2)}, u32[]{:S(2)}) collective-permute-start(bf16[896,256]{1,0:T(8,128)(2,1)S(1)} %pad_maximum_fusion.3), channel_id=1, source_target_pairs={{0,0},{1,16},{4,4},{5,20},{8,8},{9,24},{12,12},{13,28},{16,1},{17,... | collective-permute-start | bytes 1376264 | tf_op jit(solution)/shard_map/ppermute | solution.py:41
  14.7 0.7 convert_subtract_fusion
  15.8 5.1 %collective-permute-done.10 = bf16[896,256]{1,0:T(8,128)(2,1)S(1)} collective-permute-done((bf16[896,256]{1,0:T(8,128)(2,1)S(1)}, bf16[896,256]{1,0:T(8,128)(2,1)S(1)}, u32[]{:S(2)}, u32[]{:S(2)}) %collective-permute-start.10) | collective-permute-done | bytes 458784 | tf_op jit(solution)/shard_map/ppermute | solution.py:41
  20.8 0.8 copy-done.12
  22.0 1.9 collective-permute-start
  24.3 4.3 %collective-permute-done = bf16[1,4096]{1,0:T(2,128)(2,1)S(1)} collective-permute-done((bf16[1,4096]{1,0:T(2,128)(2,1)S(1)}, bf16[1,4096]{1,0:T(2,128)(2,1)S(1)}, u32[]{:S(2)}, u32[]{:S(2)}) %collective-permute-start) | collective-permute-done | bytes 8224 | tf_op jit(solution)/shard_map/ppermute | solution.py:47
  28.7 2.6 %collective-permute-start.3 = (bf16[2,32,4096]{2,1,0:T(8,128)(2,1)S(1)}, bf16[2,32,4096]{2,1,0:T(8,128)(2,1)S(1)}, u32[]{:S(2)}, u32[]{:S(2)}) collective-permute-start(bf16[2,32,4096]{2,1,0:T(8,128)(2,1)S(1)} %pad_maximum_fusion.2), channel_id=1, source_target_pairs={{0,18},{1,13},{4,22},{5,1},{8,26},{9,5},{12,30},{13,9},{16,0},{17,... | collective-permute-start | bytes 1572872 | tf_op jit(solution)/shard_map/ppermute | solution.py:29
  31.2 0.5 collective-permute-start.2
  31.8 0.6 collective-permute-start.1
  32.4 10.6 %collective-permute-done.3 = bf16[2,32,4096]{2,1,0:T(8,128)(2,1)S(1)} collective-permute-done((bf16[2,32,4096]{2,1,0:T(8,128)(2,1)S(1)}, bf16[2,32,4096]{2,1,0:T(8,128)(2,1)S(1)}, u32[]{:S(2)}, u32[]{:S(2)}) %collective-permute-start.3) | collective-permute-done | bytes 524320 | tf_op jit(solution)/shard_map/ppermute | solution.py:29
  43.1 3.7 %collective-permute-done.1 = bf16[2,32,4096]{2,1,0:T(8,128)(2,1)S(1)} collective-permute-done((bf16[2,32,4096]{2,1,0:T(8,128)(2,1)S(1)}, bf16[2,32,4096]{2,1,0:T(8,128)(2,1)S(1)}, u32[]{:S(2)}, u32[]{:S(2)}) %collective-permute-start.1) | collective-permute-done | bytes 524320 | tf_op jit(solution)/shard_map/ppermute | solution.py:29
  47.5 1.5 collective-permute-start.4
  48.9 1.7 collective-permute-start.6
  50.6 1.0 collective-permute-start.5
  51.6 9.9 %collective-permute-done.7.refs_3_ = bf16[128,4096]{1,0:T(8,128)(2,1)S(1)} collective-permute-done((bf16[128,4096]{1,0:T(8,128)(2,1)S(1)}, bf16[128,4096]{1,0:T(8,128)(2,1)S(1)}, u32[]{:S(2)}, u32[]{:S(2)}) %collective-permute-start.7) | collective-permute-done | bytes 1048608 | tf_op jit(solution)/shard_map/ppermute | solution.py:29
  61.5 2.2 %collective-permute-done.4.refs_1_ = bf16[128,4096]{1,0:T(8,128)(2,1)S(1)} collective-permute-done((bf16[128,4096]{1,0:T(8,128)(2,1)S(1)}, bf16[128,4096]{1,0:T(8,128)(2,1)S(1)}, u32[]{:S(2)}, u32[]{:S(2)}) %collective-permute-start.4) | collective-permute-done | bytes 1048608 | tf_op jit(solution)/shard_map/ppermute | solution.py:29
  63.7 11.1 %collective-permute-done.6.refs_5_ = bf16[128,4096]{1,0:T(8,128)(2,1)S(1)} collective-permute-done((bf16[128,4096]{1,0:T(8,128)(2,1)S(1)}, bf16[128,4096]{1,0:T(8,128)(2,1)S(1)}, u32[]{:S(2)}, u32[]{:S(2)}) %collective-permute-start.6) | collective-permute-done | bytes 1048608 | tf_op jit(solution)/shard_map/ppermute | solution.py:29
  74.8 1.0 copy-done.17
  75.8 1.2 collective-permute-start.11
  77.1 0.8 collective-permute-start.9
  77.9 0.7 collective-permute-start.8
  78.5 12.7 %collective-permute-done.9.refs_6_ = bf16[128,4096]{1,0:T(8,128)(2,1)S(1)} collective-permute-done((bf16[128,4096]{1,0:T(8,128)(2,1)}, bf16[128,4096]{1,0:T(8,128)(2,1)S(1)}, u32[]{:S(2)}, u32[]{:S(2)}) %collective-permute-start.9) | collective-permute-done | bytes 1048608 | tf_op jit(solution)/shard_map/ppermute | solution.py:29
  91.2 1.8 collective-permute-done.8.refs_2_
  93.1 1.0 copy-done.19
  94.0 1.8 copy-done.14
  95.8 20.5 %shard_map.101 = (bf16[128,4096]{1,0:T(8,128)(2,1)S(1)}, bf16[128,4096]{1,0:T(8,128)(2,1)S(1)}, bf16[128,4096]{1,0:T(8,128)(2,1)S(1)}, bf16[128,4096]{1,0:T(8,12...) custom-call(bf16[128,4096]{1,0:T(8,128)(2,1)} %copy-done.9, ...), custom_call_target="tpu_custom_call" | custom-call | flops 11274289152 | bytes 62914560 | tf_op jit(solution)/shard_map/pallas_call | solution.py:168
  116.4 1.0 collective-permute-start.14
  117.4 2.5 %collective-permute-start.12 = (bf16[128,4096]{1,0:T(8,128)(2,1)S(1)}, bf16[128,4096]{1,0:T(8,128)(2,1)S(1)}, u32[]{:S(2)}, u32[]{:S(2)}) collective-permute-start(bf16[128,4096]{1,0:T(8,128)(2,1)S(1)} %get-tuple-element.46), channel_id=1, source_target_pairs={{0,12},{1,19},{4,0},{5,23},{8,4},{9,27},{12,8},{13,31},{16,28},{17... | collective-permute-start | bytes 3145736 | tf_op jit(solution)/shard_map/ppermute | solution.py:29
  120.1 2.8 %collective-permute-done.15 = f32[4096]{0:T(1024)S(1)} collective-permute-done((f32[4096]{0:T(1024)S(1)}, f32[4096]{0:T(1024)S(1)}, u32[]{:S(2)}, u32[]{:S(2)}) %collective-permute-start.15) | collective-permute-done | bytes 16416 | tf_op jit(solution)/shard_map/ppermute | solution.py:236
  122.9 1.6 collective-permute-start.16
  124.5 2.2 %collective-permute-done.16 = f32[4096]{0:T(1024)S(1)} collective-permute-done((f32[4096]{0:T(1024)S(1)}, f32[4096]{0:T(1024)S(1)}, u32[]{:S(2)}, u32[]{:S(2)}) %collective-permute-start.16) | collective-permute-done | bytes 16416 | tf_op jit(solution)/shard_map/ppermute | solution.py:236
  126.7 5.4 %collective-permute-start.17 = (f32[4096]{0:T(1024)S(1)}, f32[4096]{0:T(1024)S(1)}, u32[]{:S(2)}, u32[]{:S(2)}) collective-permute-start(f32[4096]{0:T(1024)S(1)} %add.93), channel_id=1, source_target_pairs={{0,128},{1,129},{4,132},{5,133},{8,136},{9,137},{12,140},{13,141},... | collective-permute-start | bytes 49160 | tf_op jit(solution)/shard_map/ppermute | solution.py:236
  132.0 1.1 collective-permute-done.17
  133.2 1.2 add_convert_fusion.4
  134.4 0.8 collective-permute-done.13
  135.2 1.2 add_convert_fusion.3
  136.4 2.7 %add_convert_fusion = bf16[8,896,256]{2,1,0:T(8,128)(2,1)} fusion(bf16[8,896,256]{2,1,0:T(8,128)(2,1)S(1)} %collective-permute-done.14, bf16[8,896,256]{2,1,0:T(8,128)(2,1)S(1)} %copy-done.6), kind=kLoop, calls=%fused_computation | loop fusion | flops 7340032 | bytes 11010048 | tf_op jit(solution)/shard_map/convert_element_type | solution.py:270
  139.2 2.7 %collective-permute-start.20 = (bf16[128,4096]{1,0:T(8,128)(2,1)}, bf16[128,4096]{1,0:T(8,128)(2,1)S(1)}, u32[]{:S(2)}, u32[]{:S(2)}) collective-permute-start(bf16[128,4096]{1,0:T(8,128)(2,1)} %get-tuple-element.54), channel_id=1, source_target_pairs={{0,12},{1,19},{4,0},{5,23},{8,4},{9,27},{12,8},{13,31},{16,28},{17... | collective-permute-start | bytes 3145736 | tf_op jit(solution)/shard_map/ppermute | solution.py:29
  141.9 0.7 collective-permute-start.18
  142.6 0.8 collective-permute-start.21
  143.3 3.1 %collective-permute-done.22 = f32[4096]{0:T(1024)S(1)} collective-permute-done((f32[4096]{0:T(1024)S(1)}, f32[4096]{0:T(1024)S(1)}, u32[]{:S(2)}, u32[]{:S(2)}) %collective-permute-start.22) | collective-permute-done | bytes 16416 | tf_op jit(solution)/shard_map/ppermute | solution.py:236
  146.4 4.3 %collective-permute-done.23 = f32[4096]{0:T(1024)S(1)} collective-permute-done((f32[4096]{0:T(1024)S(1)}, f32[4096]{0:T(1024)S(1)}, u32[]{:S(2)}, u32[]{:S(2)}) %collective-permute-start.23) | collective-permute-done | bytes 16416 | tf_op jit(solution)/shard_map/ppermute | solution.py:236
  150.8 3.6 %collective-permute-done.19 = bf16[128,4096]{1,0:T(8,128)(2,1)S(1)} collective-permute-done((bf16[128,4096]{1,0:T(8,128)(2,1)S(1)}, bf16[128,4096]{1,0:T(8,128)(2,1)S(1)}, u32[]{:S(2)}, u32[]{:S(2)}) %collective-permute-start.19) | collective-permute-done | bytes 1048608 | tf_op jit(solution)/shard_map/ppermute | solution.py:29
  154.4 11.0 %collective-permute-done.18 = bf16[128,4096]{1,0:T(8,128)(2,1)S(1)} collective-permute-done((bf16[128,4096]{1,0:T(8,128)(2,1)}, bf16[128,4096]{1,0:T(8,128)(2,1)S(1)}, u32[]{:S(2)}, u32[]{:S(2)}) %collective-permute-start.18) | collective-permute-done | bytes 1048608 | tf_op jit(solution)/shard_map/ppermute | solution.py:29
  165.4 0.5 collective-permute-done.21
  167.0 2.7 %collective-permute-start.24 = (bf16[2,32,4096]{2,1,0:T(8,128)(2,1)S(1)}, bf16[2,32,4096]{2,1,0:T(8,128)(2,1)S(1)}, u32[]{:S(2)}, u32[]{:S(2)}) collective-permute-start(bf16[2,32,4096]{2,1,0:T(8,128)(2,1)S(1)} %get-tuple-element.72), channel_id=1, source_target_pairs={{0,18},{1,13},{4,22},{5,1},{8,26},{9,5},{12,30},{13,9},{16,0},{17,... | collective-permute-start | bytes 1572872 | tf_op jit(solution)/shard_map/ppermute | solution.py:29
  170.0 2.7 %collective-permute-done.27 = f32[4096]{0:T(1024)S(1)} collective-permute-done((f32[4096]{0:T(1024)S(1)}, f32[4096]{0:T(1024)S(1)}, u32[]{:S(2)}, u32[]{:S(2)}) %collective-permute-start.27) | collective-permute-done | bytes 16416 | tf_op jit(solution)/shard_map/ppermute | solution.py:236
  172.7 2.6 %collective-permute-start.28 = (f32[4096]{0:T(1024)S(1)}, f32[4096]{0:T(1024)S(1)}, u32[]{:S(2)}, u32[]{:S(2)}) collective-permute-start(f32[4096]{0:T(1024)S(1)} %add.101), channel_id=1, source_target_pairs={{0,8},{1,3},{4,12},{5,7},{8,0},{9,11},{12,4},{13,15},{16,24},{17,1... | collective-permute-start | bytes 49160 | tf_op jit(solution)/shard_map/ppermute | solution.py:236
  175.3 1.7 collective-permute-done.28
  177.0 6.9 %collective-permute-start.29 = (f32[4096]{0:T(1024)S(1)}, f32[4096]{0:T(1024)S(1)}, u32[]{:S(2)}, u32[]{:S(2)}) collective-permute-start(f32[4096]{0:T(1024)S(1)} %add.102), channel_id=1, source_target_pairs={{0,1},{1,0},{4,5},{5,4},{8,9},{9,8},{12,13},{13,12},{16,17},{17,16... | collective-permute-start | bytes 49160 | tf_op jit(solution)/shard_map/ppermute | solution.py:236
  183.9 0.8 collective-permute-done.29
  184.8 0.6 add.103
  185.4 4.5 %reduce-scatter.2.cloned.1.call-done = bf16[1,896,256]{2,1,0:T(8,128)(2,1)} async-done(((bf16[8,896,256]{2,1,0:T(8,128)(2,1)}), bf16[1,896,256]{2,1,0:T(8,128)(2,1)}) %reduce-scatter.2.cloned.1.call-update) | async-done | bytes 458768 | tf_op jit(solution)/shard_map/reduce_scatter | solution.py:218
  189.9 1.7 convert_add_fusion
  191.9 5.3 %collective-permute-start.30 = (bf16[1,4096]{1,0:T(2,128)(2,1)S(1)}, bf16[1,4096]{1,0:T(2,128)(2,1)S(1)}, u32[]{:S(2)}, u32[]{:S(2)}) collective-permute-start(bf16[1,4096]{1,0:T(2,128)(2,1)S(1)} %slice.78), channel_id=1, source_target_pairs={{0,1},{1,2},{2,3},{3,4},{4,5},{5,6},{6,7},{7,8},{8,9},{9,10},{10,1... | collective-permute-start | bytes 24584 | tf_op jit(solution)/shard_map/ppermute | solution.py:47
  197.2 1.9 collective-permute-start.31
  199.2 1.5 fusion.1
  200.7 1.4 fusion
  202.1 4.9 %collective-permute-done.31 = bf16[896,256]{1,0:T(8,128)(2,1)S(1)} collective-permute-done((bf16[896,256]{1,0:T(8,128)(2,1)S(1)}, bf16[896,256]{1,0:T(8,128)(2,1)S(1)}, u32[]{:S(2)}, u32[]{:S(2)}) %collective-permute-start.31) | collective-permute-done | bytes 458784 | tf_op jit(solution)/shard_map/ppermute | solution.py:41
  207.0 0.8 multiply_bitcast_fusion
  207.8 0.8 slice_convert_fusion
  (93 shorter events, 4.1 us)
Async XLA Ops:
  7.2 14.6 %copy-start = (bf16[128,4096]{1,0:T(8,128)(2,1)S(1)}, bf16[128,4096]{1,0:T(8,128)(2,1)}, u32[]{:S(2)}) copy-start(bf16[128,4096]{1,0:T(8,128)(2,1)} %param.11) | copy-start | bytes 3145732
  7.2 16.8 %copy-start.2 = (bf16[128,4096]{1,0:T(8,128)(2,1)S(1)}, bf16[128,4096]{1,0:T(8,128)(2,1)}, u32[]{:S(2)}) copy-start(bf16[128,4096]{1,0:T(8,128)(2,1)} %param.6) | copy-start | bytes 3145732
  7.2 68.6 %all-gather.3.cloned.1.call-start = ((), (), s32[]{:S(2)}) async-start(), calls=%async_computation.2 | async-start | bytes 4128768 | tf_op jit(solution)/shard_map/all_gather | solution.py:250
  10.1 10.8 %collective-permute-start.10 = (bf16[896,256]{1,0:T(8,128)(2,1)S(1)}, bf16[896,256]{1,0:T(8,128)(2,1)S(1)}, u32[]{:S(2)}, u32[]{:S(2)}) collective-permute-start(bf16[896,256]{1,0:T(8,128)(2,1)S(1)} %pad_maximum_fusion.3), channel_id=1, source_target_pairs={{0,0},{1,16},{4,4},{5,20},{8,8},{9,24},{12,12},{13,28},{16,1},{17,... | collective-permute-start | bytes 1376264 | tf_op jit(solution)/shard_map/ppermute | solution.py:41
  20.8 0.8 copy-start.12
  21.6 168.3 %reduce-scatter.2.cloned.1.call-start = ((), (), s32[]{:S(2)}) async-start(), calls=%async_computation.1 | async-start | bytes 4128768 | tf_op jit(solution)/shard_map/reduce_scatter | solution.py:218
  22.0 6.6 %collective-permute-start = (bf16[1,4096]{1,0:T(2,128)(2,1)S(1)}, bf16[1,4096]{1,0:T(2,128)(2,1)S(1)}, u32[]{:S(2)}, u32[]{:S(2)}) collective-permute-start(bf16[1,4096]{1,0:T(2,128)(2,1)S(1)} %slice.65), channel_id=1, source_target_pairs={{1,0},{2,1},{3,2},{4,3},{5,4},{6,5},{7,6},{8,7},{9,8},{10,9},{11,1... | collective-permute-start | bytes 24584 | tf_op jit(solution)/shard_map/ppermute | solution.py:47
  24.3 22.5 %copy-start.4 = (bf16[31,4096]{1,0:T(8,128)(2,1)}, bf16[31,4096]{1,0:T(8,128)(2,1)S(1)}, u32[]{:S(2)}) copy-start(bf16[31,4096]{1,0:T(8,128)(2,1)S(1)} %slice.64) | copy-start | bytes 761860
  28.7 14.3 %collective-permute-start.3 = (bf16[2,32,4096]{2,1,0:T(8,128)(2,1)S(1)}, bf16[2,32,4096]{2,1,0:T(8,128)(2,1)S(1)}, u32[]{:S(2)}, u32[]{:S(2)}) collective-permute-start(bf16[2,32,4096]{2,1,0:T(8,128)(2,1)S(1)} %pad_maximum_fusion.2), channel_id=1, source_target_pairs={{0,18},{1,13},{4,22},{5,1},{8,26},{9,5},{12,30},{13,9},{16,0},{17,... | collective-permute-start | bytes 1572872 | tf_op jit(solution)/shard_map/ppermute | solution.py:29
  31.2 11.8 %collective-permute-start.2 = (bf16[2,32,4096]{2,1,0:T(8,128)(2,1)S(1)}, bf16[2,32,4096]{2,1,0:T(8,128)(2,1)S(1)}, u32[]{:S(2)}, u32[]{:S(2)}) collective-permute-start(bf16[2,32,4096]{2,1,0:T(8,128)(2,1)S(1)} %pad_maximum_fusion.2), channel_id=1, source_target_pairs={{0,2},{1,9},{4,6},{5,13},{8,10},{9,1},{12,14},{13,5},{16,18},{17,2... | collective-permute-start | bytes 1572872 | tf_op jit(solution)/shard_map/ppermute | solution.py:29
  31.8 15.0 %collective-permute-start.1 = (bf16[2,32,4096]{2,1,0:T(8,128)(2,1)S(1)}, bf16[2,32,4096]{2,1,0:T(8,128)(2,1)S(1)}, u32[]{:S(2)}, u32[]{:S(2)}) collective-permute-start(bf16[2,32,4096]{2,1,0:T(8,128)(2,1)S(1)} %pad_maximum_fusion.2), channel_id=1, source_target_pairs={{0,16},{1,5},{4,20},{5,9},{8,24},{9,13},{12,28},{13,1},{16,2},{17,... | collective-permute-start | bytes 1572872 | tf_op jit(solution)/shard_map/ppermute | solution.py:29
  47.3 45.8 %copy-start.8 = (bf16[128,4096]{1,0:T(8,128)(2,1)}, bf16[128,4096]{1,0:T(8,128)(2,1)S(1)}, u32[]{:S(2)}) copy-start(bf16[128,4096]{1,0:T(8,128)(2,1)S(1)} %concatenate.18.refs_4_) | copy-start | bytes 3145732
  47.4 27.5 %copy-start.9 = (bf16[128,4096]{1,0:T(8,128)(2,1)}, bf16[128,4096]{1,0:T(8,128)(2,1)S(1)}, u32[]{:S(2)}) copy-start(bf16[128,4096]{1,0:T(8,128)(2,1)S(1)} %pad_maximum_fusion.refs_0_) | copy-start | bytes 3145732
  47.4 14.1 %collective-permute-start.7 = (bf16[128,4096]{1,0:T(8,128)(2,1)S(1)}, bf16[128,4096]{1,0:T(8,128)(2,1)S(1)}, u32[]{:S(2)}, u32[]{:S(2)}) collective-permute-start(bf16[128,4096]{1,0:T(8,128)(2,1)S(1)} %pad_maximum_fusion.refs_0_), channel_id=1, source_target_pairs={{0,12},{1,19},{4,0},{5,23},{8,4},{9,27},{12,8},{13,31},{16,28},{17... | collective-permute-start | bytes 3145736 | tf_op jit(solution)/shard_map/ppermute | solution.py:29
  47.5 16.3 %collective-permute-start.4 = (bf16[128,4096]{1,0:T(8,128)(2,1)S(1)}, bf16[128,4096]{1,0:T(8,128)(2,1)S(1)}, u32[]{:S(2)}, u32[]{:S(2)}) collective-permute-start(bf16[128,4096]{1,0:T(8,128)(2,1)S(1)} %pad_maximum_fusion.refs_0_), channel_id=1, source_target_pairs={{0,4},{1,17},{4,8},{5,21},{8,12},{9,25},{12,0},{13,29},{16,20},{17... | collective-permute-start | bytes 3145736 | tf_op jit(solution)/shard_map/ppermute | solution.py:29
  48.9 25.9 %collective-permute-start.6 = (bf16[128,4096]{1,0:T(8,128)(2,1)S(1)}, bf16[128,4096]{1,0:T(8,128)(2,1)S(1)}, u32[]{:S(2)}, u32[]{:S(2)}) collective-permute-start(bf16[128,4096]{1,0:T(8,128)(2,1)S(1)} %concatenate.18.refs_4_), channel_id=1, source_target_pairs={{0,4},{1,17},{4,8},{5,21},{8,12},{9,25},{12,0},{13,29},{16,20},{17... | collective-permute-start | bytes 3145736 | tf_op jit(solution)/shard_map/ppermute | solution.py:29
  50.6 25.2 %collective-permute-start.5 = (bf16[128,4096]{1,0:T(8,128)(2,1)S(1)}, bf16[128,4096]{1,0:T(8,128)(2,1)}, u32[]{:S(2)}, u32[]{:S(2)}) collective-permute-start(bf16[128,4096]{1,0:T(8,128)(2,1)S(1)} %concatenate.18.refs_4_), channel_id=1, source_target_pairs={{0,12},{1,19},{4,0},{5,23},{8,4},{9,27},{12,8},{13,31},{16,28},{17... | collective-permute-start | bytes 3145736 | tf_op jit(solution)/shard_map/ppermute | solution.py:29
  61.5 31.5 %copy-start.15 = (bf16[128,4096]{1,0:T(8,128)(2,1)}, bf16[128,4096]{1,0:T(8,128)(2,1)S(1)}, u32[]{:S(2)}) copy-start(bf16[128,4096]{1,0:T(8,128)(2,1)S(1)} %collective-permute-done.7.refs_3_) | copy-start | bytes 3145732
  63.7 29.3 %copy-start.16 = (bf16[128,4096]{1,0:T(8,128)(2,1)}, bf16[128,4096]{1,0:T(8,128)(2,1)S(1)}, u32[]{:S(2)}) copy-start(bf16[128,4096]{1,0:T(8,128)(2,1)S(1)} %collective-permute-done.4.refs_1_) | copy-start | bytes 3145732
  74.8 1.0 copy-start.17
  75.8 44.0 %copy-start.13 = (f32[4096]{0:T(1024)S(1)}, f32[4096]{0:T(1024)}, u32[]{:S(2)}) copy-start(f32[4096]{0:T(1024)} %param.8) | copy-start | bytes 49156
  75.8 17.2 %collective-permute-start.11 = (bf16[8,896,256]{2,1,0:T(8,128)(2,1)}, bf16[8,896,256]{2,1,0:T(8,128)(2,1)S(1)}, u32[]{:S(2)}, u32[]{:S(2)}) collective-permute-start(bf16[8,896,256]{2,1,0:T(8,128)(2,1)} %bitcast.43), channel_id=1, source_target_pairs={{0,1},{1,0},{4,5},{5,4},{8,9},{9,8},{12,13},{13,12},{16,17},{17,16... | collective-permute-start | bytes 11010056 | tf_op jit(solution)/shard_map/ppermute | solution.py:34
  77.1 14.2 %collective-permute-start.9 = (bf16[128,4096]{1,0:T(8,128)(2,1)}, bf16[128,4096]{1,0:T(8,128)(2,1)S(1)}, u32[]{:S(2)}, u32[]{:S(2)}) collective-permute-start(bf16[128,4096]{1,0:T(8,128)(2,1)} %collective-permute-done.5.refs_7_), channel_id=1, source_target_pairs={{0,12},{1,19},{4,0},{5,23},{8,4},{9,27},{12,8},{13,31},{16,28},{17... | collective-permute-start | bytes 3145736 | tf_op jit(solution)/shard_map/ppermute | solution.py:29
  77.9 15.2 %collective-permute-start.8 = (bf16[128,4096]{1,0:T(8,128)(2,1)S(1)}, bf16[128,4096]{1,0:T(8,128)(2,1)S(1)}, u32[]{:S(2)}, u32[]{:S(2)}) collective-permute-start(bf16[128,4096]{1,0:T(8,128)(2,1)S(1)} %collective-permute-done.4.refs_1_), channel_id=1, source_target_pairs={{0,4},{1,17},{4,8},{5,21},{8,12},{9,25},{12,0},{13,29},{16,20},{17... | collective-permute-start | bytes 3145736 | tf_op jit(solution)/shard_map/ppermute | solution.py:29
  91.2 1.8 copy-start.18
  93.0 1.0 copy-start.19
  94.0 1.8 copy-start.14
  116.4 18.8 %copy-start.7 = (bf16[128,4096]{1,0:T(8,128)(2,1)S(1)}, bf16[128,4096]{1,0:T(8,128)(2,1)}, u32[]{:S(2)}) copy-start(bf16[128,4096]{1,0:T(8,128)(2,1)} %get-tuple-element.47) | copy-start | bytes 3145732
  116.4 20.1 %collective-permute-start.14 = (bf16[8,896,256]{2,1,0:T(8,128)(2,1)}, bf16[8,896,256]{2,1,0:T(8,128)(2,1)S(1)}, u32[]{:S(2)}, u32[]{:S(2)}) collective-permute-start(bf16[8,896,256]{2,1,0:T(8,128)(2,1)} %get-tuple-element.50), channel_id=1, source_target_pairs={{0,1},{1,0},{4,5},{5,4},{8,9},{9,8},{12,13},{13,12},{16,17},{17,16... | collective-permute-start | bytes 11010056 | tf_op jit(solution)/shard_map/ppermute | solution.py:34
  117.4 15.8 %collective-permute-start.12 = (bf16[128,4096]{1,0:T(8,128)(2,1)S(1)}, bf16[128,4096]{1,0:T(8,128)(2,1)S(1)}, u32[]{:S(2)}, u32[]{:S(2)}) collective-permute-start(bf16[128,4096]{1,0:T(8,128)(2,1)S(1)} %get-tuple-element.46), channel_id=1, source_target_pairs={{0,12},{1,19},{4,0},{5,23},{8,4},{9,27},{12,8},{13,31},{16,28},{17... | collective-permute-start | bytes 3145736 | tf_op jit(solution)/shard_map/ppermute | solution.py:29
  119.8 15.4 %collective-permute-start.13 = (bf16[128,4096]{1,0:T(8,128)(2,1)}, bf16[128,4096]{1,0:T(8,128)(2,1)S(1)}, u32[]{:S(2)}, u32[]{:S(2)}) collective-permute-start(bf16[128,4096]{1,0:T(8,128)(2,1)} %get-tuple-element.48), channel_id=1, source_target_pairs={{0,4},{1,17},{4,8},{5,21},{8,12},{9,25},{12,0},{13,29},{16,20},{17... | collective-permute-start | bytes 3145736 | tf_op jit(solution)/shard_map/ppermute | solution.py:29
  119.9 3.0 %collective-permute-start.15 = (f32[4096]{0:T(1024)S(1)}, f32[4096]{0:T(1024)S(1)}, u32[]{:S(2)}, u32[]{:S(2)}) collective-permute-start(f32[4096]{0:T(1024)S(1)} %div.35), channel_id=1, source_target_pairs={{0,32},{1,33},{4,36},{5,37},{8,40},{9,41},{12,44},{13,45},{16,48},... | collective-permute-start | bytes 49160 | tf_op jit(solution)/shard_map/ppermute | solution.py:236
  122.9 3.8 %collective-permute-start.16 = (f32[4096]{0:T(1024)S(1)}, f32[4096]{0:T(1024)S(1)}, u32[]{:S(2)}, u32[]{:S(2)}) collective-permute-start(f32[4096]{0:T(1024)S(1)} %add.92), channel_id=1, source_target_pairs={{0,64},{1,65},{4,68},{5,69},{8,72},{9,73},{12,76},{13,77},{16,80},... | collective-permute-start | bytes 49160 | tf_op jit(solution)/shard_map/ppermute | solution.py:236
  126.7 6.5 %collective-permute-start.17 = (f32[4096]{0:T(1024)S(1)}, f32[4096]{0:T(1024)S(1)}, u32[]{:S(2)}, u32[]{:S(2)}) collective-permute-start(f32[4096]{0:T(1024)S(1)} %add.93), channel_id=1, source_target_pairs={{0,128},{1,129},{4,132},{5,133},{8,136},{9,137},{12,140},{13,141},... | collective-permute-start | bytes 49160 | tf_op jit(solution)/shard_map/ppermute | solution.py:236
  133.2 3.2 %copy-start.6 = (bf16[8,896,256]{2,1,0:T(8,128)(2,1)S(1)}, bf16[8,896,256]{2,1,0:T(8,128)(2,1)}, u32[]{:S(2)}) copy-start(bf16[8,896,256]{2,1,0:T(8,128)(2,1)} %get-tuple-element.49) | copy-start | bytes 11010052
  139.1 15.2 %collective-permute-start.19 = (bf16[128,4096]{1,0:T(8,128)(2,1)S(1)}, bf16[128,4096]{1,0:T(8,128)(2,1)S(1)}, u32[]{:S(2)}, u32[]{:S(2)}) collective-permute-start(bf16[128,4096]{1,0:T(8,128)(2,1)S(1)} %get-tuple-element.53), channel_id=1, source_target_pairs={{0,4},{1,17},{4,8},{5,21},{8,12},{9,25},{12,0},{13,29},{16,20},{17... | collective-permute-start | bytes 3145736 | tf_op jit(solution)/shard_map/ppermute | solution.py:29
  139.2 15.1 %collective-permute-start.20 = (bf16[128,4096]{1,0:T(8,128)(2,1)}, bf16[128,4096]{1,0:T(8,128)(2,1)S(1)}, u32[]{:S(2)}, u32[]{:S(2)}) collective-permute-start(bf16[128,4096]{1,0:T(8,128)(2,1)} %get-tuple-element.54), channel_id=1, source_target_pairs={{0,12},{1,19},{4,0},{5,23},{8,4},{9,27},{12,8},{13,31},{16,28},{17... | collective-permute-start | bytes 3145736 | tf_op jit(solution)/shard_map/ppermute | solution.py:29
  141.9 23.5 %collective-permute-start.18 = (bf16[128,4096]{1,0:T(8,128)(2,1)}, bf16[128,4096]{1,0:T(8,128)(2,1)S(1)}, u32[]{:S(2)}, u32[]{:S(2)}) collective-permute-start(bf16[128,4096]{1,0:T(8,128)(2,1)} %add_convert_fusion.4), channel_id=1, source_target_pairs={{0,12},{1,19},{4,0},{5,23},{8,4},{9,27},{12,8},{13,31},{16,28},{17... | collective-permute-start | bytes 3145736 | tf_op jit(solution)/shard_map/ppermute | solution.py:29
  142.6 23.3 %collective-permute-start.21 = (bf16[128,4096]{1,0:T(8,128)(2,1)}, bf16[128,4096]{1,0:T(8,128)(2,1)S(1)}, u32[]{:S(2)}, u32[]{:S(2)}) collective-permute-start(bf16[128,4096]{1,0:T(8,128)(2,1)} %add_convert_fusion.3), channel_id=1, source_target_pairs={{0,4},{1,17},{4,8},{5,21},{8,12},{9,25},{12,0},{13,29},{16,20},{17... | collective-permute-start | bytes 3145736 | tf_op jit(solution)/shard_map/ppermute | solution.py:29
  143.3 3.1 %collective-permute-start.22 = (f32[4096]{0:T(1024)S(1)}, f32[4096]{0:T(1024)S(1)}, u32[]{:S(2)}, u32[]{:S(2)}) collective-permute-start(f32[4096]{0:T(1024)S(1)} %add.94), channel_id=1, source_target_pairs={{0,16},{1,5},{4,20},{5,1},{8,24},{9,13},{12,28},{13,9},{16,0},{17,... | collective-permute-start | bytes 49160 | tf_op jit(solution)/shard_map/ppermute | solution.py:236
  146.4 4.3 %collective-permute-start.23 = (f32[4096]{0:T(1024)S(1)}, f32[4096]{0:T(1024)S(1)}, u32[]{:S(2)}, u32[]{:S(2)}) collective-permute-start(f32[4096]{0:T(1024)S(1)} %add.95), channel_id=1, source_target_pairs={{0,2},{1,9},{4,6},{5,13},{8,10},{9,1},{12,14},{13,5},{16,18},{17,2... | collective-permute-start | bytes 49160 | tf_op jit(solution)/shard_map/ppermute | solution.py:236
  167.0 18.4 %collective-permute-start.26 = (bf16[2,32,4096]{2,1,0:T(8,128)(2,1)S(1)}, bf16[2,32,4096]{2,1,0:T(8,128)(2,1)S(1)}, u32[]{:S(2)}, u32[]{:S(2)}) collective-permute-start(bf16[2,32,4096]{2,1,0:T(8,128)(2,1)S(1)} %get-tuple-element.71), channel_id=1, source_target_pairs={{0,16},{1,5},{4,20},{5,9},{8,24},{9,13},{12,28},{13,1},{16,2},{17,... | collective-permute-start | bytes 1572872 | tf_op jit(solution)/shard_map/ppermute | solution.py:29
  167.0 18.3 %collective-permute-start.24 = (bf16[2,32,4096]{2,1,0:T(8,128)(2,1)S(1)}, bf16[2,32,4096]{2,1,0:T(8,128)(2,1)S(1)}, u32[]{:S(2)}, u32[]{:S(2)}) collective-permute-start(bf16[2,32,4096]{2,1,0:T(8,128)(2,1)S(1)} %get-tuple-element.72), channel_id=1, source_target_pairs={{0,18},{1,13},{4,22},{5,1},{8,26},{9,5},{12,30},{13,9},{16,0},{17,... | collective-permute-start | bytes 1572872 | tf_op jit(solution)/shard_map/ppermute | solution.py:29
  169.7 15.7 %collective-permute-start.25 = (bf16[2,32,4096]{2,1,0:T(8,128)(2,1)S(1)}, bf16[2,32,4096]{2,1,0:T(8,128)(2,1)}, u32[]{:S(2)}, u32[]{:S(2)}) collective-permute-start(bf16[2,32,4096]{2,1,0:T(8,128)(2,1)S(1)} %get-tuple-element.73), channel_id=1, source_target_pairs={{0,2},{1,9},{4,6},{5,13},{8,10},{9,1},{12,14},{13,5},{16,18},{17,2... | collective-permute-start | bytes 1572872 | tf_op jit(solution)/shard_map/ppermute | solution.py:29
  169.7 3.0 %collective-permute-start.27 = (f32[4096]{0:T(1024)S(1)}, f32[4096]{0:T(1024)S(1)}, u32[]{:S(2)}, u32[]{:S(2)}) collective-permute-start(f32[4096]{0:T(1024)S(1)} %add.96), channel_id=1, source_target_pairs={{0,4},{1,17},{4,0},{5,21},{8,12},{9,25},{12,8},{13,29},{16,20},{17... | collective-permute-start | bytes 49160 | tf_op jit(solution)/shard_map/ppermute | solution.py:236
  172.7 4.3 %collective-permute-start.28 = (f32[4096]{0:T(1024)S(1)}, f32[4096]{0:T(1024)S(1)}, u32[]{:S(2)}, u32[]{:S(2)}) collective-permute-start(f32[4096]{0:T(1024)S(1)} %add.101), channel_id=1, source_target_pairs={{0,8},{1,3},{4,12},{5,7},{8,0},{9,11},{12,4},{13,15},{16,24},{17,1... | collective-permute-start | bytes 49160 | tf_op jit(solution)/shard_map/ppermute | solution.py:236
  177.0 7.7 %collective-permute-start.29 = (f32[4096]{0:T(1024)S(1)}, f32[4096]{0:T(1024)S(1)}, u32[]{:S(2)}, u32[]{:S(2)}) collective-permute-start(f32[4096]{0:T(1024)S(1)} %add.102), channel_id=1, source_target_pairs={{0,1},{1,0},{4,5},{5,4},{8,9},{9,8},{12,13},{13,12},{16,17},{17,16... | collective-permute-start | bytes 49160 | tf_op jit(solution)/shard_map/ppermute | solution.py:236
  185.4 4.5 %copy-start.10 = (bf16[2,32,4096]{2,1,0:T(8,128)(2,1)}, bf16[2,32,4096]{2,1,0:T(8,128)(2,1)S(1)}, u32[]{:S(2)}) copy-start(bf16[2,32,4096]{2,1,0:T(8,128)(2,1)S(1)} %collective-permute-done.26) | copy-start | bytes 1572868
  185.4 4.5 %copy-start.11 = (bf16[2,32,4096]{2,1,0:T(8,128)(2,1)}, bf16[2,32,4096]{2,1,0:T(8,128)(2,1)S(1)}, u32[]{:S(2)}) copy-start(bf16[2,32,4096]{2,1,0:T(8,128)(2,1)S(1)} %collective-permute-done.24) | copy-start | bytes 1572868
  189.9 7.3 %copy-start.20 = (bf16[1,896,256]{2,1,0:T(8,128)(2,1)S(1)}, bf16[1,896,256]{2,1,0:T(8,128)(2,1)}, u32[]{:S(2)}) copy-start(bf16[1,896,256]{2,1,0:T(8,128)(2,1)} %reduce-scatter.2.cloned.1.call-done) | copy-start | bytes 1376260
  189.9 9.3 %copy-start.1 = (bf16[128,4096]{1,0:T(8,128)(2,1)S(1)}, bf16[128,4096]{1,0:T(8,128)(2,1)}, u32[]{:S(2)}) copy-start(bf16[128,4096]{1,0:T(8,128)(2,1)} %param.11) | copy-start | bytes 3145732
  189.9 9.3 %copy-start.5 = (bf16[31,4096]{1,0:T(8,128)(2,1)S(1)}, bf16[31,4096]{1,0:T(8,128)(2,1)}, u32[]{:S(2)}) copy-start(bf16[31,4096]{1,0:T(8,128)(2,1)} %copy-done.4) | copy-start | bytes 761860
  191.6 9.0 %copy-start.3 = (bf16[128,4096]{1,0:T(8,128)(2,1)S(1)}, bf16[128,4096]{1,0:T(8,128)(2,1)}, u32[]{:S(2)}) copy-start(bf16[128,4096]{1,0:T(8,128)(2,1)} %param.6) | copy-start | bytes 3145732
  191.9 8.7 %collective-permute-start.30 = (bf16[1,4096]{1,0:T(2,128)(2,1)S(1)}, bf16[1,4096]{1,0:T(2,128)(2,1)S(1)}, u32[]{:S(2)}, u32[]{:S(2)}) collective-permute-start(bf16[1,4096]{1,0:T(2,128)(2,1)S(1)} %slice.78), channel_id=1, source_target_pairs={{0,1},{1,2},{2,3},{3,4},{4,5},{5,6},{6,7},{7,8},{8,9},{9,10},{10,1... | collective-permute-start | bytes 24584 | tf_op jit(solution)/shard_map/ppermute | solution.py:47
  197.2 9.8 %collective-permute-start.31 = (bf16[896,256]{1,0:T(8,128)(2,1)S(1)}, bf16[896,256]{1,0:T(8,128)(2,1)S(1)}, u32[]{:S(2)}, u32[]{:S(2)}) collective-permute-start(bf16[896,256]{1,0:T(8,128)(2,1)S(1)} %bitcast.45), channel_id=1, source_target_pairs={{0,0},{1,16},{4,4},{5,20},{8,8},{9,24},{12,12},{13,28},{16,1},{17,... | collective-permute-start | bytes 1376264 | tf_op jit(solution)/shard_map/ppermute | solution.py:41
Sparse Core Ops, SparseCore 0:
  21.8 52.5 all-gather.2
  139.2 50.5 reduce-scatter.1

commit v11 on v10

--- a/solution.py
+++ b/solution.py
@@ -212,9 +212,10 @@
     bf = jnp.bfloat16
     d2, n2 = shift(d2, second=-1), shift(n2, second=1)
     n1, d3 = shift(n1, second=-1), shift(d3, second=1)
+    d2, n2, weight_part = lax.optimization_barrier((d2, n2, weight_part))
     d1, n3 = add_all([d1, d2]).astype(bf), add_all([n3, n2]).astype(bf)
     gain = pair(pair(pair(gain_part, z=1), z=2), z=4)
-    d1, n3, weight_part, gain = lax.optimization_barrier((d1, n3, weight_part, gain))
+    d1, n3, gain = lax.optimization_barrier((d1, n3, gain))
     weight_sum = lax.psum_scatter(weight_part, "z", scatter_dimension=0, tiled=False)
     d1, n3 = shift(d1, second=-1), shift(n3, second=1)
     gain = pair(pair(gain, first=1), first=2)

time: 216 us -> 220 us (1.019)
  other arithmetic: 13.3 us -> 15.9 us
    reduce_scatter x1, waiting for transfers between devices: 4.5 us -> 0.02 us  [scatter_plane(): lax.psum_scatter(weight_part, 'z', scatter_dimension=0, tiled=False)]
    ppermute x2, waiting for transfers between devices: 0.01 us -> 3.78 us  [other_core(): return lax.ppermute(value, AXES, pairs)]
    ppermute x18, waiting for transfers between devices: 68 us -> 71.2 us  [shift(): return lax.ppermute(value, AXES, pairs)]
  transfers between devices with their start and end apart: 34 -> 34, of which waited for: 23 -> 23; matrix products, arithmetic and copies ran while one was open for 4% -> 7% of each run, Pallas kernels for 0% -> 0%
where the time goes in v11:
time: 220 us
  waiting for transfers between devices  107 us (49%)
  starting transfers between devices  50.2 us (23%)
  Pallas kernels  20.6 us (9%)
  other arithmetic  15.9 us (7%)
  between operations  14.5 us (7%)
  local copies, waits for them, and re-layouts  8.27 us (4%)
  matrix products  3.44 us (2%)
    ppermute x18, waiting for transfers between devices, shift(): return lax.ppermute(value, AXES, pairs)  71.2 us
    pallas_call x1, Pallas kernels, block(): pl.pallas_call(functools.partial(block_kernel, chunks), out_shape=[jax.Sh...  20.6 us
    ppermute x18, starting transfers between devices, shift(): return lax.ppermute(value, AXES, pairs)  18.8 us
    ppermute x8, waiting for transfers between devices, pair(): return value + lax.ppermute(value, AXES, pairs)  17.6 us
    ppermute x8, starting transfers between devices, pair(): return value + lax.ppermute(value, AXES, pairs)  15.4 us
    ppermute x2, waiting for transfers between devices, swap_low(): return lax.ppermute(value, AXES, pairs)  10 us
    ppermute x2, starting transfers between devices, from_behind(): return lax.ppermute(value, AXES, pairs)  7.44 us
    unnamed x42, local copies, waits for them, and re-layouts  6.54 us
  transfers between devices with their start and end apart: 34, of which 23 were waited for; matrix products, arithmetic and copies ran while one was open for 7% of the time, Pallas kernels for 0%

profile of v11, /device:TPU:1, one launch (start us, length us, event | category | flops | bytes accessed | tf_op | source)
XLA Modules:
  0.0 219.8 jit_solution(1675259729476277999)
XLA Ops:
  7.2 0.9 dynamic_slice.3
  8.1 1.0 fusion.20
  9.1 1.0 pad_maximum_fusion.3
  10.1 4.6 %collective-permute-start.10 = (bf16[896,256]{1,0:T(8,128)(2,1)S(1)}, bf16[896,256]{1,0:T(8,128)(2,1)S(1)}, u32[]{:S(2)}, u32[]{:S(2)}) collective-permute-start(bf16[896,256]{1,0:T(8,128)(2,1)S(1)} %pad_maximum_fusion.3), channel_id=1, source_target_pairs={{0,0},{1,16},{4,4},{5,20},{8,8},{9,24},{12,12},{13,28},{16,1},{17,... | collective-permute-start | bytes 1376264 | tf_op jit(solution)/shard_map/ppermute | solution.py:41
  14.7 0.7 convert_subtract_fusion
  15.8 5.1 %collective-permute-done.10 = bf16[896,256]{1,0:T(8,128)(2,1)S(1)} collective-permute-done((bf16[896,256]{1,0:T(8,128)(2,1)S(1)}, bf16[896,256]{1,0:T(8,128)(2,1)S(1)}, u32[]{:S(2)}, u32[]{:S(2)}) %collective-permute-start.10) | collective-permute-done | bytes 458784 | tf_op jit(solution)/shard_map/ppermute | solution.py:41
  20.8 0.8 copy-done.12
  22.0 1.9 collective-permute-start
  24.3 4.3 %collective-permute-done = bf16[1,4096]{1,0:T(2,128)(2,1)S(1)} collective-permute-done((bf16[1,4096]{1,0:T(2,128)(2,1)S(1)}, bf16[1,4096]{1,0:T(2,128)(2,1)S(1)}, u32[]{:S(2)}, u32[]{:S(2)}) %collective-permute-start) | collective-permute-done | bytes 8224 | tf_op jit(solution)/shard_map/ppermute | solution.py:47
  28.7 2.6 %collective-permute-start.3 = (bf16[2,32,4096]{2,1,0:T(8,128)(2,1)S(1)}, bf16[2,32,4096]{2,1,0:T(8,128)(2,1)S(1)}, u32[]{:S(2)}, u32[]{:S(2)}) collective-permute-start(bf16[2,32,4096]{2,1,0:T(8,128)(2,1)S(1)} %pad_maximum_fusion.2), channel_id=1, source_target_pairs={{0,18},{1,13},{4,22},{5,1},{8,26},{9,5},{12,30},{13,9},{16,0},{17,... | collective-permute-start | bytes 1572872 | tf_op jit(solution)/shard_map/ppermute | solution.py:29
  31.8 0.6 collective-permute-start.1
  32.4 10.6 %collective-permute-done.3 = bf16[2,32,4096]{2,1,0:T(8,128)(2,1)S(1)} collective-permute-done((bf16[2,32,4096]{2,1,0:T(8,128)(2,1)S(1)}, bf16[2,32,4096]{2,1,0:T(8,128)(2,1)S(1)}, u32[]{:S(2)}, u32[]{:S(2)}) %collective-permute-start.3) | collective-permute-done | bytes 524320 | tf_op jit(solution)/shard_map/ppermute | solution.py:29
  43.1 3.7 %collective-permute-done.1 = bf16[2,32,4096]{2,1,0:T(8,128)(2,1)S(1)} collective-permute-done((bf16[2,32,4096]{2,1,0:T(8,128)(2,1)S(1)}, bf16[2,32,4096]{2,1,0:T(8,128)(2,1)S(1)}, u32[]{:S(2)}, u32[]{:S(2)}) %collective-permute-start.1) | collective-permute-done | bytes 524320 | tf_op jit(solution)/shard_map/ppermute | solution.py:29
  47.5 1.5 collective-permute-start.4
  48.9 1.7 collective-permute-start.6
  50.6 1.0 collective-permute-start.5
  51.6 9.9 %collective-permute-done.7.refs_3_ = bf16[128,4096]{1,0:T(8,128)(2,1)S(1)} collective-permute-done((bf16[128,4096]{1,0:T(8,128)(2,1)S(1)}, bf16[128,4096]{1,0:T(8,128)(2,1)S(1)}, u32[]{:S(2)}, u32[]{:S(2)}) %collective-permute-start.7) | collective-permute-done | bytes 1048608 | tf_op jit(solution)/shard_map/ppermute | solution.py:29
  61.5 2.2 %collective-permute-done.4.refs_1_ = bf16[128,4096]{1,0:T(8,128)(2,1)S(1)} collective-permute-done((bf16[128,4096]{1,0:T(8,128)(2,1)S(1)}, bf16[128,4096]{1,0:T(8,128)(2,1)S(1)}, u32[]{:S(2)}, u32[]{:S(2)}) %collective-permute-start.4) | collective-permute-done | bytes 1048608 | tf_op jit(solution)/shard_map/ppermute | solution.py:29
  63.7 11.1 %collective-permute-done.6.refs_5_ = bf16[128,4096]{1,0:T(8,128)(2,1)S(1)} collective-permute-done((bf16[128,4096]{1,0:T(8,128)(2,1)S(1)}, bf16[128,4096]{1,0:T(8,128)(2,1)S(1)}, u32[]{:S(2)}, u32[]{:S(2)}) %collective-permute-start.6) | collective-permute-done | bytes 1048608 | tf_op jit(solution)/shard_map/ppermute | solution.py:29
  74.9 1.0 copy-done.17
  75.9 1.2 collective-permute-start.11
  77.1 0.8 collective-permute-start.9
  77.9 0.7 collective-permute-start.8
  78.6 12.7 %collective-permute-done.9.refs_6_ = bf16[128,4096]{1,0:T(8,128)(2,1)S(1)} collective-permute-done((bf16[128,4096]{1,0:T(8,128)(2,1)}, bf16[128,4096]{1,0:T(8,128)(2,1)S(1)}, u32[]{:S(2)}, u32[]{:S(2)}) %collective-permute-start.9) | collective-permute-done | bytes 1048608 | tf_op jit(solution)/shard_map/ppermute | solution.py:29
  91.3 2.0 collective-permute-done.8.refs_2_
  93.3 0.9 copy-done.19
  94.3 1.9 copy-done.14
  96.1 20.6 %shard_map.101 = (bf16[128,4096]{1,0:T(8,128)(2,1)S(1)}, bf16[128,4096]{1,0:T(8,128)(2,1)S(1)}, bf16[128,4096]{1,0:T(8,128)(2,1)}, bf16[128,4096]{1,0:T(8,128)(2...) custom-call(bf16[128,4096]{1,0:T(8,128)(2,1)} %copy-done.9, ...), custom_call_target="tpu_custom_call" | custom-call | flops 11274289152 | bytes 62914560 | tf_op jit(solution)/shard_map/pallas_call | solution.py:168
  116.7 1.0 copy-done
  117.7 0.7 collective-permute-start.14
  118.4 2.5 %collective-permute-start.12 = (bf16[128,4096]{1,0:T(8,128)(2,1)}, bf16[128,4096]{1,0:T(8,128)(2,1)}, u32[]{:S(2)}, u32[]{:S(2)}) collective-permute-start(bf16[128,4096]{1,0:T(8,128)(2,1)} %get-tuple-element.48), channel_id=1, source_target_pairs={{0,12},{1,19},{4,0},{5,23},{8,4},{9,27},{12,8},{13,31},{16,28},{17... | collective-permute-start | bytes 3145736 | tf_op jit(solution)/shard_map/ppermute | solution.py:29
  120.8 3.8 %collective-permute-done.14 = bf16[8,896,256]{2,1,0:T(8,128)(2,1)S(1)} collective-permute-done((bf16[8,896,256]{2,1,0:T(8,128)(2,1)}, bf16[8,896,256]{2,1,0:T(8,128)(2,1)S(1)}, u32[]{:S(2)}, u32[]{:S(2)}) %collective-permute-start.14) | collective-permute-done | bytes 3670048 | tf_op jit(solution)/shard_map/ppermute | solution.py:34
  124.6 4.7 %add_convert_fusion = bf16[8,896,256]{2,1,0:T(8,128)(2,1)} fusion(bf16[8,896,256]{2,1,0:T(8,128)(2,1)S(1)} %collective-permute-done.14, bf16[8,896,256]{2,1,0:T(8,128)(2,1)} %get-tuple-element.50), kind=kLoop, calls=%fused_computation | loop fusion | flops 7340032 | bytes 11010048 | tf_op jit(solution)/shard_map/convert_element_type | solution.py:271
  129.3 3.6 %collective-permute-done.12 = bf16[128,4096]{1,0:T(8,128)(2,1)} collective-permute-done((bf16[128,4096]{1,0:T(8,128)(2,1)}, bf16[128,4096]{1,0:T(8,128)(2,1)}, u32[]{:S(2)}, u32[]{:S(2)}) %collective-permute-start.12) | collective-permute-done | bytes 1048608 | tf_op jit(solution)/shard_map/ppermute | solution.py:29
  132.9 3.2 %collective-permute-done.13 = bf16[128,4096]{1,0:T(8,128)(2,1)} collective-permute-done((bf16[128,4096]{1,0:T(8,128)(2,1)}, bf16[128,4096]{1,0:T(8,128)(2,1)}, u32[]{:S(2)}, u32[]{:S(2)}) %collective-permute-start.13) | collective-permute-done | bytes 1048608 | tf_op jit(solution)/shard_map/ppermute | solution.py:29
  136.3 2.6 %collective-permute-done.15 = f32[4096]{0:T(1024)S(1)} collective-permute-done((f32[4096]{0:T(1024)S(1)}, f32[4096]{0:T(1024)S(1)}, u32[]{:S(2)}, u32[]{:S(2)}) %collective-permute-start.15) | collective-permute-done | bytes 16416 | tf_op jit(solution)/shard_map/ppermute | solution.py:237
  138.9 1.5 collective-permute-start.16
  140.4 2.0 collective-permute-done.16
  142.3 5.0 %collective-permute-start.17 = (f32[4096]{0:T(1024)S(1)}, f32[4096]{0:T(1024)S(1)}, u32[]{:S(2)}, u32[]{:S(2)}) collective-permute-start(f32[4096]{0:T(1024)S(1)} %add.93), channel_id=1, source_target_pairs={{0,128},{1,129},{4,132},{5,133},{8,136},{9,137},{12,140},{13,141},... | collective-permute-start | bytes 49160 | tf_op jit(solution)/shard_map/ppermute | solution.py:237
  147.3 2.7 %collective-permute-start.20 = (bf16[128,4096]{1,0:T(8,128)(2,1)}, bf16[128,4096]{1,0:T(8,128)(2,1)S(1)}, u32[]{:S(2)}, u32[]{:S(2)}) collective-permute-start(bf16[128,4096]{1,0:T(8,128)(2,1)} %get-tuple-element.58), channel_id=1, source_target_pairs={{0,12},{1,19},{4,0},{5,23},{8,4},{9,27},{12,8},{13,31},{16,28},{17... | collective-permute-start | bytes 3145736 | tf_op jit(solution)/shard_map/ppermute | solution.py:29
  150.0 1.5 add_convert_fusion.4
  151.5 1.5 add_convert_fusion.3
  153.1 1.5 collective-permute-start.21
  154.7 3.1 %collective-permute-done.22 = f32[4096]{0:T(1024)S(1)} collective-permute-done((f32[4096]{0:T(1024)S(1)}, f32[4096]{0:T(1024)S(1)}, u32[]{:S(2)}, u32[]{:S(2)}) %collective-permute-start.22) | collective-permute-done | bytes 16416 | tf_op jit(solution)/shard_map/ppermute | solution.py:237
  157.9 4.2 %collective-permute-done.23 = f32[4096]{0:T(1024)S(1)} collective-permute-done((f32[4096]{0:T(1024)S(1)}, f32[4096]{0:T(1024)S(1)}, u32[]{:S(2)}, u32[]{:S(2)}) %collective-permute-start.23) | collective-permute-done | bytes 16416 | tf_op jit(solution)/shard_map/ppermute | solution.py:237
  162.1 0.7 collective-permute-done.19
  162.8 10.6 %collective-permute-done.18 = bf16[128,4096]{1,0:T(8,128)(2,1)S(1)} collective-permute-done((bf16[128,4096]{1,0:T(8,128)(2,1)S(1)}, bf16[128,4096]{1,0:T(8,128)(2,1)S(1)}, u32[]{:S(2)}, u32[]{:S(2)}) %collective-permute-start.18) | collective-permute-done | bytes 1048608 | tf_op jit(solution)/shard_map/ppermute | solution.py:29
  173.4 0.8 collective-permute-done.21
  175.5 2.5 %collective-permute-start.24 = (bf16[2,32,4096]{2,1,0:T(8,128)(2,1)S(1)}, bf16[2,32,4096]{2,1,0:T(8,128)(2,1)S(1)}, u32[]{:S(2)}, u32[]{:S(2)}) collective-permute-start(bf16[2,32,4096]{2,1,0:T(8,128)(2,1)S(1)} %get-tuple-element.76), channel_id=1, source_target_pairs={{0,18},{1,13},{4,22},{5,1},{8,26},{9,5},{12,30},{13,9},{16,0},{17,... | collective-permute-start | bytes 1572872 | tf_op jit(solution)/shard_map/ppermute | solution.py:29
  178.0 3.0 %collective-permute-done.27 = f32[4096]{0:T(1024)S(1)} collective-permute-done((f32[4096]{0:T(1024)S(1)}, f32[4096]{0:T(1024)S(1)}, u32[]{:S(2)}, u32[]{:S(2)}) %collective-permute-start.27) | collective-permute-done | bytes 16416 | tf_op jit(solution)/shard_map/ppermute | solution.py:237
  181.0 2.4 %collective-permute-start.28 = (f32[4096]{0:T(1024)S(1)}, f32[4096]{0:T(1024)S(1)}, u32[]{:S(2)}, u32[]{:S(2)}) collective-permute-start(f32[4096]{0:T(1024)S(1)} %add.101), channel_id=1, source_target_pairs={{0,8},{1,3},{4,12},{5,7},{8,0},{9,11},{12,4},{13,15},{16,24},{17,1... | collective-permute-start | bytes 49160 | tf_op jit(solution)/shard_map/ppermute | solution.py:237
  183.4 1.9 collective-permute-done.28
  185.4 6.2 %collective-permute-start.29 = (f32[4096]{0:T(1024)S(1)}, f32[4096]{0:T(1024)S(1)}, u32[]{:S(2)}, u32[]{:S(2)}) collective-permute-start(f32[4096]{0:T(1024)S(1)} %add.102), channel_id=1, source_target_pairs={{0,1},{1,0},{4,5},{5,4},{8,9},{9,8},{12,13},{13,12},{16,17},{17,16... | collective-permute-start | bytes 49160 | tf_op jit(solution)/shard_map/ppermute | solution.py:237
  191.6 0.8 collective-permute-done.29
  192.4 0.6 add.103
  193.1 0.7 copy-done.10
  194.0 1.7 convert_add_fusion
  196.0 5.5 %collective-permute-start.30 = (bf16[1,4096]{1,0:T(2,128)(2,1)S(1)}, bf16[1,4096]{1,0:T(2,128)(2,1)S(1)}, u32[]{:S(2)}, u32[]{:S(2)}) collective-permute-start(bf16[1,4096]{1,0:T(2,128)(2,1)S(1)} %slice.78), channel_id=1, source_target_pairs={{0,1},{1,2},{2,3},{3,4},{4,5},{5,6},{6,7},{7,8},{8,9},{9,10},{10,1... | collective-permute-start | bytes 24584 | tf_op jit(solution)/shard_map/ppermute | solution.py:47
  201.5 1.9 collective-permute-start.31
  203.5 1.5 fusion.1
  205.0 1.4 fusion
  206.4 4.9 %collective-permute-done.31 = bf16[896,256]{1,0:T(8,128)(2,1)S(1)} collective-permute-done((bf16[896,256]{1,0:T(8,128)(2,1)S(1)}, bf16[896,256]{1,0:T(8,128)(2,1)S(1)}, u32[]{:S(2)}, u32[]{:S(2)}) %collective-permute-start.31) | collective-permute-done | bytes 458784 | tf_op jit(solution)/shard_map/ppermute | solution.py:41
  211.3 0.8 multiply_bitcast_fusion
  212.1 0.8 slice_convert_fusion
  (93 shorter events, 4.8 us)
Async XLA Ops:
  7.2 14.6 %copy-start.1 = (bf16[128,4096]{1,0:T(8,128)(2,1)S(1)}, bf16[128,4096]{1,0:T(8,128)(2,1)}, u32[]{:S(2)}) copy-start(bf16[128,4096]{1,0:T(8,128)(2,1)} %param.11) | copy-start | bytes 3145732
  7.2 16.8 %copy-start.3 = (bf16[128,4096]{1,0:T(8,128)(2,1)S(1)}, bf16[128,4096]{1,0:T(8,128)(2,1)}, u32[]{:S(2)}) copy-start(bf16[128,4096]{1,0:T(8,128)(2,1)} %param.6) | copy-start | bytes 3145732
  7.2 68.7 %all-gather.3.cloned.1.call-start = ((), (), s32[]{:S(2)}) async-start(), calls=%async_computation.2 | async-start | bytes 4128768 | tf_op jit(solution)/shard_map/all_gather | solution.py:251
  10.1 10.8 %collective-permute-start.10 = (bf16[896,256]{1,0:T(8,128)(2,1)S(1)}, bf16[896,256]{1,0:T(8,128)(2,1)S(1)}, u32[]{:S(2)}, u32[]{:S(2)}) collective-permute-start(bf16[896,256]{1,0:T(8,128)(2,1)S(1)} %pad_maximum_fusion.3), channel_id=1, source_target_pairs={{0,0},{1,16},{4,4},{5,20},{8,8},{9,24},{12,12},{13,28},{16,1},{17,... | collective-permute-start | bytes 1376264 | tf_op jit(solution)/shard_map/ppermute | solution.py:41
  20.8 0.8 copy-start.12
  21.6 171.4 %reduce-scatter.2.cloned.1.call-start = ((), (), s32[]{:S(2)}) async-start(), calls=%async_computation.1 | async-start | bytes 4128768 | tf_op jit(solution)/shard_map/reduce_scatter | solution.py:219
  22.0 6.6 %collective-permute-start = (bf16[1,4096]{1,0:T(2,128)(2,1)S(1)}, bf16[1,4096]{1,0:T(2,128)(2,1)S(1)}, u32[]{:S(2)}, u32[]{:S(2)}) collective-permute-start(bf16[1,4096]{1,0:T(2,128)(2,1)S(1)} %slice.65), channel_id=1, source_target_pairs={{1,0},{2,1},{3,2},{4,3},{5,4},{6,5},{7,6},{8,7},{9,8},{10,9},{11,1... | collective-permute-start | bytes 24584 | tf_op jit(solution)/shard_map/ppermute | solution.py:47
  24.3 22.5 %copy-start.5 = (bf16[31,4096]{1,0:T(8,128)(2,1)}, bf16[31,4096]{1,0:T(8,128)(2,1)S(1)}, u32[]{:S(2)}) copy-start(bf16[31,4096]{1,0:T(8,128)(2,1)S(1)} %slice.64) | copy-start | bytes 761860
  28.7 14.3 %collective-permute-start.3 = (bf16[2,32,4096]{2,1,0:T(8,128)(2,1)S(1)}, bf16[2,32,4096]{2,1,0:T(8,128)(2,1)S(1)}, u32[]{:S(2)}, u32[]{:S(2)}) collective-permute-start(bf16[2,32,4096]{2,1,0:T(8,128)(2,1)S(1)} %pad_maximum_fusion.2), channel_id=1, source_target_pairs={{0,18},{1,13},{4,22},{5,1},{8,26},{9,5},{12,30},{13,9},{16,0},{17,... | collective-permute-start | bytes 1572872 | tf_op jit(solution)/shard_map/ppermute | solution.py:29
  31.2 11.8 %collective-permute-start.2 = (bf16[2,32,4096]{2,1,0:T(8,128)(2,1)S(1)}, bf16[2,32,4096]{2,1,0:T(8,128)(2,1)S(1)}, u32[]{:S(2)}, u32[]{:S(2)}) collective-permute-start(bf16[2,32,4096]{2,1,0:T(8,128)(2,1)S(1)} %pad_maximum_fusion.2), channel_id=1, source_target_pairs={{0,2},{1,9},{4,6},{5,13},{8,10},{9,1},{12,14},{13,5},{16,18},{17,2... | collective-permute-start | bytes 1572872 | tf_op jit(solution)/shard_map/ppermute | solution.py:29
  31.8 15.0 %collective-permute-start.1 = (bf16[2,32,4096]{2,1,0:T(8,128)(2,1)S(1)}, bf16[2,32,4096]{2,1,0:T(8,128)(2,1)S(1)}, u32[]{:S(2)}, u32[]{:S(2)}) collective-permute-start(bf16[2,32,4096]{2,1,0:T(8,128)(2,1)S(1)} %pad_maximum_fusion.2), channel_id=1, source_target_pairs={{0,16},{1,5},{4,20},{5,9},{8,24},{9,13},{12,28},{13,1},{16,2},{17,... | collective-permute-start | bytes 1572872 | tf_op jit(solution)/shard_map/ppermute | solution.py:29
  47.3 46.0 %copy-start.8 = (bf16[128,4096]{1,0:T(8,128)(2,1)}, bf16[128,4096]{1,0:T(8,128)(2,1)S(1)}, u32[]{:S(2)}) copy-start(bf16[128,4096]{1,0:T(8,128)(2,1)S(1)} %concatenate.18.refs_4_) | copy-start | bytes 3145732
  47.4 45.9 %copy-start.9 = (bf16[128,4096]{1,0:T(8,128)(2,1)}, bf16[128,4096]{1,0:T(8,128)(2,1)S(1)}, u32[]{:S(2)}) copy-start(bf16[128,4096]{1,0:T(8,128)(2,1)S(1)} %pad_maximum_fusion.refs_0_) | copy-start | bytes 3145732
  47.4 14.1 %collective-permute-start.7 = (bf16[128,4096]{1,0:T(8,128)(2,1)S(1)}, bf16[128,4096]{1,0:T(8,128)(2,1)S(1)}, u32[]{:S(2)}, u32[]{:S(2)}) collective-permute-start(bf16[128,4096]{1,0:T(8,128)(2,1)S(1)} %pad_maximum_fusion.refs_0_), channel_id=1, source_target_pairs={{0,12},{1,19},{4,0},{5,23},{8,4},{9,27},{12,8},{13,31},{16,28},{17... | collective-permute-start | bytes 3145736 | tf_op jit(solution)/shard_map/ppermute | solution.py:29
  47.5 16.3 %collective-permute-start.4 = (bf16[128,4096]{1,0:T(8,128)(2,1)S(1)}, bf16[128,4096]{1,0:T(8,128)(2,1)S(1)}, u32[]{:S(2)}, u32[]{:S(2)}) collective-permute-start(bf16[128,4096]{1,0:T(8,128)(2,1)S(1)} %pad_maximum_fusion.refs_0_), channel_id=1, source_target_pairs={{0,4},{1,17},{4,8},{5,21},{8,12},{9,25},{12,0},{13,29},{16,20},{17... | collective-permute-start | bytes 3145736 | tf_op jit(solution)/shard_map/ppermute | solution.py:29
  48.9 25.9 %collective-permute-start.6 = (bf16[128,4096]{1,0:T(8,128)(2,1)S(1)}, bf16[128,4096]{1,0:T(8,128)(2,1)S(1)}, u32[]{:S(2)}, u32[]{:S(2)}) collective-permute-start(bf16[128,4096]{1,0:T(8,128)(2,1)S(1)} %concatenate.18.refs_4_), channel_id=1, source_target_pairs={{0,4},{1,17},{4,8},{5,21},{8,12},{9,25},{12,0},{13,29},{16,20},{17... | collective-permute-start | bytes 3145736 | tf_op jit(solution)/shard_map/ppermute | solution.py:29
  50.6 25.2 %collective-permute-start.5 = (bf16[128,4096]{1,0:T(8,128)(2,1)S(1)}, bf16[128,4096]{1,0:T(8,128)(2,1)}, u32[]{:S(2)}, u32[]{:S(2)}) collective-permute-start(bf16[128,4096]{1,0:T(8,128)(2,1)S(1)} %concatenate.18.refs_4_), channel_id=1, source_target_pairs={{0,12},{1,19},{4,0},{5,23},{8,4},{9,27},{12,8},{13,31},{16,28},{17... | collective-permute-start | bytes 3145736 | tf_op jit(solution)/shard_map/ppermute | solution.py:29
  61.5 31.8 %copy-start.15 = (bf16[128,4096]{1,0:T(8,128)(2,1)}, bf16[128,4096]{1,0:T(8,128)(2,1)S(1)}, u32[]{:S(2)}) copy-start(bf16[128,4096]{1,0:T(8,128)(2,1)S(1)} %collective-permute-done.7.refs_3_) | copy-start | bytes 3145732
  63.7 11.1 %copy-start.16 = (bf16[128,4096]{1,0:T(8,128)(2,1)}, bf16[128,4096]{1,0:T(8,128)(2,1)S(1)}, u32[]{:S(2)}) copy-start(bf16[128,4096]{1,0:T(8,128)(2,1)S(1)} %collective-permute-done.4.refs_1_) | copy-start | bytes 3145732
  74.9 1.0 copy-start.17
  75.9 17.4 %collective-permute-start.11 = (bf16[8,896,256]{2,1,0:T(8,128)(2,1)}, bf16[8,896,256]{2,1,0:T(8,128)(2,1)S(1)}, u32[]{:S(2)}, u32[]{:S(2)}) collective-permute-start(bf16[8,896,256]{2,1,0:T(8,128)(2,1)} %bitcast.43), channel_id=1, source_target_pairs={{0,1},{1,0},{4,5},{5,4},{8,9},{9,8},{12,13},{13,12},{16,17},{17,16... | collective-permute-start | bytes 11010056 | tf_op jit(solution)/shard_map/ppermute | solution.py:34
  77.1 14.2 %collective-permute-start.9 = (bf16[128,4096]{1,0:T(8,128)(2,1)}, bf16[128,4096]{1,0:T(8,128)(2,1)S(1)}, u32[]{:S(2)}, u32[]{:S(2)}) collective-permute-start(bf16[128,4096]{1,0:T(8,128)(2,1)} %collective-permute-done.5.refs_7_), channel_id=1, source_target_pairs={{0,12},{1,19},{4,0},{5,23},{8,4},{9,27},{12,8},{13,31},{16,28},{17... | collective-permute-start | bytes 3145736 | tf_op jit(solution)/shard_map/ppermute | solution.py:29
  77.9 15.4 %collective-permute-start.8 = (bf16[128,4096]{1,0:T(8,128)(2,1)}, bf16[128,4096]{1,0:T(8,128)(2,1)S(1)}, u32[]{:S(2)}, u32[]{:S(2)}) collective-permute-start(bf16[128,4096]{1,0:T(8,128)(2,1)} %copy-done.16), channel_id=1, source_target_pairs={{0,4},{1,17},{4,8},{5,21},{8,12},{9,25},{12,0},{13,29},{16,20},{17... | collective-permute-start | bytes 3145736 | tf_op jit(solution)/shard_map/ppermute | solution.py:29
  91.3 2.1 copy-start.18
  93.3 1.0 copy-start.19
  94.3 1.9 copy-start.14
  116.7 1.0 copy-start
  117.7 6.9 %collective-permute-start.14 = (bf16[8,896,256]{2,1,0:T(8,128)(2,1)}, bf16[8,896,256]{2,1,0:T(8,128)(2,1)S(1)}, u32[]{:S(2)}, u32[]{:S(2)}) collective-permute-start(bf16[8,896,256]{2,1,0:T(8,128)(2,1)} %get-tuple-element.51), channel_id=1, source_target_pairs={{0,1},{1,0},{4,5},{5,4},{8,9},{9,8},{12,13},{13,12},{16,17},{17,16... | collective-permute-start | bytes 11010056 | tf_op jit(solution)/shard_map/ppermute | solution.py:34
  118.4 14.5 %collective-permute-start.12 = (bf16[128,4096]{1,0:T(8,128)(2,1)}, bf16[128,4096]{1,0:T(8,128)(2,1)}, u32[]{:S(2)}, u32[]{:S(2)}) collective-permute-start(bf16[128,4096]{1,0:T(8,128)(2,1)} %get-tuple-element.48), channel_id=1, source_target_pairs={{0,12},{1,19},{4,0},{5,23},{8,4},{9,27},{12,8},{13,31},{16,28},{17... | collective-permute-start | bytes 3145736 | tf_op jit(solution)/shard_map/ppermute | solution.py:29
  120.8 15.3 %collective-permute-start.13 = (bf16[128,4096]{1,0:T(8,128)(2,1)}, bf16[128,4096]{1,0:T(8,128)(2,1)}, u32[]{:S(2)}, u32[]{:S(2)}) collective-permute-start(bf16[128,4096]{1,0:T(8,128)(2,1)} %get-tuple-element.49), channel_id=1, source_target_pairs={{0,4},{1,17},{4,8},{5,21},{8,12},{9,25},{12,0},{13,29},{16,20},{17... | collective-permute-start | bytes 3145736 | tf_op jit(solution)/shard_map/ppermute | solution.py:29
  129.3 6.8 %copy-start.13 = (f32[4096]{0:T(1024)S(1)}, f32[4096]{0:T(1024)}, u32[]{:S(2)}) copy-start(f32[4096]{0:T(1024)} %param.8) | copy-start | bytes 49156
  136.1 15.4 %copy-start.7 = (bf16[128,4096]{1,0:T(8,128)(2,1)S(1)}, bf16[128,4096]{1,0:T(8,128)(2,1)}, u32[]{:S(2)}) copy-start(bf16[128,4096]{1,0:T(8,128)(2,1)} %get-tuple-element.53) | copy-start | bytes 3145732
  136.2 2.7 %collective-permute-start.15 = (f32[4096]{0:T(1024)S(1)}, f32[4096]{0:T(1024)S(1)}, u32[]{:S(2)}, u32[]{:S(2)}) collective-permute-start(f32[4096]{0:T(1024)S(1)} %div.35), channel_id=1, source_target_pairs={{0,32},{1,33},{4,36},{5,37},{8,40},{9,41},{12,44},{13,45},{16,48},... | collective-permute-start | bytes 49160 | tf_op jit(solution)/shard_map/ppermute | solution.py:237
  138.9 3.5 %collective-permute-start.16 = (f32[4096]{0:T(1024)S(1)}, f32[4096]{0:T(1024)S(1)}, u32[]{:S(2)}, u32[]{:S(2)}) collective-permute-start(f32[4096]{0:T(1024)S(1)} %add.92), channel_id=1, source_target_pairs={{0,64},{1,65},{4,68},{5,69},{8,72},{9,73},{12,76},{13,77},{16,80},... | collective-permute-start | bytes 49160 | tf_op jit(solution)/shard_map/ppermute | solution.py:237
  142.3 7.7 %collective-permute-start.17 = (f32[4096]{0:T(1024)S(1)}, f32[4096]{0:T(1024)S(1)}, u32[]{:S(2)}, u32[]{:S(2)}) collective-permute-start(f32[4096]{0:T(1024)S(1)} %add.93), channel_id=1, source_target_pairs={{0,128},{1,129},{4,132},{5,133},{8,136},{9,137},{12,140},{13,141},... | collective-permute-start | bytes 49160 | tf_op jit(solution)/shard_map/ppermute | solution.py:237
  147.3 15.5 %collective-permute-start.19 = (bf16[128,4096]{1,0:T(8,128)(2,1)}, bf16[128,4096]{1,0:T(8,128)(2,1)S(1)}, u32[]{:S(2)}, u32[]{:S(2)}) collective-permute-start(bf16[128,4096]{1,0:T(8,128)(2,1)} %copy-done), channel_id=1, source_target_pairs={{0,4},{1,17},{4,8},{5,21},{8,12},{9,25},{12,0},{13,29},{16,20},{17... | collective-permute-start | bytes 3145736 | tf_op jit(solution)/shard_map/ppermute | solution.py:29
  147.3 15.5 %collective-permute-start.20 = (bf16[128,4096]{1,0:T(8,128)(2,1)}, bf16[128,4096]{1,0:T(8,128)(2,1)S(1)}, u32[]{:S(2)}, u32[]{:S(2)}) collective-permute-start(bf16[128,4096]{1,0:T(8,128)(2,1)} %get-tuple-element.58), channel_id=1, source_target_pairs={{0,12},{1,19},{4,0},{5,23},{8,4},{9,27},{12,8},{13,31},{16,28},{17... | collective-permute-start | bytes 3145736 | tf_op jit(solution)/shard_map/ppermute | solution.py:29
  153.0 20.4 %collective-permute-start.18 = (bf16[128,4096]{1,0:T(8,128)(2,1)S(1)}, bf16[128,4096]{1,0:T(8,128)(2,1)S(1)}, u32[]{:S(2)}, u32[]{:S(2)}) collective-permute-start(bf16[128,4096]{1,0:T(8,128)(2,1)S(1)} %add_convert_fusion.4), channel_id=1, source_target_pairs={{0,12},{1,19},{4,0},{5,23},{8,4},{9,27},{12,8},{13,31},{16,28},{17... | collective-permute-start | bytes 3145736 | tf_op jit(solution)/shard_map/ppermute | solution.py:29
  153.1 21.1 %collective-permute-start.21 = (bf16[128,4096]{1,0:T(8,128)(2,1)S(1)}, bf16[128,4096]{1,0:T(8,128)(2,1)S(1)}, u32[]{:S(2)}, u32[]{:S(2)}) collective-permute-start(bf16[128,4096]{1,0:T(8,128)(2,1)S(1)} %add_convert_fusion.3), channel_id=1, source_target_pairs={{0,4},{1,17},{4,8},{5,21},{8,12},{9,25},{12,0},{13,29},{16,20},{17... | collective-permute-start | bytes 3145736 | tf_op jit(solution)/shard_map/ppermute | solution.py:29
  154.5 3.2 %collective-permute-start.22 = (f32[4096]{0:T(1024)S(1)}, f32[4096]{0:T(1024)S(1)}, u32[]{:S(2)}, u32[]{:S(2)}) collective-permute-start(f32[4096]{0:T(1024)S(1)} %add.94), channel_id=1, source_target_pairs={{0,16},{1,5},{4,20},{5,1},{8,24},{9,13},{12,28},{13,9},{16,0},{17,... | collective-permute-start | bytes 49160 | tf_op jit(solution)/shard_map/ppermute | solution.py:237
  157.8 4.3 %collective-permute-start.23 = (f32[4096]{0:T(1024)S(1)}, f32[4096]{0:T(1024)S(1)}, u32[]{:S(2)}, u32[]{:S(2)}) collective-permute-start(f32[4096]{0:T(1024)S(1)} %add.95), channel_id=1, source_target_pairs={{0,2},{1,9},{4,6},{5,13},{8,10},{9,1},{12,14},{13,5},{16,18},{17,2... | collective-permute-start | bytes 49160 | tf_op jit(solution)/shard_map/ppermute | solution.py:237
  175.3 17.7 %collective-permute-start.26 = (bf16[2,32,4096]{2,1,0:T(8,128)(2,1)S(1)}, bf16[2,32,4096]{2,1,0:T(8,128)(2,1)S(1)}, u32[]{:S(2)}, u32[]{:S(2)}) collective-permute-start(bf16[2,32,4096]{2,1,0:T(8,128)(2,1)S(1)} %get-tuple-element.75), channel_id=1, source_target_pairs={{0,16},{1,5},{4,20},{5,9},{8,24},{9,13},{12,28},{13,1},{16,2},{17,... | collective-permute-start | bytes 1572872 | tf_op jit(solution)/shard_map/ppermute | solution.py:29
  175.5 17.5 %collective-permute-start.24 = (bf16[2,32,4096]{2,1,0:T(8,128)(2,1)S(1)}, bf16[2,32,4096]{2,1,0:T(8,128)(2,1)S(1)}, u32[]{:S(2)}, u32[]{:S(2)}) collective-permute-start(bf16[2,32,4096]{2,1,0:T(8,128)(2,1)S(1)} %get-tuple-element.76), channel_id=1, source_target_pairs={{0,18},{1,13},{4,22},{5,1},{8,26},{9,5},{12,30},{13,9},{16,0},{17,... | collective-permute-start | bytes 1572872 | tf_op jit(solution)/shard_map/ppermute | solution.py:29
  178.0 15.0 %collective-permute-start.25 = (bf16[2,32,4096]{2,1,0:T(8,128)(2,1)S(1)}, bf16[2,32,4096]{2,1,0:T(8,128)(2,1)}, u32[]{:S(2)}, u32[]{:S(2)}) collective-permute-start(bf16[2,32,4096]{2,1,0:T(8,128)(2,1)S(1)} %get-tuple-element.77), channel_id=1, source_target_pairs={{0,2},{1,9},{4,6},{5,13},{8,10},{9,1},{12,14},{13,5},{16,18},{17,2... | collective-permute-start | bytes 1572872 | tf_op jit(solution)/shard_map/ppermute | solution.py:29
  178.0 3.0 %collective-permute-start.27 = (f32[4096]{0:T(1024)S(1)}, f32[4096]{0:T(1024)S(1)}, u32[]{:S(2)}, u32[]{:S(2)}) collective-permute-start(f32[4096]{0:T(1024)S(1)} %add.96), channel_id=1, source_target_pairs={{0,4},{1,17},{4,0},{5,21},{8,12},{9,25},{12,8},{13,29},{16,20},{17... | collective-permute-start | bytes 49160 | tf_op jit(solution)/shard_map/ppermute | solution.py:237
  181.0 4.3 %collective-permute-start.28 = (f32[4096]{0:T(1024)S(1)}, f32[4096]{0:T(1024)S(1)}, u32[]{:S(2)}, u32[]{:S(2)}) collective-permute-start(f32[4096]{0:T(1024)S(1)} %add.101), channel_id=1, source_target_pairs={{0,8},{1,3},{4,12},{5,7},{8,0},{9,11},{12,4},{13,15},{16,24},{17,1... | collective-permute-start | bytes 49160 | tf_op jit(solution)/shard_map/ppermute | solution.py:237
  185.4 7.0 %collective-permute-start.29 = (f32[4096]{0:T(1024)S(1)}, f32[4096]{0:T(1024)S(1)}, u32[]{:S(2)}, u32[]{:S(2)}) collective-permute-start(f32[4096]{0:T(1024)S(1)} %add.102), channel_id=1, source_target_pairs={{0,1},{1,0},{4,5},{5,4},{8,9},{9,8},{12,13},{13,12},{16,17},{17,16... | collective-permute-start | bytes 49160 | tf_op jit(solution)/shard_map/ppermute | solution.py:237
  193.0 0.8 copy-start.10
  193.0 1.0 copy-start.11
  194.0 7.6 %copy-start.20 = (bf16[1,896,256]{2,1,0:T(8,128)(2,1)S(1)}, bf16[1,896,256]{2,1,0:T(8,128)(2,1)}, u32[]{:S(2)}) copy-start(bf16[1,896,256]{2,1,0:T(8,128)(2,1)} %reduce-scatter.2.cloned.1.call-done) | copy-start | bytes 1376260
  194.0 9.5 %copy-start.2 = (bf16[128,4096]{1,0:T(8,128)(2,1)S(1)}, bf16[128,4096]{1,0:T(8,128)(2,1)}, u32[]{:S(2)}) copy-start(bf16[128,4096]{1,0:T(8,128)(2,1)} %param.11) | copy-start | bytes 3145732
  194.0 9.5 %copy-start.6 = (bf16[31,4096]{1,0:T(8,128)(2,1)S(1)}, bf16[31,4096]{1,0:T(8,128)(2,1)}, u32[]{:S(2)}) copy-start(bf16[31,4096]{1,0:T(8,128)(2,1)} %copy-done.5) | copy-start | bytes 761860
  195.7 9.3 %copy-start.4 = (bf16[128,4096]{1,0:T(8,128)(2,1)S(1)}, bf16[128,4096]{1,0:T(8,128)(2,1)}, u32[]{:S(2)}) copy-start(bf16[128,4096]{1,0:T(8,128)(2,1)} %param.6) | copy-start | bytes 3145732
  196.0 9.0 %collective-permute-start.30 = (bf16[1,4096]{1,0:T(2,128)(2,1)S(1)}, bf16[1,4096]{1,0:T(2,128)(2,1)S(1)}, u32[]{:S(2)}, u32[]{:S(2)}) collective-permute-start(bf16[1,4096]{1,0:T(2,128)(2,1)S(1)} %slice.78), channel_id=1, source_target_pairs={{0,1},{1,2},{2,3},{3,4},{4,5},{5,6},{6,7},{7,8},{8,9},{9,10},{10,1... | collective-permute-start | bytes 24584 | tf_op jit(solution)/shard_map/ppermute | solution.py:47
  201.5 9.8 %collective-permute-start.31 = (bf16[896,256]{1,0:T(8,128)(2,1)S(1)}, bf16[896,256]{1,0:T(8,128)(2,1)S(1)}, u32[]{:S(2)}, u32[]{:S(2)}) collective-permute-start(bf16[896,256]{1,0:T(8,128)(2,1)S(1)} %bitcast.45), channel_id=1, source_target_pairs={{0,0},{1,16},{4,4},{5,20},{8,8},{9,24},{12,12},{13,28},{16,1},{17,... | collective-permute-start | bytes 1376264 | tf_op jit(solution)/shard_map/ppermute | solution.py:41
Sparse Core Ops, SparseCore 0:
  21.8 52.5 all-gather.2
  136.3 48.1 reduce-scatter.1
